TPU v7x, 32 devices: a whole 2x2x4 slice. The times are simulated.
32 devices in a mesh: wide: 8 (over y, x, core), narrow: 4 (over z).
Axes of the slice: x: 2, y: 2, z: 4, core: 2. Of those that a mesh axis runs over, the one named last changes fastest.
Arguments:
- density: float32 [256, 256, 256], P('wide', 'narrow'), may hold values from -48 to 48
Outputs:
- recon_real: float32 [256, 256, 256], P('narrow', 'wide')
- recon_imag: float32 [256, 256, 256], P('narrow', 'wide')
All inputs are finite; a program needn't handle non-finite values.
Results may differ from a plain program's by a relative error of at most 0.0003.
Values sent between devices are 32-bit elements; how exact they have to be, the bound alone decides.
No kernel may reach another device: no remote copies, remote signals or barrier semaphores. Data moves between devices by JAX's collectives and lax.ppermute only.
A program may use at most 192 MiB of HBM per device.

v0:
```python
from functools import partial
import math

import jax
import jax.numpy as jnp
from jax import lax
from jax.sharding import PartitionSpec as P


def tables(length):
    indices = jnp.arange(length, dtype=jnp.int32)
    products = indices[:, None] * indices[None, :] % length
    angles = products.astype(jnp.float32) * (2.0 * math.pi / length)
    return (jnp.cos(angles), jnp.sin(angles))


def transform(parts_in, position, inverse, pattern_last=False):
    real_part, imag_part = parts_in
    length = real_part.shape[position]
    cosine, sine = tables(length)
    if position == 1:
        pattern = "fabc,ad->fcbd" if pattern_last else "fabc,ad->fdbc"
    elif position == 2:
        pattern = "fabc,bd->fadc"
    else:
        pattern = "fabc,cd->fabd"
    contract = partial(
        jnp.einsum, pattern, precision=lax.Precision.HIGHEST, preferred_element_type=jnp.float32
    )
    real_cos = contract(real_part, cosine)
    real_sin = contract(real_part, sine)
    imag_cos = contract(imag_part, cosine)
    imag_sin = contract(imag_part, sine)
    if inverse:
        scale = 1.0 / length
        return ((real_cos - imag_sin) * scale, (imag_cos + real_sin) * scale)
    return (real_cos + imag_sin, imag_cos - real_sin)


def pass_second(parts_in):
    return transform(parts_in, 2, False)


def pass_first(parts_in):
    return transform(parts_in, 1, False)


def pass_first_last(parts_in):
    return transform(parts_in, 1, False, True)


def back_second(parts_in):
    return transform(parts_in, 2, True)


def back_third(parts_in):
    return transform(parts_in, 3, True)


def forward(real_part, imag_part, first_last):
    section = transform((real_part, imag_part), 3, False)
    section = pass_second(
        (
            lax.all_to_all(section[0], "narrow", split_axis=3, concat_axis=2, tiled=True),
            lax.all_to_all(section[1], "narrow", split_axis=3, concat_axis=2, tiled=True),
        )
    )
    final_pass = pass_first_last if first_last else pass_first
    section = final_pass(
        (
            lax.all_to_all(section[0], "wide", split_axis=2, concat_axis=1, tiled=True),
            lax.all_to_all(section[1], "wide", split_axis=2, concat_axis=1, tiled=True),
        )
    )
    return section


def inverse(real_part, imag_part):
    section = transform((real_part, imag_part), 1, True)
    section = back_second(
        (
            lax.all_to_all(section[0], "wide", split_axis=1, concat_axis=2, tiled=True),
            lax.all_to_all(section[1], "wide", split_axis=1, concat_axis=2, tiled=True),
        )
    )
    section = back_third(
        (
            lax.all_to_all(section[0], "narrow", split_axis=2, concat_axis=3, tiled=True),
            lax.all_to_all(section[1], "narrow", split_axis=2, concat_axis=3, tiled=True),
        )
    )
    return section


def wavenumbers(length, offset, count):
    indices = offset + jnp.arange(count, dtype=jnp.int32)
    signed = jnp.where(indices < length // 2, indices, indices - length)
    wave = signed.astype(jnp.float32) * (2.0 * math.pi / length)
    return (wave, indices != length // 2, indices == 0)


def per_device(density):
    length = density.shape[2]
    zeros_in = jnp.zeros((1,) + density.shape, jnp.float32)
    spec_real, spec_imag = forward(density[None], zeros_in, False)
    spec_real = spec_real[0]
    spec_imag = spec_imag[0]
    rows_y = spec_real.shape[1]
    rows_z = spec_real.shape[2]
    wave_x, usable_x, anchor_x = wavenumbers(length, 0, length)
    wave_y, usable_y, anchor_y = wavenumbers(length, lax.axis_index("wide") * rows_y, rows_y)
    wave_z, usable_z, anchor_z = wavenumbers(length, lax.axis_index("narrow") * rows_z, rows_z)
    wave_x = wave_x[:, None, None]
    wave_y = wave_y[None, :, None]
    wave_z = wave_z[None, None, :]
    squared = wave_x * wave_x + wave_y * wave_y + wave_z * wave_z
    keep = (
        usable_x[:, None, None] & usable_y[None, :, None] & usable_z[None, None, :] & (squared > 0)
    )
    squared_safe = jnp.where(squared > 0, squared, jnp.ones_like(squared))
    smooth_kernel = jnp.where(keep, jnp.exp(-0.5 * squared) / squared_safe, jnp.zeros_like(squared))
    waves = [wave_x, wave_y, wave_z]
    pairs = [(0, 0), (1, 1), (2, 2), (0, 1), (0, 2), (1, 2)]
    kernels = [smooth_kernel * waves[first] * waves[second] for first, second in pairs]
    stacked_real = jnp.stack([kernel * spec_real for kernel in kernels])
    stacked_imag = jnp.stack([kernel * spec_imag for kernel in kernels])
    tidal_real, tidal_imag = inverse(stacked_real, stacked_imag)
    tidal = [tidal_real[number] for number in range(6)]
    shear = tidal[0] * tidal[0] + tidal[1] * tidal[1] + tidal[2] * tidal[2]
    shear = shear + 2.0 * (tidal[3] * tidal[3] + tidal[4] * tidal[4] + tidal[5] * tidal[5])
    recon_real, recon_imag = forward(shear[None], zeros_in, True)
    norm_scale = 1.0 / float(length) ** 1.5
    anchor = anchor_z[:, None, None] & anchor_y[None, :, None] & anchor_x[None, None, :]
    recon_real = jnp.where(anchor, 0.0, recon_real[0] * norm_scale).astype(jnp.float32)
    recon_imag = jnp.where(anchor, 0.0, recon_imag[0] * norm_scale).astype(jnp.float32)
    return (recon_real, recon_imag)


def solution(mesh):
    in_specs = (P("wide", "narrow", None),)
    out_specs = (P("narrow", "wide", None), P("narrow", "wide", None))
    return jax.shard_map(
        per_device, mesh=mesh, in_specs=in_specs, out_specs=out_specs, check_vma=False
    )
```

profile of v0, /device:TPU:1, one launch (start us, length us, event | category | flops | bytes accessed | tf_op | source)
XLA Modules:
  0.0 1878.0 jit_solution(7576247466693412180)
XLA Ops:
  45.3 28.3 %all-to-all-done.1 = f32[4,1,131072]{2,1,0:T(1,128)} async-done(((f32[4,1,131072]{2,1,0:T(1,128)}), f32[4,1,131072]{2,1,0:T(1,128)}, u32[]{:S(2)}, u32[]{:S(2)}) %all-to-all-start.1) | async-done | bytes 2097184 | tf_op jit(solution)/shard_map/all_to_all | solution.py:65
  79.2 7.7 reduce
  90.8 6.8 copy.111
  106.1 20.2 %all-to-all-done = f32[4,1,131072]{2,1,0:T(1,128)} async-done(((f32[4,1,131072]{2,1,0:T(1,128)}), f32[4,1,131072]{2,1,0:T(1,128)}, u32[]{:S(2)}, u32[]{:S(2)}) %all-to-all-start) | async-done | bytes 2097184 | tf_op jit(solution)/shard_map/all_to_all | solution.py:64
  126.4 9.0 reduce.1
  140.9 7.1 copy.112
  165.1 7.2 reshape.355
  189.1 7.2 reshape.353
  201.5 8.1 all-to-all-start.2
  211.0 7.2 reduce.2
  241.3 7.2 reduce.3
  289.8 20.6 %fusion.77 = f32[256,12288]{0,1} fusion(f32[256,12288]{0,1:T(8,128)} %bitcast.284), kind=kOutput, calls=%fused_computation.99 | convolution fusion | flops 9664593920 | bytes 25165824
  310.4 15.2 fusion.50
  325.7 14.7 multiply_bitcast_fusion.2
  340.3 23.6 %copy.67 = f32[6,256,32,64]{3,2,0,1:T(8,128)} copy(f32[6,256,32,64]{1,3,2,0:T(8,128)} %multiply_bitcast_fusion.2) | data formatting | bytes 25165824 | tf_op jit(solution)/shard_map/mul | solution.py:36
  363.9 20.5 %reshape.359 = f32[8,1,393216]{2,1,0:T(1,128)} reshape(f32[256,6,32,64]{3,2,1,0:T(8,128)} %bitcast.286) | data formatting | bytes 25165824
  389.7 15.5 fusion.55
  405.3 17.5 fusion.79
  422.7 11.0 multiply_bitcast_fusion.3
  433.7 23.4 %copy.63 = f32[6,256,32,64]{3,2,0,1:T(8,128)} copy(f32[6,256,32,64]{1,3,2,0:T(8,128)} %multiply_bitcast_fusion.3) | data formatting | bytes 25165824 | tf_op jit(solution)/shard_map/mul | solution.py:36
  457.1 20.9 %reshape.357 = f32[8,1,393216]{2,1,0:T(1,128)} reshape(f32[256,6,32,64]{3,2,1,0:T(8,128)} %bitcast.287) | data formatting | bytes 25165824
  478.0 47.2 %all-to-all-done.5 = f32[8,1,393216]{2,1,0:T(1,128)} async-done(((f32[8,1,393216]{2,1,0:T(1,128)}), f32[8,1,393216]{2,1,0:T(1,128)}, u32[]{:S(2)}, u32[]{:S(2)}) %all-to-all-start.5) | async-done | bytes 12582944 | tf_op jit(solution)/shard_map/all_to_all | solution.py:83
  525.2 8.8 all-to-all-start.4
  534.1 36.6 %reduce.5 = f32[8,393216]{1,0:T(8,128)} reduce(f32[8,1,393216]{2,1,0:T(1,128)} %all-to-all-done.5, f32[]{:T(128)} %broadcast.567), dimensions={1}, to_apply=%all_to_all.156.reduce_sub_computation | reduce | bytes 25165828 | tf_op jit(solution)/shard_map/all_to_all | solution.py:83
  570.7 22.6 %reshape.360 = f32[256,6,32,64]{3,2,1,0:T(8,128)} reshape(f32[8,393216]{1,0:T(8,128)} %reduce.5) | data formatting | bytes 25165824
  593.3 17.9 copy.69
  611.2 58.3 %all-to-all-done.4 = f32[8,1,393216]{2,1,0:T(1,128)} async-done(((f32[8,1,393216]{2,1,0:T(1,128)}), f32[8,1,393216]{2,1,0:T(1,128)}, u32[]{:S(2)}, u32[]{:S(2)}) %all-to-all-start.4) | async-done | bytes 12582944 | tf_op jit(solution)/shard_map/all_to_all | solution.py:82
  669.6 36.9 %reduce.4 = f32[8,393216]{1,0:T(8,128)} reduce(f32[8,1,393216]{2,1,0:T(1,128)} %all-to-all-done.4, f32[]{:T(128)} %broadcast.567), dimensions={1}, to_apply=%all_to_all.152.reduce_sub_computation | reduce | bytes 25165828 | tf_op jit(solution)/shard_map/all_to_all | solution.py:82
  706.4 22.6 %reshape.358 = f32[256,6,32,64]{3,2,1,0:T(8,128)} reshape(f32[8,393216]{1,0:T(8,128)} %reduce.4) | data formatting | bytes 25165824
  729.1 17.9 copy.65
  747.0 48.7 %fusion.27 = f32[256,6,32,64]{0,3,2,1:T(8,128)} fusion(f32[6,32,256,64]{3,2,1,0:T(8,128)} %bitcast.280), kind=kOutput, calls=%fused_computation.73 | convolution fusion | flops 9664593920 | bytes 25165824 | tf_op jit(solution)/shard_map/fabc,bd->fadc/dot_general | solution.py:30
  795.6 48.5 %multiply_bitcast_fusion.1 = f32[6,32,256,64]{2,3,1,0:T(8,128)} fusion(f32[256,6,32,64]{0,3,2,1:T(8,128)} %fusion.27, f32[6,32,256,64]{3,2,1,0:T(8,128)} %bitcast.278), kind=kOutput, calls=%fused_computation.4 | convolution fusion | flops 9670885376 | bytes 37748736 | tf_op jit(solution)/shard_map/fabc,bd->fadc/dot_general | solution.py:33
  844.2 23.4 %copy.71 = f32[6,32,256,64]{3,1,0,2:T(8,128)} copy(f32[6,32,256,64]{2,3,1,0:T(8,128)} %multiply_bitcast_fusion.1) | data formatting | bytes 25165824 | tf_op jit(solution)/shard_map/mul | solution.py:36
  867.6 33.5 %reshape.361 = f32[4,1,786432]{2,1,0:T(1,128)} reshape(f32[256,6,32,64]{3,2,1,0:T(8,128)} %bitcast.290) | data formatting | bytes 25165824
  907.4 48.6 %fusion.23 = f32[256,6,32,64]{0,3,2,1:T(8,128)} fusion(f32[6,32,256,64]{3,2,1,0:T(8,128)} %bitcast.279), kind=kOutput, calls=%fused_computation.69 | convolution fusion | flops 9664593920 | bytes 25165824 | tf_op jit(solution)/shard_map/fabc,bd->fadc/dot_general | solution.py:32
  956.0 48.7 %multiply_bitcast_fusion = f32[6,32,256,64]{2,3,1,0:T(8,128)} fusion(f32[256,6,32,64]{0,3,2,1:T(8,128)} %fusion.23, f32[6,32,256,64]{3,2,1,0:T(8,128)} %bitcast.281), kind=kOutput, calls=%fused_computation.3 | convolution fusion | flops 9670885376 | bytes 37748736 | tf_op jit(solution)/shard_map/fabc,bd->fadc/dot_general | solution.py:31
  1004.6 23.4 %copy.75 = f32[6,32,256,64]{3,1,0,2:T(8,128)} copy(f32[6,32,256,64]{2,3,1,0:T(8,128)} %multiply_bitcast_fusion) | data formatting | bytes 25165824 | tf_op jit(solution)/shard_map/mul | solution.py:36
  1028.1 33.2 %reshape.363 = f32[4,1,786432]{2,1,0:T(1,128)} reshape(f32[256,6,32,64]{3,2,1,0:T(8,128)} %bitcast.291) | data formatting | bytes 25165824
  1061.3 118.5 %all-to-all-done.6 = f32[4,1,786432]{2,1,0:T(1,128)} async-done(((f32[4,1,786432]{2,1,0:T(1,128)}), f32[4,1,786432]{2,1,0:T(1,128)}, u32[]{:S(2)}, u32[]{:S(2)}) %all-to-all-start.6) | async-done | bytes 12582944 | tf_op jit(solution)/shard_map/all_to_all | solution.py:88
  1179.8 6.3 all-to-all-start.7
  1186.1 40.1 %reduce.6 = f32[4,786432]{1,0:T(4,128)} reduce(f32[4,1,786432]{2,1,0:T(1,128)} %all-to-all-done.6, f32[]{:T(128)} %broadcast.567), dimensions={1}, to_apply=%all_to_all.160.reduce_sub_computation | reduce | bytes 25165828 | tf_op jit(solution)/shard_map/all_to_all | solution.py:88
  1226.2 31.8 %reshape.362 = f32[256,6,32,64]{3,2,1,0:T(8,128)} reshape(f32[4,786432]{1,0:T(4,128)} %reduce.6) | data formatting | bytes 25165824
  1258.0 30.2 %copy.108 = f32[6,32,4,64,64]{4,2,3,1,0:T(4,128)} copy(f32[6,32,4,64,64]{4,1,0,3,2:T(8,128)} %bitcast.292) | data formatting | bytes 25165824 | tf_op jit(solution)/shard_map/all_to_all | solution.py:88
  1288.3 23.2 %all_to_all.163 = f32[6,32,64,256]{3,2,1,0:T(8,128)} reshape(f32[6,32,64,4,64]{4,3,2,1,0:T(4,128)} %bitcast.293) | data formatting | bytes 25165824 | tf_op jit(solution)/shard_map/all_to_all | solution.py:88
  1311.4 17.4 fusion.25
  1328.8 129.7 %all-to-all-done.7 = f32[4,1,786432]{2,1,0:T(1,128)} async-done(((f32[4,1,786432]{2,1,0:T(1,128)}), f32[4,1,786432]{2,1,0:T(1,128)}, u32[]{:S(2)}, u32[]{:S(2)}) %all-to-all-start.7) | async-done | bytes 12582944 | tf_op jit(solution)/shard_map/all_to_all | solution.py:89
  1458.6 39.9 %reduce.7 = f32[4,786432]{1,0:T(4,128)} reduce(f32[4,1,786432]{2,1,0:T(1,128)} %all-to-all-done.7, f32[]{:T(128)} %broadcast.567), dimensions={1}, to_apply=%all_to_all.164.reduce_sub_computation | reduce | bytes 25165828 | tf_op jit(solution)/shard_map/all_to_all | solution.py:89
  1498.5 32.1 %reshape.364 = f32[256,6,32,64]{3,2,1,0:T(8,128)} reshape(f32[4,786432]{1,0:T(4,128)} %reduce.7) | data formatting | bytes 25165824
  1530.5 30.2 %copy.107 = f32[6,32,4,64,64]{4,2,3,1,0:T(4,128)} copy(f32[6,32,4,64,64]{4,1,0,3,2:T(8,128)} %bitcast.294) | data formatting | bytes 25165824 | tf_op jit(solution)/shard_map/all_to_all | solution.py:89
  1560.8 23.2 %all_to_all.167 = f32[6,32,64,256]{3,2,1,0:T(8,128)} reshape(f32[6,32,64,4,64]{4,3,2,1,0:T(4,128)} %bitcast.295) | data formatting | bytes 25165824 | tf_op jit(solution)/shard_map/all_to_all | solution.py:89
  1583.9 19.4 %subtract_multiply_fusion = f32[6,32,64,256]{3,2,1,0:T(8,128)} fusion(f32[6,32,64,256]{3,2,1,0:T(8,128)} %fusion.25, f32[6,32,64,256]{3,2,1,0:T(8,128)} %all_to_all.167), kind=kOutput, calls=%fused_computation.2 | convolution fusion | flops 9670885376 | bytes 37748736 | tf_op jit(solution)/shard_map/fabc,cd->fabd/dot_general | solution.py:33
  1603.3 6.4 fusion.7
  1646.1 31.0 %all-to-all-done.8 = f32[4,1,131072]{2,1,0:T(1,128)} async-done(((f32[4,1,131072]{2,1,0:T(1,128)}), f32[4,1,131072]{2,1,0:T(1,128)}, u32[]{:S(2)}, u32[]{:S(2)}) %all-to-all-start.8) | async-done | bytes 2097184 | tf_op jit(solution)/shard_map/all_to_all | solution.py:64
  1682.0 7.7 reduce.9
  1693.6 6.8 copy.110
  1709.0 20.8 %all-to-all-done.9 = f32[4,1,131072]{2,1,0:T(1,128)} async-done(((f32[4,1,131072]{2,1,0:T(1,128)}), f32[4,1,131072]{2,1,0:T(1,128)}, u32[]{:S(2)}, u32[]{:S(2)}) %all-to-all-start.9) | async-done | bytes 2097184 | tf_op jit(solution)/shard_map/all_to_all | solution.py:65
  1729.7 9.0 reduce.8
  1744.3 7.1 copy.109
  1768.4 7.2 reshape.371
  1775.6 7.1 all-to-all-start.11
  1793.3 7.2 reshape.369
  1805.8 8.0 all-to-all-start.10
  1813.9 7.2 reduce.10
  1844.0 7.2 reduce.11
  (126 shorter events, 326.0 us)
Async XLA Ops:
  0.6 4.2 copy-start
  3.5 1.3 copy-start.3
  20.1 53.5 %all-to-all-start.1 = ((f32[4,1,131072]{2,1,0:T(1,128)}), f32[4,1,131072]{2,1,0:T(1,128)}, u32[]{:S(2)}, u32[]{:S(2)}) async-start(f32[4,1,131072]{2,1,0:T(1,128)} %reshape.351), calls=%async_computation.1 | async-start | bytes 4194304 | tf_op jit(solution)/shard_map/all_to_all | solution.py:65
  28.6 1.3 copy-start.4
  73.6 52.8 %all-to-all-start = ((f32[4,1,131072]{2,1,0:T(1,128)}), f32[4,1,131072]{2,1,0:T(1,128)}, u32[]{:S(2)}, u32[]{:S(2)}) async-start(f32[4,1,131072]{2,1,0:T(1,128)} %reshape.349), calls=%async_computation | async-start | bytes 4194304 | tf_op jit(solution)/shard_map/all_to_all | solution.py:64
  153.2 4.7 copy-start.8
  172.3 29.2 %all-to-all-start.3 = ((f32[8,1,65536]{2,1,0:T(1,128)}), f32[8,1,65536]{2,1,0:T(1,128)}, u32[]{:S(2)}, u32[]{:S(2)}) async-start(f32[8,1,65536]{2,1,0:T(1,128)} %reshape.355), calls=%async_computation.3 | async-start | bytes 4194304 | tf_op jit(solution)/shard_map/all_to_all | solution.py:72
  178.4 2.9 copy-start.6
  201.5 39.8 %all-to-all-start.2 = ((f32[8,1,65536]{2,1,0:T(1,128)}), f32[8,1,65536]{2,1,0:T(1,128)}, u32[]{:S(2)}, u32[]{:S(2)}) async-start(f32[8,1,65536]{2,1,0:T(1,128)} %reshape.353), calls=%async_computation.2 | async-start | bytes 4194304 | tf_op jit(solution)/shard_map/all_to_all | solution.py:71
  267.2 4.1 copy-start.12
  267.2 4.1 copy-start.13
  289.8 20.6 %copy-start.2 = (f32[6,256,32,64]{1,3,2,0:T(8,128)}, f32[6,256,32,64]{1,3,2,0:T(8,128)S(1)}, u32[]{:S(2)}) copy-start(f32[6,256,32,64]{1,3,2,0:T(8,128)S(1)} %get-tuple-element.16) | copy-start | bytes 37748740
  384.4 140.8 %all-to-all-start.5 = ((f32[8,1,393216]{2,1,0:T(1,128)}), f32[8,1,393216]{2,1,0:T(1,128)}, u32[]{:S(2)}, u32[]{:S(2)}) async-start(f32[8,1,393216]{2,1,0:T(1,128)} %reshape.359), calls=%async_computation.5 | async-start | bytes 25165824 | tf_op jit(solution)/shard_map/all_to_all | solution.py:83
  525.2 144.3 %all-to-all-start.4 = ((f32[8,1,393216]{2,1,0:T(1,128)}), f32[8,1,393216]{2,1,0:T(1,128)}, u32[]{:S(2)}, u32[]{:S(2)}) async-start(f32[8,1,393216]{2,1,0:T(1,128)} %reshape.357), calls=%async_computation.4 | async-start | bytes 25165824 | tf_op jit(solution)/shard_map/all_to_all | solution.py:82
  901.1 278.7 %all-to-all-start.6 = ((f32[4,1,786432]{2,1,0:T(1,128)}), f32[4,1,786432]{2,1,0:T(1,128)}, u32[]{:S(2)}, u32[]{:S(2)}) async-start(f32[4,1,786432]{2,1,0:T(1,128)} %reshape.361), calls=%async_computation.6 | async-start | bytes 25165824 | tf_op jit(solution)/shard_map/all_to_all | solution.py:88
  1179.8 278.8 %all-to-all-start.7 = ((f32[4,1,786432]{2,1,0:T(1,128)}), f32[4,1,786432]{2,1,0:T(1,128)}, u32[]{:S(2)}, u32[]{:S(2)}) async-start(f32[4,1,786432]{2,1,0:T(1,128)} %reshape.363), calls=%async_computation.7 | async-start | bytes 25165824 | tf_op jit(solution)/shard_map/all_to_all | solution.py:89
  1603.3 6.4 copy-start.5
  1624.9 52.2 %all-to-all-start.8 = ((f32[4,1,131072]{2,1,0:T(1,128)}), f32[4,1,131072]{2,1,0:T(1,128)}, u32[]{:S(2)}, u32[]{:S(2)}) async-start(f32[4,1,131072]{2,1,0:T(1,128)} %reshape.365), calls=%async_computation.8 | async-start | bytes 4194304 | tf_op jit(solution)/shard_map/all_to_all | solution.py:64
  1677.1 52.7 %all-to-all-start.9 = ((f32[4,1,131072]{2,1,0:T(1,128)}), f32[4,1,131072]{2,1,0:T(1,128)}, u32[]{:S(2)}, u32[]{:S(2)}) async-start(f32[4,1,131072]{2,1,0:T(1,128)} %reshape.367), calls=%async_computation.9 | async-start | bytes 4194304 | tf_op jit(solution)/shard_map/all_to_all | solution.py:65
  1756.6 4.6 copy-start.9
  1775.6 30.2 %all-to-all-start.11 = ((f32[8,1,65536]{2,1,0:T(1,128)}), f32[8,1,65536]{2,1,0:T(1,128)}, u32[]{:S(2)}, u32[]{:S(2)}) async-start(f32[8,1,65536]{2,1,0:T(1,128)} %reshape.371), calls=%async_computation.11 | async-start | bytes 4194304 | tf_op jit(solution)/shard_map/all_to_all | solution.py:72
  1782.7 2.9 copy-start.7
  1800.5 13.3 copy-start.14
  1800.5 13.4 copy-start.15
  1805.8 38.2 %all-to-all-start.10 = ((f32[8,1,65536]{2,1,0:T(1,128)}), f32[8,1,65536]{2,1,0:T(1,128)}, u32[]{:S(2)}, u32[]{:S(2)}) async-start(f32[8,1,65536]{2,1,0:T(1,128)} %reshape.369), calls=%async_computation.10 | async-start | bytes 4194304 | tf_op jit(solution)/shard_map/all_to_all | solution.py:71
  1868.9 2.9 copy-start.10
  1868.9 2.9 copy-start.11
  1875.3 2.5 copy-start.1
where the time goes:
time: 1890 us; the launch traced here: 1880 us
  local copies, waits for them, and re-layouts  679 us (36%)
  waiting for transfers between devices  465 us (25%)
  matrix products  384 us (20%)
  other arithmetic  273 us (14%)
  starting transfers between devices  76.1 us (4%)
    unnamed x58, local copies, waits for them, and re-layouts  310 us
    all_to_all x1, waiting for transfers between devices, inverse(): lax.all_to_all(section[1], 'narrow', split_axis=2, concat_axis=3, tiled=T...  130 us
    unnamed x20, matrix products  129 us
    all_to_all x1, waiting for transfers between devices, inverse(): lax.all_to_all(section[0], 'narrow', split_axis=2, concat_axis=3, tiled=T...  119 us
    mul x4, local copies, waits for them, and re-layouts, transform(): return ((real_cos - imag_sin) * scale, (imag_cos + real_sin) * scale)  93.8 us
    dot_general x4, matrix products, transform(): real_cos = contract(real_part, cosine)  74.4 us
    dot_general x3, matrix products, transform(): imag_sin = contract(imag_part, sine)  70.7 us
    dot_general x3, matrix products, transform(): real_sin = contract(real_part, sine)  58.6 us
  transfers between devices with their start and end apart: 12, of which 10 were waited for; matrix products, arithmetic and copies ran while one was open for 33% of the time, Pallas kernels for 0%

commit v1 on v0

v1 whole, which is shorter than its diff:
```python
import math

import jax
import jax.numpy as jnp
import ml_dtypes
import numpy as np
from jax import lax
from jax.experimental import pallas as pl
from jax.experimental.pallas import tpu as pltpu
from jax.sharding import PartitionSpec as P

AXES = ("wide", "narrow")
TILE = 128
LIMIT = 56 * 1024 * 1024


def angles(rows, columns, length):
    return (2.0 * math.pi / length) * (np.outer(rows, columns) % length)


def split_table(table):
    table = np.asarray(table, np.float64)
    high = table.astype(ml_dtypes.bfloat16)
    low = (table - high.astype(np.float64)).astype(ml_dtypes.bfloat16)
    return np.stack([high, low])


def split(value):
    high = value.astype(jnp.bfloat16)
    low = (value - high.astype(jnp.float32)).astype(jnp.bfloat16)
    return high, low


def product(left, right, contract=((1,), (0,))):
    def dot(a, b):
        return lax.dot_general(a, b, (contract, ((), ())), preferred_element_type=jnp.float32)

    return dot(left[0], right[0]) + (dot(left[0], right[1]) + dot(left[1], right[0]))


def pair(ref):
    return ref[0], ref[1]


def signed_wave(index, length):
    index = np.asarray(index)
    return np.where(index < length // 2, index, index - length) * (2.0 * math.pi / length)


def params(steps):
    return pltpu.CompilerParams(
        vmem_limit_bytes=LIMIT, dimension_semantics=("arbitrary",) * steps
    )


def whole(shape):
    return pl.BlockSpec(shape, lambda *_: (0,) * len(shape))


def cost(macs, moved):
    return pl.CostEstimate(flops=6 * macs, bytes_accessed=moved, transcendentals=0)


def third_kernel(table_ref, density_ref, out_ref):
    rows_x, rows_y, length = density_ref.shape
    half = out_ref.shape[0]
    flat = out_ref.reshape(half * rows_x, 2 * rows_y)
    table = pair(table_ref)
    left_half = lax.broadcasted_iota(jnp.int32, (half, 2 * rows_y), 1) < rows_y
    group = 4
    for first in range(0, rows_x, group):
        block = density_ref[first : first + group].reshape(group * rows_y, length)
        result = product(table, split(block), ((1,), (1,)))
        for inner in range(0, group, 2):
            lanes = slice(inner * rows_y, (inner + 2) * rows_y)
            real = result[:half, lanes]
            imag = result[half:, lanes]
            even = jnp.where(left_half, real, pltpu.roll(imag, rows_y, 1))
            odd = jnp.where(left_half, pltpu.roll(real, rows_y, 1), imag)
            flat[pl.ds(first + inner, half, stride=rows_x), :] = even
            flat[pl.ds(first + inner + 1, half, stride=rows_x), :] = odd


def third_pass(density):
    rows_x, rows_y, length = density.shape
    half = length // 2
    angle = angles(np.arange(half), np.arange(length), length)
    table = split_table(np.concatenate([np.cos(angle), -np.sin(angle)]))
    step = min(8, rows_x)
    return pl.pallas_call(
        third_kernel,
        grid=(rows_x // step,),
        in_specs=[
            whole(table.shape),
            pl.BlockSpec((step, rows_y, length), lambda i: (i, 0, 0)),
        ],
        out_specs=pl.BlockSpec((half, step, 2 * rows_y), lambda i: (0, i, 0)),
        out_shape=jax.ShapeDtypeStruct((half, rows_x, 2 * rows_y), jnp.float32),
        compiler_params=params(1),
        cost_estimate=cost(density.size * length, 8 * density.size),
    )(table, density)


def spectrum_kernel(
    fields, per_c, groups, pairs_x, wave_c_ref, wave_ref, row_ref, second_ref, first_ref, back_ref, in_ref, *outs
):
    wide, narrow, _, rows_x, lanes = in_ref.shape
    length = wide * rows_x
    plane = jnp.concatenate(
        [in_ref[:, n, 0].reshape(length, lanes) for n in range(narrow)], axis=1
    )
    plane = product(split(plane), pair(second_ref))
    both = product(pair(first_ref), split(plane))
    real = both[:length, :length] + both[length:, length:]
    imag = both[:length, length:] - both[length:, :length]
    wave_a = wave_ref[...]
    wave_b = row_ref[...]
    wave_c = wave_c_ref[pl.program_id(0)]
    squared = wave_a * wave_a + (wave_b * wave_b + wave_c * wave_c)
    spot_a = lax.broadcasted_iota(jnp.int32, (length, length), 0)
    spot_b = lax.broadcasted_iota(jnp.int32, (length, length), 1)
    keep = (spot_a != length // 2) & (spot_b != length // 2) & (squared > 0)
    safe = jnp.where(squared > 0, squared, 1.0)
    smooth = jnp.where(keep, jnp.exp(-0.5 * squared) / safe, 0.0) * (1.0 / float(length) ** 3)
    field = jnp.concatenate([real * smooth, imag * smooth], axis=1)
    tiles, message, tile = outs[0].shape[1:]
    devices = length // (groups * pairs_x)
    flats = [ref.reshape(devices * tiles * message, tile) for ref in outs]
    for number in range(fields):
        both = product(pair(back_ref), split(field))
        real = both[:length, :length] - both[length:, length:]
        imag = both[:length, length:] + both[length:, :length]
        value = jnp.concatenate([real, imag], axis=1)
        count = tiles // fields
        for group in range(groups):
            for x in range(pairs_x):
                start = (group * pairs_x + x) * devices
                for spot in range(count):
                    at = (number * count + spot) * message + x * per_c + pl.program_id(0)
                    flats[group][pl.ds(at, devices, stride=tiles * message), :] = value[
                        start : start + devices, spot * tile : (spot + 1) * tile
                    ]
        if number + 1 < fields:
            field = field * wave_a


def spectrum_pass(received, waves_c, devices, pairs_x):
    wide, narrow, per_c, rows_x, lanes = received.shape
    length = wide * rows_x
    rows_y = lanes // 2
    index = np.arange(length)
    angle = angles(index, index, length)
    cosine, sine = np.cos(angle), np.sin(angle)
    second = np.zeros((narrow, 2, rows_y, 2 * length))
    for n in range(narrow):
        spots = slice(n * rows_y, (n + 1) * rows_y)
        second[n, 0] = np.concatenate([cosine[spots], -sine[spots]], axis=1)
        second[n, 1] = np.concatenate([sine[spots], cosine[spots]], axis=1)
    second = split_table(second.reshape(2 * length, 2 * length))
    first = split_table(np.concatenate([cosine, sine]))
    slab = length // devices
    groups = slab // pairs_x
    order = index.reshape(devices, groups, pairs_x).transpose(1, 2, 0).reshape(-1)
    back = split_table(np.concatenate([cosine[order], sine[order]]))
    wave = signed_wave(index, length).astype(np.float32)
    fields = 3
    out_shape = (devices, fields * 2 * length // TILE, pairs_x * per_c, TILE)

    def body(*refs):
        spectrum_kernel(fields, per_c, groups, pairs_x, *refs)

    return pl.pallas_call(
        body,
        grid=(per_c,),
        in_specs=[
            pl.BlockSpec(memory_space=pltpu.SMEM),
            whole((length, 1)),
            whole((1, length)),
            whole(second.shape),
            whole(first.shape),
            whole(back.shape),
            pl.BlockSpec((wide, narrow, 1, rows_x, lanes), lambda i: (0, 0, i, 0, 0)),
        ],
        out_specs=[whole(out_shape)] * groups,
        out_shape=[jax.ShapeDtypeStruct(out_shape, jnp.float32)] * groups,
        compiler_params=params(1),
        cost_estimate=cost(per_c * 20 * length**3, 20 * per_c * length**2 * 2),
    )(waves_c, wave[:, None], wave[None, :], second, first, back, received)


def shear_kernel(
    pairs_x, row_ref, lane_ref, second_ref, third_ref, ahead_ref, last_ref, in_ref, out_ref, shear_ref
):
    step = pl.program_id(0)
    length = shear_ref.shape[1]

    @pl.when(step == 0)
    def _():
        shear_ref[...] = jnp.zeros_like(shear_ref)

    devices, tiles, message, tile = in_ref.shape
    field = jnp.concatenate(
        [in_ref[:, spot].reshape(devices * message, tile) for spot in range(tiles)], axis=1
    )
    field = field * row_ref[0] * lane_ref[0]
    field = product(split(field), pair(second_ref))
    field = jnp.concatenate([field[:, :length], field[:, length:]], axis=0)
    field = product(pair(third_ref), split(field))
    shear_ref[...] += field * field

    @pl.when(step == 5)
    def _():
        wide, narrow, _, rows_b, lanes = out_ref.shape
        ahead = product(pair(ahead_ref), split(shear_ref[...]), ((1,), (1,)))
        for spot in range(pairs_x):
            part = slice(spot * length, (spot + 1) * length)
            value = jnp.concatenate([ahead[:length, part], ahead[length:, part]], axis=1)
            value = product(split(value), pair(last_ref))
            for w in range(wide):
                for n in range(narrow):
                    out_ref[w, n, spot] = value[
                        w * rows_b : (w + 1) * rows_b, n * lanes : (n + 1) * lanes
                    ]


def shear_pass(received, wide, narrow, pairs_x, per_c):
    devices, tiles, message, tile = received.shape
    rows = devices * message
    length = tiles * tile // 6
    index = np.arange(length)
    angle = angles(index, index, length)
    cosine, sine = np.cos(angle), np.sin(angle)
    second = np.block([[cosine, sine], [-sine, cosine]])
    spots = np.arange(rows).reshape(devices, pairs_x, per_c)
    row_c = (np.arange(devices)[:, None, None] * per_c + np.arange(per_c)[None, None, :]) + 0 * spots
    row_c = row_c.reshape(-1)
    row_x = (np.arange(pairs_x)[None, :, None] + 0 * spots).reshape(-1)
    weight = np.where(row_c == 0, 1.0, 2.0)
    angle = angles(index, row_c, length)
    third = np.concatenate(
        [
            np.concatenate(
                [(row_x == x) * weight * np.cos(angle), (row_x == x) * weight * -np.sin(angle)], axis=1
            )
            for x in range(pairs_x)
        ]
    )
    ahead = np.concatenate([cosine, -sine])
    cos_z = cosine.reshape(length, narrow, 1, length // narrow)
    sin_z = sine.reshape(length, narrow, 1, length // narrow)
    last = np.concatenate(
        [
            np.concatenate([cos_z, -sin_z], axis=2).reshape(length, 2 * length),
            np.concatenate([sin_z, cos_z], axis=2).reshape(length, 2 * length),
        ]
    )
    wave = signed_wave(index, length)
    wave_rows = wave[row_c]
    wave_lanes = np.concatenate([wave, wave])
    twice = math.sqrt(2.0)
    one_row, one_lane = np.ones_like(wave_rows), np.ones_like(wave_lanes)
    row_factor = np.stack(
        [one_row, twice * one_row, twice * wave_rows, one_row, twice * wave_rows, wave_rows**2]
    ).astype(np.float32)[:, :, None]
    lane_factor = np.stack(
        [one_lane, wave_lanes, one_lane, wave_lanes**2, wave_lanes, one_lane]
    ).astype(np.float32)[:, None, :]
    tables = [split_table(table) for table in (second, third, ahead, last)]
    out_shape = (wide, narrow, pairs_x, length // wide, 2 * length // narrow)

    def body(*refs):
        shear_kernel(pairs_x, *refs)

    def which(i):
        return (0, 2 - (i >= 1).astype(jnp.int32) - (i >= 3).astype(jnp.int32), 0, 0)

    return pl.pallas_call(
        body,
        grid=(6,),
        in_specs=[
            pl.BlockSpec((1, rows, 1), lambda i: (i, 0, 0)),
            pl.BlockSpec((1, 1, 2 * length), lambda i: (i, 0, 0)),
            *[whole(table.shape) for table in tables],
            pl.BlockSpec((devices, tiles // 3, message, tile), which),
        ],
        out_specs=whole(out_shape),
        out_shape=jax.ShapeDtypeStruct(out_shape, jnp.float32),
        scratch_shapes=[pltpu.VMEM((pairs_x * length, length), jnp.float32)],
        compiler_params=params(1),
        cost_estimate=cost(60 * length**3, 4 * received.size + 4 * 2**20),
    )(row_factor, lane_factor, *tables, received)


def first_kernel(scale, anchor_ref, table_ref, *refs):
    ins, (real_ref, imag_ref, real_tile_ref, imag_tile_ref) = refs[:-4], refs[-4:]
    devices, pairs_x, rows_b, lanes = ins[0].shape
    half, length = lanes // 2, real_ref.shape[2]
    table = pair(table_ref)
    flats = [ref.reshape(devices * pairs_x * rows_b, lanes) for ref in ins]
    tile = real_tile_ref.shape[2]
    spot_c = lax.broadcasted_iota(jnp.int32, (half, length), 0)
    spot_a = lax.broadcasted_iota(jnp.int32, (half, length), 1)
    is_anchor = (anchor_ref[0] == 1) & (pl.program_id(0) == 0)
    anchor = (spot_c == 0) & (spot_a == 0) & is_anchor
    group = min(4, rows_b)
    for first in range(0, rows_b, group):
        columns = []
        for b in range(first, first + group):
            column = jnp.concatenate(
                [flat[pl.ds(b, devices * pairs_x, stride=rows_b), :] for flat in flats], axis=0
            )
            columns.append(column.T)
        result = product(split(jnp.concatenate(columns, axis=0)), table)
        for number in range(group):
            b = first + number
            here = result[number * lanes : (number + 1) * lanes]
            real = (here[:half, :length] + here[half:, length:]) * scale
            imag = (here[half:, :length] - here[:half, length:]) * scale
            if b == 0:
                real = jnp.where(anchor, 0.0, real)
                imag = jnp.where(anchor, 0.0, imag)
            for spot in range(length // tile):
                part = slice(spot * tile, (spot + 1) * tile)
                real_tile_ref[spot, pl.ds(b, half, stride=rows_b), :] = real[:, part]
                imag_tile_ref[spot, pl.ds(b, half, stride=rows_b), :] = imag[:, part]
    for spot in range(length // tile):
        part = slice(spot * tile, (spot + 1) * tile)
        real_ref[:, :, part] = real_tile_ref[spot].reshape(half, rows_b, tile)
        imag_ref[:, :, part] = imag_tile_ref[spot].reshape(half, rows_b, tile)


def first_pass(parts, is_anchor, length):
    devices, pairs_x, rows_b, lanes = parts[0].shape
    groups = len(parts)
    index = np.arange(length)
    order = index.reshape(devices, groups, pairs_x).transpose(1, 0, 2).reshape(-1)
    angle = angles(order, index, length)
    table = split_table(np.concatenate([np.cos(angle), np.sin(angle)], axis=1))
    step = min(8, rows_b)
    scale = 1.0 / float(length) ** 1.5

    def body(*refs):
        first_kernel(scale, *refs)

    out_shape = jax.ShapeDtypeStruct((lanes // 2, rows_b, length), jnp.float32)
    return pl.pallas_call(
        body,
        grid=(rows_b // step,),
        in_specs=[
            pl.BlockSpec(memory_space=pltpu.SMEM),
            whole(table.shape),
            *[pl.BlockSpec((devices, pairs_x, step, lanes), lambda i: (0, 0, i, 0))] * groups,
        ],
        out_specs=[pl.BlockSpec((lanes // 2, step, length), lambda i: (0, i, 0))] * 2,
        out_shape=[out_shape] * 2,
        scratch_shapes=[pltpu.VMEM((length // TILE, lanes // 2 * step, TILE), jnp.float32)] * 2,
        compiler_params=params(1),
        cost_estimate=cost(rows_b * lanes * length * 2 * length, 8 * rows_b * lanes * length),
    )(is_anchor, table, *parts)


def transpose(value):
    return lax.all_to_all(value, AXES, split_axis=0, concat_axis=0, tiled=True)


def solution(mesh):
    wide, narrow = mesh.shape["wide"], mesh.shape["narrow"]
    devices = wide * narrow

    def per_device(density):
        rows_x, rows_y, length = density.shape
        per_c = length // 2 // devices
        pairs_x = 2
        spot_wide, spot_narrow = lax.axis_index("wide"), lax.axis_index("narrow")
        here = spot_wide * narrow + spot_narrow
        planes = third_pass(density).reshape(devices, per_c, rows_x, 2 * rows_y)
        planes = transpose(planes).reshape(wide, narrow, per_c, rows_x, 2 * rows_y)
        waves_c = (here * per_c + jnp.arange(per_c, dtype=jnp.int32)).astype(jnp.float32)
        waves_c = waves_c * (2.0 * math.pi / length)
        chunks = spectrum_pass(planes, waves_c, devices, pairs_x)
        is_anchor = (here == 0).astype(jnp.int32).reshape(1)
        parts = []
        for chunk in chunks:
            part = shear_pass(transpose(chunk), wide, narrow, pairs_x, per_c)
            part = part.reshape((devices,) + part.shape[2:])
            parts.append(transpose(part))
        return tuple(first_pass(parts, is_anchor, length))

    return jax.shard_map(
        per_device,
        mesh=mesh,
        in_specs=(P("wide", "narrow", None),),
        out_specs=(P("narrow", "wide", None), P("narrow", "wide", None)),
        check_vma=False,
    )
```

time: 1890 us -> 375 us (0.20)
  local copies, waits for them, and re-layouts: 679 us -> 2.33 us
  matrix products: 384 us -> 0 us
  waiting for transfers between devices: 465 us -> 142 us
  other arithmetic: 273 us -> 0.49 us
  blocking collectives: 0 us -> 123 us
  Pallas kernels: 0 us -> 82.9 us
  starting transfers between devices: 76.1 us -> 22.9 us
    all_to_all x12 -> x6, waiting for transfers between devices: 465 us -> 142 us  [transpose(): return lax.all_to_all(value, AXES, split_axis=0, concat_axis=0, tiled=True)]
    unnamed x58 -> x16, local copies, waits for them, and re-layouts: 310 us -> 2.33 us
    dot_general x12 -> x0, matrix products: 255 us -> none  [the longest x4 74.4 us: transform(): real_cos = contract(real_part, cosine)]
    all_to_all x12 -> x0, other arithmetic: 216 us -> none  [the longest x1 40.1 us: inverse(): lax.all_to_all(section[0], 'narrow', split_axis=2, concat_axis=3, tiled=T...]
    all_to_all x19 -> x0, local copies, waits for them, and re-layouts: 200 us -> none  [the longest x2 53.4 us: inverse(): lax.all_to_all(section[0], 'narrow', split_axis=2, concat_axis=3, tiled=T...]
    unnamed x20 -> x0, matrix products: 129 us -> none
    all_to_all x0 -> x3, blocking collectives: none -> 123 us  [transpose(): return lax.all_to_all(value, AXES, split_axis=0, concat_axis=0, tiled=True)]
    mul x4 -> x0, local copies, waits for them, and re-layouts: 93.8 us -> none  [transform(): return ((real_cos - imag_sin) * scale, (imag_cos + real_sin) * scale)]
  transfers between devices with their start and end apart: 12 -> 6, of which waited for: 10 -> 6; matrix products, arithmetic and copies ran while one was open for 33% -> 0% of each run, Pallas kernels for 0% -> 13%
where the time goes in v1:
time: 375 us; the launch traced here: 374 us
  waiting for transfers between devices  142 us (38%)
  blocking collectives  123 us (33%)
  Pallas kernels  82.9 us (22%)
  starting transfers between devices  22.9 us (6%)
    all_to_all x6, waiting for transfers between devices, transpose(): return lax.all_to_all(value, AXES, split_axis=0, concat_axis=0, tiled=True)  142 us
    all_to_all x3, blocking collectives, transpose(): return lax.all_to_all(value, AXES, split_axis=0, concat_axis=0, tiled=True)  123 us
    pallas_call x4, Pallas kernels, shear_pass(): pl.pallas_call(body, grid=(6,), in_specs=[pl.BlockSpec((1, rows, 1), lamb...  48.7 us
    all_to_all x6, starting transfers between devices, transpose(): return lax.all_to_all(value, AXES, split_axis=0, concat_axis=0, tiled=True)  22.9 us
    pallas_call x1, Pallas kernels, spectrum_pass(): pl.pallas_call(body, grid=(per_c,), in_specs=[pl.BlockSpec(memory_space=p...  21.3 us
    pallas_call x1, Pallas kernels, first_pass(): pl.pallas_call(body, grid=(rows_b // step,), in_specs=[pl.BlockSpec(memor...  8.05 us
  transfers between devices with their start and end apart: 6, of which 6 were waited for; matrix products, arithmetic and copies ran while one was open for 0% of the time, Pallas kernels for 13%

profile of v1, /device:TPU:1, one launch (start us, length us, event | category | flops | bytes accessed | tf_op | source)
XLA Modules:
  0.0 374.1 jit_solution(15549181568841818414)
XLA Ops:
  0.6 4.9 %shard_map.311 = f32[128,32,128]{2,1,0:T(8,128)} custom-call(bf16[2,256,256]{2,1,0:T(8,128)(2,1)} %constant.41.clone.table_ref, f32[32,64,256]{2,1,0:T(8,128)} %density_ref.1), custom_call_target="tpu_custom_call" | custom-call | flops 805306368 | bytes 4194304 | tf_op jit(solution)/shard_map/pallas_call | solution.py:90
  5.5 7.1 %all-to-all-start = ((f32[32,4,32,128]{3,2,1,0:T(8,128)}), f32[32,4,32,128]{3,2,1,0:T(8,128)S(1)}, u32[]{:S(2)}, u32[]{:S(2)}) async-start(f32[32,4,32,128]{3,2,1,0:T(8,128)} %bitcast.7), calls=%async_computation | async-start | bytes 4194304 | tf_op jit(solution)/shard_map/all_to_all | solution.py:363
  12.6 0.5 convert_multiply_fusion.refs_0_
  13.1 47.8 %all-to-all-done = f32[32,4,32,128]{3,2,1,0:T(8,128)S(1)} async-done(((f32[32,4,32,128]{3,2,1,0:T(8,128)}), f32[32,4,32,128]{3,2,1,0:T(8,128)S(1)}, u32[]{:S(2)}, u32[]{:S(2)}) %all-to-all-start) | async-done | bytes 2097184 | tf_op jit(solution)/shard_map/all_to_all | solution.py:363
  60.9 0.0 copy-start
  60.9 1.3 copy-done
  62.2 21.3 %shard_map.312 = (f32[32,12,8,128]{3,2,1,0:T(8,128)}, f32[32,12,8,128]{3,2,1,0:T(8,128)}, f32[32,12,8,128]{3,2,1,0:T(8,128)}, f32[32,12,8,128]{3,2,1,0:T(8,128)}) custom-call(f32[4]{0:T(128)} %convert_multiply_fusion.refs_0_, f32[256,1]{1,0:T(8,128)} %constant.42.clone.refs_1_, f32[1,256]{1,0:T(1,128)} %constant.43.clone.refs_2_, ...), custom_call_target="tpu_custom_call" | custom-call | flops 8053063680 | bytes 10485760 | tf_op jit(solution)/shard_map/pallas_call | solution.py:172
  83.5 0.0 copy-start.3
  83.5 41.3 %all_to_all.45.refs_6_ = f32[32,12,8,128]{3,2,1,0:T(8,128)} all-to-all(f32[32,12,8,128]{3,2,1,0:T(8,128)} %get-tuple-element.6), channel_id=1, replica_groups=mesh['wide'=8,'narrow'=4] {'wide','narrow'}, dimensions={0} | all-to-all | bytes 3145728 | tf_op jit(solution)/shard_map/all_to_all | solution.py:363
  124.8 0.0 copy-done.3
  124.8 0.0 copy-start.2
  124.8 40.8 %all_to_all.46.refs_6_ = f32[32,12,8,128]{3,2,1,0:T(8,128)} all-to-all(f32[32,12,8,128]{3,2,1,0:T(8,128)S(1)} %copy-done.3), channel_id=1, replica_groups=mesh['wide'=8,'narrow'=4] {'wide','narrow'}, dimensions={0} | all-to-all | bytes 3145728 | tf_op jit(solution)/shard_map/all_to_all | solution.py:363
  165.6 0.0 copy-done.2
  165.6 40.8 %all_to_all.47.refs_6_ = f32[32,12,8,128]{3,2,1,0:T(8,128)} all-to-all(f32[32,12,8,128]{3,2,1,0:T(8,128)S(1)} %copy-done.2), channel_id=1, replica_groups=mesh['wide'=8,'narrow'=4] {'wide','narrow'}, dimensions={0} | all-to-all | bytes 3145728 | tf_op jit(solution)/shard_map/all_to_all | solution.py:363
  206.4 3.2 all-to-all-start.7
  209.6 12.2 %shard_map.313 = f32[8,4,2,32,128]{4,3,2,1,0:T(8,128)} custom-call(f32[6,256,1]{2,1,0:T(8,128)} %constant.47.clone.refs_0_, f32[6,1,512]{2,1,0:T(1,128)} %constant.48.clone.refs_1_, bf16[2,512,512]{2,1,0:T(8,128)(2,1)} %constant.49.clone.refs_2_, bf16[2,512,512]{2,1,0:T(8,128)(2,1)} %constant.50.clone.refs_3_, bf16[2,512,256]{2,1,0:T(8,128)(2,1)} %constant.51.clone.refs_4_, ...), custom_call_target="tpu_custom_call" | custom-call | flops 6039797760 | bytes 5767168 | tf_op jit(solution)/shard_map/pallas_call | solution.py:277
  221.7 25.2 %all-to-all-done.7.refs_6_ = f32[32,12,8,128]{3,2,1,0:T(8,128)S(1)} async-done(((f32[32,12,8,128]{3,2,1,0:T(8,128)}), f32[32,12,8,128]{3,2,1,0:T(8,128)S(1)}, u32[]{:S(2)}, u32[]{:S(2)}) %all-to-all-start.7) | async-done | bytes 1572896 | tf_op jit(solution)/shard_map/all_to_all | solution.py:363
  246.9 0.0 copy-start.1
  246.9 3.2 all-to-all-start.2
  250.1 12.2 %shard_map.314 = f32[8,4,2,32,128]{4,3,2,1,0:T(8,128)} custom-call(f32[6,256,1]{2,1,0:T(8,128)} %constant.47.clone.refs_0_, f32[6,1,512]{2,1,0:T(1,128)} %constant.48.clone.refs_1_, bf16[2,512,512]{2,1,0:T(8,128)(2,1)} %constant.49.clone.refs_2_, bf16[2,512,512]{2,1,0:T(8,128)(2,1)} %constant.50.clone.refs_3_, bf16[2,512,256]{2,1,0:T(8,128)(2,1)} %constant.51.clone.refs_4_, ...), custom_call_target="tpu_custom_call" | custom-call | flops 6039797760 | bytes 5767168 | tf_op jit(solution)/shard_map/pallas_call | solution.py:277
  262.3 0.0 copy-done.1
  262.3 14.2 %all-to-all-done.2.refs_2_ = f32[32,2,32,128]{3,2,1,0:T(8,128)S(1)} async-done(((f32[32,2,32,128]{3,2,1,0:T(8,128)}), f32[32,2,32,128]{3,2,1,0:T(8,128)S(1)}, u32[]{:S(2)}, u32[]{:S(2)}) %all-to-all-start.2) | async-done | bytes 1048608 | tf_op jit(solution)/shard_map/all_to_all | solution.py:363
  276.5 0.0 copy-start.4
  276.5 3.2 all-to-all-start.4
  279.6 12.2 %shard_map.315 = f32[8,4,2,32,128]{4,3,2,1,0:T(8,128)} custom-call(f32[6,256,1]{2,1,0:T(8,128)} %constant.47.clone.refs_0_, f32[6,1,512]{2,1,0:T(1,128)} %constant.48.clone.refs_1_, bf16[2,512,512]{2,1,0:T(8,128)(2,1)} %constant.49.clone.refs_2_, bf16[2,512,512]{2,1,0:T(8,128)(2,1)} %constant.50.clone.refs_3_, bf16[2,512,256]{2,1,0:T(8,128)(2,1)} %constant.51.clone.refs_4_, ...), custom_call_target="tpu_custom_call" | custom-call | flops 6039797760 | bytes 5767168 | tf_op jit(solution)/shard_map/pallas_call | solution.py:277
  291.8 0.0 copy-done.4
  291.8 14.2 %all-to-all-done.4.refs_3_ = f32[32,2,32,128]{3,2,1,0:T(8,128)S(1)} async-done(((f32[32,2,32,128]{3,2,1,0:T(8,128)}), f32[32,2,32,128]{3,2,1,0:T(8,128)S(1)}, u32[]{:S(2)}, u32[]{:S(2)}) %all-to-all-start.4) | async-done | bytes 1048608 | tf_op jit(solution)/shard_map/all_to_all | solution.py:363
  306.0 0.0 copy-start.5
  306.0 3.2 all-to-all-start.6
  309.1 12.2 %shard_map.316 = f32[8,4,2,32,128]{4,3,2,1,0:T(8,128)} custom-call(f32[6,256,1]{2,1,0:T(8,128)} %constant.47.clone.refs_0_, f32[6,1,512]{2,1,0:T(1,128)} %constant.48.clone.refs_1_, bf16[2,512,512]{2,1,0:T(8,128)(2,1)} %constant.49.clone.refs_2_, bf16[2,512,512]{2,1,0:T(8,128)(2,1)} %constant.50.clone.refs_3_, bf16[2,512,256]{2,1,0:T(8,128)(2,1)} %constant.51.clone.refs_4_, ...), custom_call_target="tpu_custom_call" | custom-call | flops 6039797760 | bytes 5767168 | tf_op jit(solution)/shard_map/pallas_call | solution.py:277
  321.3 0.0 copy-done.5
  321.3 14.2 %all-to-all-done.6.refs_4_ = f32[32,2,32,128]{3,2,1,0:T(8,128)S(1)} async-done(((f32[32,2,32,128]{3,2,1,0:T(8,128)}), f32[32,2,32,128]{3,2,1,0:T(8,128)S(1)}, u32[]{:S(2)}, u32[]{:S(2)}) %all-to-all-start.6) | async-done | bytes 1048608 | tf_op jit(solution)/shard_map/all_to_all | solution.py:363
  335.5 0.0 copy-start.6
  335.5 3.2 all-to-all-start.8
  338.7 26.4 %all-to-all-done.8.refs_5_ = f32[32,2,32,128]{3,2,1,0:T(8,128)S(1)} async-done(((f32[32,2,32,128]{3,2,1,0:T(8,128)}), f32[32,2,32,128]{3,2,1,0:T(8,128)S(1)}, u32[]{:S(2)}, u32[]{:S(2)}) %all-to-all-start.8) | async-done | bytes 1048608 | tf_op jit(solution)/shard_map/all_to_all | solution.py:363
  365.0 0.0 copy-start.7
  365.0 0.0 copy-done.6
  365.0 1.0 copy-done.7
  366.0 8.0 %shard_map.317 = (f32[64,32,256]{2,1,0:T(8,128)}, f32[64,32,256]{2,1,0:T(8,128)}) custom-call(s32[1]{0:T(128)} %bitcast.refs_0_, bf16[2,256,512]{2,1,0:T(8,128)(2,1)} %constant.53.clone.refs_1_, f32[32,2,32,128]{3,2,1,0:T(8,128)} %copy-done.4, f32[32,2,32,128]{3,2,1,0:T(8,128)} %copy-done.5, f32[32,2,32,128]{3,2,1,0:T(8,128)} %copy-done.6, ...), custom_call_target="tpu_custom_call" | custom-call | flops 3221225472 | bytes 8388608 | tf_op jit(solution)/shard_map/pallas_call | solution.py:346
Async XLA Ops:
  5.5 55.4 %all-to-all-start = ((f32[32,4,32,128]{3,2,1,0:T(8,128)}), f32[32,4,32,128]{3,2,1,0:T(8,128)S(1)}, u32[]{:S(2)}, u32[]{:S(2)}) async-start(f32[32,4,32,128]{3,2,1,0:T(8,128)} %bitcast.7), calls=%async_computation | async-start | bytes 4194304 | tf_op jit(solution)/shard_map/all_to_all | solution.py:363
  60.9 1.3 copy-start
  83.5 41.3 %copy-start.3 = (f32[32,12,8,128]{3,2,1,0:T(8,128)S(1)}, f32[32,12,8,128]{3,2,1,0:T(8,128)}, u32[]{:S(2)}) copy-start(f32[32,12,8,128]{3,2,1,0:T(8,128)} %get-tuple-element.7) | copy-start | bytes 4718596
  124.8 40.8 %copy-start.2 = (f32[32,12,8,128]{3,2,1,0:T(8,128)S(1)}, f32[32,12,8,128]{3,2,1,0:T(8,128)}, u32[]{:S(2)}) copy-start(f32[32,12,8,128]{3,2,1,0:T(8,128)} %get-tuple-element.8) | copy-start | bytes 4718596
  206.4 40.5 %all-to-all-start.7 = ((f32[32,12,8,128]{3,2,1,0:T(8,128)}), f32[32,12,8,128]{3,2,1,0:T(8,128)S(1)}, u32[]{:S(2)}, u32[]{:S(2)}) async-start(f32[32,12,8,128]{3,2,1,0:T(8,128)} %get-tuple-element.9), calls=%async_computation.7 | async-start | bytes 3145728 | tf_op jit(solution)/shard_map/all_to_all | solution.py:363
  246.9 15.4 %copy-start.1 = (f32[32,12,8,128]{3,2,1,0:T(8,128)}, f32[32,12,8,128]{3,2,1,0:T(8,128)S(1)}, u32[]{:S(2)}) copy-start(f32[32,12,8,128]{3,2,1,0:T(8,128)S(1)} %all-to-all-done.7.refs_6_) | copy-start | bytes 4718596
  246.9 29.5 %all-to-all-start.2 = ((f32[32,2,32,128]{3,2,1,0:T(8,128)}), f32[32,2,32,128]{3,2,1,0:T(8,128)S(1)}, u32[]{:S(2)}, u32[]{:S(2)}) async-start(f32[32,2,32,128]{3,2,1,0:T(8,128)} %bitcast.11), calls=%async_computation.2 | async-start | bytes 2097152 | tf_op jit(solution)/shard_map/all_to_all | solution.py:363
  276.5 15.3 %copy-start.4 = (f32[32,2,32,128]{3,2,1,0:T(8,128)}, f32[32,2,32,128]{3,2,1,0:T(8,128)S(1)}, u32[]{:S(2)}) copy-start(f32[32,2,32,128]{3,2,1,0:T(8,128)S(1)} %all-to-all-done.2.refs_2_) | copy-start | bytes 3145732
  276.5 29.5 %all-to-all-start.4 = ((f32[32,2,32,128]{3,2,1,0:T(8,128)}), f32[32,2,32,128]{3,2,1,0:T(8,128)S(1)}, u32[]{:S(2)}, u32[]{:S(2)}) async-start(f32[32,2,32,128]{3,2,1,0:T(8,128)} %bitcast.12), calls=%async_computation.4 | async-start | bytes 2097152 | tf_op jit(solution)/shard_map/all_to_all | solution.py:363
  306.0 15.4 %copy-start.5 = (f32[32,2,32,128]{3,2,1,0:T(8,128)}, f32[32,2,32,128]{3,2,1,0:T(8,128)S(1)}, u32[]{:S(2)}) copy-start(f32[32,2,32,128]{3,2,1,0:T(8,128)S(1)} %all-to-all-done.4.refs_3_) | copy-start | bytes 3145732
  306.0 29.5 %all-to-all-start.6 = ((f32[32,2,32,128]{3,2,1,0:T(8,128)}), f32[32,2,32,128]{3,2,1,0:T(8,128)S(1)}, u32[]{:S(2)}, u32[]{:S(2)}) async-start(f32[32,2,32,128]{3,2,1,0:T(8,128)} %bitcast.10), calls=%async_computation.6 | async-start | bytes 2097152 | tf_op jit(solution)/shard_map/all_to_all | solution.py:363
  335.5 29.5 %copy-start.6 = (f32[32,2,32,128]{3,2,1,0:T(8,128)}, f32[32,2,32,128]{3,2,1,0:T(8,128)S(1)}, u32[]{:S(2)}) copy-start(f32[32,2,32,128]{3,2,1,0:T(8,128)S(1)} %all-to-all-done.6.refs_4_) | copy-start | bytes 3145732
  335.5 29.5 %all-to-all-start.8 = ((f32[32,2,32,128]{3,2,1,0:T(8,128)}), f32[32,2,32,128]{3,2,1,0:T(8,128)S(1)}, u32[]{:S(2)}, u32[]{:S(2)}) async-start(f32[32,2,32,128]{3,2,1,0:T(8,128)} %bitcast.9), calls=%async_computation.8 | async-start | bytes 2097152 | tf_op jit(solution)/shard_map/all_to_all | solution.py:363
  365.0 1.0 copy-start.7

commit v2 on v1

v2 whole, which is shorter than its diff:
```python
import math

import jax
import jax.numpy as jnp
import ml_dtypes
import numpy as np
from jax import lax
from jax.experimental import pallas as pl
from jax.experimental.pallas import tpu as pltpu
from jax.sharding import PartitionSpec as P

AXES = ("wide", "narrow")
TILE = 128
LIMIT = 56 * 1024 * 1024


def angles(rows, columns, length):
    return (2.0 * math.pi / length) * (np.outer(rows, columns) % length)


def split_table(table):
    table = np.asarray(table, np.float64)
    high = table.astype(ml_dtypes.bfloat16)
    low = (table - high.astype(np.float64)).astype(ml_dtypes.bfloat16)
    return np.stack([high, low])


def split(value):
    high = value.astype(jnp.bfloat16)
    low = (value - high.astype(jnp.float32)).astype(jnp.bfloat16)
    return high, low


def product(left, right, contract=((1,), (0,))):
    (left_axis,), (right_axis,) = contract
    left = jnp.concatenate([left[0], left[0], left[1]], axis=left_axis)
    right = jnp.concatenate([right[0], right[1], right[0]], axis=right_axis)
    return lax.dot_general(
        left, right, (contract, ((), ())), preferred_element_type=jnp.float32
    )


def pair(ref):
    return ref[0], ref[1]


def signed_wave(index, length):
    index = np.asarray(index)
    return np.where(index < length // 2, index, index - length) * (2.0 * math.pi / length)


def params(steps):
    return pltpu.CompilerParams(
        vmem_limit_bytes=LIMIT, dimension_semantics=("arbitrary",) * steps
    )


def whole(shape):
    return pl.BlockSpec(shape, lambda *_: (0,) * len(shape))


def cost(macs, moved):
    return pl.CostEstimate(flops=6 * macs, bytes_accessed=moved, transcendentals=0)


def third_kernel(table_ref, density_ref, out_ref):
    rows_x, rows_y, length = density_ref.shape
    half = out_ref.shape[0]
    flat = out_ref.reshape(half * rows_x, 2 * rows_y)
    table = pair(table_ref)
    left_half = lax.broadcasted_iota(jnp.int32, (half, 2 * rows_y), 1) < rows_y
    group = 4
    for first in range(0, rows_x, group):
        block = density_ref[first : first + group].reshape(group * rows_y, length)
        result = product(table, split(block), ((1,), (1,)))
        for inner in range(0, group, 2):
            lanes = slice(inner * rows_y, (inner + 2) * rows_y)
            real = result[:half, lanes]
            imag = result[half:, lanes]
            even = jnp.where(left_half, real, pltpu.roll(imag, rows_y, 1))
            odd = jnp.where(left_half, pltpu.roll(real, rows_y, 1), imag)
            flat[pl.ds(first + inner, half, stride=rows_x), :] = even
            flat[pl.ds(first + inner + 1, half, stride=rows_x), :] = odd


def third_pass(density):
    rows_x, rows_y, length = density.shape
    half = length // 2
    angle = angles(np.arange(half), np.arange(length), length)
    table = split_table(np.concatenate([np.cos(angle), -np.sin(angle)]))
    step = min(8, rows_x)
    return pl.pallas_call(
        third_kernel,
        grid=(rows_x // step,),
        in_specs=[
            whole(table.shape),
            pl.BlockSpec((step, rows_y, length), lambda i: (i, 0, 0)),
        ],
        out_specs=pl.BlockSpec((half, step, 2 * rows_y), lambda i: (0, i, 0)),
        out_shape=jax.ShapeDtypeStruct((half, rows_x, 2 * rows_y), jnp.float32),
        compiler_params=params(1),
        cost_estimate=cost(density.size * length, 8 * density.size),
    )(table, density)


def turn(angle):
    cosine, sine = np.cos(angle), np.sin(angle)
    return np.block([[cosine, -sine], [sine, cosine]])


def spectrum_kernel(per_c, slab, wave_c_ref, a_ref, b_ref, second_ref, first_ref, back_ref, in_ref, *outs):
    wide, narrow, _, rows_x, lanes = in_ref.shape
    length = wide * rows_x
    half = length // 2

    def column(n):
        return in_ref[:, n, 0].reshape(length, lanes)

    low = jnp.concatenate([column(n) for n in range(narrow // 2)], axis=1)
    high = jnp.concatenate([column(n) for n in range(narrow // 2, narrow)], axis=1)
    planes = [
        product(split(low + high), pair(second_ref.at[0])),
        product(split(low - high), pair(second_ref.at[1])),
    ]

    def stacked(sign):
        return jnp.concatenate(
            [
                jnp.concatenate(
                    [
                        plane[:half, part * half : (part + 1) * half]
                        + sign * plane[half:, part * half : (part + 1) * half]
                        for plane in planes
                    ],
                    axis=1,
                )
                for part in range(2)
            ],
            axis=0,
        )

    wave_b = b_ref[0]
    wave_c = wave_c_ref[pl.program_id(0)]
    field = []
    for parity, sign in ((0, 1.0), (1, -1.0)):
        value = product(pair(first_ref.at[parity]), split(stacked(sign)))
        wave_a = a_ref[0, parity]
        squared = wave_a * wave_a + (wave_b * wave_b + wave_c * wave_c)
        safe = jnp.where(squared > 0, squared, 1.0)
        usable = a_ref[1, parity] * b_ref[1] * (1.0 / float(length) ** 3)
        smooth = jnp.where(squared > 0, jnp.exp(-0.5 * squared) / safe, 0.0) * usable
        field.append(value * jnp.concatenate([smooth, smooth], axis=0))
    tiles, message, tile = outs[0].shape[1:]
    devices = outs[0].shape[0]
    near = devices // 2
    count = slab // len(outs)
    flats = [ref.reshape(devices * tiles * message, tile) for ref in outs]
    for number in range(3):
        even = product(pair(back_ref.at[0]), split(field[0]))
        odd = product(pair(back_ref.at[1]), split(field[1]))
        for side, value in enumerate((even + odd, even - odd)):
            for group in range(len(outs)):
                for x in range(count):
                    for spot in range(tiles // 3):
                        parity, part = divmod(spot, 2)
                        start = part * half + (group * count + x) * near
                        at = (
                            (side * near * tiles + number * (tiles // 3) + spot) * message
                            + x * per_c
                            + pl.program_id(0)
                        )
                        flats[group][pl.ds(at, near, stride=tiles * message), :] = value[
                            start : start + near, parity * tile : (parity + 1) * tile
                        ]
        if number < 2:
            for parity in range(2):
                wave_a = a_ref[0, parity]
                field[parity] = field[parity] * jnp.concatenate([wave_a, wave_a], axis=0)


def halves(length):
    return np.arange(length).reshape(length // 2, 2).T


def spectrum_pass(received, waves_c, devices, chunks):
    wide, narrow, per_c, rows_x, lanes = received.shape
    length = wide * rows_x
    rows_y = lanes // 2
    half = length // 2
    near = np.arange(half)
    split_index = halves(length)
    slab = length // devices
    second, first, back = [], [], []
    order = near.reshape(devices // 2, slab).T.reshape(-1)
    for index in split_index:
        table = turn(-angles(index, near, length)).reshape(2, half, 2, narrow // 2, rows_y)
        second.append(table.transpose(3, 2, 4, 0, 1).reshape(length, length))
        first.append(turn(-angles(index, near, length)))
        back.append(turn(angles(order, index, length)))
    tables = [np.stack([split_table(table) for table in each]) for each in (second, first, back)]
    wave = signed_wave(split_index, length)
    a_table = np.stack([wave, split_index != half]).astype(np.float32)[..., None]
    b_table = a_table.reshape(2, 1, length)
    out_shape = (devices, 3 * 2 * length // TILE, slab // chunks * per_c, TILE)

    def body(*refs):
        spectrum_kernel(per_c, slab, *refs)

    return pl.pallas_call(
        body,
        grid=(per_c,),
        in_specs=[
            pl.BlockSpec(memory_space=pltpu.SMEM),
            whole(a_table.shape),
            whole(b_table.shape),
            *[whole(table.shape) for table in tables],
            pl.BlockSpec((wide, narrow, 1, rows_x, lanes), lambda i: (0, 0, i, 0, 0)),
        ],
        out_specs=[whole(out_shape)] * chunks,
        out_shape=[jax.ShapeDtypeStruct(out_shape, jnp.float32)] * chunks,
        compiler_params=params(1),
        cost_estimate=cost(per_c * 10 * length**3, 20 * per_c * length**2 * 2),
    )(waves_c, a_table, b_table, *tables, received)


def shear_kernel(
    pairs_x, row_ref, lane_ref, second_ref, third_ref, ahead_ref, last_ref, in_ref, out_ref, shear_ref
):
    step = pl.program_id(1)
    length = shear_ref.shape[1]
    half = length // 2

    @pl.when(step == 0)
    def _():
        shear_ref[...] = jnp.zeros_like(shear_ref)

    devices, tiles, message, tile = in_ref.shape
    field = jnp.concatenate(
        [in_ref[:, spot].reshape(devices * message, tile) for spot in range(tiles)], axis=1
    )
    field = field * row_ref[0] * lane_ref[0]
    even = product(split(field[:, :length]), pair(second_ref.at[0]))
    odd = product(split(field[:, length:]), pair(second_ref.at[1]))
    near, far = even + odd, even - odd
    field = jnp.concatenate(
        [
            jnp.concatenate([near[:, :half], far[:, :half]], axis=1),
            jnp.concatenate([near[:, half:], far[:, half:]], axis=1),
        ],
        axis=0,
    )
    field = product(pair(third_ref), split(field))
    shear_ref[...] += field * field

    @pl.when(step == 5)
    def _():
        wide, narrow, _, rows_b, lanes = out_ref.shape
        ahead = product(pair(ahead_ref), split(shear_ref[...]), ((1,), (1,)))
        for spot in range(pairs_x):
            part = slice(spot * length, (spot + 1) * length)
            value = jnp.concatenate([ahead[:length, part], ahead[length:, part]], axis=1)
            value = product(split(value), pair(last_ref))
            for w in range(wide):
                for n in range(narrow):
                    out_ref[w, n, spot] = value[
                        w * rows_b : (w + 1) * rows_b, n * lanes : (n + 1) * lanes
                    ]


def shear_pass(received, wide, narrow, pairs_x, per_c):
    devices, tiles, message, tile = received.shape
    pairs = message // (pairs_x * per_c)
    rows = devices * pairs_x * per_c
    length = tiles * tile // 6
    half = length // 2
    index = np.arange(length)
    angle = angles(index, index, length)
    cosine, sine = np.cos(angle), np.sin(angle)
    split_index = halves(length)
    second = np.stack(
        [split_table(turn(angles(np.arange(half), b, length)).T) for b in split_index]
    )
    spots = np.arange(rows).reshape(devices, pairs_x, per_c)
    row_c = (np.arange(devices)[:, None, None] * per_c + np.arange(per_c)[None, None, :]) + 0 * spots
    row_c = row_c.reshape(-1)
    row_x = (np.arange(pairs_x)[None, :, None] + 0 * spots).reshape(-1)
    weight = np.where(row_c == 0, 1.0, 2.0)
    angle = angles(index, row_c, length)
    third = np.concatenate(
        [
            np.concatenate(
                [(row_x == x) * weight * np.cos(angle), (row_x == x) * weight * -np.sin(angle)], axis=1
            )
            for x in range(pairs_x)
        ]
    )
    ahead = np.concatenate([cosine, -sine])
    cos_z = cosine.reshape(length, narrow, 1, length // narrow)
    sin_z = sine.reshape(length, narrow, 1, length // narrow)
    last = np.concatenate(
        [
            np.concatenate([cos_z, -sin_z], axis=2).reshape(length, 2 * length),
            np.concatenate([sin_z, cos_z], axis=2).reshape(length, 2 * length),
        ]
    )
    wave = signed_wave(index, length)
    wave_rows = wave[row_c]
    wave_lanes = np.stack([wave[split_index]] * 2, axis=1).reshape(-1)
    twice = math.sqrt(2.0)
    one_row, one_lane = np.ones_like(wave_rows), np.ones_like(wave_lanes)
    row_factor = np.stack(
        [one_row, twice * one_row, twice * wave_rows, one_row, twice * wave_rows, wave_rows**2]
    ).astype(np.float32)[:, :, None]
    lane_factor = np.stack(
        [one_lane, wave_lanes, one_lane, wave_lanes**2, wave_lanes, one_lane]
    ).astype(np.float32)[:, None, :]
    tables = [second] + [split_table(table) for table in (third, ahead, last)]
    block = (wide, narrow, pairs_x, length // wide, 2 * length // narrow)
    out_shape = (wide, narrow, pairs * pairs_x, length // wide, 2 * length // narrow)

    def body(*refs):
        shear_kernel(pairs_x, *refs)

    def which(p, i):
        return (0, 2 - (i >= 1).astype(jnp.int32) - (i >= 3).astype(jnp.int32), p, 0)

    return pl.pallas_call(
        body,
        grid=(pairs, 6),
        in_specs=[
            pl.BlockSpec((1, rows, 1), lambda p, i: (i, 0, 0)),
            pl.BlockSpec((1, 1, 2 * length), lambda p, i: (i, 0, 0)),
            *[whole(table.shape) for table in tables],
            pl.BlockSpec((devices, tiles // 3, pairs_x * per_c, tile), which),
        ],
        out_specs=pl.BlockSpec(block, lambda p, i: (0, 0, p, 0, 0)),
        out_shape=jax.ShapeDtypeStruct(out_shape, jnp.float32),
        scratch_shapes=[pltpu.VMEM((pairs_x * length, length), jnp.float32)],
        compiler_params=params(2),
        cost_estimate=cost(pairs * 48 * length**3, 4 * received.size + 4 * 2**20),
    )(row_factor, lane_factor, *tables, received)


def first_kernel(scale, anchor_ref, table_ref, *refs):
    ins, (real_ref, imag_ref, real_tile_ref, imag_tile_ref) = refs[:-4], refs[-4:]
    devices, count, rows_b, lanes = ins[0].shape
    half_c, length = lanes // 2, real_ref.shape[2]
    half = length // 2
    tables = [pair(table_ref.at[0]), pair(table_ref.at[1])]
    flats = [ref.reshape(devices * count * rows_b, lanes) for ref in ins]
    tile = real_tile_ref.shape[2]
    spot_c = lax.broadcasted_iota(jnp.int32, (half_c, half), 0)
    spot_a = lax.broadcasted_iota(jnp.int32, (half_c, half), 1)
    is_anchor = (anchor_ref[0] == 1) & (pl.program_id(0) == 0)
    anchor = (spot_c == 0) & (spot_a == 0) & is_anchor
    group = min(8, rows_b)
    spots = devices * count // 2
    for first in range(0, rows_b, group):
        sums = []
        for parity in range(2):
            columns = []
            for b in range(first, first + group):
                start = parity * rows_b + b
                column = jnp.concatenate(
                    [flat[pl.ds(start, spots, stride=2 * rows_b), :] for flat in flats], axis=0
                ).T
                columns.append(jnp.concatenate([column[:half_c], column[half_c:]], axis=1))
            sums.append(product(split(jnp.concatenate(columns, axis=0)), tables[parity]))
        even, odd = sums
        for side, value in enumerate((even + odd, even - odd)):
            value = value * scale
            for number in range(group):
                b = first + number
                rows = slice(number * half_c, (number + 1) * half_c)
                real, imag = value[rows, :half], value[rows, half:]
                if b == 0 and side == 0:
                    real = jnp.where(anchor, 0.0, real)
                    imag = jnp.where(anchor, 0.0, imag)
                for spot in range(half // tile):
                    part = slice(spot * tile, (spot + 1) * tile)
                    at = side * (half // tile) + spot
                    real_tile_ref[at, pl.ds(b, half_c, stride=rows_b), :] = real[:, part]
                    imag_tile_ref[at, pl.ds(b, half_c, stride=rows_b), :] = imag[:, part]
    for spot in range(length // tile):
        part = slice(spot * tile, (spot + 1) * tile)
        real_ref[:, :, part] = real_tile_ref[spot].reshape(half_c, rows_b, tile)
        imag_ref[:, :, part] = imag_tile_ref[spot].reshape(half_c, rows_b, tile)


def first_pass(parts, is_anchor, length):
    devices, count, rows_b, lanes = parts[0].shape
    groups = len(parts)
    index = np.arange(length).reshape(devices, groups, count // 2, 2)
    index = index.transpose(3, 1, 0, 2).reshape(2, -1)
    table = np.stack(
        [split_table(turn(-angles(np.arange(length // 2), x, length)).T) for x in index]
    )
    step = min(8, rows_b)
    scale = 1.0 / float(length) ** 1.5

    def body(*refs):
        first_kernel(scale, *refs)

    out_shape = jax.ShapeDtypeStruct((lanes // 2, rows_b, length), jnp.float32)
    return pl.pallas_call(
        body,
        grid=(rows_b // step,),
        in_specs=[
            pl.BlockSpec(memory_space=pltpu.SMEM),
            whole(table.shape),
            *[pl.BlockSpec((devices, count, step, lanes), lambda i: (0, 0, i, 0))] * groups,
        ],
        out_specs=[pl.BlockSpec((lanes // 2, step, length), lambda i: (0, i, 0))] * 2,
        out_shape=[out_shape] * 2,
        scratch_shapes=[pltpu.VMEM((length // TILE, lanes // 2 * step, TILE), jnp.float32)] * 2,
        compiler_params=params(1),
        cost_estimate=cost(rows_b * lanes * length * length, 8 * rows_b * lanes * length),
    )(is_anchor, table, *parts)


def transpose(value):
    return lax.all_to_all(value, AXES, split_axis=0, concat_axis=0, tiled=True)


def solution(mesh):
    wide, narrow = mesh.shape["wide"], mesh.shape["narrow"]
    devices = wide * narrow

    def per_device(density):
        rows_x, rows_y, length = density.shape
        per_c = length // 2 // devices
        pairs_x = 2
        spot_wide, spot_narrow = lax.axis_index("wide"), lax.axis_index("narrow")
        here = spot_wide * narrow + spot_narrow
        planes = third_pass(density).reshape(devices, per_c, rows_x, 2 * rows_y)
        planes = transpose(planes).reshape(wide, narrow, per_c, rows_x, 2 * rows_y)
        waves_c = (here * per_c + jnp.arange(per_c, dtype=jnp.int32)).astype(jnp.float32)
        waves_c = waves_c * (2.0 * math.pi / length)
        chunks = spectrum_pass(planes, waves_c, devices, min(2, length // devices // pairs_x))
        is_anchor = (here == 0).astype(jnp.int32).reshape(1)
        parts = []
        for chunk in chunks:
            part = shear_pass(transpose(chunk), wide, narrow, pairs_x, per_c)
            part = part.reshape((devices,) + part.shape[2:])
            parts.append(transpose(part))
        return tuple(first_pass(parts, is_anchor, length))

    return jax.shard_map(
        per_device,
        mesh=mesh,
        in_specs=(P("wide", "narrow", None),),
        out_specs=(P("narrow", "wide", None), P("narrow", "wide", None)),
        check_vma=False,
    )
```

time: 375 us -> 342 us (0.912)
  blocking collectives: 123 us -> 74.8 us
  waiting for transfers between devices: 142 us -> 176 us
  Pallas kernels: 82.9 us -> 66.7 us
  starting transfers between devices: 22.9 us -> 18.6 us
    all_to_all x3 -> x1, blocking collectives: 123 us -> 74.8 us  [transpose(): return lax.all_to_all(value, AXES, split_axis=0, concat_axis=0, tiled=True)]
    all_to_all x6 -> x4, waiting for transfers between devices: 142 us -> 176 us  [transpose(): return lax.all_to_all(value, AXES, split_axis=0, concat_axis=0, tiled=True)]
    pallas_call x4 -> x2, Pallas kernels: 48.7 us -> 38.3 us  [shear_pass(): pl.pallas_call(body, grid=(pairs, 6), in_specs=[pl.BlockSpec((1, rows, 1)...]
    pallas_call x1, Pallas kernels: 21.3 us -> 16.1 us  [spectrum_pass(): pl.pallas_call(body, grid=(per_c,), in_specs=[pl.BlockSpec(memory_space=p...]
    all_to_all x6 -> x4, starting transfers between devices: 22.9 us -> 18.6 us  [transpose(): return lax.all_to_all(value, AXES, split_axis=0, concat_axis=0, tiled=True)]
  transfers between devices with their start and end apart: 6 -> 4, of which waited for: 6 -> 4; matrix products, arithmetic and copies ran while one was open for 0% -> 0% of each run, Pallas kernels for 13% -> 11%
where the time goes in v2:
time: 342 us
  waiting for transfers between devices  176 us (51%)
  blocking collectives  74.8 us (22%)
  Pallas kernels  66.7 us (20%)
  starting transfers between devices  18.6 us (5%)
  local copies, waits for them, and re-layouts  4.27 us (1%)
    all_to_all x4, waiting for transfers between devices, transpose(): return lax.all_to_all(value, AXES, split_axis=0, concat_axis=0, tiled=True)  176 us
    all_to_all x1, blocking collectives, transpose(): return lax.all_to_all(value, AXES, split_axis=0, concat_axis=0, tiled=True)  74.8 us
    pallas_call x2, Pallas kernels, shear_pass(): pl.pallas_call(body, grid=(pairs, 6), in_specs=[pl.BlockSpec((1, rows, 1)...  38.3 us
    all_to_all x4, starting transfers between devices, transpose(): return lax.all_to_all(value, AXES, split_axis=0, concat_axis=0, tiled=True)  18.6 us
    pallas_call x1, Pallas kernels, spectrum_pass(): pl.pallas_call(body, grid=(per_c,), in_specs=[pl.BlockSpec(memory_space=p...  16.1 us
    pallas_call x1, Pallas kernels, first_pass(): pl.pallas_call(body, grid=(rows_b // step,), in_specs=[pl.BlockSpec(memor...  7.38 us
  transfers between devices with their start and end apart: 4, of which 4 were waited for; matrix products, arithmetic and copies ran while one was open for 0% of the time, Pallas kernels for 11%

profile of v2, /device:TPU:1, one launch (start us, length us, event | category | flops | bytes accessed | tf_op | source)
XLA Modules:
  0.0 341.6 jit_solution(4680567210984370775)
XLA Ops:
  0.6 4.9 %shard_map.203 = f32[128,32,128]{2,1,0:T(8,128)} custom-call(bf16[2,256,256]{2,1,0:T(8,128)(2,1)} %constant.39.clone.table_ref, f32[32,64,256]{2,1,0:T(8,128)} %density_ref.1), custom_call_target="tpu_custom_call" | custom-call | flops 805306368 | bytes 4194304 | tf_op jit(solution)/shard_map/pallas_call | solution.py:92
  5.5 7.1 %all-to-all-start = ((f32[32,4,32,128]{3,2,1,0:T(8,128)}), f32[32,4,32,128]{3,2,1,0:T(8,128)S(1)}, u32[]{:S(2)}, u32[]{:S(2)}) async-start(f32[32,4,32,128]{3,2,1,0:T(8,128)} %bitcast.5), calls=%async_computation | async-start | bytes 4194304 | tf_op jit(solution)/shard_map/all_to_all | solution.py:422
  12.6 0.5 convert_multiply_fusion.refs_0_
  13.1 47.7 %all-to-all-done = f32[32,4,32,128]{3,2,1,0:T(8,128)S(1)} async-done(((f32[32,4,32,128]{3,2,1,0:T(8,128)}), f32[32,4,32,128]{3,2,1,0:T(8,128)S(1)}, u32[]{:S(2)}, u32[]{:S(2)}) %all-to-all-start) | async-done | bytes 2097184 | tf_op jit(solution)/shard_map/all_to_all | solution.py:422
  60.9 0.0 copy-start.1
  60.9 1.3 copy-done.1
  62.2 16.1 %shard_map.204 = (f32[32,12,16,128]{3,2,1,0:T(8,128)}, f32[32,12,16,128]{3,2,1,0:T(8,128)}) custom-call(f32[4]{0:T(128)} %convert_multiply_fusion.refs_0_, f32[2,2,128,1]{3,2,1,0:T(8,128)} %constant.40.clone.refs_1_, f32[2,1,256]{2,1,0:T(1,128)} %constant.41.clone.refs_2_, bf16[2,2,256,256]{3,2,1,0:T(8,128)(2,1)} %constant.42.clone.refs_3_, ...), custom_call_target="tpu_custom_call" | custom-call | flops 4026531840 | bytes 10485760 | tf_op jit(solution)/shard_map/pallas_call | solution.py:209
  78.3 74.8 %all_to_all.25.refs_6_ = f32[32,12,16,128]{3,2,1,0:T(8,128)} all-to-all(f32[32,12,16,128]{3,2,1,0:T(8,128)} %get-tuple-element.4), channel_id=1, replica_groups=mesh['wide'=8,'narrow'=4] {'wide','narrow'}, dimensions={0} | all-to-all | bytes 6291456 | tf_op jit(solution)/shard_map/all_to_all | solution.py:422
  153.1 3.2 all-to-all-start.3
  156.2 19.2 %shard_map.205 = f32[8,4,4,32,128]{4,3,2,1,0:T(8,128)} custom-call(f32[6,256,1]{2,1,0:T(8,128)} %constant.45.clone.refs_0_, f32[6,1,512]{2,1,0:T(1,128)} %constant.46.clone.refs_1_, bf16[2,2,256,256]{3,2,1,0:T(8,128)(2,1)} %constant.43.clone.refs_4_.refs_2_, bf16[2,512,512]{2,1,0:T(8,128)(2,1)} %constant.47.clone.refs_3_, ...), custom_call_target="tpu_custom_call" | custom-call | flops 9663676416 | bytes 7340032 | tf_op jit(solution)/shard_map/pallas_call | solution.py:327
  175.4 51.0 %all-to-all-done.3.refs_6_ = f32[32,12,16,128]{3,2,1,0:T(8,128)S(1)} async-done(((f32[32,12,16,128]{3,2,1,0:T(8,128)}), f32[32,12,16,128]{3,2,1,0:T(8,128)S(1)}, u32[]{:S(2)}, u32[]{:S(2)}) %all-to-all-start.3) | async-done | bytes 3145760 | tf_op jit(solution)/shard_map/all_to_all | solution.py:422
  226.4 0.0 copy-start
  226.4 1.6 copy-done
  228.0 4.9 %all-to-all-start.2 = ((f32[32,4,32,128]{3,2,1,0:T(8,128)}), f32[32,4,32,128]{3,2,1,0:T(8,128)}, u32[]{:S(2)}, u32[]{:S(2)}) async-start(f32[32,4,32,128]{3,2,1,0:T(8,128)} %bitcast.8), calls=%async_computation.2 | async-start | bytes 4194304 | tf_op jit(solution)/shard_map/all_to_all | solution.py:422
  233.0 19.2 %shard_map.206 = f32[8,4,4,32,128]{4,3,2,1,0:T(8,128)} custom-call(f32[6,256,1]{2,1,0:T(8,128)} %constant.45.clone.refs_0_, f32[6,1,512]{2,1,0:T(1,128)} %constant.46.clone.refs_1_, bf16[2,2,256,256]{3,2,1,0:T(8,128)(2,1)} %constant.43.clone.refs_4_.refs_2_, bf16[2,512,512]{2,1,0:T(8,128)(2,1)} %constant.47.clone.refs_3_, ...), custom_call_target="tpu_custom_call" | custom-call | flops 9663676416 | bytes 7340032 | tf_op jit(solution)/shard_map/pallas_call | solution.py:327
  252.1 29.1 %all-to-all-done.2.refs_2_ = f32[32,4,32,128]{3,2,1,0:T(8,128)} async-done(((f32[32,4,32,128]{3,2,1,0:T(8,128)}), f32[32,4,32,128]{3,2,1,0:T(8,128)}, u32[]{:S(2)}, u32[]{:S(2)}) %all-to-all-start.2) | async-done | bytes 2097184 | tf_op jit(solution)/shard_map/all_to_all | solution.py:422
  281.2 3.4 all-to-all-start.4
  284.7 48.2 %all-to-all-done.4.refs_3_ = f32[32,4,32,128]{3,2,1,0:T(8,128)S(1)} async-done(((f32[32,4,32,128]{3,2,1,0:T(8,128)}), f32[32,4,32,128]{3,2,1,0:T(8,128)S(1)}, u32[]{:S(2)}, u32[]{:S(2)}) %all-to-all-start.4) | async-done | bytes 2097184 | tf_op jit(solution)/shard_map/all_to_all | solution.py:422
  332.9 0.0 copy-start.2
  332.9 1.3 copy-done.2
  334.2 7.4 %shard_map.207 = (f32[64,32,256]{2,1,0:T(8,128)}, f32[64,32,256]{2,1,0:T(8,128)}) custom-call(s32[1]{0:T(128)} %bitcast.refs_0_, bf16[2,2,256,256]{3,2,1,0:T(8,128)(2,1)} %constant.50.clone.refs_1_, f32[32,4,32,128]{3,2,1,0:T(8,128)} %all-to-all-done.2.refs_2_, f32[32,4,32,128]{3,2,1,0:T(8,128)} %copy-done.2), custom_call_target="tpu_custom_call" | custom-call | flops 1610612736 | bytes 8388608 | tf_op jit(solution)/shard_map/pallas_call | solution.py:405
Async XLA Ops:
  5.5 55.4 %all-to-all-start = ((f32[32,4,32,128]{3,2,1,0:T(8,128)}), f32[32,4,32,128]{3,2,1,0:T(8,128)S(1)}, u32[]{:S(2)}, u32[]{:S(2)}) async-start(f32[32,4,32,128]{3,2,1,0:T(8,128)} %bitcast.5), calls=%async_computation | async-start | bytes 4194304 | tf_op jit(solution)/shard_map/all_to_all | solution.py:422
  60.9 1.3 copy-start.1
  153.1 73.3 %all-to-all-start.3 = ((f32[32,12,16,128]{3,2,1,0:T(8,128)}), f32[32,12,16,128]{3,2,1,0:T(8,128)S(1)}, u32[]{:S(2)}, u32[]{:S(2)}) async-start(f32[32,12,16,128]{3,2,1,0:T(8,128)} %get-tuple-element.5), calls=%async_computation.3 | async-start | bytes 6291456 | tf_op jit(solution)/shard_map/all_to_all | solution.py:422
  226.4 1.6 copy-start
  228.0 53.2 %all-to-all-start.2 = ((f32[32,4,32,128]{3,2,1,0:T(8,128)}), f32[32,4,32,128]{3,2,1,0:T(8,128)}, u32[]{:S(2)}, u32[]{:S(2)}) async-start(f32[32,4,32,128]{3,2,1,0:T(8,128)} %bitcast.8), calls=%async_computation.2 | async-start | bytes 4194304 | tf_op jit(solution)/shard_map/all_to_all | solution.py:422
  281.2 51.7 %all-to-all-start.4 = ((f32[32,4,32,128]{3,2,1,0:T(8,128)}), f32[32,4,32,128]{3,2,1,0:T(8,128)S(1)}, u32[]{:S(2)}, u32[]{:S(2)}) async-start(f32[32,4,32,128]{3,2,1,0:T(8,128)} %bitcast.7), calls=%async_computation.4 | async-start | bytes 4194304 | tf_op jit(solution)/shard_map/all_to_all | solution.py:422
  332.9 1.3 copy-start.2

commit v3 on v2

v3 whole, which is shorter than its diff:
```python
import math

import jax
import jax.numpy as jnp
import ml_dtypes
import numpy as np
from jax import lax
from jax.experimental import pallas as pl
from jax.experimental.pallas import tpu as pltpu
from jax.sharding import PartitionSpec as P

AXES = ("wide", "narrow")
TILE = 128
LIMIT = 56 * 1024 * 1024


def angles(rows, columns, length):
    return (2.0 * math.pi / length) * (np.outer(rows, columns) % length)


def split_table(table):
    table = np.asarray(table, np.float64)
    high = table.astype(ml_dtypes.bfloat16)
    low = (table - high.astype(np.float64)).astype(ml_dtypes.bfloat16)
    return np.stack([high, low])


def split(value):
    high = value.astype(jnp.bfloat16)
    low = (value - high.astype(jnp.float32)).astype(jnp.bfloat16)
    return high, low


def product(left, right, contract=((1,), (0,))):
    (left_axis,), (right_axis,) = contract
    left = jnp.concatenate([left[0], left[0], left[1]], axis=left_axis)
    right = jnp.concatenate([right[0], right[1], right[0]], axis=right_axis)
    return lax.dot_general(
        left, right, (contract, ((), ())), preferred_element_type=jnp.float32
    )


def pair(ref):
    return ref[0], ref[1]


def signed_wave(index, length):
    index = np.asarray(index)
    return np.where(index < length // 2, index, index - length) * (2.0 * math.pi / length)


def params(steps):
    return pltpu.CompilerParams(
        vmem_limit_bytes=LIMIT, dimension_semantics=("arbitrary",) * steps
    )


def whole(shape):
    return pl.BlockSpec(shape, lambda *_: (0,) * len(shape))


def cost(macs, moved):
    return pl.CostEstimate(flops=6 * macs, bytes_accessed=moved, transcendentals=0)


def third_kernel(counts, table_ref, density_ref, *outs):
    rows_x, rows_y, length = density_ref.shape
    wide, sides, ranks = outs[0].shape[:3]
    half = length // 2
    flats = [ref.reshape(math.prod(ref.shape[:5]), 2 * rows_y) for ref in outs]
    table = pair(table_ref)
    left_half = lax.broadcasted_iota(jnp.int32, (half, 2 * rows_y), 1) < rows_y
    group = 4
    for first in range(0, rows_x, group):
        block = density_ref[first : first + group].reshape(group * rows_y, length)
        result = product(table, split(block), ((1,), (1,)))
        for inner in range(0, group, 2):
            lanes = slice(inner * rows_y, (inner + 2) * rows_y)
            real = result[:half, lanes]
            imag = result[half:, lanes]
            even = jnp.where(left_half, real, pltpu.roll(imag, rows_y, 1))
            odd = jnp.where(left_half, pltpu.roll(real, rows_y, 1), imag)
            for x, value in ((first + inner, even), (first + inner + 1, odd)):
                start = 0
                for flat, count in zip(flats, counts):
                    for c in range(count):
                        for rank in range(ranks):
                            for side in range(sides):
                                at = ((side * ranks + rank) * count + c) * rows_x + x
                                stride = sides * ranks * count * rows_x
                                flat[pl.ds(at, wide, stride=stride), :] = value[start : start + wide]
                            start += wide


def third_pass(density, wide, sides, ranks, counts):
    rows_x, rows_y, length = density.shape
    half = length // 2
    per_c = sum(counts)
    order = np.arange(half).reshape(wide, ranks, per_c).transpose(2, 1, 0).reshape(-1)
    angle = angles(order, np.arange(length), length)
    table = split_table(np.concatenate([np.cos(angle), -np.sin(angle)]))
    step = min(8, rows_x)

    def body(*refs):
        third_kernel(counts, *refs)

    return pl.pallas_call(
        body,
        grid=(rows_x // step,),
        in_specs=[
            whole(table.shape),
            pl.BlockSpec((step, rows_y, length), lambda i: (i, 0, 0)),
        ],
        out_specs=[
            pl.BlockSpec(
                (wide, sides, ranks, count, step, 2 * rows_y), lambda i: (0, 0, 0, 0, i, 0)
            )
            for count in counts
        ],
        out_shape=[
            jax.ShapeDtypeStruct((wide, sides, ranks, count, rows_x, 2 * rows_y), jnp.float32)
            for count in counts
        ],
        compiler_params=params(1),
        cost_estimate=cost(density.size * length, 12 * density.size),
    )(table, density)


PAIR = 2


def turn(angle):
    cosine, sine = np.cos(angle), np.sin(angle)
    return np.block([[cosine, -sine], [sine, cosine]])


def spectrum_kernel(
    slab, groups, side_ref, wave_c_ref, a_ref, b_ref, second_ref, first_ref, back_ref, in_ref, *refs
):
    outs = refs[-groups:]
    wide, narrow, _, rows_x, lanes = in_ref.shape
    length = wide * rows_x
    half = length // 2
    quarter = half // 2
    devices, tiles, message, tile = outs[0].shape
    count = slab // groups
    flats = [ref.reshape(devices * tiles * message, tile) for ref in outs]
    side = side_ref[0]
    sign_back = 1.0 - 2.0 * side.astype(jnp.float32)
    wave_b = b_ref[0]
    for c in range(PAIR):

        def column(n):
            return in_ref[:, n, c].reshape(length, lanes)

        low = jnp.concatenate([column(n) for n in range(narrow // 2)], axis=1)
        high = jnp.concatenate([column(n) for n in range(narrow // 2, narrow)], axis=1)
        planes = [
            product(split(low + high), pair(second_ref.at[0])),
            product(split(low - high), pair(second_ref.at[1])),
        ]

        def stacked(sign):
            return jnp.concatenate(
                [
                    jnp.concatenate(
                        [
                            plane[:half, part * half : (part + 1) * half]
                            + sign * plane[half:, part * half : (part + 1) * half]
                            for plane in planes
                        ],
                        axis=1,
                    )
                    for part in range(2)
                ],
                axis=0,
            )

        wave_c = wave_c_ref[pl.program_id(0) * PAIR + c]
        field = []
        for parity, sign in ((0, 1.0), (1, -1.0)):
            value = product(pair(first_ref.at[parity]), split(stacked(sign)))
            wave_a = a_ref[0, parity]
            squared = wave_a * wave_a + (wave_b * wave_b + wave_c * wave_c)
            safe = jnp.where(squared > 0, squared, 1.0)
            usable = a_ref[1, parity] * b_ref[1] * (1.0 / float(length) ** 3)
            smooth = jnp.where(squared > 0, jnp.exp(-0.5 * squared) / safe, 0.0) * usable
            field.append(value * jnp.concatenate([smooth, smooth], axis=0))
        for number in range(3):
            folded = jnp.concatenate(
                [
                    field[parity][part * half : part * half + quarter]
                    + sign_back * field[parity][part * half + quarter : (part + 1) * half]
                    for part in range(2)
                    for parity in range(2)
                ],
                axis=0,
            )
            value = product(pair(back_ref.at[side]), split(folded))
            for x in range(slab):
                group, within = divmod(x, count)
                for spot in range(tiles // 3):
                    parity, part = divmod(spot, 2)
                    start = part * half + x * devices
                    at = (number * (tiles // 3) + spot) * message + c * count + within
                    flats[group][pl.ds(at, devices, stride=tiles * message), :] = value[
                        start : start + devices, parity * tile : (parity + 1) * tile
                    ]
            if number < 2:
                for parity in range(2):
                    wave_a = a_ref[0, parity]
                    field[parity] = field[parity] * jnp.concatenate([wave_a, wave_a], axis=0)


def halves(length):
    return np.arange(length).reshape(length // 2, 2).T


def spectrum_pass(received, side, waves_c, devices, groups, steps, first_step, filled):
    wide, narrow, per_c, rows_x, lanes = received.shape
    length = wide * rows_x
    rows_y = lanes // 2
    half = length // 2
    near = np.arange(half)
    split_index = halves(length)
    slab = half // devices
    second, first, back = [], [], []
    order = near.reshape(devices, slab).T.reshape(-1)
    for parity, index in enumerate(split_index):
        table = turn(-angles(index, near, length)).reshape(2, half, 2, narrow // 2, rows_y)
        second.append(table.transpose(3, 2, 4, 0, 1).reshape(length, length))
        first.append(turn(-angles(index, near, length)))
        back.append(turn(angles(2 * order + parity, split_index[:, : half // 2].reshape(-1), length)))
    tables = [np.stack([split_table(table) for table in each]) for each in (second, first, back)]
    wave = signed_wave(split_index, length)
    a_table = np.stack([wave, split_index != half]).astype(np.float32)[..., None]
    b_table = a_table.reshape(2, 1, length)
    message = PAIR * slab // groups
    out_shape = (devices, 3 * 2 * length // TILE, steps * message, TILE)
    block = out_shape[:2] + (message, TILE)

    def body(*refs):
        spectrum_kernel(slab, groups, *refs)

    return pl.pallas_call(
        body,
        grid=(per_c // PAIR,),
        in_specs=[
            pl.BlockSpec(memory_space=pltpu.SMEM),
            pl.BlockSpec(memory_space=pltpu.SMEM),
            whole(a_table.shape),
            whole(b_table.shape),
            *[whole(table.shape) for table in tables],
            pl.BlockSpec((wide, narrow, PAIR, rows_x, lanes), lambda i: (0, 0, i, 0, 0)),
            *[pl.BlockSpec(memory_space=pl.ANY)] * len(filled),
        ],
        out_specs=[pl.BlockSpec(block, lambda i: (0, 0, first_step + i, 0))] * groups,
        out_shape=[jax.ShapeDtypeStruct(out_shape, jnp.float32)] * groups,
        input_output_aliases={8 + spot: spot for spot in range(len(filled))},
        compiler_params=params(1),
        cost_estimate=cost(per_c * 7 * length**3, 20 * per_c * length**2 * 2),
    )(side, waves_c, a_table, b_table, *tables, received, *filled)


def shear_kernel(
    per_c, row_ref, lane_ref, second_ref, third_ref, ahead_ref, last_ref, in_ref, out_ref, shear_ref
):
    step = pl.program_id(0)
    length = shear_ref.shape[0]
    half = length // 2
    devices, tiles, message, tile = in_ref.shape
    count = message // per_c
    flat = in_ref.reshape(devices * tiles * message, tile)

    @pl.when(step == 0)
    def _():
        shear_ref[...] = jnp.zeros_like(shear_ref)

    field = jnp.concatenate(
        [
            jnp.concatenate(
                [
                    flat[pl.ds((source * tiles + spot) * message + x, per_c, stride=count), :]
                    for x in range(count)
                    for source in range(devices)
                ],
                axis=0,
            )
            for spot in range(tiles)
        ],
        axis=1,
    )
    field = field * row_ref[0] * lane_ref[0]
    even = product(split(field[:, :length]), pair(second_ref.at[0]))
    odd = product(split(field[:, length:]), pair(second_ref.at[1]))
    near, far = even + odd, even - odd
    field = jnp.concatenate(
        [
            jnp.concatenate(
                [
                    value[x * half : (x + 1) * half, part * half : (part + 1) * half]
                    for x in range(count)
                    for value in (near, far)
                ],
                axis=1,
            )
            for part in range(2)
        ],
        axis=0,
    )
    field = product(pair(third_ref), split(field))
    shear_ref[...] += field * field

    @pl.when(step == 5)
    def _():
        wide, narrow, _, rows_b, lanes = out_ref.shape
        for x in range(count):
            shear = shear_ref[:, x * length : (x + 1) * length]
            ahead = product(pair(ahead_ref), split(shear), ((1,), (1,)))
            value = jnp.concatenate([ahead[:length], ahead[length:]], axis=1)
            value = product(split(value), pair(last_ref))
            for w in range(wide):
                for n in range(narrow):
                    out_ref[w, n, x] = value[
                        w * rows_b : (w + 1) * rows_b, n * lanes : (n + 1) * lanes
                    ]


def shear_pass(received, wide, narrow, per_c):
    devices, tiles, message, tile = received.shape
    count = message // per_c
    length = tiles * tile // 6
    half = length // 2
    index = np.arange(length)
    angle = angles(index, index, length)
    cosine, sine = np.cos(angle), np.sin(angle)
    split_index = halves(length)
    second = np.stack(
        [split_table(turn(angles(np.arange(half), b, length)).T) for b in split_index]
    )
    row_c = np.arange(half)
    weight = np.where(row_c == 0, 1.0, 2.0)
    angle = angles(index, row_c, length)
    third = np.concatenate([weight * np.cos(angle), -weight * np.sin(angle)], axis=1)
    ahead = np.concatenate([cosine, -sine])
    cos_z = cosine.reshape(length, narrow, 1, length // narrow)
    sin_z = sine.reshape(length, narrow, 1, length // narrow)
    last = np.concatenate(
        [
            np.concatenate([cos_z, -sin_z], axis=2).reshape(length, 2 * length),
            np.concatenate([sin_z, cos_z], axis=2).reshape(length, 2 * length),
        ]
    )
    wave = signed_wave(index, length)
    wave_rows = np.tile(wave[row_c], count)
    wave_lanes = np.stack([wave[split_index]] * 2, axis=1).reshape(-1)
    twice = math.sqrt(2.0)
    one_row, one_lane = np.ones_like(wave_rows), np.ones_like(wave_lanes)
    row_factor = np.stack(
        [one_row, twice * one_row, twice * wave_rows, one_row, twice * wave_rows, wave_rows**2]
    ).astype(np.float32)[:, :, None]
    lane_factor = np.stack(
        [one_lane, wave_lanes, one_lane, wave_lanes**2, wave_lanes, one_lane]
    ).astype(np.float32)[:, None, :]
    tables = [second] + [split_table(table) for table in (third, ahead, last)]
    out_shape = (wide, narrow, count, length // wide, 2 * length // narrow)

    def body(*refs):
        shear_kernel(per_c, *refs)

    def which(i):
        return (0, 2 - (i >= 1).astype(jnp.int32) - (i >= 3).astype(jnp.int32), 0, 0)

    return pl.pallas_call(
        body,
        grid=(6,),
        in_specs=[
            pl.BlockSpec((1, count * half, 1), lambda i: (i, 0, 0)),
            pl.BlockSpec((1, 1, 2 * length), lambda i: (i, 0, 0)),
            *[whole(table.shape) for table in tables],
            pl.BlockSpec((devices, tiles // 3, message, tile), which),
        ],
        out_specs=whole(out_shape),
        out_shape=jax.ShapeDtypeStruct(out_shape, jnp.float32),
        scratch_shapes=[pltpu.VMEM((length, count * length), jnp.float32)],
        compiler_params=params(1),
        cost_estimate=cost(count * 18 * length**3, 4 * received.size + 4 * 2**20),
    )(row_factor, lane_factor, *tables, received)


def first_kernel(scale, wide, sides, anchor_ref, table_ref, *refs):
    ins, (real_ref, imag_ref, real_tile_ref, imag_tile_ref) = refs[:-4], refs[-4:]
    devices, count, rows_b, lanes = ins[0].shape
    half_c, length = lanes // 2, real_ref.shape[2]
    half = length // 2
    tables = [pair(table_ref.at[0]), pair(table_ref.at[1])]
    flats = [ref.reshape(devices * count * rows_b, lanes) for ref in ins]
    tile = real_tile_ref.shape[2]
    spot_c = lax.broadcasted_iota(jnp.int32, (half_c, half), 0)
    spot_a = lax.broadcasted_iota(jnp.int32, (half_c, half), 1)
    is_anchor = (anchor_ref[0] == 1) & (pl.program_id(0) == 0)
    anchor = (spot_c == 0) & (spot_a == 0) & is_anchor
    group = min(8, rows_b)
    run = devices // wide // sides * count
    for first in range(0, rows_b, group):
        sums = []
        for parity in range(2):
            columns = []
            for b in range(first, first + group):
                column = jnp.concatenate(
                    [
                        flat[pl.ds((w * sides + parity) * run * rows_b + b, run, stride=rows_b), :]
                        for flat in flats
                        for w in range(wide)
                    ],
                    axis=0,
                ).T
                columns.append(jnp.concatenate([column[:half_c], column[half_c:]], axis=1))
            sums.append(product(split(jnp.concatenate(columns, axis=0)), tables[parity]))
        even, odd = sums
        for side, value in enumerate((even + odd, even - odd)):
            value = value * scale
            for number in range(group):
                b = first + number
                rows = slice(number * half_c, (number + 1) * half_c)
                real, imag = value[rows, :half], value[rows, half:]
                if b == 0 and side == 0:
                    real = jnp.where(anchor, 0.0, real)
                    imag = jnp.where(anchor, 0.0, imag)
                for spot in range(half // tile):
                    part = slice(spot * tile, (spot + 1) * tile)
                    at = side * (half // tile) + spot
                    real_tile_ref[at, pl.ds(b, half_c, stride=rows_b), :] = real[:, part]
                    imag_tile_ref[at, pl.ds(b, half_c, stride=rows_b), :] = imag[:, part]
    for spot in range(length // tile):
        part = slice(spot * tile, (spot + 1) * tile)
        real_ref[:, :, part] = real_tile_ref[spot].reshape(half_c, rows_b, tile)
        imag_ref[:, :, part] = imag_tile_ref[spot].reshape(half_c, rows_b, tile)


def first_pass(parts, is_anchor, length, wide, sides):
    devices, count, rows_b, lanes = parts[0].shape
    groups = len(parts)
    ranks = devices // wide // sides
    index = np.arange(length).reshape(wide, ranks, groups, count, sides)
    index = index.transpose(4, 2, 0, 1, 3).reshape(2, -1)
    table = np.stack(
        [split_table(turn(-angles(np.arange(length // 2), x, length)).T) for x in index]
    )
    step = min(8, rows_b)
    scale = 1.0 / float(length) ** 1.5

    def body(*refs):
        first_kernel(scale, wide, sides, *refs)

    out_shape = jax.ShapeDtypeStruct((lanes // 2, rows_b, length), jnp.float32)
    return pl.pallas_call(
        body,
        grid=(rows_b // step,),
        in_specs=[
            pl.BlockSpec(memory_space=pltpu.SMEM),
            whole(table.shape),
            *[pl.BlockSpec((devices, count, step, lanes), lambda i: (0, 0, i, 0))] * groups,
        ],
        out_specs=[pl.BlockSpec((lanes // 2, step, length), lambda i: (0, i, 0))] * 2,
        out_shape=[out_shape] * 2,
        scratch_shapes=[pltpu.VMEM((length // TILE, lanes // 2 * step, TILE), jnp.float32)] * 2,
        compiler_params=params(1),
        cost_estimate=cost(rows_b * lanes * length * length, 8 * rows_b * lanes * length),
    )(is_anchor, table, *parts)


def transpose(value, members=None):
    return lax.all_to_all(
        value, AXES, split_axis=0, concat_axis=0, tiled=True, axis_index_groups=members
    )


def solution(mesh):
    wide, narrow = mesh.shape["wide"], mesh.shape["narrow"]
    sides = 2
    ranks = narrow // sides
    devices = wide * ranks
    members = [
        [w * narrow + side * ranks + rank for w in range(wide) for rank in range(ranks)]
        for side in range(sides)
    ]

    def per_device(density):
        rows_x, rows_y, length = density.shape
        half = length // 2
        per_c = half // devices
        slab = half // devices
        steps = per_c // PAIR
        counts = [per_c - PAIR, PAIR] if steps > 1 else [per_c]
        groups = 2 if slab > 2 else 1
        spot_wide, spot_narrow = lax.axis_index("wide"), lax.axis_index("narrow")
        side = (spot_narrow // ranks).astype(jnp.int32).reshape(1)
        rank = spot_wide * ranks + spot_narrow % ranks
        waves_c = (rank * per_c + jnp.arange(per_c, dtype=jnp.int32)).astype(jnp.float32)
        waves_c = waves_c * (2.0 * math.pi / length)
        chunks, start = [], 0
        for planes, count in zip(third_pass(density, wide, sides, ranks, counts), counts):
            planes = transpose(planes.reshape(wide * narrow, count, rows_x, 2 * rows_y))
            planes = planes.reshape(wide, narrow, count, rows_x, 2 * rows_y)
            chunks = spectrum_pass(
                planes, side, waves_c[start : start + count], devices, groups, steps, start // PAIR, chunks
            )
            start += count
        is_anchor = ((spot_wide == 0) & (spot_narrow == 0)).astype(jnp.int32).reshape(1)
        parts = []
        for chunk in chunks:
            part = shear_pass(transpose(chunk, members), wide, narrow, per_c)
            parts.append(transpose(part.reshape((wide * narrow,) + part.shape[2:])))
        return tuple(first_pass(parts, is_anchor, length, wide, sides))

    return jax.shard_map(
        per_device,
        mesh=mesh,
        in_specs=(P("wide", "narrow", None),),
        out_specs=(P("narrow", "wide", None), P("narrow", "wide", None)),
        check_vma=False,
    )
```

time: 342 us -> 324 us (0.947)
  waiting for transfers between devices: 176 us -> 120 us
  blocking collectives: 74.8 us -> 119 us
  Pallas kernels: 66.7 us -> 61.8 us
    all_to_all x4, waiting for transfers between devices: 176 us -> 120 us  [transpose(): lax.all_to_all(value, AXES, split_axis=0, concat_axis=0, tiled=True, axis...]
    all_to_all x1 -> x2, blocking collectives: 74.8 us -> 119 us  [transpose(): lax.all_to_all(value, AXES, split_axis=0, concat_axis=0, tiled=True, axis...]
    pallas_call x4 -> x5, Pallas kernels: 59.3 us -> 54.6 us  [the longest x2 28.2 us: shear_pass(): pl.pallas_call(body, grid=(6,), in_specs=[pl.BlockSpec((1, count * half,...]
  transfers between devices with their start and end apart: 4 -> 4, of which waited for: 4 -> 4; matrix products, arithmetic and copies ran while one was open for 0% -> 0% of each run, Pallas kernels for 11% -> 13%
where the time goes in v3:
time: 324 us; the launch traced here: 323 us
  waiting for transfers between devices  120 us (37%)
  blocking collectives  119 us (37%)
  Pallas kernels  61.8 us (19%)
  starting transfers between devices  17.6 us (5%)
    all_to_all x4, waiting for transfers between devices, transpose(): lax.all_to_all(value, AXES, split_axis=0, concat_axis=0, tiled=True, axis...  120 us
    all_to_all x2, blocking collectives, transpose(): lax.all_to_all(value, AXES, split_axis=0, concat_axis=0, tiled=True, axis...  119 us
    pallas_call x2, Pallas kernels, shear_pass(): pl.pallas_call(body, grid=(6,), in_specs=[pl.BlockSpec((1, count * half,...  28.2 us
    pallas_call x2, Pallas kernels, spectrum_pass(): pl.pallas_call(body, grid=(per_c // PAIR,), in_specs=[pl.BlockSpec(memory...  19.3 us
    all_to_all x4, starting transfers between devices, transpose(): lax.all_to_all(value, AXES, split_axis=0, concat_axis=0, tiled=True, axis...  17.6 us
    pallas_call x1, Pallas kernels, first_pass(): pl.pallas_call(body, grid=(rows_b // step,), in_specs=[pl.BlockSpec(memor...  7.25 us
    pallas_call x1, Pallas kernels, third_pass(): pl.pallas_call(body, grid=(rows_x // step,), in_specs=[whole(table.shape)...  7 us
  transfers between devices with their start and end apart: 4, of which 4 were waited for; matrix products, arithmetic and copies ran while one was open for 0% of the time, Pallas kernels for 13%

profile of v3, /device:TPU:1, one launch (start us, length us, event | category | flops | bytes accessed | tf_op | source)
XLA Modules:
  0.0 322.7 jit_solution(7032263118519390559)
XLA Ops:
  0.6 7.0 %shard_map.248 = (f32[8,2,2,6,32,128]{5,4,3,2,1,0:T(8,128)}, f32[8,2,2,2,32,128]{5,4,3,2,1,0:T(8,128)}) custom-call(bf16[2,256,256]{2,1,0:T(8,128)(2,1)} %constant.62.clone.refs_0_, f32[32,64,256]{2,1,0:T(8,128)} %refs_1_.4), custom_call_target="tpu_custom_call" | custom-call | flops 805306368 | bytes 6291456 | tf_op jit(solution)/shard_map/pallas_call | solution.py:107
  7.6 78.5 %all_to_all.30 = f32[32,6,32,128]{3,2,1,0:T(8,128)} all-to-all(f32[32,6,32,128]{3,2,1,0:T(8,128)} %bitcast.11), channel_id=1, replica_groups=mesh['wide'=8,'narrow'=4] {'wide','narrow'}, dimensions={0} | all-to-all | bytes 6291456 | tf_op jit(solution)/shard_map/all_to_all | solution.py:474
  86.1 3.2 all-to-all-start
  89.3 0.0 copy-start.3
  89.3 0.6 slice.6.refs_1_
  89.9 0.0 copy-done.3
  89.9 13.0 %shard_map.249 = (f32[16,12,32,128]{3,2,1,0:T(8,128)}, f32[16,12,32,128]{3,2,1,0:T(8,128)}) custom-call(s32[1]{0:T(128)} %bitcast.1.refs_0_, f32[6]{0:T(128)} %bitcast.14, f32[2,2,128,1]{3,2,1,0:T(8,128)} %constant.63.clone.refs_2_, f32[2,1,256]{2,1,0:T(1,128)} %constant.64.clone.refs_3_, bf16[2,2,256,256]{3,2,1,0:T(8,128)(2,1)} %constant.65.clone.refs_4_, ...), custom_call_target="tpu_custom_call" | custom-call | flops 4227858432 | bytes 15728640 | tf_op jit(solution)/shard_map/pallas_call | solution.py:245
  103.0 12.7 %all-to-all-done = f32[32,2,32,128]{3,2,1,0:T(8,128)S(1)} async-done(((f32[32,2,32,128]{3,2,1,0:T(8,128)}), f32[32,2,32,128]{3,2,1,0:T(8,128)S(1)}, u32[]{:S(2)}, u32[]{:S(2)}) %all-to-all-start) | async-done | bytes 1048608 | tf_op jit(solution)/shard_map/all_to_all | solution.py:474
  115.6 0.0 copy-start
  115.6 1.0 copy-done
  116.6 6.3 %shard_map.250 = (f32[16,12,32,128]{3,2,1,0:T(8,128)}, f32[16,12,32,128]{3,2,1,0:T(8,128)}) custom-call(s32[1]{0:T(128)} %bitcast.1.refs_0_, f32[2]{0:T(128)} %slice.6.refs_1_, f32[2,2,128,1]{3,2,1,0:T(8,128)} %constant.63.clone.refs_2_, f32[2,1,256]{2,1,0:T(1,128)} %constant.64.clone.refs_3_, ...), custom_call_target="tpu_custom_call", output_to_operand_aliasing={{0}: (8, {}), {1}: (9, {})} | custom-call | flops 1409286144 | bytes 5242880 | tf_op jit(solution)/shard_map/pallas_call | solution.py:245
  122.9 40.8 %all_to_all.31.refs_6_ = f32[16,12,32,128]{3,2,1,0:T(8,128)} all-to-all(f32[16,12,32,128]{3,2,1,0:T(8,128)} %get-tuple-element.12), channel_id=1, replica_groups={{0,1,4,5,8,9,12,13,16,17,20,21,24,25,28,29},{2,3,6,7,10,11,14,15,18,19,..., dimensions={0} | all-to-all | bytes 6291456 | tf_op jit(solution)/shard_map/all_to_all | solution.py:474
  163.8 5.7 %all-to-all-start.4 = ((f32[16,12,32,128]{3,2,1,0:T(8,128)}), f32[16,12,32,128]{3,2,1,0:T(8,128)S(1)}, u32[]{:S(2)}, u32[]{:S(2)}) async-start(f32[16,12,32,128]{3,2,1,0:T(8,128)} %get-tuple-element.13), calls=%async_computation.4 | async-start | bytes 6291456 | tf_op jit(solution)/shard_map/all_to_all | solution.py:474
  169.5 14.1 %shard_map.251 = f32[8,4,4,32,128]{4,3,2,1,0:T(8,128)} custom-call(f32[6,512,1]{2,1,0:T(8,128)} %constant.68.clone.refs_0_, f32[6,1,512]{2,1,0:T(1,128)} %constant.69.clone.refs_1_, bf16[2,2,256,256]{3,2,1,0:T(8,128)(2,1)} %constant.66.clone.refs_5_.refs_2_, bf16[2,256,256]{2,1,0:T(8,128)(2,1)} %constant.70.clone.refs_3_, ...), custom_call_target="tpu_custom_call" | custom-call | flops 7247757312 | bytes 7340032 | tf_op jit(solution)/shard_map/pallas_call | solution.py:374
  183.5 25.3 %all-to-all-done.4.refs_6_ = f32[16,12,32,128]{3,2,1,0:T(8,128)S(1)} async-done(((f32[16,12,32,128]{3,2,1,0:T(8,128)}), f32[16,12,32,128]{3,2,1,0:T(8,128)S(1)}, u32[]{:S(2)}, u32[]{:S(2)}) %all-to-all-start.4) | async-done | bytes 3145760 | tf_op jit(solution)/shard_map/all_to_all | solution.py:474
  208.8 0.0 copy-start.1
  208.8 5.3 %all-to-all-start.3 = ((f32[32,4,32,128]{3,2,1,0:T(8,128)}), f32[32,4,32,128]{3,2,1,0:T(8,128)}, u32[]{:S(2)}, u32[]{:S(2)}) async-start(f32[32,4,32,128]{3,2,1,0:T(8,128)} %bitcast.13), calls=%async_computation.3 | async-start | bytes 4194304 | tf_op jit(solution)/shard_map/all_to_all | solution.py:474
  214.2 0.0 copy-done.1
  214.2 14.1 %shard_map.252 = f32[8,4,4,32,128]{4,3,2,1,0:T(8,128)} custom-call(f32[6,512,1]{2,1,0:T(8,128)} %constant.68.clone.refs_0_, f32[6,1,512]{2,1,0:T(1,128)} %constant.69.clone.refs_1_, bf16[2,2,256,256]{3,2,1,0:T(8,128)(2,1)} %constant.66.clone.refs_5_.refs_2_, bf16[2,256,256]{2,1,0:T(8,128)(2,1)} %constant.70.clone.refs_3_, ...), custom_call_target="tpu_custom_call" | custom-call | flops 7247757312 | bytes 7340032 | tf_op jit(solution)/shard_map/pallas_call | solution.py:374
  228.3 34.1 %all-to-all-done.3.refs_2_ = f32[32,4,32,128]{3,2,1,0:T(8,128)} async-done(((f32[32,4,32,128]{3,2,1,0:T(8,128)}), f32[32,4,32,128]{3,2,1,0:T(8,128)}, u32[]{:S(2)}, u32[]{:S(2)}) %all-to-all-start.3) | async-done | bytes 2097184 | tf_op jit(solution)/shard_map/all_to_all | solution.py:474
  262.5 3.4 %all-to-all-start.5 = ((f32[32,4,32,128]{3,2,1,0:T(8,128)}), f32[32,4,32,128]{3,2,1,0:T(8,128)S(1)}, u32[]{:S(2)}, u32[]{:S(2)}) async-start(f32[32,4,32,128]{3,2,1,0:T(8,128)} %bitcast.12), calls=%async_computation.5 | async-start | bytes 4194304 | tf_op jit(solution)/shard_map/all_to_all | solution.py:474
  265.9 48.2 %all-to-all-done.5.refs_3_ = f32[32,4,32,128]{3,2,1,0:T(8,128)S(1)} async-done(((f32[32,4,32,128]{3,2,1,0:T(8,128)}), f32[32,4,32,128]{3,2,1,0:T(8,128)S(1)}, u32[]{:S(2)}, u32[]{:S(2)}) %all-to-all-start.5) | async-done | bytes 2097184 | tf_op jit(solution)/shard_map/all_to_all | solution.py:474
  314.1 0.0 copy-start.2
  314.1 1.3 copy-done.2
  315.5 7.2 %shard_map.253 = (f32[64,32,256]{2,1,0:T(8,128)}, f32[64,32,256]{2,1,0:T(8,128)}) custom-call(s32[1]{0:T(128)} %bitcast.refs_0_, bf16[2,2,256,256]{3,2,1,0:T(8,128)(2,1)} %constant.73.clone.refs_1_, f32[32,4,32,128]{3,2,1,0:T(8,128)} %all-to-all-done.3.refs_2_, f32[32,4,32,128]{3,2,1,0:T(8,128)} %copy-done.2), custom_call_target="tpu_custom_call" | custom-call | flops 1610612736 | bytes 8388608 | tf_op jit(solution)/shard_map/pallas_call | solution.py:457
  (1 shorter events, 0.0 us)
Async XLA Ops:
  86.1 29.5 %all-to-all-start = ((f32[32,2,32,128]{3,2,1,0:T(8,128)}), f32[32,2,32,128]{3,2,1,0:T(8,128)S(1)}, u32[]{:S(2)}, u32[]{:S(2)}) async-start(f32[32,2,32,128]{3,2,1,0:T(8,128)} %bitcast.2), calls=%async_computation | async-start | bytes 2097152 | tf_op jit(solution)/shard_map/all_to_all | solution.py:474
  89.3 0.6 copy-start.3
  115.6 1.0 copy-start
  163.8 45.1 %all-to-all-start.4 = ((f32[16,12,32,128]{3,2,1,0:T(8,128)}), f32[16,12,32,128]{3,2,1,0:T(8,128)S(1)}, u32[]{:S(2)}, u32[]{:S(2)}) async-start(f32[16,12,32,128]{3,2,1,0:T(8,128)} %get-tuple-element.13), calls=%async_computation.4 | async-start | bytes 6291456 | tf_op jit(solution)/shard_map/all_to_all | solution.py:474
  208.8 5.4 %copy-start.1 = (f32[16,12,32,128]{3,2,1,0:T(8,128)}, f32[16,12,32,128]{3,2,1,0:T(8,128)S(1)}, u32[]{:S(2)}) copy-start(f32[16,12,32,128]{3,2,1,0:T(8,128)S(1)} %all-to-all-done.4.refs_6_) | copy-start | bytes 9437188
  208.8 53.6 %all-to-all-start.3 = ((f32[32,4,32,128]{3,2,1,0:T(8,128)}), f32[32,4,32,128]{3,2,1,0:T(8,128)}, u32[]{:S(2)}, u32[]{:S(2)}) async-start(f32[32,4,32,128]{3,2,1,0:T(8,128)} %bitcast.13), calls=%async_computation.3 | async-start | bytes 4194304 | tf_op jit(solution)/shard_map/all_to_all | solution.py:474
  262.5 51.7 %all-to-all-start.5 = ((f32[32,4,32,128]{3,2,1,0:T(8,128)}), f32[32,4,32,128]{3,2,1,0:T(8,128)S(1)}, u32[]{:S(2)}, u32[]{:S(2)}) async-start(f32[32,4,32,128]{3,2,1,0:T(8,128)} %bitcast.12), calls=%async_computation.5 | async-start | bytes 4194304 | tf_op jit(solution)/shard_map/all_to_all | solution.py:474
  314.1 1.3 copy-start.2

commit v4 on v3

--- a/solution.py
+++ b/solution.py
@@ -11,7 +11,7 @@
 
 AXES = ("wide", "narrow")
 TILE = 128
-LIMIT = 56 * 1024 * 1024
+LIMIT = 16 * 1024 * 1024
 
 
 def angles(rows, columns, length):

time: 324 us -> 325 us (level)
  local copies, waits for them, and re-layouts: 2.93 us -> 28.2 us
  Pallas kernels: 61.8 us -> 49.8 us
  waiting for transfers between devices: 120 us -> 109 us
    unnamed x8 -> x56, local copies, waits for them, and re-layouts: 2.32 us -> 28.1 us
    all_to_all x4, waiting for transfers between devices: 120 us -> 109 us  [transpose(): lax.all_to_all(value, AXES, split_axis=0, concat_axis=0, tiled=True, axis...]
    pallas_call x2, Pallas kernels: 28.2 us -> 21 us  [shear_pass(): pl.pallas_call(body, grid=(6,), in_specs=[pl.BlockSpec((1, count * half,...]
    pallas_call x2, Pallas kernels: 19.3 us -> 16 us  [spectrum_pass(): pl.pallas_call(body, grid=(per_c // PAIR,), in_specs=[pl.BlockSpec(memory...]
  transfers between devices with their start and end apart: 4 -> 4, of which waited for: 4 -> 4; matrix products, arithmetic and copies ran while one was open for 0% -> 0% of each run, Pallas kernels for 13% -> 10%
where the time goes in v4:
time: 325 us; the launch traced here: 323 us
  blocking collectives  118 us (36%)
  waiting for transfers between devices  109 us (34%)
  Pallas kernels  49.8 us (15%)
  local copies, waits for them, and re-layouts  28.2 us (9%)
  starting transfers between devices  16.9 us (5%)
    all_to_all x2, blocking collectives, transpose(): lax.all_to_all(value, AXES, split_axis=0, concat_axis=0, tiled=True, axis...  118 us
    all_to_all x4, waiting for transfers between devices, transpose(): lax.all_to_all(value, AXES, split_axis=0, concat_axis=0, tiled=True, axis...  109 us
    unnamed x56, local copies, waits for them, and re-layouts  28.1 us
    pallas_call x2, Pallas kernels, shear_pass(): pl.pallas_call(body, grid=(6,), in_specs=[pl.BlockSpec((1, count * half,...  21 us
    all_to_all x4, starting transfers between devices, transpose(): lax.all_to_all(value, AXES, split_axis=0, concat_axis=0, tiled=True, axis...  16.9 us
    pallas_call x2, Pallas kernels, spectrum_pass(): pl.pallas_call(body, grid=(per_c // PAIR,), in_specs=[pl.BlockSpec(memory...  16 us
    pallas_call x1, Pallas kernels, first_pass(): pl.pallas_call(body, grid=(rows_b // step,), in_specs=[pl.BlockSpec(memor...  6.76 us
  transfers between devices with their start and end apart: 4, of which 4 were waited for; matrix products, arithmetic and copies ran while one was open for 0% of the time, Pallas kernels for 10%

profile of v4, /device:TPU:1, one launch (start us, length us, event | category | flops | bytes accessed | tf_op | source)
XLA Modules:
  0.0 323.3 jit_solution(10214124649818805727)
XLA Ops:
  0.6 0.0 copy-start.17
  0.6 1.6 copy-done.17
  2.2 0.0 copy-start.26
  2.2 0.9 copy-done.26
  3.2 6.1 %shard_map.248 = (f32[8,2,2,6,32,128]{5,4,3,2,1,0:T(8,128)S(1)}, f32[8,2,2,2,32,128]{5,4,3,2,1,0:T(8,128)}) custom-call(bf16[2,256,256]{2,1,0:T(8,128)(2,1)S(1)} %copy-done.26, f32[32,64,256]{2,1,0:T(8,128)S(1)} %copy-done.17), custom_call_target="tpu_custom_call" | custom-call | flops 805306368 | bytes 6291456 | tf_op jit(solution)/shard_map/pallas_call | solution.py:107
  9.2 0.0 copy-start.15
  9.2 78.3 %all_to_all.30 = f32[32,6,32,128]{3,2,1,0:T(8,128)} all-to-all(f32[32,6,32,128]{3,2,1,0:T(8,128)S(1)} %bitcast.10), channel_id=1, replica_groups=mesh['wide'=8,'narrow'=4] {'wide','narrow'}, dimensions={0} | all-to-all | bytes 6291456 | tf_op jit(solution)/shard_map/all_to_all | solution.py:474
  87.5 3.2 all-to-all-start
  90.8 0.1 slice.6.refs_1_
  90.8 0.0 copy-done.15
  90.8 0.0 copy-done.16
  90.8 0.0 copy-start.3
  90.8 1.9 copy-done.3
  92.7 0.0 copy-start.7
  92.7 1.0 copy-done.7
  93.8 0.0 copy-start.11
  93.8 1.0 copy-done.11
  94.8 0.0 copy-start.13
  94.8 1.0 copy-done.13
  95.9 11.2 %shard_map.249 = (f32[16,12,32,128]{3,2,1,0:T(8,128)S(1)}, f32[16,12,32,128]{3,2,1,0:T(8,128)S(1)}) custom-call(s32[1]{0:T(128)} %bitcast.1.refs_0_, f32[6]{0:T(128)S(1)} %bitcast.13, f32[2,2,128,1]{3,2,1,0:T(8,128)S(1)} %copy-done.15, f32[2,1,256]{2,1,0:T(1,128)S(1)} %copy-done.16, bf16[2,2,256,256]{3,2,1,0:T(8,128)(2,1)S(1)} %copy-done.13, ...), custom_call_target="tpu_custom_call" | custom-call | flops 4227858432 | bytes 15728640 | tf_op jit(solution)/shard_map/pallas_call | solution.py:245
  107.1 0.0 copy-start
  107.1 1.6 copy-done
  108.7 8.4 %all-to-all-done = f32[32,2,32,128]{3,2,1,0:T(8,128)} async-done(((f32[32,2,32,128]{3,2,1,0:T(8,128)}), f32[32,2,32,128]{3,2,1,0:T(8,128)}, u32[]{:S(2)}, u32[]{:S(2)}) %all-to-all-start) | async-done | bytes 1048608 | tf_op jit(solution)/shard_map/all_to_all | solution.py:474
  117.1 0.0 copy-start.1
  117.1 1.9 copy-done.1
  119.0 0.0 copy-start.8
  119.0 1.0 copy-done.8
  120.1 0.0 copy-start.12
  120.1 1.0 copy-done.12
  121.1 0.0 copy-start.14
  121.1 1.0 copy-done.14
  122.2 4.8 %shard_map.250 = (f32[16,12,32,128]{3,2,1,0:T(8,128)S(1)}, f32[16,12,32,128]{3,2,1,0:T(8,128)S(1)}) custom-call(s32[1]{0:T(128)} %bitcast.1.refs_0_, f32[2]{0:T(128)S(1)} %slice.6.refs_1_, f32[2,2,128,1]{3,2,1,0:T(8,128)S(1)} %copy-done.15, f32[2,1,256]{2,1,0:T(1,128)S(1)} %copy-done.16, ...), custom_call_target="tpu_custom_call", output_to_operand_aliasing={{0}: (8, {}), {1}: (9, {})} | custom-call | flops 1409286144 | bytes 5242880 | tf_op jit(solution)/shard_map/pallas_call | solution.py:245
  126.9 0.0 copy-start.2
  126.9 40.0 %all_to_all.31.refs_6_ = f32[16,12,32,128]{3,2,1,0:T(8,128)} all-to-all(f32[16,12,32,128]{3,2,1,0:T(8,128)S(1)} %get-tuple-element.12), channel_id=1, replica_groups={{0,1,4,5,8,9,12,13,16,17,20,21,24,25,28,29},{2,3,6,7,10,11,14,15,18,19,..., dimensions={0} | all-to-all | bytes 6291456 | tf_op jit(solution)/shard_map/all_to_all | solution.py:474
  167.0 0.0 copy-done.2
  167.0 0.0 copy-start.25
  167.0 0.0 copy-start.27
  167.0 3.9 %all-to-all-start.4 = ((f32[16,12,32,128]{3,2,1,0:T(8,128)}), f32[16,12,32,128]{3,2,1,0:T(8,128)S(1)}, u32[]{:S(2)}, u32[]{:S(2)}) async-start(f32[16,12,32,128]{3,2,1,0:T(8,128)} %copy-done.2), calls=%async_computation.4 | async-start | bytes 6291456 | tf_op jit(solution)/shard_map/all_to_all | solution.py:474
  170.9 0.0 copy-done.25
  170.9 0.0 copy-done.27
  170.9 0.0 copy-start.4
  170.9 1.9 copy-done.4
  172.8 1.0 copy-done.9
  173.9 1.4 copy-done.18
  175.3 1.2 copy-done.20
  176.5 1.0 copy-done.23
  177.5 10.5 %shard_map.251 = f32[8,4,4,32,128]{4,3,2,1,0:T(8,128)S(1)} custom-call(f32[6,512,1]{2,1,0:T(8,128)S(1)} %copy-done.18, f32[6,1,512]{2,1,0:T(1,128)S(1)} %copy-done.27, bf16[2,2,256,256]{3,2,1,0:T(8,128)(2,1)S(1)} %copy-done.9, bf16[2,256,256]{2,1,0:T(8,128)(2,1)S(1)} %copy-done.25, bf16[2,512,256]{2,1,0:T(8,128)(2,1)S(1)} %copy-done.23, ...), custom_call_target="tpu_custom_call" | custom-call | flops 7247757312 | bytes 7340032 | tf_op jit(solution)/shard_map/pallas_call | solution.py:374
  188.1 0.0 copy-start.6
  188.1 1.3 copy-done.6
  189.4 20.9 %all-to-all-done.4.refs_6_ = f32[16,12,32,128]{3,2,1,0:T(8,128)S(1)} async-done(((f32[16,12,32,128]{3,2,1,0:T(8,128)}), f32[16,12,32,128]{3,2,1,0:T(8,128)S(1)}, u32[]{:S(2)}, u32[]{:S(2)}) %all-to-all-start.4) | async-done | bytes 3145760 | tf_op jit(solution)/shard_map/all_to_all | solution.py:474
  210.3 6.4 %all-to-all-start.3 = ((f32[32,4,32,128]{3,2,1,0:T(8,128)}), f32[32,4,32,128]{3,2,1,0:T(8,128)}, u32[]{:S(2)}, u32[]{:S(2)}) async-start(f32[32,4,32,128]{3,2,1,0:T(8,128)} %bitcast.12), calls=%async_computation.3 | async-start | bytes 4194304 | tf_op jit(solution)/shard_map/all_to_all | solution.py:474
  216.6 0.0 copy-start.10
  216.6 1.0 copy-done.10
  217.7 1.4 copy-done.19
  219.1 1.2 copy-done.21
  220.3 1.0 copy-done.24
  221.3 10.5 %shard_map.252 = f32[8,4,4,32,128]{4,3,2,1,0:T(8,128)S(1)} custom-call(f32[6,512,1]{2,1,0:T(8,128)S(1)} %copy-done.19, f32[6,1,512]{2,1,0:T(1,128)S(1)} %copy-done.27, bf16[2,2,256,256]{3,2,1,0:T(8,128)(2,1)S(1)} %copy-done.10, bf16[2,256,256]{2,1,0:T(8,128)(2,1)S(1)} %copy-done.25, bf16[2,512,256]{2,1,0:T(8,128)(2,1)S(1)} %copy-done.24, ...), custom_call_target="tpu_custom_call" | custom-call | flops 7247757312 | bytes 7340032 | tf_op jit(solution)/shard_map/pallas_call | solution.py:374
  231.9 0.0 copy-start.5
  231.9 1.3 copy-done.5
  233.2 31.7 %all-to-all-done.3.refs_2_ = f32[32,4,32,128]{3,2,1,0:T(8,128)} async-done(((f32[32,4,32,128]{3,2,1,0:T(8,128)}), f32[32,4,32,128]{3,2,1,0:T(8,128)}, u32[]{:S(2)}, u32[]{:S(2)}) %all-to-all-start.3) | async-done | bytes 2097184 | tf_op jit(solution)/shard_map/all_to_all | solution.py:474
  264.9 3.4 %all-to-all-start.5 = ((f32[32,4,32,128]{3,2,1,0:T(8,128)}), f32[32,4,32,128]{3,2,1,0:T(8,128)S(1)}, u32[]{:S(2)}, u32[]{:S(2)}) async-start(f32[32,4,32,128]{3,2,1,0:T(8,128)} %bitcast.11), calls=%async_computation.5 | async-start | bytes 4194304 | tf_op jit(solution)/shard_map/all_to_all | solution.py:474
  268.3 48.2 %all-to-all-done.5.refs_3_ = f32[32,4,32,128]{3,2,1,0:T(8,128)S(1)} async-done(((f32[32,4,32,128]{3,2,1,0:T(8,128)}), f32[32,4,32,128]{3,2,1,0:T(8,128)S(1)}, u32[]{:S(2)}, u32[]{:S(2)}) %all-to-all-start.5) | async-done | bytes 2097184 | tf_op jit(solution)/shard_map/all_to_all | solution.py:474
  316.6 0.0 copy-done.22
  316.6 6.8 %shard_map.253 = (f32[64,32,256]{2,1,0:T(8,128)}, f32[64,32,256]{2,1,0:T(8,128)}) custom-call(s32[1]{0:T(128)} %bitcast.refs_0_, bf16[2,2,256,256]{3,2,1,0:T(8,128)(2,1)S(1)} %copy-done.22, f32[32,4,32,128]{3,2,1,0:T(8,128)} %all-to-all-done.3.refs_2_, f32[32,4,32,128]{3,2,1,0:T(8,128)S(1)} %all-to-all-done.5.refs_3_), custom_call_target="tpu_custom_call" | custom-call | flops 1610612736 | bytes 8388608 | tf_op jit(solution)/shard_map/pallas_call | solution.py:457
  (10 shorter events, 0.0 us)
Async XLA Ops:
  0.6 1.6 copy-start.17
  2.2 0.9 copy-start.26
  9.2 81.6 %copy-start.15 = (f32[2,2,128,1]{3,2,1,0:T(8,128)S(1)}, f32[2,2,128,1]{3,2,1,0:T(8,128)}, u32[]{:S(2)}) copy-start(f32[2,2,128,1]{3,2,1,0:T(8,128)} %constant.63.clone.refs_2_) | copy-start | bytes 6148
  9.2 81.6 %copy-start.16 = (f32[2,1,256]{2,1,0:T(1,128)S(1)}, f32[2,1,256]{2,1,0:T(1,128)}, u32[]{:S(2)}) copy-start(f32[2,1,256]{2,1,0:T(1,128)} %constant.64.clone.refs_3_) | copy-start | bytes 6148
  87.5 29.6 %all-to-all-start = ((f32[32,2,32,128]{3,2,1,0:T(8,128)}), f32[32,2,32,128]{3,2,1,0:T(8,128)}, u32[]{:S(2)}, u32[]{:S(2)}) async-start(f32[32,2,32,128]{3,2,1,0:T(8,128)} %bitcast.2), calls=%async_computation | async-start | bytes 2097152 | tf_op jit(solution)/shard_map/all_to_all | solution.py:474
  90.8 1.9 copy-start.3
  92.7 1.0 copy-start.7
  93.8 1.0 copy-start.11
  94.8 1.0 copy-start.13
  107.1 1.6 copy-start
  117.1 1.9 copy-start.1
  119.0 1.0 copy-start.8
  120.1 1.0 copy-start.12
  121.1 1.0 copy-start.14
  126.9 40.0 %copy-start.2 = (f32[16,12,32,128]{3,2,1,0:T(8,128)}, f32[16,12,32,128]{3,2,1,0:T(8,128)S(1)}, u32[]{:S(2)}) copy-start(f32[16,12,32,128]{3,2,1,0:T(8,128)S(1)} %get-tuple-element.13) | copy-start | bytes 9437188
  167.0 4.0 %copy-start.25 = (bf16[2,256,256]{2,1,0:T(8,128)(2,1)S(1)}, bf16[2,256,256]{2,1,0:T(8,128)(2,1)}, u32[]{:S(2)}) copy-start(bf16[2,256,256]{2,1,0:T(8,128)(2,1)} %constant.70.clone.refs_3_) | copy-start | bytes 786436
  167.0 4.0 %copy-start.27 = (f32[6,1,512]{2,1,0:T(1,128)S(1)}, f32[6,1,512]{2,1,0:T(1,128)}, u32[]{:S(2)}) copy-start(f32[6,1,512]{2,1,0:T(1,128)} %constant.69.clone.refs_1_) | copy-start | bytes 36868
  167.0 43.3 %all-to-all-start.4 = ((f32[16,12,32,128]{3,2,1,0:T(8,128)}), f32[16,12,32,128]{3,2,1,0:T(8,128)S(1)}, u32[]{:S(2)}, u32[]{:S(2)}) async-start(f32[16,12,32,128]{3,2,1,0:T(8,128)} %copy-done.2), calls=%async_computation.4 | async-start | bytes 6291456 | tf_op jit(solution)/shard_map/all_to_all | solution.py:474
  170.9 1.9 copy-start.4
  172.8 1.0 copy-start.9
  173.9 1.4 copy-start.18
  175.3 1.2 copy-start.20
  176.5 1.0 copy-start.23
  188.1 1.3 copy-start.6
  210.3 54.6 %all-to-all-start.3 = ((f32[32,4,32,128]{3,2,1,0:T(8,128)}), f32[32,4,32,128]{3,2,1,0:T(8,128)}, u32[]{:S(2)}, u32[]{:S(2)}) async-start(f32[32,4,32,128]{3,2,1,0:T(8,128)} %bitcast.12), calls=%async_computation.3 | async-start | bytes 4194304 | tf_op jit(solution)/shard_map/all_to_all | solution.py:474
  216.6 1.0 copy-start.10
  217.7 1.4 copy-start.19
  219.1 1.2 copy-start.21
  220.3 1.0 copy-start.24
  231.9 1.3 copy-start.5
  233.2 83.4 %copy-start.22 = (bf16[2,2,256,256]{3,2,1,0:T(8,128)(2,1)S(1)}, bf16[2,2,256,256]{3,2,1,0:T(8,128)(2,1)}, u32[]{:S(2)}) copy-start(bf16[2,2,256,256]{3,2,1,0:T(8,128)(2,1)} %constant.73.clone.refs_1_) | copy-start | bytes 1572868
  264.9 51.7 %all-to-all-start.5 = ((f32[32,4,32,128]{3,2,1,0:T(8,128)}), f32[32,4,32,128]{3,2,1,0:T(8,128)S(1)}, u32[]{:S(2)}, u32[]{:S(2)}) async-start(f32[32,4,32,128]{3,2,1,0:T(8,128)} %bitcast.11), calls=%async_computation.5 | async-start | bytes 4194304 | tf_op jit(solution)/shard_map/all_to_all | solution.py:474

commit v5 on v4

v5 whole, which is shorter than its diff:
```python
import math

import jax
import jax.numpy as jnp
import ml_dtypes
import numpy as np
from jax import lax
from jax.experimental import pallas as pl
from jax.experimental.pallas import tpu as pltpu
from jax.sharding import PartitionSpec as P

AXES = ("wide", "narrow")
TILE = 128
LIMIT = 16 * 1024 * 1024


def angles(rows, columns, length):
    return (2.0 * math.pi / length) * (np.outer(rows, columns) % length)


def split_table(table):
    table = np.asarray(table, np.float64)
    high = table.astype(ml_dtypes.bfloat16)
    low = (table - high.astype(np.float64)).astype(ml_dtypes.bfloat16)
    return np.stack([high, low])


def split(value):
    high = value.astype(jnp.bfloat16)
    low = (value - high.astype(jnp.float32)).astype(jnp.bfloat16)
    return high, low


def product(left, right, contract=((1,), (0,))):
    (left_axis,), (right_axis,) = contract
    left = jnp.concatenate([left[0], left[0], left[1]], axis=left_axis)
    right = jnp.concatenate([right[0], right[1], right[0]], axis=right_axis)
    return lax.dot_general(
        left, right, (contract, ((), ())), preferred_element_type=jnp.float32
    )


def pair(ref):
    return ref[0], ref[1]


def signed_wave(index, length):
    index = np.asarray(index)
    return np.where(index < length // 2, index, index - length) * (2.0 * math.pi / length)


def params(steps):
    return pltpu.CompilerParams(
        vmem_limit_bytes=LIMIT, dimension_semantics=("arbitrary",) * steps
    )


def whole(shape):
    return pl.BlockSpec(shape, lambda *_: (0,) * len(shape))


def in_hbm(value):
    return pltpu.with_memory_space_constraint(jnp.asarray(value), pltpu.HBM)


def cost(macs, moved):
    return pl.CostEstimate(flops=6 * macs, bytes_accessed=moved, transcendentals=0)


def third_kernel(counts, table_ref, density_ref, *outs):
    rows_x, rows_y, length = density_ref.shape
    wide, sides, ranks = outs[0].shape[:3]
    half = length // 2
    flats = [ref.reshape(math.prod(ref.shape[:5]), 2 * rows_y) for ref in outs]
    table = pair(table_ref)
    left_half = lax.broadcasted_iota(jnp.int32, (half, 2 * rows_y), 1) < rows_y
    group = 4
    for first in range(0, rows_x, group):
        block = density_ref[first : first + group].reshape(group * rows_y, length)
        result = product(table, split(block), ((1,), (1,)))
        for inner in range(0, group, 2):
            lanes = slice(inner * rows_y, (inner + 2) * rows_y)
            real = result[:half, lanes]
            imag = result[half:, lanes]
            even = jnp.where(left_half, real, pltpu.roll(imag, rows_y, 1))
            odd = jnp.where(left_half, pltpu.roll(real, rows_y, 1), imag)
            for x, value in ((first + inner, even), (first + inner + 1, odd)):
                start = 0
                for flat, count in zip(flats, counts):
                    for c in range(count):
                        for rank in range(ranks):
                            at = (rank * count + c) * rows_x + x
                            stride = sides * ranks * count * rows_x
                            flat[pl.ds(at, wide, stride=stride), :] = value[start : start + wide]
                            start += wide
    for ref in outs:
        for side in range(1, sides):
            ref[:, side] = ref[:, 0]


def third_pass(density, wide, sides, ranks, counts):
    rows_x, rows_y, length = density.shape
    half = length // 2
    per_c = sum(counts)
    order = np.arange(half).reshape(wide, ranks, per_c).transpose(2, 1, 0).reshape(-1)
    angle = angles(order, np.arange(length), length)
    table = split_table(np.concatenate([np.cos(angle), -np.sin(angle)]))
    step = min(8, rows_x)

    def body(*refs):
        third_kernel(counts, *refs)

    return pl.pallas_call(
        body,
        grid=(rows_x // step,),
        in_specs=[
            whole(table.shape),
            pl.BlockSpec((step, rows_y, length), lambda i: (i, 0, 0)),
        ],
        out_specs=[
            pl.BlockSpec(
                (wide, sides, ranks, count, step, 2 * rows_y), lambda i: (0, 0, 0, 0, i, 0)
            )
            for count in counts
        ],
        out_shape=[
            jax.ShapeDtypeStruct((wide, sides, ranks, count, rows_x, 2 * rows_y), jnp.float32)
            for count in counts
        ],
        compiler_params=params(1),
        cost_estimate=cost(density.size * length, 12 * density.size),
    )(in_hbm(table), in_hbm(density))


PAIR = 2


def turn(angle):
    cosine, sine = np.cos(angle), np.sin(angle)
    return np.block([[cosine, -sine], [sine, cosine]])


def spectrum_kernel(slab, groups, side_ref, wave_c_ref, a_ref, b_ref, second_ref, first_ref, back_ref, in_ref, *refs):
    outs = refs[-groups:]
    wide, narrow, _, rows_x, lanes = in_ref.shape
    length = wide * rows_x
    half = length // 2
    quarter = half // 2
    devices, tiles, message, tile = outs[0].shape
    count = slab // groups
    sign_back = 1.0 - 2.0 * side_ref[0].astype(jnp.float32)

    def column(c, n):
        return in_ref[:, n, c].reshape(length, lanes)

    def columns(numbers):
        return jnp.concatenate(
            [
                jnp.concatenate([column(c, n) for n in numbers], axis=1)
                for c in range(PAIR)
            ],
            axis=0,
        )

    low, high = columns(range(narrow // 2)), columns(range(narrow // 2, narrow))
    planes = [
        product(split(low + high), pair(second_ref.at[0])),
        product(split(low - high), pair(second_ref.at[1])),
    ]

    def stacked(sign):
        return jnp.concatenate(
            [
                jnp.concatenate(
                    [
                        plane[c * length : c * length + half, part * half : (part + 1) * half]
                        + sign
                        * plane[c * length + half : (c + 1) * length, part * half : (part + 1) * half]
                        for c in range(PAIR)
                        for plane in planes
                    ],
                    axis=1,
                )
                for part in range(2)
            ],
            axis=0,
        )

    squared_b, scale_b = b_ref[0], b_ref[1]
    field = []
    for parity, sign in ((0, 1.0), (1, -1.0)):
        value = product(pair(first_ref.at[parity]), split(stacked(sign)))
        smooth = []
        for c in range(PAIR):
            wave_c = wave_c_ref[pl.program_id(0) * PAIR + c]
            scale_c = wave_c_ref[wave_c_ref.shape[0] // 2 + pl.program_id(0) * PAIR + c]
            squared = a_ref[1, parity] + (squared_b + wave_c * wave_c)
            inverse = scale_c / jnp.where(squared > 0, squared, 1.0)
            smooth.append(jnp.where(squared > 0, inverse * scale_b, 0.0) * a_ref[2, parity])
        smooth = jnp.concatenate(smooth, axis=1)
        field.append(value * jnp.concatenate([smooth, smooth], axis=0))
    upper = lax.broadcasted_iota(jnp.int32, (devices, message, tile), 1) < count
    for number in range(3):
        folded = jnp.concatenate(
            [
                field[parity][part * half : part * half + quarter]
                + sign_back * field[parity][part * half + quarter : (part + 1) * half]
                for part in range(2)
                for parity in range(2)
            ],
            axis=0,
        )
        values = [
            product(
                pair(back_ref.at[0, c % back_ref.shape[1]]),
                split(folded[:, c * length : (c + 1) * length]),
            )
            for c in range(PAIR)
        ]
        for spot in range(tiles // 3):
            parity, part = divmod(spot, 2)
            at = number * (tiles // 3) + spot
            here = [
                value[part * half : (part + 1) * half, parity * tile : (parity + 1) * tile]
                for value in values
            ]
            if groups == 2:
                even, odd = [value.reshape(devices, message, tile) for value in here]
                outs[0][:, at] = jnp.where(upper, even, odd)
                outs[1][:, at] = jnp.where(upper, odd, even)
            else:
                flat = outs[0].reshape(devices * tiles * message, tile)
                for c in range(PAIR):
                    for x in range(slab):
                        start = at * message + c * count + x
                        flat[pl.ds(start, devices, stride=tiles * message), :] = here[c][
                            x * devices : (x + 1) * devices
                        ]
        if number < 2:
            for parity in range(2):
                wave_a = a_ref[0, parity]
                field[parity] = field[parity] * jnp.concatenate([wave_a, wave_a], axis=0)


def halves(length):
    return np.arange(length).reshape(length // 2, 2).T


def spectrum_pass(received, side, waves_c, devices, groups, steps, first_step, filled):
    wide, narrow, per_c, rows_x, lanes = received.shape
    length = wide * rows_x
    rows_y = lanes // 2
    half = length // 2
    near = np.arange(half)
    split_index = halves(length)
    slab = half // devices
    second, first, back = [], [], []
    if groups == 2:
        orders = [
            near.reshape(devices, 2, slab // 2)[:, ::step].reshape(-1) for step in (1, -1)
        ]
    else:
        orders = [near.reshape(devices, slab).T.reshape(-1)]
    for parity, index in enumerate(split_index):
        table = turn(-angles(index, near, length)).reshape(2, half, 2, narrow // 2, rows_y)
        second.append(split_table(table.transpose(3, 2, 4, 0, 1).reshape(length, length)))
        first.append(split_table(turn(-angles(index, near, length))))
        columns = split_index[:, : half // 2].reshape(-1)
        back.append(
            [split_table(turn(angles(2 * order + parity, columns, length))) for order in orders]
        )
    tables = [np.stack(second), np.stack(first), np.stack([np.stack(each) for each in back])]
    wave = signed_wave(split_index, length)
    scale = np.where(split_index == half, 0.0, np.exp(-0.5 * wave**2))
    a_table = np.stack([wave, wave**2, scale]).astype(np.float32)[..., None]
    b_table = np.stack([wave**2, scale]).astype(np.float32).reshape(2, 1, length)
    message = PAIR * slab // groups
    out_shape = (devices, 3 * 2 * length // TILE, steps * message, TILE)
    block = out_shape[:2] + (message, TILE)

    def body(*refs):
        spectrum_kernel(slab, groups, *refs)

    def fixed(shape):
        return pl.BlockSpec(shape, lambda *_: (0,) * len(shape))

    return pl.pallas_call(
        body,
        grid_spec=pltpu.PrefetchScalarGridSpec(
            num_scalar_prefetch=2,
            grid=(per_c // PAIR,),
            in_specs=[
                fixed(a_table.shape),
                fixed(b_table.shape),
                fixed(tables[0].shape),
                fixed(tables[1].shape),
                pl.BlockSpec((1,) + tables[2].shape[1:], lambda i, s, _: (s[0], 0, 0, 0, 0)),
                pl.BlockSpec((wide, narrow, PAIR, rows_x, lanes), lambda i, *_: (0, 0, i, 0, 0)),
                *[pl.BlockSpec(memory_space=pl.ANY)] * len(filled),
            ],
            out_specs=[pl.BlockSpec(block, lambda i, *_: (0, 0, first_step + i, 0))] * groups,
        ),
        out_shape=[pltpu.HBM(out_shape, jnp.float32)] * groups,
        input_output_aliases={8 + spot: spot for spot in range(len(filled))},
        compiler_params=params(1),
        cost_estimate=cost(per_c * 7 * length**3, 20 * per_c * length**2 * 2),
    )(
        side,
        waves_c,
        *[in_hbm(table) for table in (a_table, b_table, *tables)],
        in_hbm(received),
        *[in_hbm(each) for each in filled],
    )


def shear_kernel(
    per_c, group, joined, row_ref, lane_ref, second_ref, third_ref, ahead_ref, last_ref, in_ref, out_ref, shear_ref
):
    step = pl.program_id(0)
    length = shear_ref.shape[0]
    half = length // 2
    devices, tiles, message, tile = in_ref.shape
    count = message // per_c
    flat = in_ref.reshape(devices * tiles * message, tile)

    @pl.when(step == 0)
    def _():
        shear_ref[...] = jnp.zeros_like(shear_ref)

    field = jnp.concatenate(
        [
            jnp.concatenate(
                [
                    flat[pl.ds((source * tiles + spot) * message + x, per_c, stride=count), :]
                    for x in range(count)
                    for source in range(devices)
                ],
                axis=0,
            )
            for spot in range(tiles)
        ],
        axis=1,
    )
    field = field * row_ref[0] * lane_ref[0]
    even = product(split(field[:, :length]), pair(second_ref.at[0]))
    odd = product(split(field[:, length:]), pair(second_ref.at[1]))
    near, far = even + odd, even - odd
    field = jnp.concatenate(
        [
            jnp.concatenate(
                [
                    value[x * half : (x + 1) * half, part * half : (part + 1) * half]
                    for x in range(count)
                    for value in (near, far)
                ],
                axis=1,
            )
            for part in range(2)
        ],
        axis=0,
    )
    field = product(pair(third_ref), split(field))
    shear_ref[...] += field * field

    @pl.when(step == 5)
    def _():
        ahead = jnp.concatenate(
            [shear_ref[:, x * length : (x + 1) * length] for x in range(count)], axis=0
        )
        ahead = product(split(ahead), pair(ahead_ref))
        ahead = jnp.concatenate(
            [
                jnp.concatenate(
                    [
                        ahead[x * length : (x + 1) * length, part * length : (part + 1) * length]
                        for x in range(count)
                    ],
                    axis=1,
                )
                for part in range(2)
            ],
            axis=0,
        )
        value = product(pair(last_ref), split(ahead))
        wide, narrow, message_out, _ = out_ref.shape
        rows_b = length // wide
        slots = tile // rows_b
        rows = 2 * length // slots
        run = rows // (2 * narrow * joined)
        out = out_ref.reshape(wide * narrow * message_out, tile)
        lane = lax.broadcasted_iota(jnp.int32, (rows, tile), 1) // rows_b
        for x in range(count):
            for w in range(wide):
                block, place = divmod(w, slots)
                lanes = slice(x * length + block * tile, x * length + (block + 1) * tile)
                moved = None
                for slot in range(slots):
                    piece = value[slot * rows : (slot + 1) * rows, lanes]
                    if slot != place:
                        piece = pltpu.roll(piece, (slot - place) * rows_b % tile, 1)
                    moved = piece if moved is None else jnp.where(lane == slot, piece, moved)
                for n in range(narrow):
                    for part in range(2):
                        for join in range(joined):
                            start = ((n * 2 + part) * joined + join) * run
                            piece = moved[start : start + run]
                            at = (w * narrow + n) * message_out
                            if joined == 2:
                                at += part * 2 * count + (join ^ group) * count + x
                                out[pl.ds(at, run, stride=4 * count), :] = piece
                            else:
                                at += (x * 2 + part) * run
                                out[pl.ds(at, run), :] = piece


def shear_pass(received, wide, narrow, per_c, group, joined):
    devices, tiles, message, tile = received.shape
    count = message // per_c
    length = tiles * tile // 6
    half = length // 2
    index = np.arange(length)
    angle = angles(index, index, length)
    cosine, sine = np.cos(angle), np.sin(angle)
    split_index = halves(length)
    second = np.stack(
        [split_table(turn(angles(np.arange(half), b, length)).T) for b in split_index]
    )
    row_c = np.arange(half) ^ group
    weight = np.where(row_c == 0, 1.0, 2.0)
    angle = angles(index, row_c, length)
    third = np.concatenate([weight * np.cos(angle), -weight * np.sin(angle)], axis=1)
    ahead = np.concatenate([cosine, -sine], axis=1)
    slots = TILE * wide // length
    order = index.reshape(narrow, -1, joined, slots).transpose(3, 0, 2, 1)
    angle = angles(order.reshape(-1), index, length)
    last = np.stack(
        [
            np.concatenate([np.cos(angle), np.sin(angle)], axis=1),
            np.concatenate([-np.sin(angle), np.cos(angle)], axis=1),
        ]
    )
    last = last.reshape(2, slots, narrow, -1, 2 * length).transpose(1, 2, 0, 3, 4)
    last = last.reshape(2 * length, 2 * length)
    wave = signed_wave(index, length)
    wave_rows = np.tile(wave[row_c], count)
    wave_lanes = np.stack([wave[split_index]] * 2, axis=1).reshape(-1)
    twice = math.sqrt(2.0)
    one_row, one_lane = np.ones_like(wave_rows), np.ones_like(wave_lanes)
    row_factor = np.stack(
        [one_row, twice * one_row, twice * wave_rows, one_row, twice * wave_rows, wave_rows**2]
    ).astype(np.float32)[:, :, None]
    lane_factor = np.stack(
        [one_lane, wave_lanes, one_lane, wave_lanes**2, wave_lanes, one_lane]
    ).astype(np.float32)[:, None, :]
    tables = [second] + [split_table(table) for table in (third, ahead, last)]
    out_shape = (wide, narrow, count * 2 * length // (narrow * slots), TILE)

    def body(*refs):
        shear_kernel(per_c, group, joined, *refs)

    def which(i):
        return (0, 2 - (i >= 1).astype(jnp.int32) - (i >= 3).astype(jnp.int32), 0, 0)

    return pl.pallas_call(
        body,
        grid=(6,),
        in_specs=[
            pl.BlockSpec((1, count * half, 1), lambda i: (i, 0, 0)),
            pl.BlockSpec((1, 1, 2 * length), lambda i: (i, 0, 0)),
            *[whole(table.shape) for table in tables],
            pl.BlockSpec((devices, tiles // 3, message, tile), which),
        ],
        out_specs=whole(out_shape),
        out_shape=pltpu.HBM(out_shape, jnp.float32),
        scratch_shapes=[pltpu.VMEM((length, count * length), jnp.float32)],
        compiler_params=params(1),
        cost_estimate=cost(count * 18 * length**3, 4 * received.size + 4 * 2**20),
    )(*[in_hbm(value) for value in (row_factor, lane_factor, *tables, received)])


def first_kernel(count, rows_b, anchor_ref, table_ref, *refs):
    ins, (real_ref, imag_ref) = refs[:-2], refs[-2:]
    wide, sides, ranks, rows, lanes = ins[0].shape
    length = real_ref.shape[2]
    half = length // 2
    slots = lanes // rows_b
    joined = len(ins)
    steps = real_ref.shape[0] // (slots * joined)
    spot_row = lax.broadcasted_iota(jnp.int32, (lanes, half), 0)
    spot_a = lax.broadcasted_iota(jnp.int32, (lanes, half), 1)
    is_anchor = (anchor_ref[0] == 1) & (pl.program_id(0) == 0)
    anchor = (spot_row == 0) & (spot_a == 0) & is_anchor
    upper = lax.broadcasted_iota(jnp.int32, (wide * ranks, joined * count, lanes), 1) < count

    def gathered(side, step, join, part):
        if joined == 2:
            at = pl.ds((step * 2 + part) * 2 * count, 2 * count)
            own, other = [
                ref[:, side, :, at].reshape(wide * ranks, 2 * count, lanes)
                for ref in (ins if join == 0 else ins[::-1])
            ]
            return jnp.where(upper, own, other).reshape(half, lanes)
        flat = ins[0].reshape(wide * sides * ranks * rows, lanes)
        run = rows // count
        return jnp.concatenate(
            [
                flat[
                    pl.ds((w * sides + side) * ranks * rows + part * steps + step, ranks * count, stride=run),
                    :,
                ]
                for w in range(wide)
            ],
            axis=0,
        )

    for join in range(joined):
        sums = []
        for side in range(sides):
            left = jnp.concatenate(
                [
                    jnp.concatenate([gathered(side, step, join, part).T for part in range(2)], axis=1)
                    for step in range(steps)
                ],
                axis=0,
            )
            sums.append(product(split(left), pair(table_ref.at[join, side])))
        even, odd = sums
        for far, value in enumerate((even + odd, even - odd)):
            for step in range(steps):
                at = (step * joined + join) * slots
                columns = slice(far * half, (far + 1) * half)
                for part, ref in enumerate((real_ref, imag_ref)):
                    here = value[step * lanes : (step + 1) * lanes, part * half : (part + 1) * half]
                    if at == 0 and far == 0:
                        here = jnp.where(anchor, 0.0, here)
                    ref[at : at + slots, :, columns] = here.reshape(slots, rows_b, half)


def first_pass(parts, is_anchor, length, wide, sides, count):
    devices, rows, lanes = parts[0].shape
    joined = len(parts)
    ranks = devices // wide // sides
    rows_b = length // wide
    slots = lanes // rows_b
    scale = 1.0 / float(length) ** 1.5
    index = np.arange(length).reshape(wide * ranks, joined, count, sides)
    tables = []
    for join in range(joined):
        order = index[:, :: 1 - 2 * join].transpose(3, 0, 1, 2).reshape(sides, -1)
        tables.append(
            [split_table(scale * turn(-angles(np.arange(length // 2), x, length)).T) for x in order]
        )
    table = np.stack([np.stack(each) for each in tables])
    total = rows // (2 * joined * count) if joined == 2 else rows // (2 * count)
    grid = 4 if joined == 2 and total % 4 == 0 else 1
    parts = [part.reshape(wide, sides, ranks, rows, lanes) for part in parts]

    def body(*refs):
        first_kernel(count, rows_b, *refs)

    rows_c = total * joined * slots
    out_shape = jax.ShapeDtypeStruct((rows_c, rows_b, length), jnp.float32)
    return pl.pallas_call(
        body,
        grid=(grid,),
        in_specs=[
            pl.BlockSpec(memory_space=pltpu.SMEM),
            whole(table.shape),
            *[pl.BlockSpec((wide, sides, ranks, rows // grid, lanes), lambda i: (0, 0, 0, i, 0))]
            * joined,
        ],
        out_specs=[pl.BlockSpec((rows_c // grid, rows_b, length), lambda i: (i, 0, 0))] * 2,
        out_shape=[out_shape] * 2,
        compiler_params=params(1),
        cost_estimate=cost(rows_c * 2 * rows_b * length * length, 16 * rows_c * rows_b * length),
    )(is_anchor, table, *parts)


def transpose(value, members=None):
    return lax.all_to_all(
        value, AXES, split_axis=0, concat_axis=0, tiled=True, axis_index_groups=members
    )


def solution(mesh):
    wide, narrow = mesh.shape["wide"], mesh.shape["narrow"]
    sides = 2
    ranks = narrow // sides
    devices = wide * ranks
    members = [
        [w * narrow + side * ranks + rank for w in range(wide) for rank in range(ranks)]
        for side in range(sides)
    ]

    def per_device(density):
        rows_x, rows_y, length = density.shape
        half = length // 2
        per_c = half // devices
        slab = half // devices
        steps = per_c // PAIR
        counts = [per_c - PAIR, PAIR] if steps > 1 else [per_c]
        groups = 2 if slab > 2 else 1
        spot_wide, spot_narrow = lax.axis_index("wide"), lax.axis_index("narrow")
        side = (spot_narrow // ranks).astype(jnp.int32).reshape(1)
        rank = spot_wide * ranks + spot_narrow % ranks
        waves_c = (rank * per_c + jnp.arange(per_c, dtype=jnp.int32)).astype(jnp.float32)
        waves_c = waves_c * (2.0 * math.pi / length)
        scales_c = jnp.exp(-0.5 * waves_c * waves_c) * (1.0 / float(length) ** 3)
        chunks, start = [], 0
        for planes, count in zip(third_pass(density, wide, sides, ranks, counts), counts):
            planes = transpose(planes.reshape(wide * narrow, count, rows_x, 2 * rows_y))
            planes = planes.reshape(wide, narrow, count, rows_x, 2 * rows_y)
            spots = slice(start, start + count)
            both_c = jnp.concatenate([waves_c[spots], scales_c[spots]])
            chunks = spectrum_pass(
                planes, side, both_c, devices, groups, steps, start // PAIR, chunks
            )
            start += count
        is_anchor = ((spot_wide == 0) & (spot_narrow == 0)).astype(jnp.int32).reshape(1)
        parts = []
        for group, chunk in enumerate(chunks):
            part = shear_pass(transpose(chunk, members), wide, narrow, per_c, group, groups)
            parts.append(transpose(part.reshape((wide * narrow,) + part.shape[2:])))
        return tuple(first_pass(parts, is_anchor, length, wide, sides, slab // groups))

    return jax.shard_map(
        per_device,
        mesh=mesh,
        in_specs=(P("wide", "narrow", None),),
        out_specs=(P("narrow", "wide", None), P("narrow", "wide", None)),
        check_vma=False,
    )
```

time: 325 us -> 320 us (0.985)
  local copies, waits for them, and re-layouts: 28.2 us -> 2.75 us
  waiting for transfers between devices: 109 us -> 124 us
  Pallas kernels: 49.8 us -> 54.9 us
    unnamed x56 -> x6, local copies, waits for them, and re-layouts: 28.1 us -> 2.6 us
    all_to_all x4, waiting for transfers between devices: 109 us -> 124 us  [transpose(): lax.all_to_all(value, AXES, split_axis=0, concat_axis=0, tiled=True, axis...]
    pallas_call x2, Pallas kernels: 21 us -> 28.5 us  [shear_pass(): pl.pallas_call(body, grid=(6,), in_specs=[pl.BlockSpec((1, count * half,...]
  transfers between devices with their start and end apart: 4 -> 4, of which waited for: 4 -> 4; matrix products, arithmetic and copies ran while one was open for 0% -> 0% of each run, Pallas kernels for 10% -> 12%
where the time goes in v5:
time: 320 us; the launch traced here: 319 us
  waiting for transfers between devices  124 us (39%)
  blocking collectives  119 us (37%)
  Pallas kernels  54.9 us (17%)
  starting transfers between devices  17.6 us (6%)
    all_to_all x4, waiting for transfers between devices, transpose(): lax.all_to_all(value, AXES, split_axis=0, concat_axis=0, tiled=True, axis...  124 us
    all_to_all x2, blocking collectives, transpose(): lax.all_to_all(value, AXES, split_axis=0, concat_axis=0, tiled=True, axis...  119 us
    pallas_call x2, Pallas kernels, shear_pass(): pl.pallas_call(body, grid=(6,), in_specs=[pl.BlockSpec((1, count * half,...  28.5 us
    all_to_all x4, starting transfers between devices, transpose(): lax.all_to_all(value, AXES, split_axis=0, concat_axis=0, tiled=True, axis...  17.6 us
    pallas_call x2, Pallas kernels, spectrum_pass(): pl.pallas_call(body, grid_spec=pltpu.PrefetchScalarGridSpec(num_scalar_pr...  15.1 us
  transfers between devices with their start and end apart: 4, of which 4 were waited for; matrix products, arithmetic and copies ran while one was open for 0% of the time, Pallas kernels for 12%

profile of v5, /device:TPU:1, one launch (start us, length us, event | category | flops | bytes accessed | tf_op | source)
XLA Modules:
  0.0 319.1 jit_solution(16549875981749819267)
XLA Ops:
  0.6 5.6 %shard_map.248 = (f32[8,2,2,6,32,128]{5,4,3,2,1,0:T(8,128)S(1)}, f32[8,2,2,2,32,128]{5,4,3,2,1,0:T(8,128)}) custom-call(bf16[2,256,256]{2,1,0:T(8,128)(2,1)} %constant.71.clone.refs_0_, f32[32,64,256]{2,1,0:T(8,128)} %refs_1_.4), custom_call_target="tpu_custom_call" | custom-call | flops 805306368 | bytes 6291456 | tf_op jit(solution)/shard_map/pallas_call | solution.py:113
  6.2 78.3 %all_to_all.30 = f32[32,6,32,128]{3,2,1,0:T(8,128)} all-to-all(f32[32,6,32,128]{3,2,1,0:T(8,128)S(1)} %bitcast.12), channel_id=1, replica_groups=mesh['wide'=8,'narrow'=4] {'wide','narrow'}, dimensions={0} | all-to-all | bytes 6291456 | tf_op jit(solution)/shard_map/all_to_all | solution.py:580
  84.5 3.2 all-to-all-start
  87.7 0.1 slice.13
  87.8 0.1 slice.12
  87.8 0.1 pad_maximum_fusion.1.refs_1_
  87.9 0.1 pad_maximum_fusion.refs_1_
  88.0 9.6 %shard_map.249 = (f32[16,12,32,128]{3,2,1,0:T(8,128)}, f32[16,12,32,128]{3,2,1,0:T(8,128)}) custom-call(s32[1]{0:T(128)} %bitcast.1.refs_0_, f32[12]{0:T(128)S(1)} %pad_maximum_fusion.1.refs_1_, f32[3,2,128,1]{3,2,1,0:T(8,128)} %constant.72.clone.refs_2_, f32[2,1,256]{2,1,0:T(1,128)} %constant.73.clone.refs_3_, ...), custom_call_target="tpu_custom_call" | custom-call | flops 4227858432 | bytes 15728640 | tf_op jit(solution)/shard_map/pallas_call | solution.py:287
  97.6 16.4 %all-to-all-done = f32[32,2,32,128]{3,2,1,0:T(8,128)S(1)} async-done(((f32[32,2,32,128]{3,2,1,0:T(8,128)}), f32[32,2,32,128]{3,2,1,0:T(8,128)S(1)}, u32[]{:S(2)}, u32[]{:S(2)}) %all-to-all-start) | async-done | bytes 1048608 | tf_op jit(solution)/shard_map/all_to_all | solution.py:580
  114.0 0.0 copy-start.1
  114.0 1.0 copy-done.1
  115.0 5.5 %shard_map.250 = (f32[16,12,32,128]{3,2,1,0:T(8,128)}, f32[16,12,32,128]{3,2,1,0:T(8,128)}) custom-call(s32[1]{0:T(128)} %bitcast.1.refs_0_, f32[4]{0:T(128)S(1)} %pad_maximum_fusion.refs_1_, f32[3,2,128,1]{3,2,1,0:T(8,128)} %constant.72.clone.refs_2_, f32[2,1,256]{2,1,0:T(1,128)} %constant.73.clone.refs_3_, ...), custom_call_target="tpu_custom_call", output_to_operand_aliasing={{0}: (8, {}), {1}: (9, {})} | custom-call | flops 1409286144 | bytes 5242880 | tf_op jit(solution)/shard_map/pallas_call | solution.py:287
  120.5 40.8 %all_to_all.31.refs_6_ = f32[16,12,32,128]{3,2,1,0:T(8,128)} all-to-all(f32[16,12,32,128]{3,2,1,0:T(8,128)} %get-tuple-element.12), channel_id=1, replica_groups={{0,1,4,5,8,9,12,13,16,17,20,21,24,25,28,29},{2,3,6,7,10,11,14,15,18,19,..., dimensions={0} | all-to-all | bytes 6291456 | tf_op jit(solution)/shard_map/all_to_all | solution.py:580
  161.4 5.7 %all-to-all-start.4 = ((f32[16,12,32,128]{3,2,1,0:T(8,128)}), f32[16,12,32,128]{3,2,1,0:T(8,128)S(1)}, u32[]{:S(2)}, u32[]{:S(2)}) async-start(f32[16,12,32,128]{3,2,1,0:T(8,128)} %get-tuple-element.13), calls=%async_computation.4 | async-start | bytes 6291456 | tf_op jit(solution)/shard_map/all_to_all | solution.py:580
  167.1 14.2 %shard_map.251 = f32[8,4,128,128]{3,2,1,0:T(8,128)} custom-call(f32[6,512,1]{2,1,0:T(8,128)} %constant.77.clone.refs_0_, f32[6,1,512]{2,1,0:T(1,128)} %constant.78.clone.refs_1_, bf16[2,2,256,256]{3,2,1,0:T(8,128)(2,1)} %constant.75.clone.refs_5_.refs_2_, bf16[2,256,256]{2,1,0:T(8,128)(2,1)} %constant.79.clone.refs_3_, ...), custom_call_target="tpu_custom_call" | custom-call | flops 7247757312 | bytes 7340032 | tf_op jit(solution)/shard_map/pallas_call | solution.py:464
  181.3 25.1 %all-to-all-done.4.refs_6_ = f32[16,12,32,128]{3,2,1,0:T(8,128)S(1)} async-done(((f32[16,12,32,128]{3,2,1,0:T(8,128)}), f32[16,12,32,128]{3,2,1,0:T(8,128)S(1)}, u32[]{:S(2)}, u32[]{:S(2)}) %all-to-all-start.4) | async-done | bytes 3145760 | tf_op jit(solution)/shard_map/all_to_all | solution.py:580
  206.4 0.0 copy-start.2
  206.4 1.6 copy-done.2
  208.1 5.3 %all-to-all-start.3 = ((f32[32,128,128]{2,1,0:T(8,128)}), f32[32,128,128]{2,1,0:T(8,128)S(1)}, u32[]{:S(2)}, u32[]{:S(2)}) async-start(f32[32,128,128]{2,1,0:T(8,128)} %bitcast.17), calls=%async_computation.3 | async-start | bytes 4194304 | tf_op jit(solution)/shard_map/all_to_all | solution.py:580
  213.4 14.2 %shard_map.252 = f32[8,4,128,128]{3,2,1,0:T(8,128)} custom-call(f32[6,512,1]{2,1,0:T(8,128)} %constant.82.clone.refs_0_, f32[6,1,512]{2,1,0:T(1,128)} %constant.78.clone.refs_1_, bf16[2,2,256,256]{3,2,1,0:T(8,128)(2,1)} %constant.75.clone.refs_5_.refs_2_, bf16[2,256,256]{2,1,0:T(8,128)(2,1)} %constant.83.clone.refs_3_, ...), custom_call_target="tpu_custom_call" | custom-call | flops 7247757312 | bytes 7340032 | tf_op jit(solution)/shard_map/pallas_call | solution.py:464
  227.6 34.0 %all-to-all-done.3 = f32[32,128,128]{2,1,0:T(8,128)S(1)} async-done(((f32[32,128,128]{2,1,0:T(8,128)}), f32[32,128,128]{2,1,0:T(8,128)S(1)}, u32[]{:S(2)}, u32[]{:S(2)}) %all-to-all-start.3) | async-done | bytes 2097184 | tf_op jit(solution)/shard_map/all_to_all | solution.py:580
  261.6 0.0 copy-start
  261.6 3.5 %all-to-all-start.5 = ((f32[32,128,128]{2,1,0:T(8,128)}), f32[32,128,128]{2,1,0:T(8,128)}, u32[]{:S(2)}, u32[]{:S(2)}) async-start(f32[32,128,128]{2,1,0:T(8,128)} %bitcast.16), calls=%async_computation.5 | async-start | bytes 4194304 | tf_op jit(solution)/shard_map/all_to_all | solution.py:580
  265.1 48.3 %all-to-all-done.5 = f32[32,128,128]{2,1,0:T(8,128)} async-done(((f32[32,128,128]{2,1,0:T(8,128)}), f32[32,128,128]{2,1,0:T(8,128)}, u32[]{:S(2)}, u32[]{:S(2)}) %all-to-all-start.5) | async-done | bytes 2097184 | tf_op jit(solution)/shard_map/all_to_all | solution.py:580
  313.4 0.0 copy-done
  313.4 5.7 %shard_map.253 = (f32[64,32,256]{2,1,0:T(8,128)}, f32[64,32,256]{2,1,0:T(8,128)}) custom-call(s32[1]{0:T(128)} %bitcast.refs_0_, bf16[2,2,2,256,256]{4,3,2,1,0:T(8,128)(2,1)S(1)} %copy-done, f32[8,2,2,128,128]{4,3,2,1,0:T(8,128)S(1)} %bitcast.13, f32[8,2,2,128,128]{4,3,2,1,0:T(8,128)} %bitcast.9.refs_3_), custom_call_target="tpu_custom_call" | custom-call | flops 1610612736 | bytes 8388608 | tf_op jit(solution)/shard_map/pallas_call | solution.py:563
  (1 shorter events, 0.0 us)
Async XLA Ops:
  84.5 29.5 %all-to-all-start = ((f32[32,2,32,128]{3,2,1,0:T(8,128)}), f32[32,2,32,128]{3,2,1,0:T(8,128)S(1)}, u32[]{:S(2)}, u32[]{:S(2)}) async-start(f32[32,2,32,128]{3,2,1,0:T(8,128)} %bitcast.2), calls=%async_computation | async-start | bytes 2097152 | tf_op jit(solution)/shard_map/all_to_all | solution.py:580
  114.0 1.0 copy-start.1
  161.4 45.0 %all-to-all-start.4 = ((f32[16,12,32,128]{3,2,1,0:T(8,128)}), f32[16,12,32,128]{3,2,1,0:T(8,128)S(1)}, u32[]{:S(2)}, u32[]{:S(2)}) async-start(f32[16,12,32,128]{3,2,1,0:T(8,128)} %get-tuple-element.13), calls=%async_computation.4 | async-start | bytes 6291456 | tf_op jit(solution)/shard_map/all_to_all | solution.py:580
  206.4 1.6 copy-start.2
  208.1 53.5 %all-to-all-start.3 = ((f32[32,128,128]{2,1,0:T(8,128)}), f32[32,128,128]{2,1,0:T(8,128)S(1)}, u32[]{:S(2)}, u32[]{:S(2)}) async-start(f32[32,128,128]{2,1,0:T(8,128)} %bitcast.17), calls=%async_computation.3 | async-start | bytes 4194304 | tf_op jit(solution)/shard_map/all_to_all | solution.py:580
  261.6 51.8 %copy-start = (bf16[2,2,2,256,256]{4,3,2,1,0:T(8,128)(2,1)S(1)}, bf16[2,2,2,256,256]{4,3,2,1,0:T(8,128)(2,1)}, u32[]{:S(2)}) copy-start(bf16[2,2,2,256,256]{4,3,2,1,0:T(8,128)(2,1)} %constant.84.clone.refs_1_) | copy-start | bytes 3145732
  261.6 51.8 %all-to-all-start.5 = ((f32[32,128,128]{2,1,0:T(8,128)}), f32[32,128,128]{2,1,0:T(8,128)}, u32[]{:S(2)}, u32[]{:S(2)}) async-start(f32[32,128,128]{2,1,0:T(8,128)} %bitcast.16), calls=%async_computation.5 | async-start | bytes 4194304 | tf_op jit(solution)/shard_map/all_to_all | solution.py:580

commit v6 on v5

--- a/solution.py
+++ b/solution.py
@@ -59,8 +59,12 @@
     return pl.BlockSpec(shape, lambda *_: (0,) * len(shape))
 
 
+def keep(value, near):
+    return pltpu.with_memory_space_constraint(jnp.asarray(value), pltpu.VMEM if near else pltpu.HBM)
+
+
 def in_hbm(value):
-    return pltpu.with_memory_space_constraint(jnp.asarray(value), pltpu.HBM)
+    return keep(value, False)
 
 
 def cost(macs, moved):
@@ -308,13 +312,26 @@
         side,
         waves_c,
         *[in_hbm(table) for table in (a_table, b_table, *tables)],
-        in_hbm(received),
+        received,
         *[in_hbm(each) for each in filled],
     )
 
 
 def shear_kernel(
-    per_c, group, joined, row_ref, lane_ref, second_ref, third_ref, ahead_ref, last_ref, in_ref, out_ref, shear_ref
+    per_c,
+    group,
+    joined,
+    _,
+    row_ref,
+    lane_ref,
+    second_ref,
+    third_ref,
+    ahead_ref,
+    last_ref,
+    in_ref,
+    own_ref,
+    other_ref,
+    shear_ref,
 ):
     step = pl.program_id(0)
     length = shear_ref.shape[0]
@@ -381,13 +398,14 @@
             ],
             axis=0,
         )
-        value = product(pair(last_ref), split(ahead))
-        wide, narrow, message_out, _ = out_ref.shape
+        value = product(pair(last_ref.at[0]), split(ahead))
+        wide, ranks, message_out, _ = own_ref.shape
+        narrow = 2 * ranks
         rows_b = length // wide
         slots = tile // rows_b
         rows = 2 * length // slots
         run = rows // (2 * narrow * joined)
-        out = out_ref.reshape(wide * narrow * message_out, tile)
+        outs = [ref.reshape(wide * ranks * message_out, tile) for ref in (own_ref, other_ref)]
         lane = lax.broadcasted_iota(jnp.int32, (rows, tile), 1) // rows_b
         for x in range(count):
             for w in range(wide):
@@ -400,11 +418,12 @@
                         piece = pltpu.roll(piece, (slot - place) * rows_b % tile, 1)
                     moved = piece if moved is None else jnp.where(lane == slot, piece, moved)
                 for n in range(narrow):
+                    out = outs[n // ranks]
                     for part in range(2):
                         for join in range(joined):
                             start = ((n * 2 + part) * joined + join) * run
                             piece = moved[start : start + run]
-                            at = (w * narrow + n) * message_out
+                            at = (w * ranks + n % ranks) * message_out
                             if joined == 2:
                                 at += part * 2 * count + (join ^ group) * count + x
                                 out[pl.ds(at, run, stride=4 * count), :] = piece
@@ -413,7 +432,7 @@
                                 out[pl.ds(at, run), :] = piece
 
 
-def shear_pass(received, wide, narrow, per_c, group, joined):
+def shear_pass(received, side, wide, narrow, per_c, group, joined):
     devices, tiles, message, tile = received.shape
     count = message // per_c
     length = tiles * tile // 6
@@ -440,7 +459,12 @@
         ]
     )
     last = last.reshape(2, slots, narrow, -1, 2 * length).transpose(1, 2, 0, 3, 4)
-    last = last.reshape(2 * length, 2 * length)
+    last = np.stack(
+        [
+            split_table(np.roll(last, -own, axis=1).reshape(2 * length, 2 * length))
+            for own in (0, narrow // 2)
+        ]
+    )
     wave = signed_wave(index, length)
     wave_rows = np.tile(wave[row_c], count)
     wave_lanes = np.stack([wave[split_index]] * 2, axis=1).reshape(-1)
@@ -452,39 +476,46 @@
     lane_factor = np.stack(
         [one_lane, wave_lanes, one_lane, wave_lanes**2, wave_lanes, one_lane]
     ).astype(np.float32)[:, None, :]
-    tables = [second] + [split_table(table) for table in (third, ahead, last)]
-    out_shape = (wide, narrow, count * 2 * length // (narrow * slots), TILE)
+    tables = [second, split_table(third), split_table(ahead)]
+    out_shape = (wide, narrow // 2, count * 2 * length // (narrow * slots), TILE)
 
     def body(*refs):
         shear_kernel(per_c, group, joined, *refs)
 
-    def which(i):
+    def which(i, _):
         return (0, 2 - (i >= 1).astype(jnp.int32) - (i >= 3).astype(jnp.int32), 0, 0)
 
     return pl.pallas_call(
         body,
-        grid=(6,),
-        in_specs=[
-            pl.BlockSpec((1, count * half, 1), lambda i: (i, 0, 0)),
-            pl.BlockSpec((1, 1, 2 * length), lambda i: (i, 0, 0)),
-            *[whole(table.shape) for table in tables],
-            pl.BlockSpec((devices, tiles // 3, message, tile), which),
-        ],
-        out_specs=whole(out_shape),
-        out_shape=pltpu.HBM(out_shape, jnp.float32),
-        scratch_shapes=[pltpu.VMEM((length, count * length), jnp.float32)],
+        grid_spec=pltpu.PrefetchScalarGridSpec(
+            num_scalar_prefetch=1,
+            grid=(6,),
+            in_specs=[
+                pl.BlockSpec((1, count * half, 1), lambda i, _: (i, 0, 0)),
+                pl.BlockSpec((1, 1, 2 * length), lambda i, _: (i, 0, 0)),
+                *[whole(table.shape) for table in tables],
+                pl.BlockSpec((1,) + last.shape[1:], lambda i, s: (s[0], 0, 0, 0)),
+                pl.BlockSpec((devices, tiles // 3, message, tile), which),
+            ],
+            out_specs=[whole(out_shape)] * 2,
+            scratch_shapes=[pltpu.VMEM((length, count * length), jnp.float32)],
+        ),
+        out_shape=[pltpu.HBM(out_shape, jnp.float32)] * 2,
         compiler_params=params(1),
         cost_estimate=cost(count * 18 * length**3, 4 * received.size + 4 * 2**20),
-    )(*[in_hbm(value) for value in (row_factor, lane_factor, *tables, received)])
-
-
-def first_kernel(count, rows_b, anchor_ref, table_ref, *refs):
+    )(side, *[in_hbm(value) for value in (row_factor, lane_factor, *tables, last)], received)
+
+
+def first_kernel(count, rows_b, side_ref, anchor_ref, table_ref, *refs):
     ins, (real_ref, imag_ref) = refs[:-2], refs[-2:]
-    wide, sides, ranks, rows, lanes = ins[0].shape
+    wide, ranks, rows, lanes = ins[0].shape
     length = real_ref.shape[2]
     half = length // 2
     slots = lanes // rows_b
-    joined = len(ins)
+    joined = len(ins) // 2
+    sources = ins[:joined], ins[joined:]
+    side = side_ref[0]
+    sign = 1.0 - 2.0 * side.astype(jnp.float32)
     steps = real_ref.shape[0] // (slots * joined)
     spot_row = lax.broadcasted_iota(jnp.int32, (lanes, half), 0)
     spot_a = lax.broadcasted_iota(jnp.int32, (lanes, half), 1)
@@ -492,40 +523,30 @@
     anchor = (spot_row == 0) & (spot_a == 0) & is_anchor
     upper = lax.broadcasted_iota(jnp.int32, (wide * ranks, joined * count, lanes), 1) < count
 
-    def gathered(side, step, join, part):
+    def gathered(source, step, join, part):
         if joined == 2:
             at = pl.ds((step * 2 + part) * 2 * count, 2 * count)
             own, other = [
-                ref[:, side, :, at].reshape(wide * ranks, 2 * count, lanes)
-                for ref in (ins if join == 0 else ins[::-1])
+                ref[:, :, at].reshape(wide * ranks, 2 * count, lanes)
+                for ref in (source if join == 0 else source[::-1])
             ]
             return jnp.where(upper, own, other).reshape(half, lanes)
-        flat = ins[0].reshape(wide * sides * ranks * rows, lanes)
-        run = rows // count
-        return jnp.concatenate(
-            [
-                flat[
-                    pl.ds((w * sides + side) * ranks * rows + part * steps + step, ranks * count, stride=run),
-                    :,
-                ]
-                for w in range(wide)
-            ],
-            axis=0,
-        )
+        flat = source[0].reshape(wide * ranks * rows, lanes)
+        return flat[pl.ds(part * steps + step, half, stride=rows // count), :]
 
     for join in range(joined):
         sums = []
-        for side in range(sides):
+        for parity, source in ((side, sources[0]), (1 - side, sources[1])):
             left = jnp.concatenate(
                 [
-                    jnp.concatenate([gathered(side, step, join, part).T for part in range(2)], axis=1)
+                    jnp.concatenate([gathered(source, step, join, part).T for part in range(2)], axis=1)
                     for step in range(steps)
                 ],
                 axis=0,
             )
-            sums.append(product(split(left), pair(table_ref.at[join, side])))
-        even, odd = sums
-        for far, value in enumerate((even + odd, even - odd)):
+            sums.append(product(split(left), pair(table_ref.at[join, parity])))
+        own, other = sums
+        for far, value in enumerate((own + other, (own - other) * sign)):
             for step in range(steps):
                 at = (step * joined + join) * slots
                 columns = slice(far * half, (far + 1) * half)
@@ -536,10 +557,10 @@
                     ref[at : at + slots, :, columns] = here.reshape(slots, rows_b, half)
 
 
-def first_pass(parts, is_anchor, length, wide, sides, count):
+def first_pass(parts, side, is_anchor, length, wide, sides, count):
     devices, rows, lanes = parts[0].shape
-    joined = len(parts)
-    ranks = devices // wide // sides
+    joined = len(parts) // 2
+    ranks = devices // wide
     rows_b = length // wide
     slots = lanes // rows_b
     scale = 1.0 / float(length) ** 1.5
@@ -553,7 +574,7 @@
     table = np.stack([np.stack(each) for each in tables])
     total = rows // (2 * joined * count) if joined == 2 else rows // (2 * count)
     grid = 4 if joined == 2 and total % 4 == 0 else 1
-    parts = [part.reshape(wide, sides, ranks, rows, lanes) for part in parts]
+    parts = [part.reshape(wide, ranks, rows, lanes) for part in parts]
 
     def body(*refs):
         first_kernel(count, rows_b, *refs)
@@ -565,15 +586,16 @@
         grid=(grid,),
         in_specs=[
             pl.BlockSpec(memory_space=pltpu.SMEM),
+            pl.BlockSpec(memory_space=pltpu.SMEM),
             whole(table.shape),
-            *[pl.BlockSpec((wide, sides, ranks, rows // grid, lanes), lambda i: (0, 0, 0, i, 0))]
-            * joined,
+            *[pl.BlockSpec((wide, ranks, rows // grid, lanes), lambda i: (0, 0, i, 0))]
+            * (2 * joined),
         ],
         out_specs=[pl.BlockSpec((rows_c // grid, rows_b, length), lambda i: (i, 0, 0))] * 2,
         out_shape=[out_shape] * 2,
         compiler_params=params(1),
         cost_estimate=cost(rows_c * 2 * rows_b * length * length, 16 * rows_c * rows_b * length),
-    )(is_anchor, table, *parts)
+    )(side, is_anchor, table, *parts)
 
 
 def transpose(value, members=None):
@@ -613,15 +635,19 @@
             spots = slice(start, start + count)
             both_c = jnp.concatenate([waves_c[spots], scales_c[spots]])
             chunks = spectrum_pass(
-                planes, side, both_c, devices, groups, steps, start // PAIR, chunks
+                keep(planes, start > 0), side, both_c, devices, groups, steps, start // PAIR, chunks
             )
             start += count
         is_anchor = ((spot_wide == 0) & (spot_narrow == 0)).astype(jnp.int32).reshape(1)
-        parts = []
+        across = [(n, (n + ranks) % narrow) for n in range(narrow)]
+        owns, others = [], []
         for group, chunk in enumerate(chunks):
-            part = shear_pass(transpose(chunk, members), wide, narrow, per_c, group, groups)
-            parts.append(transpose(part.reshape((wide * narrow,) + part.shape[2:])))
-        return tuple(first_pass(parts, is_anchor, length, wide, sides, slab // groups))
+            received = keep(transpose(chunk, members), group > 0)
+            own, other = shear_pass(received, side, wide, narrow, per_c, group, groups)
+            other = lax.ppermute(other, "narrow", across)
+            owns.append(transpose(own.reshape((devices,) + own.shape[2:]), members))
+            others.append(transpose(other.reshape((devices,) + other.shape[2:]), members))
+        return tuple(first_pass(owns + others, side, is_anchor, length, wide, sides, slab // groups))
 
     return jax.shard_map(
         per_device,

time: 320 us -> 360 us (1.12)
  waiting for transfers between devices: 124 us -> 152 us
  starting transfers between devices: 17.6 us -> 29.9 us
    ppermute x0 -> x2, waiting for transfers between devices: none -> 95.7 us  [per_device(): other = lax.ppermute(other, 'narrow', across)]
    all_to_all x4 -> x6, waiting for transfers between devices: 124 us -> 56.7 us  [transpose(): lax.all_to_all(value, AXES, split_axis=0, concat_axis=0, tiled=True, axis...]
    all_to_all x4 -> x6, starting transfers between devices: 17.6 us -> 29 us  [transpose(): lax.all_to_all(value, AXES, split_axis=0, concat_axis=0, tiled=True, axis...]
  transfers between devices with their start and end apart: 4 -> 8, of which waited for: 4 -> 6; matrix products, arithmetic and copies ran while one was open for 0% -> 0% of each run, Pallas kernels for 12% -> 11%
where the time goes in v6:
time: 360 us; the launch traced here: 359 us
  waiting for transfers between devices  152 us (42%)
  blocking collectives  119 us (33%)
  Pallas kernels  54 us (15%)
  starting transfers between devices  29.9 us (8%)
    all_to_all x2, blocking collectives, transpose(): lax.all_to_all(value, AXES, split_axis=0, concat_axis=0, tiled=True, axis...  119 us
    ppermute x2, waiting for transfers between devices, per_device(): other = lax.ppermute(other, 'narrow', across)  95.7 us
    all_to_all x6, waiting for transfers between devices, transpose(): lax.all_to_all(value, AXES, split_axis=0, concat_axis=0, tiled=True, axis...  56.7 us
    all_to_all x6, starting transfers between devices, transpose(): lax.all_to_all(value, AXES, split_axis=0, concat_axis=0, tiled=True, axis...  29 us
    pallas_call x2, Pallas kernels, shear_pass(): pl.pallas_call(body, grid_spec=pltpu.PrefetchScalarGridSpec(num_scalar_pr...  28.1 us
    pallas_call x2, Pallas kernels, spectrum_pass(): pl.pallas_call(body, grid_spec=pltpu.PrefetchScalarGridSpec(num_scalar_pr...  14.8 us
  transfers between devices with their start and end apart: 8, of which 6 were waited for; matrix products, arithmetic and copies ran while one was open for 0% of the time, Pallas kernels for 11%

profile of v6, /device:TPU:1, one launch (start us, length us, event | category | flops | bytes accessed | tf_op | source)
XLA Modules:
  0.0 358.5 jit_solution(4505497056106393900)
XLA Ops:
  0.6 5.6 %shard_map.248 = (f32[8,2,2,6,32,128]{5,4,3,2,1,0:T(8,128)S(1)}, f32[8,2,2,2,32,128]{5,4,3,2,1,0:T(8,128)}) custom-call(bf16[2,256,256]{2,1,0:T(8,128)(2,1)} %constant.71.clone.refs_0_, f32[32,64,256]{2,1,0:T(8,128)} %refs_1_.3), custom_call_target="tpu_custom_call" | custom-call | flops 805306368 | bytes 6291456 | tf_op jit(solution)/shard_map/pallas_call | solution.py:117
  6.2 78.3 %all_to_all.40 = f32[32,6,32,128]{3,2,1,0:T(8,128)} all-to-all(f32[32,6,32,128]{3,2,1,0:T(8,128)S(1)} %bitcast.17), channel_id=1, replica_groups=mesh['wide'=8,'narrow'=4] {'wide','narrow'}, dimensions={0} | all-to-all | bytes 6291456 | tf_op jit(solution)/shard_map/all_to_all | solution.py:602
  84.5 3.2 all-to-all-start
  87.7 0.1 slice.13
  87.8 0.1 slice.12
  87.8 0.1 pad_maximum_fusion.1.refs_1_
  87.9 0.1 pad_maximum_fusion.refs_1_
  88.0 9.6 %shard_map.249 = (f32[16,12,32,128]{3,2,1,0:T(8,128)}, f32[16,12,32,128]{3,2,1,0:T(8,128)}) custom-call(s32[1]{0:T(128)} %bitcast.refs_0_, f32[12]{0:T(128)S(1)} %pad_maximum_fusion.1.refs_1_, f32[3,2,128,1]{3,2,1,0:T(8,128)} %constant.72.clone.refs_2_, f32[2,1,256]{2,1,0:T(1,128)} %constant.73.clone.refs_3_, ...), custom_call_target="tpu_custom_call" | custom-call | flops 4227858432 | bytes 15728640 | tf_op jit(solution)/shard_map/pallas_call | solution.py:291
  97.6 16.4 %all-to-all-done = f32[32,2,32,128]{3,2,1,0:T(8,128)S(1)} async-done(((f32[32,2,32,128]{3,2,1,0:T(8,128)}), f32[32,2,32,128]{3,2,1,0:T(8,128)S(1)}, u32[]{:S(2)}, u32[]{:S(2)}) %all-to-all-start) | async-done | bytes 1048608 | tf_op jit(solution)/shard_map/all_to_all | solution.py:602
  114.0 5.2 %shard_map.250 = (f32[16,12,32,128]{3,2,1,0:T(8,128)}, f32[16,12,32,128]{3,2,1,0:T(8,128)}) custom-call(s32[1]{0:T(128)} %bitcast.refs_0_, f32[4]{0:T(128)S(1)} %pad_maximum_fusion.refs_1_, f32[3,2,128,1]{3,2,1,0:T(8,128)} %constant.72.clone.refs_2_, f32[2,1,256]{2,1,0:T(1,128)} %constant.73.clone.refs_3_, ...), custom_call_target="tpu_custom_call", output_to_operand_aliasing={{0}: (8, {}), {1}: (9, {})} | custom-call | flops 1409286144 | bytes 5242880 | tf_op jit(solution)/shard_map/pallas_call | solution.py:291
  119.2 40.8 %all_to_all.41.refs_7_ = f32[16,12,32,128]{3,2,1,0:T(8,128)} all-to-all(f32[16,12,32,128]{3,2,1,0:T(8,128)} %get-tuple-element.16), channel_id=1, replica_groups={{0,1,4,5,8,9,12,13,16,17,20,21,24,25,28,29},{2,3,6,7,10,11,14,15,18,19,..., dimensions={0} | all-to-all | bytes 6291456 | tf_op jit(solution)/shard_map/all_to_all | solution.py:602
  160.0 5.4 %all-to-all-start.4 = ((f32[16,12,32,128]{3,2,1,0:T(8,128)}), f32[16,12,32,128]{3,2,1,0:T(8,128)S(1)}, u32[]{:S(2)}, u32[]{:S(2)}) async-start(f32[16,12,32,128]{3,2,1,0:T(8,128)} %get-tuple-element.18), calls=%async_computation.4 | async-start | bytes 6291456 | tf_op jit(solution)/shard_map/all_to_all | solution.py:602
  165.4 14.3 %shard_map.251 = (f32[8,2,128,128]{3,2,1,0:T(8,128)}, f32[8,2,128,128]{3,2,1,0:T(8,128)}) custom-call(s32[1]{0:T(128)} %bitcast.refs_0_, f32[6,512,1]{2,1,0:T(8,128)} %constant.77.clone.refs_1_, f32[6,1,512]{2,1,0:T(1,128)} %constant.78.clone.refs_2_, bf16[2,2,256,256]{3,2,1,0:T(8,128)(2,1)} %constant.75.clone.refs_5_.refs_3_, ...), custom_call_target="tpu_custom_call" | custom-call | flops 7247757312 | bytes 7340032 | tf_op jit(solution)/shard_map/pallas_call | solution.py:488
  179.7 25.1 %all-to-all-done.4.refs_7_ = f32[16,12,32,128]{3,2,1,0:T(8,128)S(1)} async-done(((f32[16,12,32,128]{3,2,1,0:T(8,128)}), f32[16,12,32,128]{3,2,1,0:T(8,128)S(1)}, u32[]{:S(2)}, u32[]{:S(2)}) %all-to-all-start.4) | async-done | bytes 3145760 | tf_op jit(solution)/shard_map/all_to_all | solution.py:602
  204.8 6.5 %all-to-all-start.3 = ((f32[16,128,128]{2,1,0:T(8,128)}), f32[16,128,128]{2,1,0:T(8,128)}, u32[]{:S(2)}, u32[]{:S(2)}) async-start(f32[16,128,128]{2,1,0:T(8,128)} %bitcast.23), calls=%async_computation.3 | async-start | bytes 2097152 | tf_op jit(solution)/shard_map/all_to_all | solution.py:602
  211.2 13.9 %shard_map.252 = (f32[8,2,128,128]{3,2,1,0:T(8,128)}, f32[8,2,128,128]{3,2,1,0:T(8,128)}) custom-call(s32[1]{0:T(128)} %bitcast.refs_0_, f32[6,512,1]{2,1,0:T(8,128)} %constant.82.clone.refs_1_, f32[6,1,512]{2,1,0:T(1,128)} %constant.78.clone.refs_2_, bf16[2,2,256,256]{3,2,1,0:T(8,128)(2,1)} %constant.75.clone.refs_5_.refs_3_, ...), custom_call_target="tpu_custom_call" | custom-call | flops 7247757312 | bytes 7340032 | tf_op jit(solution)/shard_map/pallas_call | solution.py:488
  225.1 0.8 all-to-all-done.3
  225.9 4.3 %all-to-all-start.5 = ((f32[16,128,128]{2,1,0:T(8,128)}), f32[16,128,128]{2,1,0:T(8,128)S(1)}, u32[]{:S(2)}, u32[]{:S(2)}) async-start(f32[16,128,128]{2,1,0:T(8,128)} %bitcast.22), calls=%async_computation.5 | async-start | bytes 2097152 | tf_op jit(solution)/shard_map/all_to_all | solution.py:602
  230.2 0.0 collective-permute-start.1
  230.2 48.3 %collective-permute-done.1 = f32[8,2,128,128]{3,2,1,0:T(8,128)} collective-permute-done((f32[8,2,128,128]{3,2,1,0:T(8,128)}, f32[8,2,128,128]{3,2,1,0:T(8,128)}, u32[]{:S(2)}, u32[]{:S(2)}) %collective-permute-start.1) | collective-permute-done | bytes 1048608 | tf_op jit(solution)/shard_map/ppermute | solution.py:647
  278.6 0.0 all-to-all-done.5
  278.6 4.8 %all-to-all-start.7 = ((f32[16,128,128]{2,1,0:T(8,128)}), f32[16,128,128]{2,1,0:T(8,128)S(1)}, u32[]{:S(2)}, u32[]{:S(2)}) async-start(f32[16,128,128]{2,1,0:T(8,128)} %bitcast.12), calls=%async_computation.7 | async-start | bytes 2097152 | tf_op jit(solution)/shard_map/all_to_all | solution.py:602
  283.4 0.9 collective-permute-start
  284.3 47.3 %collective-permute-done = f32[8,2,128,128]{3,2,1,0:T(8,128)S(1)} collective-permute-done((f32[8,2,128,128]{3,2,1,0:T(8,128)}, f32[8,2,128,128]{3,2,1,0:T(8,128)S(1)}, u32[]{:S(2)}, u32[]{:S(2)}) %collective-permute-start) | collective-permute-done | bytes 1048608 | tf_op jit(solution)/shard_map/ppermute | solution.py:647
  331.6 0.0 copy-start.1
  331.6 0.0 all-to-all-done.7
  331.6 1.0 copy-done.1
  332.6 4.8 %all-to-all-start.6 = ((f32[16,128,128]{2,1,0:T(8,128)}), f32[16,128,128]{2,1,0:T(8,128)S(1)}, u32[]{:S(2)}, u32[]{:S(2)}) async-start(f32[16,128,128]{2,1,0:T(8,128)} %bitcast.24), calls=%async_computation.6 | async-start | bytes 2097152 | tf_op jit(solution)/shard_map/all_to_all | solution.py:602
  337.4 14.4 %all-to-all-done.6 = f32[16,128,128]{2,1,0:T(8,128)S(1)} async-done(((f32[16,128,128]{2,1,0:T(8,128)}), f32[16,128,128]{2,1,0:T(8,128)S(1)}, u32[]{:S(2)}, u32[]{:S(2)}) %all-to-all-start.6) | async-done | bytes 1048608 | tf_op jit(solution)/shard_map/all_to_all | solution.py:602
  351.8 0.0 copy-start
  351.8 1.2 copy-done
  353.0 5.5 %shard_map.253 = (f32[64,32,256]{2,1,0:T(8,128)}, f32[64,32,256]{2,1,0:T(8,128)}) custom-call(s32[1]{0:T(128)} %bitcast.refs_0_, s32[1]{0:T(128)} %bitcast.1.refs_1_, bf16[2,2,2,256,256]{4,3,2,1,0:T(8,128)(2,1)S(1)} %copy-done, f32[8,2,128,128]{3,2,1,0:T(8,128)} %bitcast.7.refs_3_, f32[8,2,128,128]{3,2,1,0:T(8,128)S(1)} %bitcast.18, ...), custom_call_target="tpu_custom_call" | custom-call | flops 1610612736 | bytes 8388608 | tf_op jit(solution)/shard_map/pallas_call | solution.py:584
  (1 shorter events, 0.0 us)
Async XLA Ops:
  84.5 29.5 %all-to-all-start = ((f32[32,2,32,128]{3,2,1,0:T(8,128)}), f32[32,2,32,128]{3,2,1,0:T(8,128)S(1)}, u32[]{:S(2)}, u32[]{:S(2)}) async-start(f32[32,2,32,128]{3,2,1,0:T(8,128)} %bitcast.2), calls=%async_computation | async-start | bytes 2097152 | tf_op jit(solution)/shard_map/all_to_all | solution.py:602
  160.0 44.7 %all-to-all-start.4 = ((f32[16,12,32,128]{3,2,1,0:T(8,128)}), f32[16,12,32,128]{3,2,1,0:T(8,128)S(1)}, u32[]{:S(2)}, u32[]{:S(2)}) async-start(f32[16,12,32,128]{3,2,1,0:T(8,128)} %get-tuple-element.18), calls=%async_computation.4 | async-start | bytes 6291456 | tf_op jit(solution)/shard_map/all_to_all | solution.py:602
  204.8 21.1 %all-to-all-start.3 = ((f32[16,128,128]{2,1,0:T(8,128)}), f32[16,128,128]{2,1,0:T(8,128)}, u32[]{:S(2)}, u32[]{:S(2)}) async-start(f32[16,128,128]{2,1,0:T(8,128)} %bitcast.23), calls=%async_computation.3 | async-start | bytes 2097152 | tf_op jit(solution)/shard_map/all_to_all | solution.py:602
  225.9 52.7 %all-to-all-start.5 = ((f32[16,128,128]{2,1,0:T(8,128)}), f32[16,128,128]{2,1,0:T(8,128)S(1)}, u32[]{:S(2)}, u32[]{:S(2)}) async-start(f32[16,128,128]{2,1,0:T(8,128)} %bitcast.22), calls=%async_computation.5 | async-start | bytes 2097152 | tf_op jit(solution)/shard_map/all_to_all | solution.py:602
  230.2 48.3 %collective-permute-start.1 = (f32[8,2,128,128]{3,2,1,0:T(8,128)}, f32[8,2,128,128]{3,2,1,0:T(8,128)}, u32[]{:S(2)}, u32[]{:S(2)}) collective-permute-start(f32[8,2,128,128]{3,2,1,0:T(8,128)} %get-tuple-element.21), channel_id=1, source_target_pairs={{0,2},{1,3},{2,0},{3,1},{4,6},{5,7},{6,4},{7,5},{8,10},{9,11},{10,... | collective-permute-start | bytes 3145736 | tf_op jit(solution)/shard_map/ppermute | solution.py:647
  278.6 53.1 %all-to-all-start.7 = ((f32[16,128,128]{2,1,0:T(8,128)}), f32[16,128,128]{2,1,0:T(8,128)S(1)}, u32[]{:S(2)}, u32[]{:S(2)}) async-start(f32[16,128,128]{2,1,0:T(8,128)} %bitcast.12), calls=%async_computation.7 | async-start | bytes 2097152 | tf_op jit(solution)/shard_map/all_to_all | solution.py:602
  283.4 48.2 %collective-permute-start = (f32[8,2,128,128]{3,2,1,0:T(8,128)}, f32[8,2,128,128]{3,2,1,0:T(8,128)S(1)}, u32[]{:S(2)}, u32[]{:S(2)}) collective-permute-start(f32[8,2,128,128]{3,2,1,0:T(8,128)} %get-tuple-element.20), channel_id=1, source_target_pairs={{0,2},{1,3},{2,0},{3,1},{4,6},{5,7},{6,4},{7,5},{8,10},{9,11},{10,... | collective-permute-start | bytes 3145736 | tf_op jit(solution)/shard_map/ppermute | solution.py:647
  331.6 1.0 copy-start.1
  332.6 19.2 %all-to-all-start.6 = ((f32[16,128,128]{2,1,0:T(8,128)}), f32[16,128,128]{2,1,0:T(8,128)S(1)}, u32[]{:S(2)}, u32[]{:S(2)}) async-start(f32[16,128,128]{2,1,0:T(8,128)} %bitcast.24), calls=%async_computation.6 | async-start | bytes 2097152 | tf_op jit(solution)/shard_map/all_to_all | solution.py:602
  351.8 1.2 copy-start

commit v7 on v5

--- a/solution.py
+++ b/solution.py
@@ -59,8 +59,12 @@
     return pl.BlockSpec(shape, lambda *_: (0,) * len(shape))
 
 
+def keep(value, space):
+    return pltpu.with_memory_space_constraint(jnp.asarray(value), space)
+
+
 def in_hbm(value):
-    return pltpu.with_memory_space_constraint(jnp.asarray(value), pltpu.HBM)
+    return keep(value, pltpu.HBM)
 
 
 def cost(macs, moved):
@@ -124,7 +128,7 @@
             for count in counts
         ],
         out_shape=[
-            jax.ShapeDtypeStruct((wide, sides, ranks, count, rows_x, 2 * rows_y), jnp.float32)
+            pltpu.VMEM((wide, sides, ranks, count, rows_x, 2 * rows_y), jnp.float32)
             for count in counts
         ],
         compiler_params=params(1),
@@ -300,7 +304,7 @@
             ],
             out_specs=[pl.BlockSpec(block, lambda i, *_: (0, 0, first_step + i, 0))] * groups,
         ),
-        out_shape=[pltpu.HBM(out_shape, jnp.float32)] * groups,
+        out_shape=[pltpu.VMEM(out_shape, jnp.float32)] * groups,
         input_output_aliases={8 + spot: spot for spot in range(len(filled))},
         compiler_params=params(1),
         cost_estimate=cost(per_c * 7 * length**3, 20 * per_c * length**2 * 2),
@@ -308,8 +312,8 @@
         side,
         waves_c,
         *[in_hbm(table) for table in (a_table, b_table, *tables)],
-        in_hbm(received),
-        *[in_hbm(each) for each in filled],
+        received,
+        *[keep(each, pltpu.VMEM) for each in filled],
     )
 
 
@@ -471,11 +475,11 @@
             pl.BlockSpec((devices, tiles // 3, message, tile), which),
         ],
         out_specs=whole(out_shape),
-        out_shape=pltpu.HBM(out_shape, jnp.float32),
+        out_shape=pltpu.VMEM(out_shape, jnp.float32),
         scratch_shapes=[pltpu.VMEM((length, count * length), jnp.float32)],
         compiler_params=params(1),
         cost_estimate=cost(count * 18 * length**3, 4 * received.size + 4 * 2**20),
-    )(*[in_hbm(value) for value in (row_factor, lane_factor, *tables, received)])
+    )(*[in_hbm(value) for value in (row_factor, lane_factor, *tables)], received)
 
 
 def first_kernel(count, rows_b, anchor_ref, table_ref, *refs):
@@ -573,7 +577,7 @@
         out_shape=[out_shape] * 2,
         compiler_params=params(1),
         cost_estimate=cost(rows_c * 2 * rows_b * length * length, 16 * rows_c * rows_b * length),
-    )(is_anchor, table, *parts)
+    )(is_anchor, table, *[keep(part, pltpu.VMEM) for part in parts])
 
 
 def transpose(value, members=None):
@@ -612,6 +616,7 @@
             planes = planes.reshape(wide, narrow, count, rows_x, 2 * rows_y)
             spots = slice(start, start + count)
             both_c = jnp.concatenate([waves_c[spots], scales_c[spots]])
+            planes = keep(planes, pltpu.VMEM if start else pltpu.HBM)
             chunks = spectrum_pass(
                 planes, side, both_c, devices, groups, steps, start // PAIR, chunks
             )
@@ -619,7 +624,8 @@
         is_anchor = ((spot_wide == 0) & (spot_narrow == 0)).astype(jnp.int32).reshape(1)
         parts = []
         for group, chunk in enumerate(chunks):
-            part = shear_pass(transpose(chunk, members), wide, narrow, per_c, group, groups)
+            received = keep(transpose(chunk, members), pltpu.VMEM if group else pltpu.HBM)
+            part = shear_pass(received, wide, narrow, per_c, group, groups)
             parts.append(transpose(part.reshape((wide * narrow,) + part.shape[2:])))
         return tuple(first_pass(parts, is_anchor, length, wide, sides, slab // groups))
 

time: 320 us -> 316 us (0.988)
  Pallas kernels: 54.9 us -> 50.1 us
  local copies, waits for them, and re-layouts: 2.75 us -> 6.31 us
    unnamed x6 -> x12, local copies, waits for them, and re-layouts: 2.6 us -> 6.17 us
  transfers between devices with their start and end apart: 4 -> 4, of which waited for: 4 -> 4; matrix products, arithmetic and copies ran while one was open for 0% -> 0% of each run, Pallas kernels for 12% -> 11%
where the time goes in v7:
time: 316 us
  waiting for transfers between devices  123 us (39%)
  blocking collectives  118 us (37%)
  Pallas kernels  50.1 us (16%)
  starting transfers between devices  16.8 us (5%)
  local copies, waits for them, and re-layouts  6.31 us (2%)
    all_to_all x4, waiting for transfers between devices, transpose(): lax.all_to_all(value, AXES, split_axis=0, concat_axis=0, tiled=True, axis...  123 us
    all_to_all x2, blocking collectives, transpose(): lax.all_to_all(value, AXES, split_axis=0, concat_axis=0, tiled=True, axis...  118 us
    pallas_call x2, Pallas kernels, shear_pass(): pl.pallas_call(body, grid=(6,), in_specs=[pl.BlockSpec((1, count * half,...  25.5 us
    all_to_all x4, starting transfers between devices, transpose(): lax.all_to_all(value, AXES, split_axis=0, concat_axis=0, tiled=True, axis...  16.8 us
    pallas_call x2, Pallas kernels, spectrum_pass(): pl.pallas_call(body, grid_spec=pltpu.PrefetchScalarGridSpec(num_scalar_pr...  13.4 us
  transfers between devices with their start and end apart: 4, of which 4 were waited for; matrix products, arithmetic and copies ran while one was open for 0% of the time, Pallas kernels for 11%

profile of v7, /device:TPU:1, one launch (start us, length us, event | category | flops | bytes accessed | tf_op | source)
XLA Modules:
  0.0 315.6 jit_solution(269659650276402023)
XLA Ops:
  0.6 5.6 %shard_map.248 = (f32[8,2,2,6,32,128]{5,4,3,2,1,0:T(8,128)S(1)}, f32[8,2,2,2,32,128]{5,4,3,2,1,0:T(8,128)}) custom-call(bf16[2,256,256]{2,1,0:T(8,128)(2,1)} %constant.71.clone.refs_0_, f32[32,64,256]{2,1,0:T(8,128)} %refs_1_.4), custom_call_target="tpu_custom_call" | custom-call | flops 805306368 | bytes 6291456 | tf_op jit(solution)/shard_map/pallas_call | solution.py:117
  6.2 78.3 %all_to_all.30 = f32[32,6,32,128]{3,2,1,0:T(8,128)} all-to-all(f32[32,6,32,128]{3,2,1,0:T(8,128)S(1)} %bitcast.12), channel_id=1, replica_groups=mesh['wide'=8,'narrow'=4] {'wide','narrow'}, dimensions={0} | all-to-all | bytes 6291456 | tf_op jit(solution)/shard_map/all_to_all | solution.py:584
  84.5 3.2 %all-to-all-start = ((f32[32,2,32,128]{3,2,1,0:T(8,128)}), f32[32,2,32,128]{3,2,1,0:T(8,128)}, u32[]{:S(2)}, u32[]{:S(2)}) async-start(f32[32,2,32,128]{3,2,1,0:T(8,128)} %bitcast.2), calls=%async_computation | async-start | bytes 2097152 | tf_op jit(solution)/shard_map/all_to_all | solution.py:584
  87.8 0.1 slice.13
  87.8 0.1 slice.12
  87.9 0.1 pad_maximum_fusion.1.refs_1_
  88.0 0.1 pad_maximum_fusion.refs_1_
  88.1 9.0 %shard_map.249 = (f32[16,12,32,128]{3,2,1,0:T(8,128)S(1)}, f32[16,12,32,128]{3,2,1,0:T(8,128)S(1)}) custom-call(s32[1]{0:T(128)} %bitcast.1.refs_0_, f32[12]{0:T(128)S(1)} %pad_maximum_fusion.1.refs_1_, f32[3,2,128,1]{3,2,1,0:T(8,128)} %constant.72.clone.refs_2_, f32[2,1,256]{2,1,0:T(1,128)} %constant.73.clone.refs_3_, ...), custom_call_target="tpu_custom_call" | custom-call | flops 4227858432 | bytes 15728640 | tf_op jit(solution)/shard_map/pallas_call | solution.py:291
  97.1 0.0 copy-start
  97.1 1.6 copy-done
  98.7 15.4 %all-to-all-done = f32[32,2,32,128]{3,2,1,0:T(8,128)} async-done(((f32[32,2,32,128]{3,2,1,0:T(8,128)}), f32[32,2,32,128]{3,2,1,0:T(8,128)}, u32[]{:S(2)}, u32[]{:S(2)}) %all-to-all-start) | async-done | bytes 1048608 | tf_op jit(solution)/shard_map/all_to_all | solution.py:584
  114.1 0.0 copy-start.1
  114.1 1.9 copy-done.1
  116.0 4.4 %shard_map.250 = (f32[16,12,32,128]{3,2,1,0:T(8,128)S(1)}, f32[16,12,32,128]{3,2,1,0:T(8,128)S(1)}) custom-call(s32[1]{0:T(128)} %bitcast.1.refs_0_, f32[4]{0:T(128)S(1)} %pad_maximum_fusion.refs_1_, f32[3,2,128,1]{3,2,1,0:T(8,128)} %constant.72.clone.refs_2_, f32[2,1,256]{2,1,0:T(1,128)} %constant.73.clone.refs_3_, ...), custom_call_target="tpu_custom_call", output_to_operand_aliasing={{0}: (8, {}), {1}: (9, {})} | custom-call | flops 1409286144 | bytes 5242880 | tf_op jit(solution)/shard_map/pallas_call | solution.py:291
  120.4 0.0 copy-start.2
  120.4 40.0 %all_to_all.31.refs_6_ = f32[16,12,32,128]{3,2,1,0:T(8,128)} all-to-all(f32[16,12,32,128]{3,2,1,0:T(8,128)S(1)} %get-tuple-element.12), channel_id=1, replica_groups={{0,1,4,5,8,9,12,13,16,17,20,21,24,25,28,29},{2,3,6,7,10,11,14,15,18,19,..., dimensions={0} | all-to-all | bytes 6291456 | tf_op jit(solution)/shard_map/all_to_all | solution.py:584
  160.5 0.0 copy-done.2
  160.5 3.8 %all-to-all-start.4 = ((f32[16,12,32,128]{3,2,1,0:T(8,128)}), f32[16,12,32,128]{3,2,1,0:T(8,128)S(1)}, u32[]{:S(2)}, u32[]{:S(2)}) async-start(f32[16,12,32,128]{3,2,1,0:T(8,128)} %copy-done.2), calls=%async_computation.4 | async-start | bytes 6291456 | tf_op jit(solution)/shard_map/all_to_all | solution.py:584
  164.3 12.9 %shard_map.251 = f32[8,4,128,128]{3,2,1,0:T(8,128)S(1)} custom-call(f32[6,512,1]{2,1,0:T(8,128)} %constant.77.clone.refs_0_, f32[6,1,512]{2,1,0:T(1,128)} %constant.78.clone.refs_1_, bf16[2,2,256,256]{3,2,1,0:T(8,128)(2,1)} %constant.75.clone.refs_5_.refs_2_, bf16[2,256,256]{2,1,0:T(8,128)(2,1)} %constant.79.clone.refs_3_, ...), custom_call_target="tpu_custom_call" | custom-call | flops 7247757312 | bytes 7340032 | tf_op jit(solution)/shard_map/pallas_call | solution.py:468
  177.2 0.0 copy-start.4
  177.2 1.3 copy-done.4
  178.5 25.1 %all-to-all-done.4.refs_6_ = f32[16,12,32,128]{3,2,1,0:T(8,128)S(1)} async-done(((f32[16,12,32,128]{3,2,1,0:T(8,128)}), f32[16,12,32,128]{3,2,1,0:T(8,128)S(1)}, u32[]{:S(2)}, u32[]{:S(2)}) %all-to-all-start.4) | async-done | bytes 3145760 | tf_op jit(solution)/shard_map/all_to_all | solution.py:584
  203.6 6.3 %all-to-all-start.3 = ((f32[32,128,128]{2,1,0:T(8,128)}), f32[32,128,128]{2,1,0:T(8,128)}, u32[]{:S(2)}, u32[]{:S(2)}) async-start(f32[32,128,128]{2,1,0:T(8,128)} %bitcast.15), calls=%async_computation.3 | async-start | bytes 4194304 | tf_op jit(solution)/shard_map/all_to_all | solution.py:584
  210.0 12.6 %shard_map.252 = f32[8,4,128,128]{3,2,1,0:T(8,128)S(1)} custom-call(f32[6,512,1]{2,1,0:T(8,128)} %constant.82.clone.refs_0_, f32[6,1,512]{2,1,0:T(1,128)} %constant.78.clone.refs_1_, bf16[2,2,256,256]{3,2,1,0:T(8,128)(2,1)} %constant.75.clone.refs_5_.refs_2_, bf16[2,256,256]{2,1,0:T(8,128)(2,1)} %constant.83.clone.refs_3_, ...), custom_call_target="tpu_custom_call" | custom-call | flops 7247757312 | bytes 7340032 | tf_op jit(solution)/shard_map/pallas_call | solution.py:468
  222.5 0.0 copy-start.3
  222.5 1.3 copy-done.3
  223.9 34.4 %all-to-all-done.3 = f32[32,128,128]{2,1,0:T(8,128)} async-done(((f32[32,128,128]{2,1,0:T(8,128)}), f32[32,128,128]{2,1,0:T(8,128)}, u32[]{:S(2)}, u32[]{:S(2)}) %all-to-all-start.3) | async-done | bytes 2097184 | tf_op jit(solution)/shard_map/all_to_all | solution.py:584
  258.3 0.0 copy-start.5
  258.3 3.4 %all-to-all-start.5 = ((f32[32,128,128]{2,1,0:T(8,128)}), f32[32,128,128]{2,1,0:T(8,128)S(1)}, u32[]{:S(2)}, u32[]{:S(2)}) async-start(f32[32,128,128]{2,1,0:T(8,128)} %bitcast.13), calls=%async_computation.5 | async-start | bytes 4194304 | tf_op jit(solution)/shard_map/all_to_all | solution.py:584
  261.7 48.2 %all-to-all-done.5 = f32[32,128,128]{2,1,0:T(8,128)S(1)} async-done(((f32[32,128,128]{2,1,0:T(8,128)}), f32[32,128,128]{2,1,0:T(8,128)S(1)}, u32[]{:S(2)}, u32[]{:S(2)}) %all-to-all-start.5) | async-done | bytes 2097184 | tf_op jit(solution)/shard_map/all_to_all | solution.py:584
  309.9 0.0 copy-done.5
  309.9 5.7 %shard_map.253 = (f32[64,32,256]{2,1,0:T(8,128)}, f32[64,32,256]{2,1,0:T(8,128)}) custom-call(s32[1]{0:T(128)} %bitcast.refs_0_, bf16[2,2,2,256,256]{4,3,2,1,0:T(8,128)(2,1)S(1)} %copy-done.5, f32[8,2,2,128,128]{4,3,2,1,0:T(8,128)} %bitcast.7.refs_2_, f32[8,2,2,128,128]{4,3,2,1,0:T(8,128)S(1)} %bitcast.14), custom_call_target="tpu_custom_call" | custom-call | flops 1610612736 | bytes 8388608 | tf_op jit(solution)/shard_map/pallas_call | solution.py:567
  (1 shorter events, 0.0 us)
Async XLA Ops:
  84.5 29.6 %all-to-all-start = ((f32[32,2,32,128]{3,2,1,0:T(8,128)}), f32[32,2,32,128]{3,2,1,0:T(8,128)}, u32[]{:S(2)}, u32[]{:S(2)}) async-start(f32[32,2,32,128]{3,2,1,0:T(8,128)} %bitcast.2), calls=%async_computation | async-start | bytes 2097152 | tf_op jit(solution)/shard_map/all_to_all | solution.py:584
  97.1 1.7 copy-start
  114.1 1.9 copy-start.1
  120.4 40.0 %copy-start.2 = (f32[16,12,32,128]{3,2,1,0:T(8,128)}, f32[16,12,32,128]{3,2,1,0:T(8,128)S(1)}, u32[]{:S(2)}) copy-start(f32[16,12,32,128]{3,2,1,0:T(8,128)S(1)} %get-tuple-element.13) | copy-start | bytes 9437188
  160.5 43.2 %all-to-all-start.4 = ((f32[16,12,32,128]{3,2,1,0:T(8,128)}), f32[16,12,32,128]{3,2,1,0:T(8,128)S(1)}, u32[]{:S(2)}, u32[]{:S(2)}) async-start(f32[16,12,32,128]{3,2,1,0:T(8,128)} %copy-done.2), calls=%async_computation.4 | async-start | bytes 6291456 | tf_op jit(solution)/shard_map/all_to_all | solution.py:584
  177.2 1.3 copy-start.4
  203.6 54.6 %all-to-all-start.3 = ((f32[32,128,128]{2,1,0:T(8,128)}), f32[32,128,128]{2,1,0:T(8,128)}, u32[]{:S(2)}, u32[]{:S(2)}) async-start(f32[32,128,128]{2,1,0:T(8,128)} %bitcast.15), calls=%async_computation.3 | async-start | bytes 4194304 | tf_op jit(solution)/shard_map/all_to_all | solution.py:584
  222.5 1.3 copy-start.3
  258.3 51.7 %copy-start.5 = (bf16[2,2,2,256,256]{4,3,2,1,0:T(8,128)(2,1)S(1)}, bf16[2,2,2,256,256]{4,3,2,1,0:T(8,128)(2,1)}, u32[]{:S(2)}) copy-start(bf16[2,2,2,256,256]{4,3,2,1,0:T(8,128)(2,1)} %constant.84.clone.refs_1_) | copy-start | bytes 3145732
  258.3 51.7 %all-to-all-start.5 = ((f32[32,128,128]{2,1,0:T(8,128)}), f32[32,128,128]{2,1,0:T(8,128)S(1)}, u32[]{:S(2)}, u32[]{:S(2)}) async-start(f32[32,128,128]{2,1,0:T(8,128)} %bitcast.13), calls=%async_computation.5 | async-start | bytes 4194304 | tf_op jit(solution)/shard_map/all_to_all | solution.py:584

commit v8 on v7

--- a/solution.py
+++ b/solution.py
@@ -144,7 +144,7 @@
     return np.block([[cosine, -sine], [sine, cosine]])
 
 
-def spectrum_kernel(slab, groups, side_ref, wave_c_ref, a_ref, b_ref, second_ref, first_ref, back_ref, in_ref, *refs):
+def spectrum_kernel(slab, groups, first_c, side_ref, start_ref, a_ref, b_ref, second_ref, first_ref, back_ref, in_ref, *refs):
     outs = refs[-groups:]
     wide, narrow, _, rows_x, lanes = in_ref.shape
     length = wide * rows_x
@@ -196,8 +196,9 @@
         value = product(pair(first_ref.at[parity]), split(stacked(sign)))
         smooth = []
         for c in range(PAIR):
-            wave_c = wave_c_ref[pl.program_id(0) * PAIR + c]
-            scale_c = wave_c_ref[wave_c_ref.shape[0] // 2 + pl.program_id(0) * PAIR + c]
+            spot_c = start_ref[0] + (first_c + pl.program_id(0) * PAIR + c)
+            wave_c = jnp.full_like(squared_b, spot_c.astype(jnp.float32)) * (2.0 * math.pi / length)
+            scale_c = jnp.exp(-0.5 * wave_c * wave_c) * (1.0 / float(length) ** 3)
             squared = a_ref[1, parity] + (squared_b + wave_c * wave_c)
             inverse = scale_c / jnp.where(squared > 0, squared, 1.0)
             smooth.append(jnp.where(squared > 0, inverse * scale_b, 0.0) * a_ref[2, parity])
@@ -250,7 +251,7 @@
     return np.arange(length).reshape(length // 2, 2).T
 
 
-def spectrum_pass(received, side, waves_c, devices, groups, steps, first_step, filled):
+def spectrum_pass(received, side, start_c, devices, groups, steps, first_step, filled):
     wide, narrow, per_c, rows_x, lanes = received.shape
     length = wide * rows_x
     rows_y = lanes // 2
@@ -283,7 +284,7 @@
     block = out_shape[:2] + (message, TILE)
 
     def body(*refs):
-        spectrum_kernel(slab, groups, *refs)
+        spectrum_kernel(slab, groups, first_step * PAIR, *refs)
 
     def fixed(shape):
         return pl.BlockSpec(shape, lambda *_: (0,) * len(shape))
@@ -310,7 +311,7 @@
         cost_estimate=cost(per_c * 7 * length**3, 20 * per_c * length**2 * 2),
     )(
         side,
-        waves_c,
+        start_c,
         *[in_hbm(table) for table in (a_table, b_table, *tables)],
         received,
         *[keep(each, pltpu.VMEM) for each in filled],
@@ -607,24 +608,20 @@
         spot_wide, spot_narrow = lax.axis_index("wide"), lax.axis_index("narrow")
         side = (spot_narrow // ranks).astype(jnp.int32).reshape(1)
         rank = spot_wide * ranks + spot_narrow % ranks
-        waves_c = (rank * per_c + jnp.arange(per_c, dtype=jnp.int32)).astype(jnp.float32)
-        waves_c = waves_c * (2.0 * math.pi / length)
-        scales_c = jnp.exp(-0.5 * waves_c * waves_c) * (1.0 / float(length) ** 3)
+        start_c = (rank * per_c).astype(jnp.int32).reshape(1)
         chunks, start = [], 0
         for planes, count in zip(third_pass(density, wide, sides, ranks, counts), counts):
             planes = transpose(planes.reshape(wide * narrow, count, rows_x, 2 * rows_y))
             planes = planes.reshape(wide, narrow, count, rows_x, 2 * rows_y)
-            spots = slice(start, start + count)
-            both_c = jnp.concatenate([waves_c[spots], scales_c[spots]])
-            planes = keep(planes, pltpu.VMEM if start else pltpu.HBM)
+            planes = keep(planes, pltpu.VMEM)
             chunks = spectrum_pass(
-                planes, side, both_c, devices, groups, steps, start // PAIR, chunks
+                planes, side, start_c, devices, groups, steps, start // PAIR, chunks
             )
             start += count
         is_anchor = ((spot_wide == 0) & (spot_narrow == 0)).astype(jnp.int32).reshape(1)
         parts = []
         for group, chunk in enumerate(chunks):
-            received = keep(transpose(chunk, members), pltpu.VMEM if group else pltpu.HBM)
+            received = keep(transpose(chunk, members), pltpu.VMEM)
             part = shear_pass(received, wide, narrow, per_c, group, groups)
             parts.append(transpose(part.reshape((wide * narrow,) + part.shape[2:])))
         return tuple(first_pass(parts, is_anchor, length, wide, sides, slab // groups))

time: 316 us -> 316 us (level)
  local copies, waits for them, and re-layouts: 6.31 us -> 9.93 us
    unnamed x12 -> x16, local copies, waits for them, and re-layouts: 6.17 us -> 9.93 us
where the time goes in v8:
time: 316 us; the launch traced here: 315 us
  waiting for transfers between devices  121 us (38%)
  blocking collectives  118 us (37%)
  Pallas kernels  48.5 us (15%)
  starting transfers between devices  16.8 us (5%)
  local copies, waits for them, and re-layouts  9.93 us (3%)
    all_to_all x4, waiting for transfers between devices, transpose(): lax.all_to_all(value, AXES, split_axis=0, concat_axis=0, tiled=True, axis...  121 us
    all_to_all x2, blocking collectives, transpose(): lax.all_to_all(value, AXES, split_axis=0, concat_axis=0, tiled=True, axis...  118 us
    pallas_call x2, Pallas kernels, shear_pass(): pl.pallas_call(body, grid=(6,), in_specs=[pl.BlockSpec((1, count * half,...  25.1 us
    all_to_all x4, starting transfers between devices, transpose(): lax.all_to_all(value, AXES, split_axis=0, concat_axis=0, tiled=True, axis...  16.8 us
    pallas_call x2, Pallas kernels, spectrum_pass(): pl.pallas_call(body, grid_spec=pltpu.PrefetchScalarGridSpec(num_scalar_pr...  12.1 us
    unnamed x16, local copies, waits for them, and re-layouts  9.93 us
  transfers between devices with their start and end apart: 4, of which 4 were waited for; matrix products, arithmetic and copies ran while one was open for 0% of the time, Pallas kernels for 11%

profile of v8, /device:TPU:1, one launch (start us, length us, event | category | flops | bytes accessed | tf_op | source)
XLA Modules:
  0.0 315.1 jit_solution(18096383637347721482)
XLA Ops:
  0.6 5.6 %shard_map.248 = (f32[8,2,2,6,32,128]{5,4,3,2,1,0:T(8,128)S(1)}, f32[8,2,2,2,32,128]{5,4,3,2,1,0:T(8,128)}) custom-call(bf16[2,256,256]{2,1,0:T(8,128)(2,1)} %constant.64.clone.refs_0_, f32[32,64,256]{2,1,0:T(8,128)} %refs_1_.4), custom_call_target="tpu_custom_call" | custom-call | flops 805306368 | bytes 6291456 | tf_op jit(solution)/shard_map/pallas_call | solution.py:117
  6.2 78.3 %all_to_all.30 = f32[32,6,32,128]{3,2,1,0:T(8,128)} all-to-all(f32[32,6,32,128]{3,2,1,0:T(8,128)S(1)} %bitcast.12), channel_id=1, replica_groups=mesh['wide'=8,'narrow'=4] {'wide','narrow'}, dimensions={0} | all-to-all | bytes 6291456 | tf_op jit(solution)/shard_map/all_to_all | solution.py:585
  84.5 3.2 %all-to-all-start = ((f32[32,2,32,128]{3,2,1,0:T(8,128)}), f32[32,2,32,128]{3,2,1,0:T(8,128)}, u32[]{:S(2)}, u32[]{:S(2)}) async-start(f32[32,2,32,128]{3,2,1,0:T(8,128)} %bitcast.3), calls=%async_computation | async-start | bytes 2097152 | tf_op jit(solution)/shard_map/all_to_all | solution.py:585
  87.7 0.0 copy-start.3
  87.8 1.9 copy-done.3
  89.6 8.3 %shard_map.249 = (f32[16,12,32,128]{3,2,1,0:T(8,128)S(1)}, f32[16,12,32,128]{3,2,1,0:T(8,128)S(1)}) custom-call(s32[1]{0:T(128)} %bitcast.1.refs_0_, s32[1]{0:T(128)} %bitcast.2.refs_1_, f32[3,2,128,1]{3,2,1,0:T(8,128)} %constant.65.clone.refs_2_, f32[2,1,256]{2,1,0:T(1,128)} %constant.66.clone.refs_3_, bf16[2,2,256,256]{3,2,1,0:T(8,128)(2,1)} %constant.67.clone.refs_4_, ...), custom_call_target="tpu_custom_call" | custom-call | flops 4227858432 | bytes 15728640 | tf_op jit(solution)/shard_map/pallas_call | solution.py:292
  97.9 0.0 copy-start
  98.0 1.6 copy-done
  99.6 14.5 %all-to-all-done = f32[32,2,32,128]{3,2,1,0:T(8,128)} async-done(((f32[32,2,32,128]{3,2,1,0:T(8,128)}), f32[32,2,32,128]{3,2,1,0:T(8,128)}, u32[]{:S(2)}, u32[]{:S(2)}) %all-to-all-start) | async-done | bytes 1048608 | tf_op jit(solution)/shard_map/all_to_all | solution.py:585
  114.1 0.0 copy-start.1
  114.1 1.9 copy-done.1
  116.0 3.8 %shard_map.250 = (f32[16,12,32,128]{3,2,1,0:T(8,128)S(1)}, f32[16,12,32,128]{3,2,1,0:T(8,128)S(1)}) custom-call(s32[1]{0:T(128)} %bitcast.1.refs_0_, s32[1]{0:T(128)} %bitcast.2.refs_1_, f32[3,2,128,1]{3,2,1,0:T(8,128)} %constant.65.clone.refs_2_, f32[2,1,256]{2,1,0:T(1,128)} %constant.66.clone.refs_3_, ...), custom_call_target="tpu_custom_call", output_to_operand_aliasing={{0}: (8, {}), {1}: (9, {})} | custom-call | flops 1409286144 | bytes 5242880 | tf_op jit(solution)/shard_map/pallas_call | solution.py:292
  119.9 0.0 copy-start.2
  119.9 40.0 %all_to_all.31.refs_6_ = f32[16,12,32,128]{3,2,1,0:T(8,128)} all-to-all(f32[16,12,32,128]{3,2,1,0:T(8,128)S(1)} %get-tuple-element.12), channel_id=1, replica_groups={{0,1,4,5,8,9,12,13,16,17,20,21,24,25,28,29},{2,3,6,7,10,11,14,15,18,19,..., dimensions={0} | all-to-all | bytes 6291456 | tf_op jit(solution)/shard_map/all_to_all | solution.py:585
  159.9 0.0 copy-done.2
  159.9 3.8 %all-to-all-start.4 = ((f32[16,12,32,128]{3,2,1,0:T(8,128)}), f32[16,12,32,128]{3,2,1,0:T(8,128)S(1)}, u32[]{:S(2)}, u32[]{:S(2)}) async-start(f32[16,12,32,128]{3,2,1,0:T(8,128)} %copy-done.2), calls=%async_computation.4 | async-start | bytes 6291456 | tf_op jit(solution)/shard_map/all_to_all | solution.py:585
  163.7 0.0 copy-start.4
  163.7 1.9 copy-done.4
  165.6 12.5 %shard_map.251 = f32[8,4,128,128]{3,2,1,0:T(8,128)S(1)} custom-call(f32[6,512,1]{2,1,0:T(8,128)} %constant.70.clone.refs_0_, f32[6,1,512]{2,1,0:T(1,128)} %constant.71.clone.refs_1_, bf16[2,2,256,256]{3,2,1,0:T(8,128)(2,1)} %constant.68.clone.refs_5_.refs_2_, bf16[2,256,256]{2,1,0:T(8,128)(2,1)} %constant.72.clone.refs_3_, ...), custom_call_target="tpu_custom_call" | custom-call | flops 7247757312 | bytes 7340032 | tf_op jit(solution)/shard_map/pallas_call | solution.py:469
  178.2 0.0 copy-start.6
  178.2 1.3 copy-done.6
  179.5 23.6 %all-to-all-done.4.refs_6_ = f32[16,12,32,128]{3,2,1,0:T(8,128)S(1)} async-done(((f32[16,12,32,128]{3,2,1,0:T(8,128)}), f32[16,12,32,128]{3,2,1,0:T(8,128)S(1)}, u32[]{:S(2)}, u32[]{:S(2)}) %all-to-all-start.4) | async-done | bytes 3145760 | tf_op jit(solution)/shard_map/all_to_all | solution.py:585
  203.1 6.3 %all-to-all-start.3 = ((f32[32,128,128]{2,1,0:T(8,128)}), f32[32,128,128]{2,1,0:T(8,128)}, u32[]{:S(2)}, u32[]{:S(2)}) async-start(f32[32,128,128]{2,1,0:T(8,128)} %bitcast.15), calls=%async_computation.3 | async-start | bytes 4194304 | tf_op jit(solution)/shard_map/all_to_all | solution.py:585
  209.4 12.6 %shard_map.252 = f32[8,4,128,128]{3,2,1,0:T(8,128)S(1)} custom-call(f32[6,512,1]{2,1,0:T(8,128)} %constant.75.clone.refs_0_, f32[6,1,512]{2,1,0:T(1,128)} %constant.71.clone.refs_1_, bf16[2,2,256,256]{3,2,1,0:T(8,128)(2,1)} %constant.68.clone.refs_5_.refs_2_, bf16[2,256,256]{2,1,0:T(8,128)(2,1)} %constant.76.clone.refs_3_, ...), custom_call_target="tpu_custom_call" | custom-call | flops 7247757312 | bytes 7340032 | tf_op jit(solution)/shard_map/pallas_call | solution.py:469
  222.0 0.0 copy-start.5
  222.0 1.3 copy-done.5
  223.3 34.4 %all-to-all-done.3 = f32[32,128,128]{2,1,0:T(8,128)} async-done(((f32[32,128,128]{2,1,0:T(8,128)}), f32[32,128,128]{2,1,0:T(8,128)}, u32[]{:S(2)}, u32[]{:S(2)}) %all-to-all-start.3) | async-done | bytes 2097184 | tf_op jit(solution)/shard_map/all_to_all | solution.py:585
  257.7 0.0 copy-start.7
  257.7 3.4 %all-to-all-start.5 = ((f32[32,128,128]{2,1,0:T(8,128)}), f32[32,128,128]{2,1,0:T(8,128)S(1)}, u32[]{:S(2)}, u32[]{:S(2)}) async-start(f32[32,128,128]{2,1,0:T(8,128)} %bitcast.13), calls=%async_computation.5 | async-start | bytes 4194304 | tf_op jit(solution)/shard_map/all_to_all | solution.py:585
  261.2 48.2 %all-to-all-done.5 = f32[32,128,128]{2,1,0:T(8,128)S(1)} async-done(((f32[32,128,128]{2,1,0:T(8,128)}), f32[32,128,128]{2,1,0:T(8,128)S(1)}, u32[]{:S(2)}, u32[]{:S(2)}) %all-to-all-start.5) | async-done | bytes 2097184 | tf_op jit(solution)/shard_map/all_to_all | solution.py:585
  309.4 0.0 copy-done.7
  309.4 5.7 %shard_map.253 = (f32[64,32,256]{2,1,0:T(8,128)}, f32[64,32,256]{2,1,0:T(8,128)}) custom-call(s32[1]{0:T(128)} %bitcast.refs_0_, bf16[2,2,2,256,256]{4,3,2,1,0:T(8,128)(2,1)S(1)} %copy-done.7, f32[8,2,2,128,128]{4,3,2,1,0:T(8,128)} %bitcast.8.refs_2_, f32[8,2,2,128,128]{4,3,2,1,0:T(8,128)S(1)} %bitcast.14), custom_call_target="tpu_custom_call" | custom-call | flops 1610612736 | bytes 8388608 | tf_op jit(solution)/shard_map/pallas_call | solution.py:568
Async XLA Ops:
  84.5 29.6 %all-to-all-start = ((f32[32,2,32,128]{3,2,1,0:T(8,128)}), f32[32,2,32,128]{3,2,1,0:T(8,128)}, u32[]{:S(2)}, u32[]{:S(2)}) async-start(f32[32,2,32,128]{3,2,1,0:T(8,128)} %bitcast.3), calls=%async_computation | async-start | bytes 2097152 | tf_op jit(solution)/shard_map/all_to_all | solution.py:585
  87.7 1.9 copy-start.3
  97.9 1.6 copy-start
  114.1 1.9 copy-start.1
  119.9 40.0 %copy-start.2 = (f32[16,12,32,128]{3,2,1,0:T(8,128)}, f32[16,12,32,128]{3,2,1,0:T(8,128)S(1)}, u32[]{:S(2)}) copy-start(f32[16,12,32,128]{3,2,1,0:T(8,128)S(1)} %get-tuple-element.13) | copy-start | bytes 9437188
  159.9 43.2 %all-to-all-start.4 = ((f32[16,12,32,128]{3,2,1,0:T(8,128)}), f32[16,12,32,128]{3,2,1,0:T(8,128)S(1)}, u32[]{:S(2)}, u32[]{:S(2)}) async-start(f32[16,12,32,128]{3,2,1,0:T(8,128)} %copy-done.2), calls=%async_computation.4 | async-start | bytes 6291456 | tf_op jit(solution)/shard_map/all_to_all | solution.py:585
  163.7 1.9 copy-start.4
  178.2 1.3 copy-start.6
  203.1 54.6 %all-to-all-start.3 = ((f32[32,128,128]{2,1,0:T(8,128)}), f32[32,128,128]{2,1,0:T(8,128)}, u32[]{:S(2)}, u32[]{:S(2)}) async-start(f32[32,128,128]{2,1,0:T(8,128)} %bitcast.15), calls=%async_computation.3 | async-start | bytes 4194304 | tf_op jit(solution)/shard_map/all_to_all | solution.py:585
  222.0 1.3 copy-start.5
  257.7 51.7 %copy-start.7 = (bf16[2,2,2,256,256]{4,3,2,1,0:T(8,128)(2,1)S(1)}, bf16[2,2,2,256,256]{4,3,2,1,0:T(8,128)(2,1)}, u32[]{:S(2)}) copy-start(bf16[2,2,2,256,256]{4,3,2,1,0:T(8,128)(2,1)} %constant.77.clone.refs_1_) | copy-start | bytes 3145732
  257.7 51.7 %all-to-all-start.5 = ((f32[32,128,128]{2,1,0:T(8,128)}), f32[32,128,128]{2,1,0:T(8,128)S(1)}, u32[]{:S(2)}, u32[]{:S(2)}) async-start(f32[32,128,128]{2,1,0:T(8,128)} %bitcast.13), calls=%async_computation.5 | async-start | bytes 4194304 | tf_op jit(solution)/shard_map/all_to_all | solution.py:585

commit v9 on v8

--- a/solution.py
+++ b/solution.py
@@ -72,14 +72,15 @@
 
 
 def third_kernel(counts, table_ref, density_ref, *outs):
-    rows_x, rows_y, length = density_ref.shape
-    wide, sides, ranks = outs[0].shape[:3]
+    step_x, rows_y, length = density_ref.shape
+    wide, sides, ranks, _, rows_x, _ = outs[0].shape
     half = length // 2
     flats = [ref.reshape(math.prod(ref.shape[:5]), 2 * rows_y) for ref in outs]
     table = pair(table_ref)
     left_half = lax.broadcasted_iota(jnp.int32, (half, 2 * rows_y), 1) < rows_y
     group = 4
-    for first in range(0, rows_x, group):
+    start_x = pl.program_id(0) * step_x
+    for first in range(0, step_x, group):
         block = density_ref[first : first + group].reshape(group * rows_y, length)
         result = product(table, split(block), ((1,), (1,)))
         for inner in range(0, group, 2):
@@ -93,13 +94,14 @@
                 for flat, count in zip(flats, counts):
                     for c in range(count):
                         for rank in range(ranks):
-                            at = (rank * count + c) * rows_x + x
+                            at = (rank * count + c) * rows_x + x + start_x
                             stride = sides * ranks * count * rows_x
                             flat[pl.ds(at, wide, stride=stride), :] = value[start : start + wide]
                             start += wide
     for ref in outs:
+        rows = pl.ds(pl.multiple_of(start_x, step_x), step_x)
         for side in range(1, sides):
-            ref[:, side] = ref[:, 0]
+            ref[:, side, :, :, rows] = ref[:, 0, :, :, rows]
 
 
 def third_pass(density, wide, sides, ranks, counts):
@@ -122,10 +124,7 @@
             pl.BlockSpec((step, rows_y, length), lambda i: (i, 0, 0)),
         ],
         out_specs=[
-            pl.BlockSpec(
-                (wide, sides, ranks, count, step, 2 * rows_y), lambda i: (0, 0, 0, 0, i, 0)
-            )
-            for count in counts
+            whole((wide, sides, ranks, count, rows_x, 2 * rows_y)) for count in counts
         ],
         out_shape=[
             pltpu.VMEM((wide, sides, ranks, count, rows_x, 2 * rows_y), jnp.float32)
@@ -280,6 +279,7 @@
     a_table = np.stack([wave, wave**2, scale]).astype(np.float32)[..., None]
     b_table = np.stack([wave**2, scale]).astype(np.float32).reshape(2, 1, length)
     message = PAIR * slab // groups
+    spaces = [pltpu.VMEM, pltpu.HBM][:groups]
     out_shape = (devices, 3 * 2 * length // TILE, steps * message, TILE)
     block = out_shape[:2] + (message, TILE)
 
@@ -305,7 +305,7 @@
             ],
             out_specs=[pl.BlockSpec(block, lambda i, *_: (0, 0, first_step + i, 0))] * groups,
         ),
-        out_shape=[pltpu.VMEM(out_shape, jnp.float32)] * groups,
+        out_shape=[space(out_shape, jnp.float32) for space in spaces],
         input_output_aliases={8 + spot: spot for spot in range(len(filled))},
         compiler_params=params(1),
         cost_estimate=cost(per_c * 7 * length**3, 20 * per_c * length**2 * 2),
@@ -314,7 +314,7 @@
         start_c,
         *[in_hbm(table) for table in (a_table, b_table, *tables)],
         received,
-        *[keep(each, pltpu.VMEM) for each in filled],
+        *[keep(each, space) for each, space in zip(filled, spaces)],
     )
 
 
@@ -476,7 +476,7 @@
             pl.BlockSpec((devices, tiles // 3, message, tile), which),
         ],
         out_specs=whole(out_shape),
-        out_shape=pltpu.VMEM(out_shape, jnp.float32),
+        out_shape=pltpu.HBM(out_shape, jnp.float32),
         scratch_shapes=[pltpu.VMEM((length, count * length), jnp.float32)],
         compiler_params=params(1),
         cost_estimate=cost(count * 18 * length**3, 4 * received.size + 4 * 2**20),
@@ -494,12 +494,14 @@
     spot_row = lax.broadcasted_iota(jnp.int32, (lanes, half), 0)
     spot_a = lax.broadcasted_iota(jnp.int32, (lanes, half), 1)
     is_anchor = (anchor_ref[0] == 1) & (pl.program_id(0) == 0)
+    start = pl.program_id(0) * steps
     anchor = (spot_row == 0) & (spot_a == 0) & is_anchor
     upper = lax.broadcasted_iota(jnp.int32, (wide * ranks, joined * count, lanes), 1) < count
 
     def gathered(side, step, join, part):
         if joined == 2:
-            at = pl.ds((step * 2 + part) * 2 * count, 2 * count)
+            at = ((start + step) * 2 + part) * 2 * count
+            at = pl.ds(pl.multiple_of(at, 2 * count), 2 * count)
             own, other = [
                 ref[:, side, :, at].reshape(wide * ranks, 2 * count, lanes)
                 for ref in (ins if join == 0 else ins[::-1])
@@ -571,8 +573,7 @@
         in_specs=[
             pl.BlockSpec(memory_space=pltpu.SMEM),
             whole(table.shape),
-            *[pl.BlockSpec((wide, sides, ranks, rows // grid, lanes), lambda i: (0, 0, 0, i, 0))]
-            * joined,
+            *[whole((wide, sides, ranks, rows, lanes))] * joined,
         ],
         out_specs=[pl.BlockSpec((rows_c // grid, rows_b, length), lambda i: (i, 0, 0))] * 2,
         out_shape=[out_shape] * 2,
@@ -613,7 +614,7 @@
         for planes, count in zip(third_pass(density, wide, sides, ranks, counts), counts):
             planes = transpose(planes.reshape(wide * narrow, count, rows_x, 2 * rows_y))
             planes = planes.reshape(wide, narrow, count, rows_x, 2 * rows_y)
-            planes = keep(planes, pltpu.VMEM)
+            planes = keep(planes, pltpu.VMEM if start else pltpu.HBM)
             chunks = spectrum_pass(
                 planes, side, start_c, devices, groups, steps, start // PAIR, chunks
             )
@@ -621,7 +622,7 @@
         is_anchor = ((spot_wide == 0) & (spot_narrow == 0)).astype(jnp.int32).reshape(1)
         parts = []
         for group, chunk in enumerate(chunks):
-            received = keep(transpose(chunk, members), pltpu.VMEM)
+            received = keep(transpose(chunk, members), pltpu.VMEM if group else pltpu.HBM)
             part = shear_pass(received, wide, narrow, per_c, group, groups)
             parts.append(transpose(part.reshape((wide * narrow,) + part.shape[2:])))
         return tuple(first_pass(parts, is_anchor, length, wide, sides, slab // groups))

time: 316 us -> 315 us (level)
  local copies, waits for them, and re-layouts: 9.93 us -> 0.01 us
  Pallas kernels: 48.5 us -> 53.5 us
  waiting for transfers between devices: 121 us -> 125 us
    unnamed x16 -> x2, local copies, waits for them, and re-layouts: 9.93 us -> 0.01 us
    all_to_all x4, waiting for transfers between devices: 121 us -> 125 us  [transpose(): lax.all_to_all(value, AXES, split_axis=0, concat_axis=0, tiled=True, axis...]
  transfers between devices with their start and end apart: 4 -> 4, of which waited for: 4 -> 4; matrix products, arithmetic and copies ran while one was open for 0% -> 0% of each run, Pallas kernels for 11% -> 12%
where the time goes in v9:
time: 315 us; the launch traced here: 314 us
  waiting for transfers between devices  125 us (40%)
  blocking collectives  118 us (37%)
  Pallas kernels  53.5 us (17%)
  starting transfers between devices  16.8 us (5%)
    all_to_all x4, waiting for transfers between devices, transpose(): lax.all_to_all(value, AXES, split_axis=0, concat_axis=0, tiled=True, axis...  125 us
    all_to_all x2, blocking collectives, transpose(): lax.all_to_all(value, AXES, split_axis=0, concat_axis=0, tiled=True, axis...  118 us
    pallas_call x2, Pallas kernels, shear_pass(): pl.pallas_call(body, grid=(6,), in_specs=[pl.BlockSpec((1, count * half,...  28.1 us
    all_to_all x4, starting transfers between devices, transpose(): lax.all_to_all(value, AXES, split_axis=0, concat_axis=0, tiled=True, axis...  16.8 us
    pallas_call x2, Pallas kernels, spectrum_pass(): pl.pallas_call(body, grid_spec=pltpu.PrefetchScalarGridSpec(num_scalar_pr...  13.9 us
  transfers between devices with their start and end apart: 4, of which 4 were waited for; matrix products, arithmetic and copies ran while one was open for 0% of the time, Pallas kernels for 12%

profile of v9, /device:TPU:1, one launch (start us, length us, event | category | flops | bytes accessed | tf_op | source)
XLA Modules:
  0.0 314.4 jit_solution(12958725832504104082)
XLA Ops:
  0.6 5.8 %shard_map.248 = (f32[8,2,2,6,32,128]{5,4,3,2,1,0:T(8,128)S(1)}, f32[8,2,2,2,32,128]{5,4,3,2,1,0:T(8,128)}) custom-call(bf16[2,256,256]{2,1,0:T(8,128)(2,1)} %constant.64.clone.refs_0_, f32[32,64,256]{2,1,0:T(8,128)} %refs_1_.4), custom_call_target="tpu_custom_call" | custom-call | flops 805306368 | bytes 6291456 | tf_op jit(solution)/shard_map/pallas_call | solution.py:119
  6.5 78.3 %all_to_all.30 = f32[32,6,32,128]{3,2,1,0:T(8,128)} all-to-all(f32[32,6,32,128]{3,2,1,0:T(8,128)S(1)} %bitcast.11), channel_id=1, replica_groups=mesh['wide'=8,'narrow'=4] {'wide','narrow'}, dimensions={0} | all-to-all | bytes 6291456 | tf_op jit(solution)/shard_map/all_to_all | solution.py:586
  84.8 3.2 %all-to-all-start = ((f32[32,2,32,128]{3,2,1,0:T(8,128)}), f32[32,2,32,128]{3,2,1,0:T(8,128)}, u32[]{:S(2)}, u32[]{:S(2)}) async-start(f32[32,2,32,128]{3,2,1,0:T(8,128)} %bitcast.3), calls=%async_computation | async-start | bytes 2097152 | tf_op jit(solution)/shard_map/all_to_all | solution.py:586
  88.0 9.1 %shard_map.249 = (f32[16,12,32,128]{3,2,1,0:T(8,128)S(1)}, f32[16,12,32,128]{3,2,1,0:T(8,128)}) custom-call(s32[1]{0:T(128)} %bitcast.1.refs_0_, s32[1]{0:T(128)} %bitcast.2.refs_1_, f32[3,2,128,1]{3,2,1,0:T(8,128)} %constant.65.clone.refs_2_, f32[2,1,256]{2,1,0:T(1,128)} %constant.66.clone.refs_3_, bf16[2,2,256,256]{3,2,1,0:T(8,128)(2,1)} %constant.67.clone.refs_4_, ...), custom_call_target="tpu_custom_call" | custom-call | flops 4227858432 | bytes 15728640 | tf_op jit(solution)/shard_map/pallas_call | solution.py:292
  97.1 17.3 %all-to-all-done = f32[32,2,32,128]{3,2,1,0:T(8,128)} async-done(((f32[32,2,32,128]{3,2,1,0:T(8,128)}), f32[32,2,32,128]{3,2,1,0:T(8,128)}, u32[]{:S(2)}, u32[]{:S(2)}) %all-to-all-start) | async-done | bytes 1048608 | tf_op jit(solution)/shard_map/all_to_all | solution.py:586
  114.4 4.8 %shard_map.250 = (f32[16,12,32,128]{3,2,1,0:T(8,128)S(1)}, f32[16,12,32,128]{3,2,1,0:T(8,128)}) custom-call(s32[1]{0:T(128)} %bitcast.1.refs_0_, s32[1]{0:T(128)} %bitcast.2.refs_1_, f32[3,2,128,1]{3,2,1,0:T(8,128)} %constant.65.clone.refs_2_, f32[2,1,256]{2,1,0:T(1,128)} %constant.66.clone.refs_3_, ...), custom_call_target="tpu_custom_call", output_to_operand_aliasing={{0}: (8, {}), {1}: (9, {})} | custom-call | flops 1409286144 | bytes 5242880 | tf_op jit(solution)/shard_map/pallas_call | solution.py:292
  119.2 40.0 %all_to_all.31.refs_6_ = f32[16,12,32,128]{3,2,1,0:T(8,128)} all-to-all(f32[16,12,32,128]{3,2,1,0:T(8,128)S(1)} %get-tuple-element.12), channel_id=1, replica_groups={{0,1,4,5,8,9,12,13,16,17,20,21,24,25,28,29},{2,3,6,7,10,11,14,15,18,19,..., dimensions={0} | all-to-all | bytes 6291456 | tf_op jit(solution)/shard_map/all_to_all | solution.py:586
  159.2 3.8 %all-to-all-start.4 = ((f32[16,12,32,128]{3,2,1,0:T(8,128)}), f32[16,12,32,128]{3,2,1,0:T(8,128)S(1)}, u32[]{:S(2)}, u32[]{:S(2)}) async-start(f32[16,12,32,128]{3,2,1,0:T(8,128)} %get-tuple-element.13), calls=%async_computation.4 | async-start | bytes 6291456 | tf_op jit(solution)/shard_map/all_to_all | solution.py:586
  163.0 14.2 %shard_map.251 = f32[8,4,128,128]{3,2,1,0:T(8,128)} custom-call(f32[6,512,1]{2,1,0:T(8,128)} %constant.70.clone.refs_0_, f32[6,1,512]{2,1,0:T(1,128)} %constant.71.clone.refs_1_, bf16[2,2,256,256]{3,2,1,0:T(8,128)(2,1)} %constant.68.clone.refs_5_.refs_2_, bf16[2,256,256]{2,1,0:T(8,128)(2,1)} %constant.72.clone.refs_3_, ...), custom_call_target="tpu_custom_call" | custom-call | flops 7247757312 | bytes 7340032 | tf_op jit(solution)/shard_map/pallas_call | solution.py:469
  177.2 25.1 %all-to-all-done.4.refs_6_ = f32[16,12,32,128]{3,2,1,0:T(8,128)S(1)} async-done(((f32[16,12,32,128]{3,2,1,0:T(8,128)}), f32[16,12,32,128]{3,2,1,0:T(8,128)S(1)}, u32[]{:S(2)}, u32[]{:S(2)}) %all-to-all-start.4) | async-done | bytes 3145760 | tf_op jit(solution)/shard_map/all_to_all | solution.py:586
  202.3 6.3 %all-to-all-start.3 = ((f32[32,128,128]{2,1,0:T(8,128)}), f32[32,128,128]{2,1,0:T(8,128)}, u32[]{:S(2)}, u32[]{:S(2)}) async-start(f32[32,128,128]{2,1,0:T(8,128)} %bitcast.15), calls=%async_computation.3 | async-start | bytes 4194304 | tf_op jit(solution)/shard_map/all_to_all | solution.py:586
  208.7 13.9 %shard_map.252 = f32[8,4,128,128]{3,2,1,0:T(8,128)} custom-call(f32[6,512,1]{2,1,0:T(8,128)} %constant.75.clone.refs_0_, f32[6,1,512]{2,1,0:T(1,128)} %constant.71.clone.refs_1_, bf16[2,2,256,256]{3,2,1,0:T(8,128)(2,1)} %constant.68.clone.refs_5_.refs_2_, bf16[2,256,256]{2,1,0:T(8,128)(2,1)} %constant.76.clone.refs_3_, ...), custom_call_target="tpu_custom_call" | custom-call | flops 7247757312 | bytes 7340032 | tf_op jit(solution)/shard_map/pallas_call | solution.py:469
  222.6 34.4 %all-to-all-done.3 = f32[32,128,128]{2,1,0:T(8,128)} async-done(((f32[32,128,128]{2,1,0:T(8,128)}), f32[32,128,128]{2,1,0:T(8,128)}, u32[]{:S(2)}, u32[]{:S(2)}) %all-to-all-start.3) | async-done | bytes 2097184 | tf_op jit(solution)/shard_map/all_to_all | solution.py:586
  257.0 0.0 copy-start
  257.0 3.4 %all-to-all-start.5 = ((f32[32,128,128]{2,1,0:T(8,128)}), f32[32,128,128]{2,1,0:T(8,128)S(1)}, u32[]{:S(2)}, u32[]{:S(2)}) async-start(f32[32,128,128]{2,1,0:T(8,128)} %bitcast.14), calls=%async_computation.5 | async-start | bytes 4194304 | tf_op jit(solution)/shard_map/all_to_all | solution.py:586
  260.4 48.2 %all-to-all-done.5 = f32[32,128,128]{2,1,0:T(8,128)S(1)} async-done(((f32[32,128,128]{2,1,0:T(8,128)}), f32[32,128,128]{2,1,0:T(8,128)S(1)}, u32[]{:S(2)}, u32[]{:S(2)}) %all-to-all-start.5) | async-done | bytes 2097184 | tf_op jit(solution)/shard_map/all_to_all | solution.py:586
  308.7 0.0 copy-done
  308.7 5.7 %shard_map.253 = (f32[64,32,256]{2,1,0:T(8,128)}, f32[64,32,256]{2,1,0:T(8,128)}) custom-call(s32[1]{0:T(128)} %bitcast.refs_0_, bf16[2,2,2,256,256]{4,3,2,1,0:T(8,128)(2,1)S(1)} %copy-done, f32[8,2,2,128,128]{4,3,2,1,0:T(8,128)} %bitcast.8.refs_2_, f32[8,2,2,128,128]{4,3,2,1,0:T(8,128)S(1)} %bitcast.12), custom_call_target="tpu_custom_call" | custom-call | flops 1610612736 | bytes 8388608 | tf_op jit(solution)/shard_map/pallas_call | solution.py:570
Async XLA Ops:
  84.8 29.6 %all-to-all-start = ((f32[32,2,32,128]{3,2,1,0:T(8,128)}), f32[32,2,32,128]{3,2,1,0:T(8,128)}, u32[]{:S(2)}, u32[]{:S(2)}) async-start(f32[32,2,32,128]{3,2,1,0:T(8,128)} %bitcast.3), calls=%async_computation | async-start | bytes 2097152 | tf_op jit(solution)/shard_map/all_to_all | solution.py:586
  159.2 43.2 %all-to-all-start.4 = ((f32[16,12,32,128]{3,2,1,0:T(8,128)}), f32[16,12,32,128]{3,2,1,0:T(8,128)S(1)}, u32[]{:S(2)}, u32[]{:S(2)}) async-start(f32[16,12,32,128]{3,2,1,0:T(8,128)} %get-tuple-element.13), calls=%async_computation.4 | async-start | bytes 6291456 | tf_op jit(solution)/shard_map/all_to_all | solution.py:586
  202.3 54.6 %all-to-all-start.3 = ((f32[32,128,128]{2,1,0:T(8,128)}), f32[32,128,128]{2,1,0:T(8,128)}, u32[]{:S(2)}, u32[]{:S(2)}) async-start(f32[32,128,128]{2,1,0:T(8,128)} %bitcast.15), calls=%async_computation.3 | async-start | bytes 4194304 | tf_op jit(solution)/shard_map/all_to_all | solution.py:586
  257.0 51.7 %copy-start = (bf16[2,2,2,256,256]{4,3,2,1,0:T(8,128)(2,1)S(1)}, bf16[2,2,2,256,256]{4,3,2,1,0:T(8,128)(2,1)}, u32[]{:S(2)}) copy-start(bf16[2,2,2,256,256]{4,3,2,1,0:T(8,128)(2,1)} %constant.77.clone.refs_1_) | copy-start | bytes 3145732
  257.0 51.7 %all-to-all-start.5 = ((f32[32,128,128]{2,1,0:T(8,128)}), f32[32,128,128]{2,1,0:T(8,128)S(1)}, u32[]{:S(2)}, u32[]{:S(2)}) async-start(f32[32,128,128]{2,1,0:T(8,128)} %bitcast.14), calls=%async_computation.5 | async-start | bytes 4194304 | tf_op jit(solution)/shard_map/all_to_all | solution.py:586

commit v10 on v9

--- a/solution.py
+++ b/solution.py
@@ -77,27 +77,22 @@
     half = length // 2
     flats = [ref.reshape(math.prod(ref.shape[:5]), 2 * rows_y) for ref in outs]
     table = pair(table_ref)
-    left_half = lax.broadcasted_iota(jnp.int32, (half, 2 * rows_y), 1) < rows_y
     group = 4
     start_x = pl.program_id(0) * step_x
     for first in range(0, step_x, group):
         block = density_ref[first : first + group].reshape(group * rows_y, length)
-        result = product(table, split(block), ((1,), (1,)))
-        for inner in range(0, group, 2):
-            lanes = slice(inner * rows_y, (inner + 2) * rows_y)
-            real = result[:half, lanes]
-            imag = result[half:, lanes]
-            even = jnp.where(left_half, real, pltpu.roll(imag, rows_y, 1))
-            odd = jnp.where(left_half, pltpu.roll(real, rows_y, 1), imag)
-            for x, value in ((first + inner, even), (first + inner + 1, odd)):
-                start = 0
-                for flat, count in zip(flats, counts):
-                    for c in range(count):
-                        for rank in range(ranks):
-                            at = (rank * count + c) * rows_x + x + start_x
-                            stride = sides * ranks * count * rows_x
-                            flat[pl.ds(at, wide, stride=stride), :] = value[start : start + wide]
-                            start += wide
+        result = product(split(block), table)
+        for inner in range(group):
+            rows = slice(inner * rows_y, (inner + 1) * rows_y)
+            value = jnp.concatenate([result[rows, :half], result[rows, half:]], axis=0).T
+            start = 0
+            for flat, count in zip(flats, counts):
+                for c in range(count):
+                    for rank in range(ranks):
+                        at = (rank * count + c) * rows_x + first + inner + start_x
+                        stride = sides * ranks * count * rows_x
+                        flat[pl.ds(at, wide, stride=stride), :] = value[start : start + wide]
+                        start += wide
     for ref in outs:
         rows = pl.ds(pl.multiple_of(start_x, step_x), step_x)
         for side in range(1, sides):
@@ -109,8 +104,8 @@
     half = length // 2
     per_c = sum(counts)
     order = np.arange(half).reshape(wide, ranks, per_c).transpose(2, 1, 0).reshape(-1)
-    angle = angles(order, np.arange(length), length)
-    table = split_table(np.concatenate([np.cos(angle), -np.sin(angle)]))
+    angle = angles(np.arange(length), order, length)
+    table = split_table(np.concatenate([np.cos(angle), -np.sin(angle)], axis=1))
     step = min(8, rows_x)
 
     def body(*refs):
@@ -498,18 +493,18 @@
     anchor = (spot_row == 0) & (spot_a == 0) & is_anchor
     upper = lax.broadcasted_iota(jnp.int32, (wide * ranks, joined * count, lanes), 1) < count
 
-    def gathered(side, step, join, part):
+    def gathered(side, step, part):
         if joined == 2:
             at = ((start + step) * 2 + part) * 2 * count
             at = pl.ds(pl.multiple_of(at, 2 * count), 2 * count)
             own, other = [
-                ref[:, side, :, at].reshape(wide * ranks, 2 * count, lanes)
-                for ref in (ins if join == 0 else ins[::-1])
+                ref[:, side, :, at].reshape(wide * ranks, 2 * count, lanes) for ref in ins
             ]
-            return jnp.where(upper, own, other).reshape(half, lanes)
+            both = [jnp.where(upper, own, other), jnp.where(upper, other, own)]
+            return [value.reshape(half, lanes).T for value in both]
         flat = ins[0].reshape(wide * sides * ranks * rows, lanes)
         run = rows // count
-        return jnp.concatenate(
+        value = jnp.concatenate(
             [
                 flat[
                     pl.ds((w * sides + side) * ranks * rows + part * steps + step, ranks * count, stride=run),
@@ -519,18 +514,23 @@
             ],
             axis=0,
         )
-
+        return [value.T]
+
+    lefts = []
+    for side in range(sides):
+        tiles = [[gathered(side, step, part) for part in range(2)] for step in range(steps)]
+        lefts.append(
+            [
+                jnp.concatenate(
+                    [jnp.concatenate([part[join] for part in parts], axis=1) for parts in tiles], axis=0
+                )
+                for join in range(joined)
+            ]
+        )
     for join in range(joined):
-        sums = []
-        for side in range(sides):
-            left = jnp.concatenate(
-                [
-                    jnp.concatenate([gathered(side, step, join, part).T for part in range(2)], axis=1)
-                    for step in range(steps)
-                ],
-                axis=0,
-            )
-            sums.append(product(split(left), pair(table_ref.at[join, side])))
+        sums = [
+            product(split(lefts[side][join]), pair(table_ref.at[join, side])) for side in range(sides)
+        ]
         even, odd = sums
         for far, value in enumerate((even + odd, even - odd)):
             for step in range(steps):

time: 315 us -> 315 us (level)
  no operation moved by 1% of the time
where the time goes in v10:
time: 315 us; the launch traced here: 314 us
  waiting for transfers between devices  125 us (40%)
  blocking collectives  118 us (37%)
  Pallas kernels  53.4 us (17%)
  starting transfers between devices  16.8 us (5%)
    all_to_all x4, waiting for transfers between devices, transpose(): lax.all_to_all(value, AXES, split_axis=0, concat_axis=0, tiled=True, axis...  125 us
    all_to_all x2, blocking collectives, transpose(): lax.all_to_all(value, AXES, split_axis=0, concat_axis=0, tiled=True, axis...  118 us
    pallas_call x2, Pallas kernels, shear_pass(): pl.pallas_call(body, grid=(6,), in_specs=[pl.BlockSpec((1, count * half,...  28.1 us
    all_to_all x4, starting transfers between devices, transpose(): lax.all_to_all(value, AXES, split_axis=0, concat_axis=0, tiled=True, axis...  16.8 us
    pallas_call x2, Pallas kernels, spectrum_pass(): pl.pallas_call(body, grid_spec=pltpu.PrefetchScalarGridSpec(num_scalar_pr...  13.9 us
  transfers between devices with their start and end apart: 4, of which 4 were waited for; matrix products, arithmetic and copies ran while one was open for 0% of the time, Pallas kernels for 12%

profile of v10, /device:TPU:1, one launch (start us, length us, event | category | flops | bytes accessed | tf_op | source)
XLA Modules:
  0.0 314.3 jit_solution(106730284788291485)
XLA Ops:
  0.6 5.8 %shard_map.248 = (f32[8,2,2,6,32,128]{5,4,3,2,1,0:T(8,128)S(1)}, f32[8,2,2,2,32,128]{5,4,3,2,1,0:T(8,128)}) custom-call(bf16[2,256,256]{2,1,0:T(8,128)(2,1)} %constant.64.clone.refs_0_, f32[32,64,256]{2,1,0:T(8,128)} %refs_1_.4), custom_call_target="tpu_custom_call" | custom-call | flops 805306368 | bytes 6291456 | tf_op jit(solution)/shard_map/pallas_call | solution.py:114
  6.4 78.3 %all_to_all.30 = f32[32,6,32,128]{3,2,1,0:T(8,128)} all-to-all(f32[32,6,32,128]{3,2,1,0:T(8,128)S(1)} %bitcast.11), channel_id=1, replica_groups=mesh['wide'=8,'narrow'=4] {'wide','narrow'}, dimensions={0} | all-to-all | bytes 6291456 | tf_op jit(solution)/shard_map/all_to_all | solution.py:586
  84.7 3.2 %all-to-all-start = ((f32[32,2,32,128]{3,2,1,0:T(8,128)}), f32[32,2,32,128]{3,2,1,0:T(8,128)}, u32[]{:S(2)}, u32[]{:S(2)}) async-start(f32[32,2,32,128]{3,2,1,0:T(8,128)} %bitcast.3), calls=%async_computation | async-start | bytes 2097152 | tf_op jit(solution)/shard_map/all_to_all | solution.py:586
  87.9 9.1 %shard_map.249 = (f32[16,12,32,128]{3,2,1,0:T(8,128)S(1)}, f32[16,12,32,128]{3,2,1,0:T(8,128)}) custom-call(s32[1]{0:T(128)} %bitcast.1.refs_0_, s32[1]{0:T(128)} %bitcast.2.refs_1_, f32[3,2,128,1]{3,2,1,0:T(8,128)} %constant.65.clone.refs_2_, f32[2,1,256]{2,1,0:T(1,128)} %constant.66.clone.refs_3_, bf16[2,2,256,256]{3,2,1,0:T(8,128)(2,1)} %constant.67.clone.refs_4_, ...), custom_call_target="tpu_custom_call" | custom-call | flops 4227858432 | bytes 15728640 | tf_op jit(solution)/shard_map/pallas_call | solution.py:287
  97.1 17.2 %all-to-all-done = f32[32,2,32,128]{3,2,1,0:T(8,128)} async-done(((f32[32,2,32,128]{3,2,1,0:T(8,128)}), f32[32,2,32,128]{3,2,1,0:T(8,128)}, u32[]{:S(2)}, u32[]{:S(2)}) %all-to-all-start) | async-done | bytes 1048608 | tf_op jit(solution)/shard_map/all_to_all | solution.py:586
  114.3 4.8 %shard_map.250 = (f32[16,12,32,128]{3,2,1,0:T(8,128)S(1)}, f32[16,12,32,128]{3,2,1,0:T(8,128)}) custom-call(s32[1]{0:T(128)} %bitcast.1.refs_0_, s32[1]{0:T(128)} %bitcast.2.refs_1_, f32[3,2,128,1]{3,2,1,0:T(8,128)} %constant.65.clone.refs_2_, f32[2,1,256]{2,1,0:T(1,128)} %constant.66.clone.refs_3_, ...), custom_call_target="tpu_custom_call", output_to_operand_aliasing={{0}: (8, {}), {1}: (9, {})} | custom-call | flops 1409286144 | bytes 5242880 | tf_op jit(solution)/shard_map/pallas_call | solution.py:287
  119.1 40.0 %all_to_all.31.refs_6_ = f32[16,12,32,128]{3,2,1,0:T(8,128)} all-to-all(f32[16,12,32,128]{3,2,1,0:T(8,128)S(1)} %get-tuple-element.12), channel_id=1, replica_groups={{0,1,4,5,8,9,12,13,16,17,20,21,24,25,28,29},{2,3,6,7,10,11,14,15,18,19,..., dimensions={0} | all-to-all | bytes 6291456 | tf_op jit(solution)/shard_map/all_to_all | solution.py:586
  159.1 3.8 %all-to-all-start.4 = ((f32[16,12,32,128]{3,2,1,0:T(8,128)}), f32[16,12,32,128]{3,2,1,0:T(8,128)S(1)}, u32[]{:S(2)}, u32[]{:S(2)}) async-start(f32[16,12,32,128]{3,2,1,0:T(8,128)} %get-tuple-element.13), calls=%async_computation.4 | async-start | bytes 6291456 | tf_op jit(solution)/shard_map/all_to_all | solution.py:586
  162.9 14.2 %shard_map.251 = f32[8,4,128,128]{3,2,1,0:T(8,128)} custom-call(f32[6,512,1]{2,1,0:T(8,128)} %constant.70.clone.refs_0_, f32[6,1,512]{2,1,0:T(1,128)} %constant.71.clone.refs_1_, bf16[2,2,256,256]{3,2,1,0:T(8,128)(2,1)} %constant.68.clone.refs_5_.refs_2_, bf16[2,256,256]{2,1,0:T(8,128)(2,1)} %constant.72.clone.refs_3_, ...), custom_call_target="tpu_custom_call" | custom-call | flops 7247757312 | bytes 7340032 | tf_op jit(solution)/shard_map/pallas_call | solution.py:464
  177.1 25.1 %all-to-all-done.4.refs_6_ = f32[16,12,32,128]{3,2,1,0:T(8,128)S(1)} async-done(((f32[16,12,32,128]{3,2,1,0:T(8,128)}), f32[16,12,32,128]{3,2,1,0:T(8,128)S(1)}, u32[]{:S(2)}, u32[]{:S(2)}) %all-to-all-start.4) | async-done | bytes 3145760 | tf_op jit(solution)/shard_map/all_to_all | solution.py:586
  202.3 6.3 %all-to-all-start.3 = ((f32[32,128,128]{2,1,0:T(8,128)}), f32[32,128,128]{2,1,0:T(8,128)}, u32[]{:S(2)}, u32[]{:S(2)}) async-start(f32[32,128,128]{2,1,0:T(8,128)} %bitcast.15), calls=%async_computation.3 | async-start | bytes 4194304 | tf_op jit(solution)/shard_map/all_to_all | solution.py:586
  208.6 13.9 %shard_map.252 = f32[8,4,128,128]{3,2,1,0:T(8,128)} custom-call(f32[6,512,1]{2,1,0:T(8,128)} %constant.75.clone.refs_0_, f32[6,1,512]{2,1,0:T(1,128)} %constant.71.clone.refs_1_, bf16[2,2,256,256]{3,2,1,0:T(8,128)(2,1)} %constant.68.clone.refs_5_.refs_2_, bf16[2,256,256]{2,1,0:T(8,128)(2,1)} %constant.76.clone.refs_3_, ...), custom_call_target="tpu_custom_call" | custom-call | flops 7247757312 | bytes 7340032 | tf_op jit(solution)/shard_map/pallas_call | solution.py:464
  222.5 34.4 %all-to-all-done.3 = f32[32,128,128]{2,1,0:T(8,128)} async-done(((f32[32,128,128]{2,1,0:T(8,128)}), f32[32,128,128]{2,1,0:T(8,128)}, u32[]{:S(2)}, u32[]{:S(2)}) %all-to-all-start.3) | async-done | bytes 2097184 | tf_op jit(solution)/shard_map/all_to_all | solution.py:586
  256.9 0.0 copy-start
  256.9 3.4 %all-to-all-start.5 = ((f32[32,128,128]{2,1,0:T(8,128)}), f32[32,128,128]{2,1,0:T(8,128)S(1)}, u32[]{:S(2)}, u32[]{:S(2)}) async-start(f32[32,128,128]{2,1,0:T(8,128)} %bitcast.14), calls=%async_computation.5 | async-start | bytes 4194304 | tf_op jit(solution)/shard_map/all_to_all | solution.py:586
  260.3 48.2 %all-to-all-done.5 = f32[32,128,128]{2,1,0:T(8,128)S(1)} async-done(((f32[32,128,128]{2,1,0:T(8,128)}), f32[32,128,128]{2,1,0:T(8,128)S(1)}, u32[]{:S(2)}, u32[]{:S(2)}) %all-to-all-start.5) | async-done | bytes 2097184 | tf_op jit(solution)/shard_map/all_to_all | solution.py:586
  308.6 0.0 copy-done
  308.6 5.7 %shard_map.253 = (f32[64,32,256]{2,1,0:T(8,128)}, f32[64,32,256]{2,1,0:T(8,128)}) custom-call(s32[1]{0:T(128)} %bitcast.refs_0_, bf16[2,2,2,256,256]{4,3,2,1,0:T(8,128)(2,1)S(1)} %copy-done, f32[8,2,2,128,128]{4,3,2,1,0:T(8,128)} %bitcast.8.refs_2_, f32[8,2,2,128,128]{4,3,2,1,0:T(8,128)S(1)} %bitcast.12), custom_call_target="tpu_custom_call" | custom-call | flops 1610612736 | bytes 8388608 | tf_op jit(solution)/shard_map/pallas_call | solution.py:570
Async XLA Ops:
  84.7 29.6 %all-to-all-start = ((f32[32,2,32,128]{3,2,1,0:T(8,128)}), f32[32,2,32,128]{3,2,1,0:T(8,128)}, u32[]{:S(2)}, u32[]{:S(2)}) async-start(f32[32,2,32,128]{3,2,1,0:T(8,128)} %bitcast.3), calls=%async_computation | async-start | bytes 2097152 | tf_op jit(solution)/shard_map/all_to_all | solution.py:586
  159.1 43.2 %all-to-all-start.4 = ((f32[16,12,32,128]{3,2,1,0:T(8,128)}), f32[16,12,32,128]{3,2,1,0:T(8,128)S(1)}, u32[]{:S(2)}, u32[]{:S(2)}) async-start(f32[16,12,32,128]{3,2,1,0:T(8,128)} %get-tuple-element.13), calls=%async_computation.4 | async-start | bytes 6291456 | tf_op jit(solution)/shard_map/all_to_all | solution.py:586
  202.3 54.6 %all-to-all-start.3 = ((f32[32,128,128]{2,1,0:T(8,128)}), f32[32,128,128]{2,1,0:T(8,128)}, u32[]{:S(2)}, u32[]{:S(2)}) async-start(f32[32,128,128]{2,1,0:T(8,128)} %bitcast.15), calls=%async_computation.3 | async-start | bytes 4194304 | tf_op jit(solution)/shard_map/all_to_all | solution.py:586
  256.9 51.7 %copy-start = (bf16[2,2,2,256,256]{4,3,2,1,0:T(8,128)(2,1)S(1)}, bf16[2,2,2,256,256]{4,3,2,1,0:T(8,128)(2,1)}, u32[]{:S(2)}) copy-start(bf16[2,2,2,256,256]{4,3,2,1,0:T(8,128)(2,1)} %constant.77.clone.refs_1_) | copy-start | bytes 3145732
  256.9 51.7 %all-to-all-start.5 = ((f32[32,128,128]{2,1,0:T(8,128)}), f32[32,128,128]{2,1,0:T(8,128)S(1)}, u32[]{:S(2)}, u32[]{:S(2)}) async-start(f32[32,128,128]{2,1,0:T(8,128)} %bitcast.14), calls=%async_computation.5 | async-start | bytes 4194304 | tf_op jit(solution)/shard_map/all_to_all | solution.py:586

commit v11 on v10

--- a/solution.py
+++ b/solution.py
@@ -106,7 +106,7 @@
     order = np.arange(half).reshape(wide, ranks, per_c).transpose(2, 1, 0).reshape(-1)
     angle = angles(np.arange(length), order, length)
     table = split_table(np.concatenate([np.cos(angle), -np.sin(angle)], axis=1))
-    step = min(8, rows_x)
+    step = max(rows_x // 2, min(8, rows_x))
 
     def body(*refs):
         third_kernel(counts, *refs)
@@ -138,8 +138,18 @@
     return np.block([[cosine, -sine], [sine, cosine]])
 
 
-def spectrum_kernel(slab, groups, first_c, side_ref, start_ref, a_ref, b_ref, second_ref, first_ref, back_ref, in_ref, *refs):
-    outs = refs[-groups:]
+def hand_on(sources, targets):
+    @pl.when(pl.program_id(0) == 0)
+    def _():
+        for source, target in zip(sources, targets):
+            target[...] = source[...]
+
+
+def spectrum_kernel(slab, groups, first_c, filled, side_ref, start_ref, *refs):
+    tables, in_ref, outs = refs[:5], refs[5], refs[6 + filled :]
+    a_ref, b_ref, second_ref, first_ref, back_ref = tables
+    hand_on(tables, outs[groups:])
+    outs = outs[:groups]
     wide, narrow, _, rows_x, lanes = in_ref.shape
     length = wide * rows_x
     half = length // 2
@@ -245,7 +255,7 @@
     return np.arange(length).reshape(length // 2, 2).T
 
 
-def spectrum_pass(received, side, start_c, devices, groups, steps, first_step, filled):
+def spectrum_pass(received, side, start_c, devices, groups, steps, first_step, filled, carried):
     wide, narrow, per_c, rows_x, lanes = received.shape
     length = wide * rows_x
     rows_y = lanes // 2
@@ -279,43 +289,56 @@
     block = out_shape[:2] + (message, TILE)
 
     def body(*refs):
-        spectrum_kernel(slab, groups, first_step * PAIR, *refs)
+        spectrum_kernel(slab, groups, first_step * PAIR, len(filled), *refs)
 
     def fixed(shape):
         return pl.BlockSpec(shape, lambda *_: (0,) * len(shape))
 
-    return pl.pallas_call(
+    tables = [a_table, b_table, *tables]
+    table_specs = [fixed(table.shape) for table in tables[:4]]
+    carry = [pltpu.VMEM(table.shape, table.dtype) for table in tables[:4]]
+    carry.append(pltpu.VMEM((1,) + tables[4].shape[1:], tables[4].dtype))
+    if carried:
+        tables, last_spec = [keep(table, pltpu.VMEM) for table in carried], fixed(carry[4].shape)
+    else:
+        tables = [in_hbm(table) for table in tables]
+        last_spec = pl.BlockSpec(carry[4].shape, lambda i, s, _: (s[0], 0, 0, 0, 0))
+    if first_step + per_c // PAIR == steps:
+        carry = []
+    result = pl.pallas_call(
         body,
         grid_spec=pltpu.PrefetchScalarGridSpec(
             num_scalar_prefetch=2,
             grid=(per_c // PAIR,),
             in_specs=[
-                fixed(a_table.shape),
-                fixed(b_table.shape),
-                fixed(tables[0].shape),
-                fixed(tables[1].shape),
-                pl.BlockSpec((1,) + tables[2].shape[1:], lambda i, s, _: (s[0], 0, 0, 0, 0)),
+                *table_specs,
+                last_spec,
                 pl.BlockSpec((wide, narrow, PAIR, rows_x, lanes), lambda i, *_: (0, 0, i, 0, 0)),
                 *[pl.BlockSpec(memory_space=pl.ANY)] * len(filled),
             ],
-            out_specs=[pl.BlockSpec(block, lambda i, *_: (0, 0, first_step + i, 0))] * groups,
+            out_specs=[pl.BlockSpec(block, lambda i, *_: (0, 0, first_step + i, 0))] * groups
+            + [fixed(each.shape) for each in carry],
         ),
-        out_shape=[space(out_shape, jnp.float32) for space in spaces],
+        out_shape=[space(out_shape, jnp.float32) for space in spaces] + carry,
         input_output_aliases={8 + spot: spot for spot in range(len(filled))},
         compiler_params=params(1),
         cost_estimate=cost(per_c * 7 * length**3, 20 * per_c * length**2 * 2),
     )(
         side,
         start_c,
-        *[in_hbm(table) for table in (a_table, b_table, *tables)],
+        *tables,
         received,
         *[keep(each, space) for each, space in zip(filled, spaces)],
     )
+    return result[:groups], result[groups:]
 
 
 def shear_kernel(
-    per_c, group, joined, row_ref, lane_ref, second_ref, third_ref, ahead_ref, last_ref, in_ref, out_ref, shear_ref
+    per_c, group, joined, row_ref, lane_ref, second_ref, third_ref, ahead_ref, last_ref, in_ref, *refs
 ):
+    shear_ref = refs[-1]
+    out_ref, carry_refs = refs[len(refs) // 2 - 1], refs[: len(refs) // 2 - 1]
+    hand_on(carry_refs, refs[len(refs) // 2 : -1])
     step = pl.program_id(0)
     length = shear_ref.shape[0]
     half = length // 2
@@ -413,7 +436,7 @@
                                 out[pl.ds(at, run), :] = piece
 
 
-def shear_pass(received, wide, narrow, per_c, group, joined):
+def shear_pass(received, wide, narrow, per_c, group, joined, carry):
     devices, tiles, message, tile = received.shape
     count = message // per_c
     length = tiles * tile // 6
@@ -469,13 +492,19 @@
             pl.BlockSpec((1, 1, 2 * length), lambda i: (i, 0, 0)),
             *[whole(table.shape) for table in tables],
             pl.BlockSpec((devices, tiles // 3, message, tile), which),
+            *[whole(each.shape) for each in carry],
         ],
-        out_specs=whole(out_shape),
-        out_shape=pltpu.HBM(out_shape, jnp.float32),
+        out_specs=[whole(out_shape)] + [whole(each.shape) for each in carry],
+        out_shape=[pltpu.HBM(out_shape, jnp.float32)]
+        + [pltpu.VMEM(each.shape, each.dtype) for each in carry],
         scratch_shapes=[pltpu.VMEM((length, count * length), jnp.float32)],
         compiler_params=params(1),
         cost_estimate=cost(count * 18 * length**3, 4 * received.size + 4 * 2**20),
-    )(*[in_hbm(value) for value in (row_factor, lane_factor, *tables)], received)
+    )(
+        *[in_hbm(value) for value in (row_factor, lane_factor, *tables)],
+        received,
+        *[in_hbm(each) for each in carry],
+    )
 
 
 def first_kernel(count, rows_b, anchor_ref, table_ref, *refs):
@@ -543,21 +572,24 @@
                     ref[at : at + slots, :, columns] = here.reshape(slots, rows_b, half)
 
 
-def first_pass(parts, is_anchor, length, wide, sides, count):
+def first_table(length, devices, joined, count, sides):
+    scale = 1.0 / float(length) ** 1.5
+    index = np.arange(length).reshape(devices, joined, count, sides)
+    tables = []
+    for join in range(joined):
+        order = index[:, :: 1 - 2 * join].transpose(3, 0, 1, 2).reshape(sides, -1)
+        tables.append(
+            [split_table(scale * turn(-angles(np.arange(length // 2), x, length)).T) for x in order]
+        )
+    return np.stack([np.stack(each) for each in tables])
+
+
+def first_pass(parts, table, is_anchor, length, wide, sides, count):
     devices, rows, lanes = parts[0].shape
     joined = len(parts)
     ranks = devices // wide // sides
     rows_b = length // wide
     slots = lanes // rows_b
-    scale = 1.0 / float(length) ** 1.5
-    index = np.arange(length).reshape(wide * ranks, joined, count, sides)
-    tables = []
-    for join in range(joined):
-        order = index[:, :: 1 - 2 * join].transpose(3, 0, 1, 2).reshape(sides, -1)
-        tables.append(
-            [split_table(scale * turn(-angles(np.arange(length // 2), x, length)).T) for x in order]
-        )
-    table = np.stack([np.stack(each) for each in tables])
     total = rows // (2 * joined * count) if joined == 2 else rows // (2 * count)
     grid = 4 if joined == 2 and total % 4 == 0 else 1
     parts = [part.reshape(wide, sides, ranks, rows, lanes) for part in parts]
@@ -579,7 +611,7 @@
         out_shape=[out_shape] * 2,
         compiler_params=params(1),
         cost_estimate=cost(rows_c * 2 * rows_b * length * length, 16 * rows_c * rows_b * length),
-    )(is_anchor, table, *[keep(part, pltpu.VMEM) for part in parts])
+    )(is_anchor, keep(table, pltpu.VMEM), *[keep(part, pltpu.VMEM) for part in parts])
 
 
 def transpose(value, members=None):
@@ -610,22 +642,24 @@
         side = (spot_narrow // ranks).astype(jnp.int32).reshape(1)
         rank = spot_wide * ranks + spot_narrow % ranks
         start_c = (rank * per_c).astype(jnp.int32).reshape(1)
-        chunks, start = [], 0
+        chunks, carried, start = [], [], 0
         for planes, count in zip(third_pass(density, wide, sides, ranks, counts), counts):
             planes = transpose(planes.reshape(wide * narrow, count, rows_x, 2 * rows_y))
             planes = planes.reshape(wide, narrow, count, rows_x, 2 * rows_y)
             planes = keep(planes, pltpu.VMEM if start else pltpu.HBM)
-            chunks = spectrum_pass(
-                planes, side, start_c, devices, groups, steps, start // PAIR, chunks
+            chunks, carried = spectrum_pass(
+                planes, side, start_c, devices, groups, steps, start // PAIR, chunks, carried
             )
             start += count
         is_anchor = ((spot_wide == 0) & (spot_narrow == 0)).astype(jnp.int32).reshape(1)
         parts = []
+        table = first_table(length, devices, groups, slab // groups, sides)
         for group, chunk in enumerate(chunks):
+            carry = [table] if group == groups - 1 else []
             received = keep(transpose(chunk, members), pltpu.VMEM if group else pltpu.HBM)
-            part = shear_pass(received, wide, narrow, per_c, group, groups)
+            part, *carry = shear_pass(received, wide, narrow, per_c, group, groups, carry)
             parts.append(transpose(part.reshape((wide * narrow,) + part.shape[2:])))
-        return tuple(first_pass(parts, is_anchor, length, wide, sides, slab // groups))
+        return tuple(first_pass(parts, *carry, is_anchor, length, wide, sides, slab // groups))
 
     return jax.shard_map(
         per_device,

time: 315 us -> 313 us (level)
  no operation moved by 1% of the time
where the time goes in v11:
time: 313 us
  waiting for transfers between devices  124 us (40%)
  blocking collectives  118 us (38%)
  Pallas kernels  51.7 us (17%)
  starting transfers between devices  17.3 us (6%)
    all_to_all x4, waiting for transfers between devices, transpose(): lax.all_to_all(value, AXES, split_axis=0, concat_axis=0, tiled=True, axis...  124 us
    all_to_all x2, blocking collectives, transpose(): lax.all_to_all(value, AXES, split_axis=0, concat_axis=0, tiled=True, axis...  118 us
    pallas_call x2, Pallas kernels, shear_pass(): pl.pallas_call(body, grid=(6,), in_specs=[pl.BlockSpec((1, count * half,...  28.5 us
    all_to_all x4, starting transfers between devices, transpose(): lax.all_to_all(value, AXES, split_axis=0, concat_axis=0, tiled=True, axis...  17.3 us
    pallas_call x2, Pallas kernels, spectrum_pass(): pl.pallas_call(body, grid_spec=pltpu.PrefetchScalarGridSpec(num_scalar_pr...  12.5 us
  transfers between devices with their start and end apart: 4, of which 4 were waited for; matrix products, arithmetic and copies ran while one was open for 0% of the time, Pallas kernels for 12%

profile of v11, /device:TPU:1, one launch (start us, length us, event | category | flops | bytes accessed | tf_op | source)
XLA Modules:
  0.0 312.6 jit_solution(15206691741222217733)
XLA Ops:
  0.6 5.0 %shard_map.203 = (f32[8,2,2,6,32,128]{5,4,3,2,1,0:T(8,128)S(1)}, f32[8,2,2,2,32,128]{5,4,3,2,1,0:T(8,128)}) custom-call(bf16[2,256,256]{2,1,0:T(8,128)(2,1)} %constant.64.clone.refs_0_, f32[32,64,256]{2,1,0:T(8,128)} %refs_1_.3), custom_call_target="tpu_custom_call" | custom-call | flops 805306368 | bytes 6291456 | tf_op jit(solution)/shard_map/pallas_call | solution.py:114
  5.6 78.3 %all_to_all.30 = f32[32,6,32,128]{3,2,1,0:T(8,128)} all-to-all(f32[32,6,32,128]{3,2,1,0:T(8,128)S(1)} %bitcast.12), channel_id=1, replica_groups=mesh['wide'=8,'narrow'=4] {'wide','narrow'}, dimensions={0} | all-to-all | bytes 6291456 | tf_op jit(solution)/shard_map/all_to_all | solution.py:618
  83.9 3.2 %all-to-all-start.1 = ((f32[32,2,32,128]{3,2,1,0:T(8,128)}), f32[32,2,32,128]{3,2,1,0:T(8,128)S(1)}, u32[]{:S(2)}, u32[]{:S(2)}) async-start(f32[32,2,32,128]{3,2,1,0:T(8,128)} %bitcast.5), calls=%async_computation.1 | async-start | bytes 2097152 | tf_op jit(solution)/shard_map/all_to_all | solution.py:618
  87.1 9.3 %shard_map.204 = (f32[16,12,32,128]{3,2,1,0:T(8,128)}, f32[16,12,32,128]{3,2,1,0:T(8,128)}, f32[3,2,128,1]{3,2,1,0:T(8,128)S(1)}, f32[2,1,256]{2,1,0:T(1,128)S(1...) custom-call(s32[1]{0:T(128)} %bitcast.1.refs_0_, ...), custom_call_target="tpu_custom_call" | custom-call | flops 4227858432 | bytes 15728640 | tf_op jit(solution)/shard_map/pallas_call | solution.py:308
  96.4 17.1 %all-to-all-done.1 = f32[32,2,32,128]{3,2,1,0:T(8,128)S(1)} async-done(((f32[32,2,32,128]{3,2,1,0:T(8,128)}), f32[32,2,32,128]{3,2,1,0:T(8,128)S(1)}, u32[]{:S(2)}, u32[]{:S(2)}) %all-to-all-start.1) | async-done | bytes 1048608 | tf_op jit(solution)/shard_map/all_to_all | solution.py:618
  113.4 3.2 %shard_map.205 = (f32[16,12,32,128]{3,2,1,0:T(8,128)}, f32[16,12,32,128]{3,2,1,0:T(8,128)}) custom-call(s32[1]{0:T(128)} %bitcast.1.refs_0_, s32[1]{0:T(128)} %bitcast.2.refs_1_, f32[3,2,128,1]{3,2,1,0:T(8,128)S(1)} %get-tuple-element.16.refs_2_, f32[2,1,256]{2,1,0:T(1,128)S(1)} %get-tuple-element.17.refs_3_, ...), custom_call_target="tpu_custom_call", output_to_operand_aliasing={{0}: (8, {}), {1}: (9, {})} | custom-call | flops 1409286144 | bytes 5242880 | tf_op jit(solution)/shard_map/pallas_call | solution.py:308
  116.6 40.1 %all_to_all.31.refs_6_ = f32[16,12,32,128]{3,2,1,0:T(8,128)S(1)} all-to-all(f32[16,12,32,128]{3,2,1,0:T(8,128)} %get-tuple-element.24), channel_id=1, replica_groups={{0,1,4,5,8,9,12,13,16,17,20,21,24,25,28,29},{2,3,6,7,10,11,14,15,18,19,..., dimensions={0} | all-to-all | bytes 6291456 | tf_op jit(solution)/shard_map/all_to_all | solution.py:618
  156.8 4.4 %all-to-all-start.3 = ((f32[16,12,32,128]{3,2,1,0:T(8,128)}), f32[16,12,32,128]{3,2,1,0:T(8,128)}, u32[]{:S(2)}, u32[]{:S(2)}) async-start(f32[16,12,32,128]{3,2,1,0:T(8,128)} %get-tuple-element.26), calls=%async_computation.3 | async-start | bytes 6291456 | tf_op jit(solution)/shard_map/all_to_all | solution.py:618
  161.1 14.3 %shard_map.206 = (f32[8,4,128,128]{3,2,1,0:T(8,128)}, bf16[2,2,2,256,256]{4,3,2,1,0:T(8,128)(2,1)S(1)}) custom-call(f32[6,512,1]{2,1,0:T(8,128)} %constant.75.clone.refs_0_, f32[6,1,512]{2,1,0:T(1,128)} %constant.71.clone.refs_1_, bf16[2,2,256,256]{3,2,1,0:T(8,128)(2,1)} %constant.68.clone.refs_5_.refs_2_, bf16[2,256,256]{2,1,0:T(8,128)(2,1)} %constant.76.clone.refs_3_, ...), custom_call_target="tpu_custom_call" | custom-call | flops 7247757312 | bytes 7340032 | tf_op jit(solution)/shard_map/pallas_call | solution.py:487
  175.4 0.0 copy-start
  175.4 1.0 copy-done
  176.4 24.2 %all-to-all-done.3.refs_6_ = f32[16,12,32,128]{3,2,1,0:T(8,128)} async-done(((f32[16,12,32,128]{3,2,1,0:T(8,128)}), f32[16,12,32,128]{3,2,1,0:T(8,128)}, u32[]{:S(2)}, u32[]{:S(2)}) %all-to-all-start.3) | async-done | bytes 3145760 | tf_op jit(solution)/shard_map/all_to_all | solution.py:618
  200.6 6.3 %all-to-all-start.5 = ((f32[32,128,128]{2,1,0:T(8,128)}), f32[32,128,128]{2,1,0:T(8,128)S(1)}, u32[]{:S(2)}, u32[]{:S(2)}) async-start(f32[32,128,128]{2,1,0:T(8,128)} %bitcast.16), calls=%async_computation.5 | async-start | bytes 4194304 | tf_op jit(solution)/shard_map/all_to_all | solution.py:618
  206.9 14.2 %shard_map.207 = f32[8,4,128,128]{3,2,1,0:T(8,128)} custom-call(f32[6,512,1]{2,1,0:T(8,128)} %constant.70.clone.refs_0_, f32[6,1,512]{2,1,0:T(1,128)} %constant.71.clone.refs_1_, bf16[2,2,256,256]{3,2,1,0:T(8,128)(2,1)} %constant.68.clone.refs_5_.refs_2_, bf16[2,256,256]{2,1,0:T(8,128)(2,1)} %constant.72.clone.refs_3_, ...), custom_call_target="tpu_custom_call" | custom-call | flops 7247757312 | bytes 7340032 | tf_op jit(solution)/shard_map/pallas_call | solution.py:487
  221.2 34.0 %all-to-all-done.5 = f32[32,128,128]{2,1,0:T(8,128)S(1)} async-done(((f32[32,128,128]{2,1,0:T(8,128)}), f32[32,128,128]{2,1,0:T(8,128)S(1)}, u32[]{:S(2)}, u32[]{:S(2)}) %all-to-all-start.5) | async-done | bytes 2097184 | tf_op jit(solution)/shard_map/all_to_all | solution.py:618
  255.2 0.0 copy-start.1
  255.2 3.5 %all-to-all-start.4 = ((f32[32,128,128]{2,1,0:T(8,128)}), f32[32,128,128]{2,1,0:T(8,128)}, u32[]{:S(2)}, u32[]{:S(2)}) async-start(f32[32,128,128]{2,1,0:T(8,128)} %bitcast.15), calls=%async_computation.4 | async-start | bytes 4194304 | tf_op jit(solution)/shard_map/all_to_all | solution.py:618
  258.7 48.3 %all-to-all-done.4 = f32[32,128,128]{2,1,0:T(8,128)} async-done(((f32[32,128,128]{2,1,0:T(8,128)}), f32[32,128,128]{2,1,0:T(8,128)}, u32[]{:S(2)}, u32[]{:S(2)}) %all-to-all-start.4) | async-done | bytes 2097184 | tf_op jit(solution)/shard_map/all_to_all | solution.py:618
  306.9 0.0 copy-done.1
  306.9 5.7 %shard_map.208 = (f32[64,32,256]{2,1,0:T(8,128)}, f32[64,32,256]{2,1,0:T(8,128)}) custom-call(s32[1]{0:T(128)} %bitcast.refs_0_, bf16[2,2,2,256,256]{4,3,2,1,0:T(8,128)(2,1)S(1)} %copy-done.1, f32[8,2,2,128,128]{4,3,2,1,0:T(8,128)} %bitcast.8.refs_2_, f32[8,2,2,128,128]{4,3,2,1,0:T(8,128)S(1)} %bitcast.13), custom_call_target="tpu_custom_call" | custom-call | flops 1610612736 | bytes 8388608 | tf_op jit(solution)/shard_map/pallas_call | solution.py:602
Async XLA Ops:
  83.9 29.5 %all-to-all-start.1 = ((f32[32,2,32,128]{3,2,1,0:T(8,128)}), f32[32,2,32,128]{3,2,1,0:T(8,128)S(1)}, u32[]{:S(2)}, u32[]{:S(2)}) async-start(f32[32,2,32,128]{3,2,1,0:T(8,128)} %bitcast.5), calls=%async_computation.1 | async-start | bytes 2097152 | tf_op jit(solution)/shard_map/all_to_all | solution.py:618
  156.8 43.8 %all-to-all-start.3 = ((f32[16,12,32,128]{3,2,1,0:T(8,128)}), f32[16,12,32,128]{3,2,1,0:T(8,128)}, u32[]{:S(2)}, u32[]{:S(2)}) async-start(f32[16,12,32,128]{3,2,1,0:T(8,128)} %get-tuple-element.26), calls=%async_computation.3 | async-start | bytes 6291456 | tf_op jit(solution)/shard_map/all_to_all | solution.py:618
  175.4 1.0 copy-start
  200.6 54.6 %all-to-all-start.5 = ((f32[32,128,128]{2,1,0:T(8,128)}), f32[32,128,128]{2,1,0:T(8,128)S(1)}, u32[]{:S(2)}, u32[]{:S(2)}) async-start(f32[32,128,128]{2,1,0:T(8,128)} %bitcast.16), calls=%async_computation.5 | async-start | bytes 4194304 | tf_op jit(solution)/shard_map/all_to_all | solution.py:618
  255.2 51.8 %copy-start.1 = (bf16[2,2,2,256,256]{4,3,2,1,0:T(8,128)(2,1)S(1)}, bf16[2,2,2,256,256]{4,3,2,1,0:T(8,128)(2,1)}, u32[]{:S(2)}) copy-start(bf16[2,2,2,256,256]{4,3,2,1,0:T(8,128)(2,1)} %copy-done) | copy-start | bytes 3145732
  255.2 51.8 %all-to-all-start.4 = ((f32[32,128,128]{2,1,0:T(8,128)}), f32[32,128,128]{2,1,0:T(8,128)}, u32[]{:S(2)}, u32[]{:S(2)}) async-start(f32[32,128,128]{2,1,0:T(8,128)} %bitcast.15), calls=%async_computation.4 | async-start | bytes 4194304 | tf_op jit(solution)/shard_map/all_to_all | solution.py:618

commit v12 on v11

--- a/solution.py
+++ b/solution.py
@@ -507,30 +507,54 @@
     )
 
 
-def first_kernel(count, rows_b, anchor_ref, table_ref, *refs):
+def turned_tile(ref, side, at):
+    wide, _, ranks, _, lanes = ref.shape
+    return ref[:, side, :, at].reshape(wide * ranks * at.size, lanes).T
+
+
+def turned_kernel(in_ref, out_ref):
+    sides, tiles, size, _ = out_ref.shape
+    message = in_ref.shape[3] // tiles
+    for side in range(sides):
+        for tile in range(tiles):
+            out_ref[side, tile] = turned_tile(in_ref, side, pl.ds(tile * message, message))
+
+
+def turned_pass(part, wide, sides, message):
+    devices, rows, lanes = part.shape
+    part = part.reshape(wide, sides, devices // wide // sides, rows, lanes)
+    out_shape = (sides, rows // message, lanes, devices // sides * message)
+    return pl.pallas_call(
+        turned_kernel,
+        grid=(1,),
+        in_specs=[whole(part.shape)],
+        out_specs=whole(out_shape),
+        out_shape=pltpu.VMEM(out_shape, jnp.float32),
+        compiler_params=params(1),
+        cost_estimate=cost(0, 8 * part.size),
+    )(keep(part, pltpu.VMEM))
+
+
+def first_kernel(count, rows_b, joined, anchor_ref, table_ref, *refs):
     ins, (real_ref, imag_ref) = refs[:-2], refs[-2:]
-    wide, sides, ranks, rows, lanes = ins[0].shape
+    wide, sides, ranks, rows, lanes = ins[-1].shape
     length = real_ref.shape[2]
     half = length // 2
     slots = lanes // rows_b
-    joined = len(ins)
     steps = real_ref.shape[0] // (slots * joined)
     spot_row = lax.broadcasted_iota(jnp.int32, (lanes, half), 0)
     spot_a = lax.broadcasted_iota(jnp.int32, (lanes, half), 1)
     is_anchor = (anchor_ref[0] == 1) & (pl.program_id(0) == 0)
     start = pl.program_id(0) * steps
     anchor = (spot_row == 0) & (spot_a == 0) & is_anchor
-    upper = lax.broadcasted_iota(jnp.int32, (wide * ranks, joined * count, lanes), 1) < count
+    upper = lax.broadcasted_iota(jnp.int32, (lanes, half), 1) % (2 * count) < count
 
     def gathered(side, step, part):
         if joined == 2:
-            at = ((start + step) * 2 + part) * 2 * count
-            at = pl.ds(pl.multiple_of(at, 2 * count), 2 * count)
-            own, other = [
-                ref[:, side, :, at].reshape(wide * ranks, 2 * count, lanes) for ref in ins
-            ]
-            both = [jnp.where(upper, own, other), jnp.where(upper, other, own)]
-            return [value.reshape(half, lanes).T for value in both]
+            tile = (start + step) * 2 + part
+            at = pl.ds(pl.multiple_of(tile * 2 * count, 2 * count), 2 * count)
+            own, other = ins[0][side, tile], turned_tile(ins[1], side, at)
+            return [jnp.where(upper, own, other), jnp.where(upper, other, own)]
         flat = ins[0].reshape(wide * sides * ranks * rows, lanes)
         run = rows // count
         value = jnp.concatenate(
@@ -590,12 +614,13 @@
     ranks = devices // wide // sides
     rows_b = length // wide
     slots = lanes // rows_b
+    turned = [turned_pass(parts[0], wide, sides, 2 * count)] if joined == 2 else []
     total = rows // (2 * joined * count) if joined == 2 else rows // (2 * count)
     grid = 4 if joined == 2 and total % 4 == 0 else 1
-    parts = [part.reshape(wide, sides, ranks, rows, lanes) for part in parts]
+    parts = turned + [parts[-1].reshape(wide, sides, ranks, rows, lanes)]
 
     def body(*refs):
-        first_kernel(count, rows_b, *refs)
+        first_kernel(count, rows_b, joined, *refs)
 
     rows_c = total * joined * slots
     out_shape = jax.ShapeDtypeStruct((rows_c, rows_b, length), jnp.float32)
@@ -605,7 +630,7 @@
         in_specs=[
             pl.BlockSpec(memory_space=pltpu.SMEM),
             whole(table.shape),
-            *[whole((wide, sides, ranks, rows, lanes))] * joined,
+            *[whole(part.shape) for part in parts],
         ],
         out_specs=[pl.BlockSpec((rows_c // grid, rows_b, length), lambda i: (i, 0, 0))] * 2,
         out_shape=[out_shape] * 2,

time: 313 us -> 320 us (1.022)
  local copies, waits for them, and re-layouts: 1 us -> 11.9 us
  waiting for transfers between devices: 124 us -> 118 us
    unnamed x4 -> x20, local copies, waits for them, and re-layouts: 1 us -> 11.9 us
    all_to_all x4, waiting for transfers between devices: 124 us -> 118 us  [transpose(): lax.all_to_all(value, AXES, split_axis=0, concat_axis=0, tiled=True, axis...]
where the time goes in v12:
time: 320 us; the launch traced here: 319 us
  blocking collectives  118 us (37%)
  waiting for transfers between devices  118 us (37%)
  Pallas kernels  53.2 us (17%)
  starting transfers between devices  16.8 us (5%)
  local copies, waits for them, and re-layouts  11.9 us (4%)
    all_to_all x4, waiting for transfers between devices, transpose(): lax.all_to_all(value, AXES, split_axis=0, concat_axis=0, tiled=True, axis...  118 us
    all_to_all x2, blocking collectives, transpose(): lax.all_to_all(value, AXES, split_axis=0, concat_axis=0, tiled=True, axis...  118 us
    pallas_call x2, Pallas kernels, shear_pass(): pl.pallas_call(body, grid=(6,), in_specs=[pl.BlockSpec((1, count * half,...  28.5 us
    all_to_all x4, starting transfers between devices, transpose(): lax.all_to_all(value, AXES, split_axis=0, concat_axis=0, tiled=True, axis...  16.8 us
    pallas_call x2, Pallas kernels, spectrum_pass(): pl.pallas_call(body, grid_spec=pltpu.PrefetchScalarGridSpec(num_scalar_pr...  13.4 us
    unnamed x20, local copies, waits for them, and re-layouts  11.9 us
  transfers between devices with their start and end apart: 4, of which 4 were waited for; matrix products, arithmetic and copies ran while one was open for 0% of the time, Pallas kernels for 12%

profile of v12, /device:TPU:1, one launch (start us, length us, event | category | flops | bytes accessed | tf_op | source)
XLA Modules:
  0.0 319.2 jit_solution(3559021084716224212)
XLA Ops:
  0.6 5.0 %shard_map.203 = (f32[8,2,2,6,32,128]{5,4,3,2,1,0:T(8,128)S(1)}, f32[8,2,2,2,32,128]{5,4,3,2,1,0:T(8,128)}) custom-call(bf16[2,256,256]{2,1,0:T(8,128)(2,1)} %constant.64.clone.refs_0_, f32[32,64,256]{2,1,0:T(8,128)} %refs_1_.3), custom_call_target="tpu_custom_call" | custom-call | flops 805306368 | bytes 6291456 | tf_op jit(solution)/shard_map/pallas_call | solution.py:114
  5.6 78.3 %all_to_all.30 = f32[32,6,32,128]{3,2,1,0:T(8,128)} all-to-all(f32[32,6,32,128]{3,2,1,0:T(8,128)S(1)} %bitcast.12), channel_id=1, replica_groups=mesh['wide'=8,'narrow'=4] {'wide','narrow'}, dimensions={0} | all-to-all | bytes 6291456 | tf_op jit(solution)/shard_map/all_to_all | solution.py:643
  83.9 3.2 %all-to-all-start.1 = ((f32[32,2,32,128]{3,2,1,0:T(8,128)}), f32[32,2,32,128]{3,2,1,0:T(8,128)}, u32[]{:S(2)}, u32[]{:S(2)}) async-start(f32[32,2,32,128]{3,2,1,0:T(8,128)} %bitcast.5), calls=%async_computation.1 | async-start | bytes 2097152 | tf_op jit(solution)/shard_map/all_to_all | solution.py:643
  87.2 9.3 %shard_map.204 = (f32[16,12,32,128]{3,2,1,0:T(8,128)S(1)}, f32[16,12,32,128]{3,2,1,0:T(8,128)}, f32[3,2,128,1]{3,2,1,0:T(8,128)S(1)}, f32[2,1,256]{2,1,0:T(1,128...) custom-call(s32[1]{0:T(128)} %bitcast.1.refs_0_, ...), custom_call_target="tpu_custom_call" | custom-call | flops 4227858432 | bytes 15728640 | tf_op jit(solution)/shard_map/pallas_call | solution.py:308
  96.4 0.0 copy-start.4
  96.4 0.8 copy-done.4
  97.2 0.0 copy-start.6
  97.2 0.8 copy-done.6
  98.0 0.0 copy-start.8
  98.0 0.8 copy-done.8
  98.8 14.8 %all-to-all-done.1 = f32[32,2,32,128]{3,2,1,0:T(8,128)} async-done(((f32[32,2,32,128]{3,2,1,0:T(8,128)}), f32[32,2,32,128]{3,2,1,0:T(8,128)}, u32[]{:S(2)}, u32[]{:S(2)}) %all-to-all-start.1) | async-done | bytes 1048608 | tf_op jit(solution)/shard_map/all_to_all | solution.py:643
  113.5 0.0 copy-start.5
  113.5 1.0 copy-done.5
  114.6 0.0 copy-start.7
  114.6 1.0 copy-done.7
  115.6 0.0 copy-start.9
  115.6 1.0 copy-done.9
  116.7 4.2 %shard_map.205 = (f32[16,12,32,128]{3,2,1,0:T(8,128)S(1)}, f32[16,12,32,128]{3,2,1,0:T(8,128)}) custom-call(s32[1]{0:T(128)} %bitcast.1.refs_0_, s32[1]{0:T(128)} %bitcast.2.refs_1_, f32[3,2,128,1]{3,2,1,0:T(8,128)S(1)} %get-tuple-element.16.refs_2_, f32[2,1,256]{2,1,0:T(1,128)S(1)} %get-tuple-element.17.refs_3_, ...), custom_call_target="tpu_custom_call", output_to_operand_aliasing={{0}: (8, {}), {1}: (9, {})} | custom-call | flops 1409286144 | bytes 5242880 | tf_op jit(solution)/shard_map/pallas_call | solution.py:308
  120.8 40.0 %all_to_all.31.refs_6_ = f32[16,12,32,128]{3,2,1,0:T(8,128)} all-to-all(f32[16,12,32,128]{3,2,1,0:T(8,128)S(1)} %get-tuple-element.26), channel_id=1, replica_groups={{0,1,4,5,8,9,12,13,16,17,20,21,24,25,28,29},{2,3,6,7,10,11,14,15,18,19,..., dimensions={0} | all-to-all | bytes 6291456 | tf_op jit(solution)/shard_map/all_to_all | solution.py:643
  160.9 3.8 %all-to-all-start.2 = ((f32[16,12,32,128]{3,2,1,0:T(8,128)}), f32[16,12,32,128]{3,2,1,0:T(8,128)S(1)}, u32[]{:S(2)}, u32[]{:S(2)}) async-start(f32[16,12,32,128]{3,2,1,0:T(8,128)} %get-tuple-element.24), calls=%async_computation.2 | async-start | bytes 6291456 | tf_op jit(solution)/shard_map/all_to_all | solution.py:643
  164.7 14.2 %shard_map.207 = f32[8,4,128,128]{3,2,1,0:T(8,128)} custom-call(f32[6,512,1]{2,1,0:T(8,128)} %constant.70.clone.refs_0_, f32[6,1,512]{2,1,0:T(1,128)} %constant.71.clone.refs_1_, bf16[2,2,256,256]{3,2,1,0:T(8,128)(2,1)} %constant.68.clone.refs_5_.refs_2_, bf16[2,256,256]{2,1,0:T(8,128)(2,1)} %constant.72.clone.refs_3_, ...), custom_call_target="tpu_custom_call" | custom-call | flops 7247757312 | bytes 7340032 | tf_op jit(solution)/shard_map/pallas_call | solution.py:487
  178.9 25.1 %all-to-all-done.2.refs_6_ = f32[16,12,32,128]{3,2,1,0:T(8,128)S(1)} async-done(((f32[16,12,32,128]{3,2,1,0:T(8,128)}), f32[16,12,32,128]{3,2,1,0:T(8,128)S(1)}, u32[]{:S(2)}, u32[]{:S(2)}) %all-to-all-start.2) | async-done | bytes 3145760 | tf_op jit(solution)/shard_map/all_to_all | solution.py:643
  204.0 0.0 copy-start
  204.0 1.6 copy-done
  205.7 6.3 %all-to-all-start.4 = ((f32[32,128,128]{2,1,0:T(8,128)}), f32[32,128,128]{2,1,0:T(8,128)S(1)}, u32[]{:S(2)}, u32[]{:S(2)}) async-start(f32[32,128,128]{2,1,0:T(8,128)} %bitcast.15), calls=%async_computation.4 | async-start | bytes 4194304 | tf_op jit(solution)/shard_map/all_to_all | solution.py:643
  212.0 0.0 copy-start.1
  212.0 1.9 copy-done.1
  213.9 14.2 %shard_map.206 = (f32[8,4,128,128]{3,2,1,0:T(8,128)}, bf16[2,2,2,256,256]{4,3,2,1,0:T(8,128)(2,1)S(1)}) custom-call(f32[6,512,1]{2,1,0:T(8,128)} %constant.75.clone.refs_0_, f32[6,1,512]{2,1,0:T(1,128)} %constant.71.clone.refs_1_, bf16[2,2,256,256]{3,2,1,0:T(8,128)(2,1)} %constant.68.clone.refs_5_.refs_2_, bf16[2,256,256]{2,1,0:T(8,128)(2,1)} %constant.76.clone.refs_3_, ...), custom_call_target="tpu_custom_call" | custom-call | flops 7247757312 | bytes 7340032 | tf_op jit(solution)/shard_map/pallas_call | solution.py:487
  228.1 32.1 %all-to-all-done.4 = f32[32,128,128]{2,1,0:T(8,128)S(1)} async-done(((f32[32,128,128]{2,1,0:T(8,128)}), f32[32,128,128]{2,1,0:T(8,128)S(1)}, u32[]{:S(2)}, u32[]{:S(2)}) %all-to-all-start.4) | async-done | bytes 2097184 | tf_op jit(solution)/shard_map/all_to_all | solution.py:643
  260.2 3.5 %all-to-all-start.5 = ((f32[32,128,128]{2,1,0:T(8,128)}), f32[32,128,128]{2,1,0:T(8,128)}, u32[]{:S(2)}, u32[]{:S(2)}) async-start(f32[32,128,128]{2,1,0:T(8,128)} %bitcast.14), calls=%async_computation.5 | async-start | bytes 4194304 | tf_op jit(solution)/shard_map/all_to_all | solution.py:643
  263.7 0.6 shard_map.208.refs_2_
  264.3 0.0 copy-start.2
  264.3 1.3 copy-done.2
  265.6 46.4 %all-to-all-done.5 = f32[32,128,128]{2,1,0:T(8,128)} async-done(((f32[32,128,128]{2,1,0:T(8,128)}), f32[32,128,128]{2,1,0:T(8,128)}, u32[]{:S(2)}, u32[]{:S(2)}) %all-to-all-start.5) | async-done | bytes 2097184 | tf_op jit(solution)/shard_map/all_to_all | solution.py:643
  312.0 0.0 copy-start.3
  312.0 1.6 copy-done.3
  313.6 5.7 %shard_map.209 = (f32[64,32,256]{2,1,0:T(8,128)}, f32[64,32,256]{2,1,0:T(8,128)}) custom-call(s32[1]{0:T(128)} %bitcast.refs_0_, bf16[2,2,2,256,256]{4,3,2,1,0:T(8,128)(2,1)S(1)} %get-tuple-element.25.refs_1_, f32[2,16,128,128]{3,2,1,0:T(8,128)S(1)} %copy-done.3, f32[8,2,2,128,128]{4,3,2,1,0:T(8,128)} %bitcast.10.refs_3_), custom_call_target="tpu_custom_call" | custom-call | flops 1610612736 | bytes 8388608 | tf_op jit(solution)/shard_map/pallas_call | solution.py:627
Async XLA Ops:
  83.9 29.6 %all-to-all-start.1 = ((f32[32,2,32,128]{3,2,1,0:T(8,128)}), f32[32,2,32,128]{3,2,1,0:T(8,128)}, u32[]{:S(2)}, u32[]{:S(2)}) async-start(f32[32,2,32,128]{3,2,1,0:T(8,128)} %bitcast.5), calls=%async_computation.1 | async-start | bytes 2097152 | tf_op jit(solution)/shard_map/all_to_all | solution.py:643
  96.4 0.8 copy-start.4
  97.2 0.8 copy-start.6
  98.0 0.8 copy-start.8
  113.5 1.0 copy-start.5
  114.6 1.0 copy-start.7
  115.6 1.0 copy-start.9
  160.9 43.2 %all-to-all-start.2 = ((f32[16,12,32,128]{3,2,1,0:T(8,128)}), f32[16,12,32,128]{3,2,1,0:T(8,128)S(1)}, u32[]{:S(2)}, u32[]{:S(2)}) async-start(f32[16,12,32,128]{3,2,1,0:T(8,128)} %get-tuple-element.24), calls=%async_computation.2 | async-start | bytes 6291456 | tf_op jit(solution)/shard_map/all_to_all | solution.py:643
  204.0 1.6 copy-start
  205.7 54.5 %all-to-all-start.4 = ((f32[32,128,128]{2,1,0:T(8,128)}), f32[32,128,128]{2,1,0:T(8,128)S(1)}, u32[]{:S(2)}, u32[]{:S(2)}) async-start(f32[32,128,128]{2,1,0:T(8,128)} %bitcast.15), calls=%async_computation.4 | async-start | bytes 4194304 | tf_op jit(solution)/shard_map/all_to_all | solution.py:643
  212.0 1.9 copy-start.1
  260.2 51.8 %all-to-all-start.5 = ((f32[32,128,128]{2,1,0:T(8,128)}), f32[32,128,128]{2,1,0:T(8,128)}, u32[]{:S(2)}, u32[]{:S(2)}) async-start(f32[32,128,128]{2,1,0:T(8,128)} %bitcast.14), calls=%async_computation.5 | async-start | bytes 4194304 | tf_op jit(solution)/shard_map/all_to_all | solution.py:643
  264.3 1.3 copy-start.2
  312.0 1.6 copy-start.3

commit v13 on v11

--- a/solution.py
+++ b/solution.py
@@ -334,11 +334,23 @@
 
 
 def shear_kernel(
-    per_c, group, joined, row_ref, lane_ref, second_ref, third_ref, ahead_ref, last_ref, in_ref, *refs
+    per_c,
+    group,
+    joined,
+    own_first,
+    _,
+    row_ref,
+    lane_ref,
+    second_ref,
+    third_ref,
+    ahead_ref,
+    last_ref,
+    in_ref,
+    *refs,
 ):
-    shear_ref = refs[-1]
-    out_ref, carry_refs = refs[len(refs) // 2 - 1], refs[: len(refs) // 2 - 1]
-    hand_on(carry_refs, refs[len(refs) // 2 : -1])
+    outs, shear_ref = refs[:-1], refs[-1]
+    if not own_first:
+        outs = outs[-1:]
     step = pl.program_id(0)
     length = shear_ref.shape[0]
     half = length // 2
@@ -404,13 +416,14 @@
             ],
             axis=0,
         )
-        value = product(pair(last_ref), split(ahead))
-        wide, narrow, message_out, _ = out_ref.shape
+        value = product(pair(last_ref.at[0]), split(ahead))
+        wide, ranks, message_out, _ = outs[0].shape
+        narrow = 2 * ranks if own_first else ranks
         rows_b = length // wide
         slots = tile // rows_b
         rows = 2 * length // slots
         run = rows // (2 * narrow * joined)
-        out = out_ref.reshape(wide * narrow * message_out, tile)
+        flats = [ref.reshape(wide * ranks * message_out, tile) for ref in outs]
         lane = lax.broadcasted_iota(jnp.int32, (rows, tile), 1) // rows_b
         for x in range(count):
             for w in range(wide):
@@ -427,16 +440,20 @@
                         for join in range(joined):
                             start = ((n * 2 + part) * joined + join) * run
                             piece = moved[start : start + run]
-                            at = (w * narrow + n) * message_out
-                            if joined == 2:
+                            at = (w * ranks + n % ranks) * message_out
+                            if own_first:
+                                flat = flats[n // ranks * 2 + part]
+                                at += (join ^ group) * count + x
+                                flat[pl.ds(at, run, stride=2 * count), :] = piece
+                            elif joined == 2:
                                 at += part * 2 * count + (join ^ group) * count + x
-                                out[pl.ds(at, run, stride=4 * count), :] = piece
+                                flats[0][pl.ds(at, run, stride=4 * count), :] = piece
                             else:
                                 at += (x * 2 + part) * run
-                                out[pl.ds(at, run), :] = piece
-
-
-def shear_pass(received, wide, narrow, per_c, group, joined, carry):
+                                flats[0][pl.ds(at, run), :] = piece
+
+
+def shear_pass(received, side, wide, narrow, per_c, group, joined, after):
     devices, tiles, message, tile = received.shape
     count = message // per_c
     length = tiles * tile // 6
@@ -463,7 +480,13 @@
         ]
     )
     last = last.reshape(2, slots, narrow, -1, 2 * length).transpose(1, 2, 0, 3, 4)
-    last = last.reshape(2 * length, 2 * length)
+    own_first = joined == 2 and group == 0
+    last = np.stack(
+        [
+            split_table(np.roll(last, -own, axis=1).reshape(2 * length, 2 * length))
+            for own in ((0, narrow // 2) if own_first else (0,))
+        ]
+    )
     wave = signed_wave(index, length)
     wave_rows = np.tile(wave[row_c], count)
     wave_lanes = np.stack([wave[split_index]] * 2, axis=1).reshape(-1)
@@ -475,45 +498,55 @@
     lane_factor = np.stack(
         [one_lane, wave_lanes, one_lane, wave_lanes**2, wave_lanes, one_lane]
     ).astype(np.float32)[:, None, :]
-    tables = [second] + [split_table(table) for table in (third, ahead, last)]
-    out_shape = (wide, narrow, count * 2 * length // (narrow * slots), TILE)
+    tables = [second, split_table(third), split_table(ahead)]
+    rows_out = count * 2 * length // (narrow * slots)
+    if own_first:
+        out_shapes = [(wide, narrow // 2, rows_out // 2, TILE)] * 4
+    else:
+        out_shapes = [(wide, narrow, rows_out, TILE)]
 
     def body(*refs):
-        shear_kernel(per_c, group, joined, *refs)
-
-    def which(i):
+        shear_kernel(per_c, group, joined, own_first, *refs)
+
+    def which(i, _):
         return (0, 2 - (i >= 1).astype(jnp.int32) - (i >= 3).astype(jnp.int32), 0, 0)
+
+    def own_table(i, s):
+        return (s[0] if own_first else 0, 0, 0, 0)
 
     return pl.pallas_call(
         body,
-        grid=(6,),
-        in_specs=[
-            pl.BlockSpec((1, count * half, 1), lambda i: (i, 0, 0)),
-            pl.BlockSpec((1, 1, 2 * length), lambda i: (i, 0, 0)),
-            *[whole(table.shape) for table in tables],
-            pl.BlockSpec((devices, tiles // 3, message, tile), which),
-            *[whole(each.shape) for each in carry],
-        ],
-        out_specs=[whole(out_shape)] + [whole(each.shape) for each in carry],
-        out_shape=[pltpu.HBM(out_shape, jnp.float32)]
-        + [pltpu.VMEM(each.shape, each.dtype) for each in carry],
-        scratch_shapes=[pltpu.VMEM((length, count * length), jnp.float32)],
+        grid_spec=pltpu.PrefetchScalarGridSpec(
+            num_scalar_prefetch=1,
+            grid=(6,),
+            in_specs=[
+                pl.BlockSpec((1, count * half, 1), lambda i, _: (i, 0, 0)),
+                pl.BlockSpec((1, 1, 2 * length), lambda i, _: (i, 0, 0)),
+                *[whole(table.shape) for table in tables],
+                pl.BlockSpec((1,) + last.shape[1:], own_table),
+                pl.BlockSpec((devices, tiles // 3, message, tile), which),
+                *[pl.BlockSpec(memory_space=pl.ANY)] * len(after),
+            ],
+            out_specs=[whole(out_shape) for out_shape in out_shapes],
+            scratch_shapes=[pltpu.VMEM((length, count * length), jnp.float32)],
+        ),
+        out_shape=[pltpu.HBM(out_shape, jnp.float32) for out_shape in out_shapes],
         compiler_params=params(1),
         cost_estimate=cost(count * 18 * length**3, 4 * received.size + 4 * 2**20),
     )(
-        *[in_hbm(value) for value in (row_factor, lane_factor, *tables)],
+        side,
+        *[in_hbm(value) for value in (row_factor, lane_factor, *tables, last)],
         received,
-        *[in_hbm(each) for each in carry],
-    )
-
-
-def first_kernel(count, rows_b, anchor_ref, table_ref, *refs):
+        *[in_hbm(each) for each in after],
+    )
+
+
+def first_kernel(count, rows_b, joined, own_ref, anchor_ref, table_ref, *refs):
     ins, (real_ref, imag_ref) = refs[:-2], refs[-2:]
-    wide, sides, ranks, rows, lanes = ins[0].shape
+    wide, sides, ranks, rows, lanes = ins[-1].shape
     length = real_ref.shape[2]
     half = length // 2
     slots = lanes // rows_b
-    joined = len(ins)
     steps = real_ref.shape[0] // (slots * joined)
     spot_row = lax.broadcasted_iota(jnp.int32, (lanes, half), 0)
     spot_a = lax.broadcasted_iota(jnp.int32, (lanes, half), 1)
@@ -524,10 +557,13 @@
 
     def gathered(side, step, part):
         if joined == 2:
-            at = ((start + step) * 2 + part) * 2 * count
-            at = pl.ds(pl.multiple_of(at, 2 * count), 2 * count)
+            at = (start + step) * 2 * count
+            near = pl.ds(pl.multiple_of(at, 2 * count), 2 * count)
+            far = pl.ds(pl.multiple_of(2 * at + part * 2 * count, 2 * count), 2 * count)
+            arrived = own_ref[0] ^ side
             own, other = [
-                ref[:, side, :, at].reshape(wide * ranks, 2 * count, lanes) for ref in ins
+                value.reshape(wide * ranks, 2 * count, lanes)
+                for value in (ins[part][:, :, arrived, near], ins[2][:, side, :, far])
             ]
             both = [jnp.where(upper, own, other), jnp.where(upper, other, own)]
             return [value.reshape(half, lanes).T for value in both]
@@ -584,18 +620,20 @@
     return np.stack([np.stack(each) for each in tables])
 
 
-def first_pass(parts, table, is_anchor, length, wide, sides, count):
-    devices, rows, lanes = parts[0].shape
-    joined = len(parts)
+def first_pass(parts, table, side, is_anchor, length, wide, sides, count):
+    devices, rows, lanes = parts[-1].shape
+    joined = min(2, len(parts))
     ranks = devices // wide // sides
     rows_b = length // wide
     slots = lanes // rows_b
     total = rows // (2 * joined * count) if joined == 2 else rows // (2 * count)
     grid = 4 if joined == 2 and total % 4 == 0 else 1
-    parts = [part.reshape(wide, sides, ranks, rows, lanes) for part in parts]
+    parts = [part.reshape(wide, ranks, 2, rows // 2, lanes) for part in parts[:-1]] + [
+        parts[-1].reshape(wide, sides, ranks, rows, lanes)
+    ]
 
     def body(*refs):
-        first_kernel(count, rows_b, *refs)
+        first_kernel(count, rows_b, joined, *refs)
 
     rows_c = total * joined * slots
     out_shape = jax.ShapeDtypeStruct((rows_c, rows_b, length), jnp.float32)
@@ -604,14 +642,15 @@
         grid=(grid,),
         in_specs=[
             pl.BlockSpec(memory_space=pltpu.SMEM),
+            pl.BlockSpec(memory_space=pltpu.SMEM),
             whole(table.shape),
-            *[whole((wide, sides, ranks, rows, lanes))] * joined,
+            *[whole(part.shape) for part in parts],
         ],
         out_specs=[pl.BlockSpec((rows_c // grid, rows_b, length), lambda i: (i, 0, 0))] * 2,
         out_shape=[out_shape] * 2,
         compiler_params=params(1),
         cost_estimate=cost(rows_c * 2 * rows_b * length * length, 16 * rows_c * rows_b * length),
-    )(is_anchor, keep(table, pltpu.VMEM), *[keep(part, pltpu.VMEM) for part in parts])
+    )(side, is_anchor, in_hbm(table), *[keep(part, pltpu.VMEM) for part in parts])
 
 
 def transpose(value, members=None):
@@ -652,14 +691,21 @@
             )
             start += count
         is_anchor = ((spot_wide == 0) & (spot_narrow == 0)).astype(jnp.int32).reshape(1)
-        parts = []
+        across = [(n, (n + ranks) % narrow) for n in range(narrow)]
+        parts, after = [], []
         table = first_table(length, devices, groups, slab // groups, sides)
         for group, chunk in enumerate(chunks):
-            carry = [table] if group == groups - 1 else []
             received = keep(transpose(chunk, members), pltpu.VMEM if group else pltpu.HBM)
-            part, *carry = shear_pass(received, wide, narrow, per_c, group, groups, carry)
-            parts.append(transpose(part.reshape((wide * narrow,) + part.shape[2:])))
-        return tuple(first_pass(parts, *carry, is_anchor, length, wide, sides, slab // groups))
+            result = shear_pass(received, side, wide, narrow, per_c, group, groups, after)
+            result = [part.reshape((-1,) + part.shape[2:]) for part in result]
+            if len(result) == 1:
+                parts.append(transpose(result[0]))
+                continue
+            for own, other in zip(result[:2], result[2:]):
+                after = [lax.ppermute(other, "narrow", across)]
+                both = jnp.concatenate([own[:, None], after[0][:, None]], axis=1)
+                parts.append(transpose(both, members))
+        return tuple(first_pass(parts, table, side, is_anchor, length, wide, sides, slab // groups))
 
     return jax.shard_map(
         per_device,

time: 313 us -> 331 us (1.058)
  starting transfers between devices: 17.3 us -> 28.5 us
  local copies, waits for them, and re-layouts: 1 us -> 7.38 us
  waiting for transfers between devices: 124 us -> 119 us
    all_to_all x4 -> x5, waiting for transfers between devices: 124 us -> 63.6 us  [transpose(): lax.all_to_all(value, AXES, split_axis=0, concat_axis=0, tiled=True, axis...]
    ppermute x0 -> x2, waiting for transfers between devices: none -> 55.8 us  [per_device(): after = [lax.ppermute(other, 'narrow', across)]]
    all_to_all x4 -> x5, starting transfers between devices: 17.3 us -> 25.6 us  [transpose(): lax.all_to_all(value, AXES, split_axis=0, concat_axis=0, tiled=True, axis...]
    unnamed x4 -> x14, local copies, waits for them, and re-layouts: 1 us -> 6.29 us
  transfers between devices with their start and end apart: 4 -> 7, of which waited for: 4 -> 5; matrix products, arithmetic and copies ran while one was open for 0% -> 1% of each run, Pallas kernels for 12% -> 11%
where the time goes in v13:
time: 331 us; the launch traced here: 330 us
  waiting for transfers between devices  119 us (36%)
  blocking collectives  118 us (36%)
  Pallas kernels  52.4 us (16%)
  starting transfers between devices  28.5 us (9%)
  local copies, waits for them, and re-layouts  7.38 us (2%)
    all_to_all x2, blocking collectives, transpose(): lax.all_to_all(value, AXES, split_axis=0, concat_axis=0, tiled=True, axis...  118 us
    all_to_all x5, waiting for transfers between devices, transpose(): lax.all_to_all(value, AXES, split_axis=0, concat_axis=0, tiled=True, axis...  63.6 us
    ppermute x2, waiting for transfers between devices, per_device(): after = [lax.ppermute(other, 'narrow', across)]  55.8 us
    pallas_call x2, Pallas kernels, shear_pass(): pl.pallas_call(body, grid_spec=pltpu.PrefetchScalarGridSpec(num_scalar_pr...  27.9 us
    all_to_all x5, starting transfers between devices, transpose(): lax.all_to_all(value, AXES, split_axis=0, concat_axis=0, tiled=True, axis...  25.6 us
    pallas_call x2, Pallas kernels, spectrum_pass(): pl.pallas_call(body, grid_spec=pltpu.PrefetchScalarGridSpec(num_scalar_pr...  13.4 us
  transfers between devices with their start and end apart: 7, of which 5 were waited for; matrix products, arithmetic and copies ran while one was open for 1% of the time, Pallas kernels for 11%

profile of v13, /device:TPU:1, one launch (start us, length us, event | category | flops | bytes accessed | tf_op | source)
XLA Modules:
  0.0 330.0 jit_solution(9743759524653176662)
XLA Ops:
  0.6 5.0 %shard_map.203 = (f32[8,2,2,6,32,128]{5,4,3,2,1,0:T(8,128)S(1)}, f32[8,2,2,2,32,128]{5,4,3,2,1,0:T(8,128)}) custom-call(bf16[2,256,256]{2,1,0:T(8,128)(2,1)} %constant.66.clone.refs_0_, f32[32,64,256]{2,1,0:T(8,128)} %refs_1_.3), custom_call_target="tpu_custom_call" | custom-call | flops 805306368 | bytes 6291456 | tf_op jit(solution)/shard_map/pallas_call | solution.py:114
  5.6 78.3 %all_to_all.35 = f32[32,6,32,128]{3,2,1,0:T(8,128)} all-to-all(f32[32,6,32,128]{3,2,1,0:T(8,128)S(1)} %bitcast.19), channel_id=1, replica_groups=mesh['wide'=8,'narrow'=4] {'wide','narrow'}, dimensions={0} | all-to-all | bytes 6291456 | tf_op jit(solution)/shard_map/all_to_all | solution.py:657
  83.9 3.2 all-to-all-start.1
  87.2 9.3 %shard_map.204 = (f32[16,12,32,128]{3,2,1,0:T(8,128)S(1)}, f32[16,12,32,128]{3,2,1,0:T(8,128)}, f32[3,2,128,1]{3,2,1,0:T(8,128)S(1)}, f32[2,1,256]{2,1,0:T(1,128...) custom-call(s32[1]{0:T(128)} %bitcast.refs_0_, ...), custom_call_target="tpu_custom_call" | custom-call | flops 4227858432 | bytes 15728640 | tf_op jit(solution)/shard_map/pallas_call | solution.py:308
  96.4 0.0 copy-start
  96.4 0.8 copy-done
  97.2 0.0 copy-start.2
  97.2 0.8 copy-done.2
  98.0 0.0 copy-start.4
  98.0 0.8 copy-done.4
  98.8 14.7 %all-to-all-done.1 = f32[32,2,32,128]{3,2,1,0:T(8,128)} async-done(((f32[32,2,32,128]{3,2,1,0:T(8,128)}), f32[32,2,32,128]{3,2,1,0:T(8,128)}, u32[]{:S(2)}, u32[]{:S(2)}) %all-to-all-start.1) | async-done | bytes 1048608 | tf_op jit(solution)/shard_map/all_to_all | solution.py:657
  113.5 0.0 copy-start.1
  113.5 1.0 copy-done.1
  114.6 0.0 copy-start.3
  114.6 1.0 copy-done.3
  115.6 0.0 copy-start.5
  115.6 1.0 copy-done.5
  116.7 4.2 %shard_map.205 = (f32[16,12,32,128]{3,2,1,0:T(8,128)S(1)}, f32[16,12,32,128]{3,2,1,0:T(8,128)}) custom-call(s32[1]{0:T(128)} %bitcast.refs_0_, s32[1]{0:T(128)} %bitcast.2.refs_1_, f32[3,2,128,1]{3,2,1,0:T(8,128)S(1)} %get-tuple-element.18.refs_2_, f32[2,1,256]{2,1,0:T(1,128)S(1)} %get-tuple-element.19.refs_3_, ...), custom_call_target="tpu_custom_call", output_to_operand_aliasing={{0}: (8, {}), {1}: (9, {})} | custom-call | flops 1409286144 | bytes 5242880 | tf_op jit(solution)/shard_map/pallas_call | solution.py:308
  120.8 40.0 %all_to_all.36.refs_7_ = f32[16,12,32,128]{3,2,1,0:T(8,128)} all-to-all(f32[16,12,32,128]{3,2,1,0:T(8,128)S(1)} %get-tuple-element.26), channel_id=1, replica_groups={{0,1,4,5,8,9,12,13,16,17,20,21,24,25,28,29},{2,3,6,7,10,11,14,15,18,19,..., dimensions={0} | all-to-all | bytes 6291456 | tf_op jit(solution)/shard_map/all_to_all | solution.py:657
  160.9 3.8 %all-to-all-start.5 = ((f32[16,12,32,128]{3,2,1,0:T(8,128)}), f32[16,12,32,128]{3,2,1,0:T(8,128)S(1)}, u32[]{:S(2)}, u32[]{:S(2)}) async-start(f32[16,12,32,128]{3,2,1,0:T(8,128)} %get-tuple-element.31), calls=%async_computation.5 | async-start | bytes 6291456 | tf_op jit(solution)/shard_map/all_to_all | solution.py:657
  164.7 14.1 %shard_map.206 = (f32[8,2,64,128]{3,2,1,0:T(8,128)}, f32[8,2,64,128]{3,2,1,0:T(8,128)}, f32[8,2,64,128]{3,2,1,0:T(8,128)}, f32[8,2,64,128]{3,2,1,0:T(8,128)}) custom-call(s32[1]{0:T(128)} %bitcast.refs_0_, f32[6,512,1]{2,1,0:T(8,128)} %constant.72.clone.refs_1_, f32[6,1,512]{2,1,0:T(1,128)} %constant.73.clone.refs_2_, ...), custom_call_target="tpu_custom_call" | custom-call | flops 7247757312 | bytes 7340032 | tf_op jit(solution)/shard_map/pallas_call | solution.py:517
  178.7 1.3 collective-permute-start
  180.1 33.7 %collective-permute-done = f32[16,64,128]{2,1,0:T(8,128)S(1)} collective-permute-done((f32[16,64,128]{2,1,0:T(8,128)}, f32[16,64,128]{2,1,0:T(8,128)S(1)}, u32[]{:S(2)}, u32[]{:S(2)}) %collective-permute-start) | collective-permute-done | bytes 524320 | tf_op jit(solution)/shard_map/ppermute | solution.py:705
  213.8 2.1 pad_maximum_fusion
  215.9 0.0 all-to-all-done.5.refs_7_
  215.9 6.1 %all-to-all-start.3 = ((f32[16,2,64,128]{3,2,1,0:T(8,128)}), f32[16,2,64,128]{3,2,1,0:T(8,128)}, u32[]{:S(2)}, u32[]{:S(2)}) async-start(f32[16,2,64,128]{3,2,1,0:T(8,128)} %pad_maximum_fusion), calls=%async_computation.3 | async-start | bytes 2097152 | tf_op jit(solution)/shard_map/all_to_all | solution.py:657
  222.0 1.6 collective-permute-start.1
  223.6 22.1 %collective-permute-done.1.refs_8_ = f32[16,64,128]{2,1,0:T(8,128)S(1)} collective-permute-done((f32[16,64,128]{2,1,0:T(8,128)}, f32[16,64,128]{2,1,0:T(8,128)S(1)}, u32[]{:S(2)}, u32[]{:S(2)}) %collective-permute-start.1) | collective-permute-done | bytes 524320 | tf_op jit(solution)/shard_map/ppermute | solution.py:705
  245.7 0.0 copy-start.6
  245.7 0.8 copy-done.6
  246.5 1.1 pad_maximum_fusion.1
  247.6 1.1 copy.27
  248.7 0.0 all-to-all-done.3
  248.7 7.1 %all-to-all-start.4 = ((f32[16,2,64,128]{3,2,1,0:T(8,128)}), f32[16,2,64,128]{3,2,1,0:T(8,128)}, u32[]{:S(2)}, u32[]{:S(2)}) async-start(f32[16,2,64,128]{3,2,1,0:T(8,128)} %copy.27), calls=%async_computation.4 | async-start | bytes 2097152 | tf_op jit(solution)/shard_map/all_to_all | solution.py:657
  255.8 13.9 %shard_map.207 = f32[8,4,128,128]{3,2,1,0:T(8,128)} custom-call(s32[1]{0:T(128)} %bitcast.refs_0_, f32[6,512,1]{2,1,0:T(8,128)} %constant.77.clone.refs_1_, f32[6,1,512]{2,1,0:T(1,128)} %constant.73.clone.refs_2_, bf16[2,2,256,256]{3,2,1,0:T(8,128)(2,1)} %constant.70.clone.refs_5_.refs_3_, bf16[2,256,256]{2,1,0:T(8,128)(2,1)} %constant.78.clone.refs_4_, ...), custom_call_target="tpu_custom_call" | custom-call | flops 7247757312 | bytes 7340032 | tf_op jit(solution)/shard_map/pallas_call | solution.py:517
  269.6 0.6 all-to-all-done.4
  270.3 5.4 %all-to-all-start.6 = ((f32[32,128,128]{2,1,0:T(8,128)}), f32[32,128,128]{2,1,0:T(8,128)S(1)}, u32[]{:S(2)}, u32[]{:S(2)}) async-start(f32[32,128,128]{2,1,0:T(8,128)} %bitcast.22), calls=%async_computation.6 | async-start | bytes 4194304 | tf_op jit(solution)/shard_map/all_to_all | solution.py:657
  275.7 48.2 %all-to-all-done.6 = f32[32,128,128]{2,1,0:T(8,128)S(1)} async-done(((f32[32,128,128]{2,1,0:T(8,128)}), f32[32,128,128]{2,1,0:T(8,128)S(1)}, u32[]{:S(2)}, u32[]{:S(2)}) %all-to-all-start.6) | async-done | bytes 2097184 | tf_op jit(solution)/shard_map/all_to_all | solution.py:657
  324.0 6.0 %shard_map.208 = (f32[64,32,256]{2,1,0:T(8,128)}, f32[64,32,256]{2,1,0:T(8,128)}) custom-call(s32[1]{0:T(128)} %bitcast.refs_0_, s32[1]{0:T(128)} %bitcast.1.refs_1_, bf16[2,2,2,256,256]{4,3,2,1,0:T(8,128)(2,1)} %constant.80.clone.refs_2_, f32[8,2,2,64,128]{4,3,2,1,0:T(8,128)} %bitcast.11.refs_3_, f32[8,2,2,64,128]{4,3,2,1,0:T(8,128)} %bitcast.15.refs_4_, ...), custom_call_target="tpu_custom_call" | custom-call | flops 1610612736 | bytes 8388608 | tf_op jit(solution)/shard_map/pallas_call | solution.py:640
Async XLA Ops:
  83.9 29.6 %all-to-all-start.1 = ((f32[32,2,32,128]{3,2,1,0:T(8,128)}), f32[32,2,32,128]{3,2,1,0:T(8,128)}, u32[]{:S(2)}, u32[]{:S(2)}) async-start(f32[32,2,32,128]{3,2,1,0:T(8,128)} %bitcast.5), calls=%async_computation.1 | async-start | bytes 2097152 | tf_op jit(solution)/shard_map/all_to_all | solution.py:657
  96.4 0.8 copy-start
  97.2 0.8 copy-start.2
  98.0 0.8 copy-start.4
  113.5 1.0 copy-start.1
  114.6 1.0 copy-start.3
  115.6 1.0 copy-start.5
  160.9 55.1 %all-to-all-start.5 = ((f32[16,12,32,128]{3,2,1,0:T(8,128)}), f32[16,12,32,128]{3,2,1,0:T(8,128)S(1)}, u32[]{:S(2)}, u32[]{:S(2)}) async-start(f32[16,12,32,128]{3,2,1,0:T(8,128)} %get-tuple-element.31), calls=%async_computation.5 | async-start | bytes 6291456 | tf_op jit(solution)/shard_map/all_to_all | solution.py:657
  178.7 35.0 %collective-permute-start = (f32[16,64,128]{2,1,0:T(8,128)}, f32[16,64,128]{2,1,0:T(8,128)S(1)}, u32[]{:S(2)}, u32[]{:S(2)}) collective-permute-start(f32[16,64,128]{2,1,0:T(8,128)} %bitcast.28), channel_id=1, source_target_pairs={{0,2},{1,3},{2,0},{3,1},{4,6},{5,7},{6,4},{7,5},{8,10},{9,11},{10,... | collective-permute-start | bytes 1572872 | tf_op jit(solution)/shard_map/ppermute | solution.py:705
  215.9 32.8 %all-to-all-start.3 = ((f32[16,2,64,128]{3,2,1,0:T(8,128)}), f32[16,2,64,128]{3,2,1,0:T(8,128)}, u32[]{:S(2)}, u32[]{:S(2)}) async-start(f32[16,2,64,128]{3,2,1,0:T(8,128)} %pad_maximum_fusion), calls=%async_computation.3 | async-start | bytes 2097152 | tf_op jit(solution)/shard_map/all_to_all | solution.py:657
  222.0 23.7 %collective-permute-start.1 = (f32[16,64,128]{2,1,0:T(8,128)}, f32[16,64,128]{2,1,0:T(8,128)S(1)}, u32[]{:S(2)}, u32[]{:S(2)}) collective-permute-start(f32[16,64,128]{2,1,0:T(8,128)} %bitcast.27), channel_id=1, source_target_pairs={{0,2},{1,3},{2,0},{3,1},{4,6},{5,7},{6,4},{7,5},{8,10},{9,11},{10,... | collective-permute-start | bytes 1572872 | tf_op jit(solution)/shard_map/ppermute | solution.py:705
  245.7 0.8 copy-start.6
  248.7 21.5 %all-to-all-start.4 = ((f32[16,2,64,128]{3,2,1,0:T(8,128)}), f32[16,2,64,128]{3,2,1,0:T(8,128)}, u32[]{:S(2)}, u32[]{:S(2)}) async-start(f32[16,2,64,128]{3,2,1,0:T(8,128)} %copy.27), calls=%async_computation.4 | async-start | bytes 2097152 | tf_op jit(solution)/shard_map/all_to_all | solution.py:657
  270.3 53.7 %all-to-all-start.6 = ((f32[32,128,128]{2,1,0:T(8,128)}), f32[32,128,128]{2,1,0:T(8,128)S(1)}, u32[]{:S(2)}, u32[]{:S(2)}) async-start(f32[32,128,128]{2,1,0:T(8,128)} %bitcast.22), calls=%async_computation.6 | async-start | bytes 4194304 | tf_op jit(solution)/shard_map/all_to_all | solution.py:657

commit v14 on v11

--- a/solution.py
+++ b/solution.py
@@ -40,6 +40,15 @@
     )
 
 
+def product_wide(left, right):
+    width = right[0].shape[1]
+    high = jnp.dot(
+        left[0], jnp.concatenate(right, axis=1), preferred_element_type=jnp.float32
+    )
+    low = jnp.dot(left[1], right[0], preferred_element_type=jnp.float32)
+    return high[:, :width] + (high[:, width:] + low)
+
+
 def pair(ref):
     return ref[0], ref[1]
 
@@ -49,9 +58,9 @@
     return np.where(index < length // 2, index, index - length) * (2.0 * math.pi / length)
 
 
-def params(steps):
+def params(steps, limit=LIMIT):
     return pltpu.CompilerParams(
-        vmem_limit_bytes=LIMIT, dimension_semantics=("arbitrary",) * steps
+        vmem_limit_bytes=limit, dimension_semantics=("arbitrary",) * steps
     )
 
 
@@ -81,7 +90,7 @@
     start_x = pl.program_id(0) * step_x
     for first in range(0, step_x, group):
         block = density_ref[first : first + group].reshape(group * rows_y, length)
-        result = product(split(block), table)
+        result = product_wide(split(block), table)
         for inner in range(group):
             rows = slice(inner * rows_y, (inner + 1) * rows_y)
             value = jnp.concatenate([result[rows, :half], result[rows, half:]], axis=0).T
@@ -498,7 +507,7 @@
         out_shape=[pltpu.HBM(out_shape, jnp.float32)]
         + [pltpu.VMEM(each.shape, each.dtype) for each in carry],
         scratch_shapes=[pltpu.VMEM((length, count * length), jnp.float32)],
-        compiler_params=params(1),
+        compiler_params=params(1, 60 * 1024 * 1024),
         cost_estimate=cost(count * 18 * length**3, 4 * received.size + 4 * 2**20),
     )(
         *[in_hbm(value) for value in (row_factor, lane_factor, *tables)],
@@ -591,7 +600,7 @@
     rows_b = length // wide
     slots = lanes // rows_b
     total = rows // (2 * joined * count) if joined == 2 else rows // (2 * count)
-    grid = 4 if joined == 2 and total % 4 == 0 else 1
+    grid = total if joined == 2 else 1
     parts = [part.reshape(wide, sides, ranks, rows, lanes) for part in parts]
 
     def body(*refs):
@@ -611,7 +620,7 @@
         out_shape=[out_shape] * 2,
         compiler_params=params(1),
         cost_estimate=cost(rows_c * 2 * rows_b * length * length, 16 * rows_c * rows_b * length),
-    )(is_anchor, keep(table, pltpu.VMEM), *[keep(part, pltpu.VMEM) for part in parts])
+    )(is_anchor, in_hbm(table), *[keep(part, pltpu.VMEM) for part in parts])
 
 
 def transpose(value, members=None):
@@ -655,11 +664,10 @@
         parts = []
         table = first_table(length, devices, groups, slab // groups, sides)
         for group, chunk in enumerate(chunks):
-            carry = [table] if group == groups - 1 else []
-            received = keep(transpose(chunk, members), pltpu.VMEM if group else pltpu.HBM)
-            part, *carry = shear_pass(received, wide, narrow, per_c, group, groups, carry)
+            received = in_hbm(transpose(chunk, members))
+            (part,) = shear_pass(received, wide, narrow, per_c, group, groups, [])
             parts.append(transpose(part.reshape((wide * narrow,) + part.shape[2:])))
-        return tuple(first_pass(parts, *carry, is_anchor, length, wide, sides, slab // groups))
+        return tuple(first_pass(parts, table, is_anchor, length, wide, sides, slab // groups))
 
     return jax.shard_map(
         per_device,

time: 313 us -> 320 us (1.022)
  local copies, waits for them, and re-layouts: 1 us -> 7.16 us
    unnamed x4 -> x14, local copies, waits for them, and re-layouts: 1 us -> 7.16 us
where the time goes in v14:
time: 320 us; the launch traced here: 319 us
  waiting for transfers between devices  122 us (38%)
  blocking collectives  118 us (37%)
  Pallas kernels  54.3 us (17%)
  starting transfers between devices  16.8 us (5%)
  local copies, waits for them, and re-layouts  7.16 us (2%)
    all_to_all x4, waiting for transfers between devices, transpose(): lax.all_to_all(value, AXES, split_axis=0, concat_axis=0, tiled=True, axis...  122 us
    all_to_all x2, blocking collectives, transpose(): lax.all_to_all(value, AXES, split_axis=0, concat_axis=0, tiled=True, axis...  118 us
    pallas_call x2, Pallas kernels, shear_pass(): pl.pallas_call(body, grid=(6,), in_specs=[pl.BlockSpec((1, count * half,...  28.5 us
    all_to_all x4, starting transfers between devices, transpose(): lax.all_to_all(value, AXES, split_axis=0, concat_axis=0, tiled=True, axis...  16.8 us
    pallas_call x2, Pallas kernels, spectrum_pass(): pl.pallas_call(body, grid_spec=pltpu.PrefetchScalarGridSpec(num_scalar_pr...  13.4 us
    pallas_call x1, Pallas kernels, first_pass(): pl.pallas_call(body, grid=(grid,), in_specs=[pl.BlockSpec(memory_space=pl...  7.43 us
    unnamed x14, local copies, waits for them, and re-layouts  7.16 us
  transfers between devices with their start and end apart: 4, of which 4 were waited for; matrix products, arithmetic and copies ran while one was open for 0% of the time, Pallas kernels for 12%

profile of v14, /device:TPU:1, one launch (start us, length us, event | category | flops | bytes accessed | tf_op | source)
XLA Modules:
  0.0 319.4 jit_solution(12713692071228866091)
XLA Ops:
  0.6 5.0 %shard_map.203 = (f32[8,2,2,6,32,128]{5,4,3,2,1,0:T(8,128)S(1)}, f32[8,2,2,2,32,128]{5,4,3,2,1,0:T(8,128)}) custom-call(bf16[2,256,256]{2,1,0:T(8,128)(2,1)} %constant.64.clone.refs_0_, f32[32,64,256]{2,1,0:T(8,128)} %refs_1_.4), custom_call_target="tpu_custom_call" | custom-call | flops 805306368 | bytes 6291456 | tf_op jit(solution)/shard_map/pallas_call | solution.py:123
  5.6 78.3 %all_to_all.30 = f32[32,6,32,128]{3,2,1,0:T(8,128)} all-to-all(f32[32,6,32,128]{3,2,1,0:T(8,128)S(1)} %bitcast.11), channel_id=1, replica_groups=mesh['wide'=8,'narrow'=4] {'wide','narrow'}, dimensions={0} | all-to-all | bytes 6291456 | tf_op jit(solution)/shard_map/all_to_all | solution.py:627
  83.9 3.2 %all-to-all-start.1 = ((f32[32,2,32,128]{3,2,1,0:T(8,128)}), f32[32,2,32,128]{3,2,1,0:T(8,128)}, u32[]{:S(2)}, u32[]{:S(2)}) async-start(f32[32,2,32,128]{3,2,1,0:T(8,128)} %bitcast.5), calls=%async_computation.1 | async-start | bytes 2097152 | tf_op jit(solution)/shard_map/all_to_all | solution.py:627
  87.2 9.3 %shard_map.204 = (f32[16,12,32,128]{3,2,1,0:T(8,128)S(1)}, f32[16,12,32,128]{3,2,1,0:T(8,128)}, f32[3,2,128,1]{3,2,1,0:T(8,128)S(1)}, f32[2,1,256]{2,1,0:T(1,128...) custom-call(s32[1]{0:T(128)} %bitcast.1.refs_0_, ...), custom_call_target="tpu_custom_call" | custom-call | flops 4227858432 | bytes 15728640 | tf_op jit(solution)/shard_map/pallas_call | solution.py:317
  96.4 0.0 copy-start
  96.4 0.8 copy-done
  97.2 0.0 copy-start.2
  97.2 0.8 copy-done.2
  98.0 0.0 copy-start.4
  98.0 0.8 copy-done.4
  98.8 14.7 %all-to-all-done.1 = f32[32,2,32,128]{3,2,1,0:T(8,128)} async-done(((f32[32,2,32,128]{3,2,1,0:T(8,128)}), f32[32,2,32,128]{3,2,1,0:T(8,128)}, u32[]{:S(2)}, u32[]{:S(2)}) %all-to-all-start.1) | async-done | bytes 1048608 | tf_op jit(solution)/shard_map/all_to_all | solution.py:627
  113.5 0.0 copy-start.1
  113.5 1.0 copy-done.1
  114.6 0.0 copy-start.3
  114.6 1.0 copy-done.3
  115.6 0.0 copy-start.5
  115.6 1.0 copy-done.5
  116.7 4.2 %shard_map.205 = (f32[16,12,32,128]{3,2,1,0:T(8,128)S(1)}, f32[16,12,32,128]{3,2,1,0:T(8,128)}) custom-call(s32[1]{0:T(128)} %bitcast.1.refs_0_, s32[1]{0:T(128)} %bitcast.2.refs_1_, f32[3,2,128,1]{3,2,1,0:T(8,128)S(1)} %get-tuple-element.14.refs_2_, f32[2,1,256]{2,1,0:T(1,128)S(1)} %get-tuple-element.15.refs_3_, ...), custom_call_target="tpu_custom_call", output_to_operand_aliasing={{0}: (8, {}), {1}: (9, {})} | custom-call | flops 1409286144 | bytes 5242880 | tf_op jit(solution)/shard_map/pallas_call | solution.py:317
  120.8 40.0 %all_to_all.31.refs_6_ = f32[16,12,32,128]{3,2,1,0:T(8,128)} all-to-all(f32[16,12,32,128]{3,2,1,0:T(8,128)S(1)} %get-tuple-element.22), channel_id=1, replica_groups={{0,1,4,5,8,9,12,13,16,17,20,21,24,25,28,29},{2,3,6,7,10,11,14,15,18,19,..., dimensions={0} | all-to-all | bytes 6291456 | tf_op jit(solution)/shard_map/all_to_all | solution.py:627
  160.9 3.8 %all-to-all-start.4 = ((f32[16,12,32,128]{3,2,1,0:T(8,128)}), f32[16,12,32,128]{3,2,1,0:T(8,128)S(1)}, u32[]{:S(2)}, u32[]{:S(2)}) async-start(f32[16,12,32,128]{3,2,1,0:T(8,128)} %get-tuple-element.23), calls=%async_computation.4 | async-start | bytes 6291456 | tf_op jit(solution)/shard_map/all_to_all | solution.py:627
  164.7 14.2 %shard_map.206 = f32[8,4,128,128]{3,2,1,0:T(8,128)} custom-call(f32[6,512,1]{2,1,0:T(8,128)} %constant.70.clone.refs_0_, f32[6,1,512]{2,1,0:T(1,128)} %constant.71.clone.refs_1_, bf16[2,2,256,256]{3,2,1,0:T(8,128)(2,1)} %constant.68.clone.refs_5_.refs_2_, bf16[2,256,256]{2,1,0:T(8,128)(2,1)} %constant.72.clone.refs_3_, ...), custom_call_target="tpu_custom_call" | custom-call | flops 7247757312 | bytes 7340032 | tf_op jit(solution)/shard_map/pallas_call | solution.py:496
  178.9 25.1 %all-to-all-done.4.refs_6_ = f32[16,12,32,128]{3,2,1,0:T(8,128)S(1)} async-done(((f32[16,12,32,128]{3,2,1,0:T(8,128)}), f32[16,12,32,128]{3,2,1,0:T(8,128)S(1)}, u32[]{:S(2)}, u32[]{:S(2)}) %all-to-all-start.4) | async-done | bytes 3145760 | tf_op jit(solution)/shard_map/all_to_all | solution.py:627
  204.0 0.0 copy-start.6
  204.0 1.6 copy-done.6
  205.7 6.3 %all-to-all-start.3 = ((f32[32,128,128]{2,1,0:T(8,128)}), f32[32,128,128]{2,1,0:T(8,128)S(1)}, u32[]{:S(2)}, u32[]{:S(2)}) async-start(f32[32,128,128]{2,1,0:T(8,128)} %bitcast.15), calls=%async_computation.3 | async-start | bytes 4194304 | tf_op jit(solution)/shard_map/all_to_all | solution.py:627
  212.0 14.2 %shard_map.207 = f32[8,4,128,128]{3,2,1,0:T(8,128)} custom-call(f32[6,512,1]{2,1,0:T(8,128)} %constant.75.clone.refs_0_, f32[6,1,512]{2,1,0:T(1,128)} %constant.71.clone.refs_1_, bf16[2,2,256,256]{3,2,1,0:T(8,128)(2,1)} %constant.68.clone.refs_5_.refs_2_, bf16[2,256,256]{2,1,0:T(8,128)(2,1)} %constant.76.clone.refs_3_, ...), custom_call_target="tpu_custom_call" | custom-call | flops 7247757312 | bytes 7340032 | tf_op jit(solution)/shard_map/pallas_call | solution.py:496
  226.2 34.0 %all-to-all-done.3 = f32[32,128,128]{2,1,0:T(8,128)S(1)} async-done(((f32[32,128,128]{2,1,0:T(8,128)}), f32[32,128,128]{2,1,0:T(8,128)S(1)}, u32[]{:S(2)}, u32[]{:S(2)}) %all-to-all-start.3) | async-done | bytes 2097184 | tf_op jit(solution)/shard_map/all_to_all | solution.py:627
  260.2 3.5 %all-to-all-start.5 = ((f32[32,128,128]{2,1,0:T(8,128)}), f32[32,128,128]{2,1,0:T(8,128)}, u32[]{:S(2)}, u32[]{:S(2)}) async-start(f32[32,128,128]{2,1,0:T(8,128)} %bitcast.14), calls=%async_computation.5 | async-start | bytes 4194304 | tf_op jit(solution)/shard_map/all_to_all | solution.py:627
  263.7 48.3 %all-to-all-done.5 = f32[32,128,128]{2,1,0:T(8,128)} async-done(((f32[32,128,128]{2,1,0:T(8,128)}), f32[32,128,128]{2,1,0:T(8,128)}, u32[]{:S(2)}, u32[]{:S(2)}) %all-to-all-start.5) | async-done | bytes 2097184 | tf_op jit(solution)/shard_map/all_to_all | solution.py:627
  312.0 7.4 %shard_map.208 = (f32[64,32,256]{2,1,0:T(8,128)}, f32[64,32,256]{2,1,0:T(8,128)}) custom-call(s32[1]{0:T(128)} %bitcast.refs_0_, bf16[2,2,2,256,256]{4,3,2,1,0:T(8,128)(2,1)} %constant.77.clone.refs_1_, f32[8,2,2,128,128]{4,3,2,1,0:T(8,128)S(1)} %bitcast.12, f32[8,2,2,128,128]{4,3,2,1,0:T(8,128)} %bitcast.10.refs_3_), custom_call_target="tpu_custom_call" | custom-call | flops 1610612736 | bytes 8388608 | tf_op jit(solution)/shard_map/pallas_call | solution.py:611
Async XLA Ops:
  83.9 29.6 %all-to-all-start.1 = ((f32[32,2,32,128]{3,2,1,0:T(8,128)}), f32[32,2,32,128]{3,2,1,0:T(8,128)}, u32[]{:S(2)}, u32[]{:S(2)}) async-start(f32[32,2,32,128]{3,2,1,0:T(8,128)} %bitcast.5), calls=%async_computation.1 | async-start | bytes 2097152 | tf_op jit(solution)/shard_map/all_to_all | solution.py:627
  96.4 0.8 copy-start
  97.2 0.8 copy-start.2
  98.0 0.8 copy-start.4
  113.5 1.0 copy-start.1
  114.6 1.0 copy-start.3
  115.6 1.0 copy-start.5
  160.9 43.2 %all-to-all-start.4 = ((f32[16,12,32,128]{3,2,1,0:T(8,128)}), f32[16,12,32,128]{3,2,1,0:T(8,128)S(1)}, u32[]{:S(2)}, u32[]{:S(2)}) async-start(f32[16,12,32,128]{3,2,1,0:T(8,128)} %get-tuple-element.23), calls=%async_computation.4 | async-start | bytes 6291456 | tf_op jit(solution)/shard_map/all_to_all | solution.py:627
  204.0 1.7 copy-start.6
  205.7 54.5 %all-to-all-start.3 = ((f32[32,128,128]{2,1,0:T(8,128)}), f32[32,128,128]{2,1,0:T(8,128)S(1)}, u32[]{:S(2)}, u32[]{:S(2)}) async-start(f32[32,128,128]{2,1,0:T(8,128)} %bitcast.15), calls=%async_computation.3 | async-start | bytes 4194304 | tf_op jit(solution)/shard_map/all_to_all | solution.py:627
  260.2 51.8 %all-to-all-start.5 = ((f32[32,128,128]{2,1,0:T(8,128)}), f32[32,128,128]{2,1,0:T(8,128)}, u32[]{:S(2)}, u32[]{:S(2)}) async-start(f32[32,128,128]{2,1,0:T(8,128)} %bitcast.14), calls=%async_computation.5 | async-start | bytes 4194304 | tf_op jit(solution)/shard_map/all_to_all | solution.py:627

commit v15 on v11

--- a/solution.py
+++ b/solution.py
@@ -77,7 +77,7 @@
     half = length // 2
     flats = [ref.reshape(math.prod(ref.shape[:5]), 2 * rows_y) for ref in outs]
     table = pair(table_ref)
-    group = 4
+    group = step_x
     start_x = pl.program_id(0) * step_x
     for first in range(0, step_x, group):
         block = density_ref[first : first + group].reshape(group * rows_y, length)
@@ -284,7 +284,7 @@
     a_table = np.stack([wave, wave**2, scale]).astype(np.float32)[..., None]
     b_table = np.stack([wave**2, scale]).astype(np.float32).reshape(2, 1, length)
     message = PAIR * slab // groups
-    spaces = [pltpu.VMEM, pltpu.HBM][:groups]
+    spaces = [pltpu.HBM] * groups
     out_shape = (devices, 3 * 2 * length // TILE, steps * message, TILE)
     block = out_shape[:2] + (message, TILE)
 
@@ -336,9 +336,7 @@
 def shear_kernel(
     per_c, group, joined, row_ref, lane_ref, second_ref, third_ref, ahead_ref, last_ref, in_ref, *refs
 ):
-    shear_ref = refs[-1]
-    out_ref, carry_refs = refs[len(refs) // 2 - 1], refs[: len(refs) // 2 - 1]
-    hand_on(carry_refs, refs[len(refs) // 2 : -1])
+    out_ref, shear_ref = refs
     step = pl.program_id(0)
     length = shear_ref.shape[0]
     half = length // 2
@@ -436,7 +434,7 @@
                                 out[pl.ds(at, run), :] = piece
 
 
-def shear_pass(received, wide, narrow, per_c, group, joined, carry):
+def shear_pass(received, wide, narrow, per_c, group, joined):
     devices, tiles, message, tile = received.shape
     count = message // per_c
     length = tiles * tile // 6
@@ -492,18 +490,15 @@
             pl.BlockSpec((1, 1, 2 * length), lambda i: (i, 0, 0)),
             *[whole(table.shape) for table in tables],
             pl.BlockSpec((devices, tiles // 3, message, tile), which),
-            *[whole(each.shape) for each in carry],
         ],
-        out_specs=[whole(out_shape)] + [whole(each.shape) for each in carry],
-        out_shape=[pltpu.HBM(out_shape, jnp.float32)]
-        + [pltpu.VMEM(each.shape, each.dtype) for each in carry],
+        out_specs=[whole(out_shape)],
+        out_shape=[pltpu.HBM(out_shape, jnp.float32)],
         scratch_shapes=[pltpu.VMEM((length, count * length), jnp.float32)],
         compiler_params=params(1),
         cost_estimate=cost(count * 18 * length**3, 4 * received.size + 4 * 2**20),
     )(
         *[in_hbm(value) for value in (row_factor, lane_factor, *tables)],
         received,
-        *[in_hbm(each) for each in carry],
     )
 
 
@@ -529,7 +524,7 @@
             own, other = [
                 ref[:, side, :, at].reshape(wide * ranks, 2 * count, lanes) for ref in ins
             ]
-            both = [jnp.where(upper, own, other), jnp.where(upper, other, own)]
+            both = jnp.where(upper, own, other), pltpu.roll(jnp.where(upper, other, own), count, 1)
             return [value.reshape(half, lanes).T for value in both]
         flat = ins[0].reshape(wide * sides * ranks * rows, lanes)
         run = rows // count
@@ -545,43 +540,35 @@
         )
         return [value.T]
 
-    lefts = []
+    sums = []
     for side in range(sides):
         tiles = [[gathered(side, step, part) for part in range(2)] for step in range(steps)]
-        lefts.append(
+        left = jnp.concatenate(
             [
-                jnp.concatenate(
-                    [jnp.concatenate([part[join] for part in parts], axis=1) for parts in tiles], axis=0
-                )
+                jnp.concatenate([part[join] for part in parts], axis=1)
+                for parts in tiles
                 for join in range(joined)
-            ]
-        )
-    for join in range(joined):
-        sums = [
-            product(split(lefts[side][join]), pair(table_ref.at[join, side])) for side in range(sides)
-        ]
-        even, odd = sums
-        for far, value in enumerate((even + odd, even - odd)):
-            for step in range(steps):
-                at = (step * joined + join) * slots
-                columns = slice(far * half, (far + 1) * half)
-                for part, ref in enumerate((real_ref, imag_ref)):
-                    here = value[step * lanes : (step + 1) * lanes, part * half : (part + 1) * half]
-                    if at == 0 and far == 0:
-                        here = jnp.where(anchor, 0.0, here)
-                    ref[at : at + slots, :, columns] = here.reshape(slots, rows_b, half)
-
-
-def first_table(length, devices, joined, count, sides):
+            ],
+            axis=0,
+        )
+        sums.append(product(split(left), pair(table_ref.at[side])))
+    even, odd = sums
+    for far, value in enumerate((even + odd, even - odd)):
+        columns = slice(far * half, (far + 1) * half)
+        for at in range(steps * joined):
+            for part, ref in enumerate((real_ref, imag_ref)):
+                here = value[at * lanes : (at + 1) * lanes, part * half : (part + 1) * half]
+                if at == 0 and far == 0:
+                    here = jnp.where(anchor, 0.0, here)
+                ref[at * slots : (at + 1) * slots, :, columns] = here.reshape(slots, rows_b, half)
+
+
+def first_table(length, devices, sides):
     scale = 1.0 / float(length) ** 1.5
-    index = np.arange(length).reshape(devices, joined, count, sides)
-    tables = []
-    for join in range(joined):
-        order = index[:, :: 1 - 2 * join].transpose(3, 0, 1, 2).reshape(sides, -1)
-        tables.append(
-            [split_table(scale * turn(-angles(np.arange(length // 2), x, length)).T) for x in order]
-        )
-    return np.stack([np.stack(each) for each in tables])
+    order = np.arange(length).reshape(devices, -1, sides).transpose(2, 0, 1).reshape(sides, -1)
+    return np.stack(
+        [split_table(scale * turn(-angles(np.arange(length // 2), x, length)).T) for x in order]
+    )
 
 
 def first_pass(parts, table, is_anchor, length, wide, sides, count):
@@ -611,7 +598,7 @@
         out_shape=[out_shape] * 2,
         compiler_params=params(1),
         cost_estimate=cost(rows_c * 2 * rows_b * length * length, 16 * rows_c * rows_b * length),
-    )(is_anchor, keep(table, pltpu.VMEM), *[keep(part, pltpu.VMEM) for part in parts])
+    )(is_anchor, in_hbm(table), *[keep(part, pltpu.VMEM) for part in parts])
 
 
 def transpose(value, members=None):
@@ -653,13 +640,12 @@
             start += count
         is_anchor = ((spot_wide == 0) & (spot_narrow == 0)).astype(jnp.int32).reshape(1)
         parts = []
-        table = first_table(length, devices, groups, slab // groups, sides)
+        table = first_table(length, devices, sides)
         for group, chunk in enumerate(chunks):
-            carry = [table] if group == groups - 1 else []
             received = keep(transpose(chunk, members), pltpu.VMEM if group else pltpu.HBM)
-            part, *carry = shear_pass(received, wide, narrow, per_c, group, groups, carry)
+            (part,) = shear_pass(received, wide, narrow, per_c, group, groups)
             parts.append(transpose(part.reshape((wide * narrow,) + part.shape[2:])))
-        return tuple(first_pass(parts, *carry, is_anchor, length, wide, sides, slab // groups))
+        return tuple(first_pass(parts, table, is_anchor, length, wide, sides, slab // groups))
 
     return jax.shard_map(
         per_device,

time: 313 us -> 314 us (level)
  no operation moved by 1% of the time
where the time goes in v15:
time: 314 us
  waiting for transfers between devices  125 us (40%)
  blocking collectives  119 us (38%)
  Pallas kernels  51.6 us (16%)
  starting transfers between devices  17.3 us (6%)
    all_to_all x4, waiting for transfers between devices, transpose(): lax.all_to_all(value, AXES, split_axis=0, concat_axis=0, tiled=True, axis...  125 us
    all_to_all x2, blocking collectives, transpose(): lax.all_to_all(value, AXES, split_axis=0, concat_axis=0, tiled=True, axis...  119 us
    pallas_call x2, Pallas kernels, shear_pass(): pl.pallas_call(body, grid=(6,), in_specs=[pl.BlockSpec((1, count * half,...  28.1 us
    all_to_all x4, starting transfers between devices, transpose(): lax.all_to_all(value, AXES, split_axis=0, concat_axis=0, tiled=True, axis...  17.3 us
    pallas_call x2, Pallas kernels, spectrum_pass(): pl.pallas_call(body, grid_spec=pltpu.PrefetchScalarGridSpec(num_scalar_pr...  12.5 us
  transfers between devices with their start and end apart: 4, of which 4 were waited for; matrix products, arithmetic and copies ran while one was open for 0% of the time, Pallas kernels for 12%

profile of v15, /device:TPU:1, one launch (start us, length us, event | category | flops | bytes accessed | tf_op | source)
XLA Modules:
  0.0 313.5 jit_solution(5076803915795158620)
XLA Ops:
  0.6 4.9 %shard_map.203 = (f32[8,2,2,6,32,128]{5,4,3,2,1,0:T(8,128)S(1)}, f32[8,2,2,2,32,128]{5,4,3,2,1,0:T(8,128)}) custom-call(bf16[2,256,256]{2,1,0:T(8,128)(2,1)} %constant.64.clone.refs_0_, f32[32,64,256]{2,1,0:T(8,128)} %refs_1_.4), custom_call_target="tpu_custom_call" | custom-call | flops 805306368 | bytes 6291456 | tf_op jit(solution)/shard_map/pallas_call | solution.py:114
  5.5 78.3 %all_to_all.30 = f32[32,6,32,128]{3,2,1,0:T(8,128)} all-to-all(f32[32,6,32,128]{3,2,1,0:T(8,128)S(1)} %bitcast.12), channel_id=1, replica_groups=mesh['wide'=8,'narrow'=4] {'wide','narrow'}, dimensions={0} | all-to-all | bytes 6291456 | tf_op jit(solution)/shard_map/all_to_all | solution.py:605
  83.8 3.2 %all-to-all-start.1 = ((f32[32,2,32,128]{3,2,1,0:T(8,128)}), f32[32,2,32,128]{3,2,1,0:T(8,128)S(1)}, u32[]{:S(2)}, u32[]{:S(2)}) async-start(f32[32,2,32,128]{3,2,1,0:T(8,128)} %bitcast.5), calls=%async_computation.1 | async-start | bytes 2097152 | tf_op jit(solution)/shard_map/all_to_all | solution.py:605
  87.0 9.3 %shard_map.204 = (f32[16,12,32,128]{3,2,1,0:T(8,128)}, f32[16,12,32,128]{3,2,1,0:T(8,128)}, f32[3,2,128,1]{3,2,1,0:T(8,128)S(1)}, f32[2,1,256]{2,1,0:T(1,128)S(1...) custom-call(s32[1]{0:T(128)} %bitcast.1.refs_0_, ...), custom_call_target="tpu_custom_call" | custom-call | flops 4227858432 | bytes 15728640 | tf_op jit(solution)/shard_map/pallas_call | solution.py:308
  96.3 17.1 %all-to-all-done.1 = f32[32,2,32,128]{3,2,1,0:T(8,128)S(1)} async-done(((f32[32,2,32,128]{3,2,1,0:T(8,128)}), f32[32,2,32,128]{3,2,1,0:T(8,128)S(1)}, u32[]{:S(2)}, u32[]{:S(2)}) %all-to-all-start.1) | async-done | bytes 1048608 | tf_op jit(solution)/shard_map/all_to_all | solution.py:605
  113.3 3.2 %shard_map.205 = (f32[16,12,32,128]{3,2,1,0:T(8,128)}, f32[16,12,32,128]{3,2,1,0:T(8,128)}) custom-call(s32[1]{0:T(128)} %bitcast.1.refs_0_, s32[1]{0:T(128)} %bitcast.2.refs_1_, f32[3,2,128,1]{3,2,1,0:T(8,128)S(1)} %get-tuple-element.14.refs_2_, f32[2,1,256]{2,1,0:T(1,128)S(1)} %get-tuple-element.15.refs_3_, ...), custom_call_target="tpu_custom_call", output_to_operand_aliasing={{0}: (8, {}), {1}: (9, {})} | custom-call | flops 1409286144 | bytes 5242880 | tf_op jit(solution)/shard_map/pallas_call | solution.py:308
  116.5 40.8 %all_to_all.31.refs_6_ = f32[16,12,32,128]{3,2,1,0:T(8,128)} all-to-all(f32[16,12,32,128]{3,2,1,0:T(8,128)} %get-tuple-element.22), channel_id=1, replica_groups={{0,1,4,5,8,9,12,13,16,17,20,21,24,25,28,29},{2,3,6,7,10,11,14,15,18,19,..., dimensions={0} | all-to-all | bytes 6291456 | tf_op jit(solution)/shard_map/all_to_all | solution.py:605
  157.4 5.3 %all-to-all-start.4 = ((f32[16,12,32,128]{3,2,1,0:T(8,128)}), f32[16,12,32,128]{3,2,1,0:T(8,128)S(1)}, u32[]{:S(2)}, u32[]{:S(2)}) async-start(f32[16,12,32,128]{3,2,1,0:T(8,128)} %get-tuple-element.23), calls=%async_computation.4 | async-start | bytes 6291456 | tf_op jit(solution)/shard_map/all_to_all | solution.py:605
  162.7 14.2 %shard_map.206 = f32[8,4,128,128]{3,2,1,0:T(8,128)} custom-call(f32[6,512,1]{2,1,0:T(8,128)} %constant.70.clone.refs_0_, f32[6,1,512]{2,1,0:T(1,128)} %constant.71.clone.refs_1_, bf16[2,2,256,256]{3,2,1,0:T(8,128)(2,1)} %constant.68.clone.refs_5_.refs_2_, bf16[2,256,256]{2,1,0:T(8,128)(2,1)} %constant.72.clone.refs_3_, ...), custom_call_target="tpu_custom_call" | custom-call | flops 7247757312 | bytes 7340032 | tf_op jit(solution)/shard_map/pallas_call | solution.py:485
  176.9 25.1 %all-to-all-done.4.refs_6_ = f32[16,12,32,128]{3,2,1,0:T(8,128)S(1)} async-done(((f32[16,12,32,128]{3,2,1,0:T(8,128)}), f32[16,12,32,128]{3,2,1,0:T(8,128)S(1)}, u32[]{:S(2)}, u32[]{:S(2)}) %all-to-all-start.4) | async-done | bytes 3145760 | tf_op jit(solution)/shard_map/all_to_all | solution.py:605
  202.1 5.3 %all-to-all-start.3 = ((f32[32,128,128]{2,1,0:T(8,128)}), f32[32,128,128]{2,1,0:T(8,128)}, u32[]{:S(2)}, u32[]{:S(2)}) async-start(f32[32,128,128]{2,1,0:T(8,128)} %bitcast.16), calls=%async_computation.3 | async-start | bytes 4194304 | tf_op jit(solution)/shard_map/all_to_all | solution.py:605
  207.4 13.9 %shard_map.207 = f32[8,4,128,128]{3,2,1,0:T(8,128)} custom-call(f32[6,512,1]{2,1,0:T(8,128)} %constant.75.clone.refs_0_, f32[6,1,512]{2,1,0:T(1,128)} %constant.71.clone.refs_1_, bf16[2,2,256,256]{3,2,1,0:T(8,128)(2,1)} %constant.68.clone.refs_5_.refs_2_, bf16[2,256,256]{2,1,0:T(8,128)(2,1)} %constant.76.clone.refs_3_, ...), custom_call_target="tpu_custom_call" | custom-call | flops 7247757312 | bytes 7340032 | tf_op jit(solution)/shard_map/pallas_call | solution.py:485
  221.3 34.4 %all-to-all-done.3 = f32[32,128,128]{2,1,0:T(8,128)} async-done(((f32[32,128,128]{2,1,0:T(8,128)}), f32[32,128,128]{2,1,0:T(8,128)}, u32[]{:S(2)}, u32[]{:S(2)}) %all-to-all-start.3) | async-done | bytes 2097184 | tf_op jit(solution)/shard_map/all_to_all | solution.py:605
  255.7 3.4 %all-to-all-start.5 = ((f32[32,128,128]{2,1,0:T(8,128)}), f32[32,128,128]{2,1,0:T(8,128)S(1)}, u32[]{:S(2)}, u32[]{:S(2)}) async-start(f32[32,128,128]{2,1,0:T(8,128)} %bitcast.15), calls=%async_computation.5 | async-start | bytes 4194304 | tf_op jit(solution)/shard_map/all_to_all | solution.py:605
  259.1 48.2 %all-to-all-done.5 = f32[32,128,128]{2,1,0:T(8,128)S(1)} async-done(((f32[32,128,128]{2,1,0:T(8,128)}), f32[32,128,128]{2,1,0:T(8,128)S(1)}, u32[]{:S(2)}, u32[]{:S(2)}) %all-to-all-start.5) | async-done | bytes 2097184 | tf_op jit(solution)/shard_map/all_to_all | solution.py:605
  307.4 6.2 %shard_map.208 = (f32[64,32,256]{2,1,0:T(8,128)}, f32[64,32,256]{2,1,0:T(8,128)}) custom-call(s32[1]{0:T(128)} %bitcast.refs_0_, bf16[2,2,256,256]{3,2,1,0:T(8,128)(2,1)} %constant.77.clone.refs_1_, f32[8,2,2,128,128]{4,3,2,1,0:T(8,128)} %bitcast.8.refs_2_, f32[8,2,2,128,128]{4,3,2,1,0:T(8,128)S(1)} %bitcast.13), custom_call_target="tpu_custom_call" | custom-call | flops 1610612736 | bytes 8388608 | tf_op jit(solution)/shard_map/pallas_call | solution.py:589
Async XLA Ops:
  83.8 29.5 %all-to-all-start.1 = ((f32[32,2,32,128]{3,2,1,0:T(8,128)}), f32[32,2,32,128]{3,2,1,0:T(8,128)S(1)}, u32[]{:S(2)}, u32[]{:S(2)}) async-start(f32[32,2,32,128]{3,2,1,0:T(8,128)} %bitcast.5), calls=%async_computation.1 | async-start | bytes 2097152 | tf_op jit(solution)/shard_map/all_to_all | solution.py:605
  157.4 44.7 %all-to-all-start.4 = ((f32[16,12,32,128]{3,2,1,0:T(8,128)}), f32[16,12,32,128]{3,2,1,0:T(8,128)S(1)}, u32[]{:S(2)}, u32[]{:S(2)}) async-start(f32[16,12,32,128]{3,2,1,0:T(8,128)} %get-tuple-element.23), calls=%async_computation.4 | async-start | bytes 6291456 | tf_op jit(solution)/shard_map/all_to_all | solution.py:605
  202.1 53.6 %all-to-all-start.3 = ((f32[32,128,128]{2,1,0:T(8,128)}), f32[32,128,128]{2,1,0:T(8,128)}, u32[]{:S(2)}, u32[]{:S(2)}) async-start(f32[32,128,128]{2,1,0:T(8,128)} %bitcast.16), calls=%async_computation.3 | async-start | bytes 4194304 | tf_op jit(solution)/shard_map/all_to_all | solution.py:605
  255.7 51.7 %all-to-all-start.5 = ((f32[32,128,128]{2,1,0:T(8,128)}), f32[32,128,128]{2,1,0:T(8,128)S(1)}, u32[]{:S(2)}, u32[]{:S(2)}) async-start(f32[32,128,128]{2,1,0:T(8,128)} %bitcast.15), calls=%async_computation.5 | async-start | bytes 4194304 | tf_op jit(solution)/shard_map/all_to_all | solution.py:605

commit v16 on v15

--- a/solution.py
+++ b/solution.py
@@ -502,25 +502,35 @@
     )
 
 
-def first_kernel(count, rows_b, anchor_ref, table_ref, *refs):
-    ins, (real_ref, imag_ref) = refs[:-2], refs[-2:]
-    wide, sides, ranks, rows, lanes = ins[0].shape
-    length = real_ref.shape[2]
+def first_kernel(count, rows_b, joined, pieces, anchor_ref, table_in, *refs):
+    ins, (real_out, imag_out) = list(refs[:joined]), refs[joined : joined + 2]
+    table_ref, real_ref, imag_ref, first_ref, in_sems, out_sems = refs[joined + 2 :]
+    wide, sides, ranks, rows, lanes = ins[-1].shape
+    rows_c, _, length = real_ref.shape
     half = length // 2
     slots = lanes // rows_b
-    joined = len(ins)
-    steps = real_ref.shape[0] // (slots * joined)
+    steps = rows_c // (slots * joined) // pieces
+    table_copy = pltpu.make_async_copy(table_in, table_ref, in_sems.at[pieces])
+    table_copy.start()
+    in_copies = []
+    if joined == 2:
+        for piece in range(pieces):
+            at = pl.ds(piece * (rows // pieces), rows // pieces)
+            copy = pltpu.make_async_copy(
+                ins[0].at[:, :, :, at], first_ref.at[:, :, :, at], in_sems.at[piece]
+            )
+            copy.start()
+            in_copies.append(copy)
+        ins[0] = first_ref
+    table_copy.wait()
     spot_row = lax.broadcasted_iota(jnp.int32, (lanes, half), 0)
     spot_a = lax.broadcasted_iota(jnp.int32, (lanes, half), 1)
-    is_anchor = (anchor_ref[0] == 1) & (pl.program_id(0) == 0)
-    start = pl.program_id(0) * steps
-    anchor = (spot_row == 0) & (spot_a == 0) & is_anchor
+    anchor = (spot_row == 0) & (spot_a == 0) & (anchor_ref[0] == 1)
     upper = lax.broadcasted_iota(jnp.int32, (wide * ranks, joined * count, lanes), 1) < count
 
     def gathered(side, step, part):
         if joined == 2:
-            at = ((start + step) * 2 + part) * 2 * count
-            at = pl.ds(pl.multiple_of(at, 2 * count), 2 * count)
+            at = pl.ds((step * 2 + part) * 2 * count, 2 * count)
             own, other = [
                 ref[:, side, :, at].reshape(wide * ranks, 2 * count, lanes) for ref in ins
             ]
@@ -540,27 +550,42 @@
         )
         return [value.T]
 
-    sums = []
-    for side in range(sides):
-        tiles = [[gathered(side, step, part) for part in range(2)] for step in range(steps)]
-        left = jnp.concatenate(
-            [
-                jnp.concatenate([part[join] for part in parts], axis=1)
-                for parts in tiles
-                for join in range(joined)
-            ],
-            axis=0,
-        )
-        sums.append(product(split(left), pair(table_ref.at[side])))
-    even, odd = sums
-    for far, value in enumerate((even + odd, even - odd)):
-        columns = slice(far * half, (far + 1) * half)
-        for at in range(steps * joined):
-            for part, ref in enumerate((real_ref, imag_ref)):
-                here = value[at * lanes : (at + 1) * lanes, part * half : (part + 1) * half]
-                if at == 0 and far == 0:
-                    here = jnp.where(anchor, 0.0, here)
-                ref[at * slots : (at + 1) * slots, :, columns] = here.reshape(slots, rows_b, half)
+    out_copies = []
+    for piece in range(pieces):
+        if in_copies:
+            in_copies[piece].wait()
+        sums = []
+        for side in range(sides):
+            tiles = [
+                [gathered(side, piece * steps + step, part) for part in range(2)] for step in range(steps)
+            ]
+            left = jnp.concatenate(
+                [
+                    jnp.concatenate([part[join] for part in parts], axis=1)
+                    for parts in tiles
+                    for join in range(joined)
+                ],
+                axis=0,
+            )
+            sums.append(product(split(left), pair(table_ref.at[side])))
+        even, odd = sums
+        first = piece * steps * joined * slots
+        for far, value in enumerate((even + odd, even - odd)):
+            columns = slice(far * half, (far + 1) * half)
+            for at in range(steps * joined):
+                for part, ref in enumerate((real_ref, imag_ref)):
+                    here = value[at * lanes : (at + 1) * lanes, part * half : (part + 1) * half]
+                    if first + at == 0 and far == 0:
+                        here = jnp.where(anchor, 0.0, here)
+                    spots = slice(first + at * slots, first + (at + 1) * slots)
+                    ref[spots, :, columns] = here.reshape(slots, rows_b, half)
+        at = pl.ds(first, steps * joined * slots)
+        for part, (ref, out) in enumerate(((real_ref, real_out), (imag_ref, imag_out))):
+            copy = pltpu.make_async_copy(ref.at[at], out.at[at], out_sems.at[2 * piece + part])
+            copy.start()
+            out_copies.append(copy)
+    for copy in out_copies:
+        copy.wait()
 
 
 def first_table(length, devices, sides):
@@ -577,28 +602,44 @@
     ranks = devices // wide // sides
     rows_b = length // wide
     slots = lanes // rows_b
-    total = rows // (2 * joined * count) if joined == 2 else rows // (2 * count)
-    grid = 4 if joined == 2 and total % 4 == 0 else 1
+    total = rows // (2 * joined * count)
+    pieces = 4 if joined == 2 and total % 4 == 0 else 1
     parts = [part.reshape(wide, sides, ranks, rows, lanes) for part in parts]
 
     def body(*refs):
-        first_kernel(count, rows_b, *refs)
+        first_kernel(count, rows_b, joined, pieces, *refs)
 
     rows_c = total * joined * slots
-    out_shape = jax.ShapeDtypeStruct((rows_c, rows_b, length), jnp.float32)
+    out_shape = (rows_c, rows_b, length)
+    first_shape = parts[0].shape if joined == 2 else (8, TILE)
+    anywhere = pl.BlockSpec(memory_space=pl.ANY)
     return pl.pallas_call(
         body,
-        grid=(grid,),
+        grid=(1,),
         in_specs=[
             pl.BlockSpec(memory_space=pltpu.SMEM),
-            whole(table.shape),
-            *[whole((wide, sides, ranks, rows, lanes))] * joined,
-        ],
-        out_specs=[pl.BlockSpec((rows_c // grid, rows_b, length), lambda i: (i, 0, 0))] * 2,
-        out_shape=[out_shape] * 2,
+            anywhere,
+            *[anywhere] * (joined - 1),
+            whole(parts[-1].shape),
+        ],
+        out_specs=[anywhere] * 2,
+        out_shape=[pltpu.HBM(out_shape, jnp.float32)] * 2,
+        scratch_shapes=[
+            pltpu.VMEM(table.shape, table.dtype),
+            pltpu.VMEM(out_shape, jnp.float32),
+            pltpu.VMEM(out_shape, jnp.float32),
+            pltpu.VMEM(first_shape, jnp.float32),
+            pltpu.SemaphoreType.DMA((pieces + 1,)),
+            pltpu.SemaphoreType.DMA((2 * pieces,)),
+        ],
         compiler_params=params(1),
         cost_estimate=cost(rows_c * 2 * rows_b * length * length, 16 * rows_c * rows_b * length),
-    )(is_anchor, in_hbm(table), *[keep(part, pltpu.VMEM) for part in parts])
+    )(
+        is_anchor,
+        in_hbm(table),
+        *[in_hbm(part) for part in parts[:-1]],
+        keep(parts[-1], pltpu.VMEM),
+    )
 
 
 def transpose(value, members=None):

time: 314 us -> 314 us (level)
  no operation moved by 1% of the time
where the time goes in v16:
time: 314 us; the launch traced here: 313 us
  waiting for transfers between devices  125 us (40%)
  blocking collectives  119 us (38%)
  Pallas kernels  51.1 us (16%)
  starting transfers between devices  17.3 us (6%)
    all_to_all x4, waiting for transfers between devices, transpose(): lax.all_to_all(value, AXES, split_axis=0, concat_axis=0, tiled=True, axis...  125 us
    all_to_all x2, blocking collectives, transpose(): lax.all_to_all(value, AXES, split_axis=0, concat_axis=0, tiled=True, axis...  119 us
    pallas_call x2, Pallas kernels, shear_pass(): pl.pallas_call(body, grid=(6,), in_specs=[pl.BlockSpec((1, count * half,...  28.1 us
    all_to_all x4, starting transfers between devices, transpose(): lax.all_to_all(value, AXES, split_axis=0, concat_axis=0, tiled=True, axis...  17.3 us
    pallas_call x2, Pallas kernels, spectrum_pass(): pl.pallas_call(body, grid_spec=pltpu.PrefetchScalarGridSpec(num_scalar_pr...  12.5 us
  transfers between devices with their start and end apart: 4, of which 4 were waited for; matrix products, arithmetic and copies ran while one was open for 0% of the time, Pallas kernels for 12%

profile of v16, /device:TPU:1, one launch (start us, length us, event | category | flops | bytes accessed | tf_op | source)
XLA Modules:
  0.0 313.2 jit_solution(8605715263938121565)
XLA Ops:
  0.6 4.9 %shard_map.203 = (f32[8,2,2,6,32,128]{5,4,3,2,1,0:T(8,128)S(1)}, f32[8,2,2,2,32,128]{5,4,3,2,1,0:T(8,128)}) custom-call(bf16[2,256,256]{2,1,0:T(8,128)(2,1)} %constant.64.clone.refs_0_, f32[32,64,256]{2,1,0:T(8,128)} %refs_1_.4), custom_call_target="tpu_custom_call" | custom-call | flops 805306368 | bytes 6291456 | tf_op jit(solution)/shard_map/pallas_call | solution.py:114
  5.5 78.3 %all_to_all.30 = f32[32,6,32,128]{3,2,1,0:T(8,128)} all-to-all(f32[32,6,32,128]{3,2,1,0:T(8,128)S(1)} %bitcast.12), channel_id=1, replica_groups=mesh['wide'=8,'narrow'=4] {'wide','narrow'}, dimensions={0} | all-to-all | bytes 6291456 | tf_op jit(solution)/shard_map/all_to_all | solution.py:646
  83.8 3.2 %all-to-all-start.1 = ((f32[32,2,32,128]{3,2,1,0:T(8,128)}), f32[32,2,32,128]{3,2,1,0:T(8,128)S(1)}, u32[]{:S(2)}, u32[]{:S(2)}) async-start(f32[32,2,32,128]{3,2,1,0:T(8,128)} %bitcast.5), calls=%async_computation.1 | async-start | bytes 2097152 | tf_op jit(solution)/shard_map/all_to_all | solution.py:646
  87.0 9.3 %shard_map.204 = (f32[16,12,32,128]{3,2,1,0:T(8,128)}, f32[16,12,32,128]{3,2,1,0:T(8,128)}, f32[3,2,128,1]{3,2,1,0:T(8,128)S(1)}, f32[2,1,256]{2,1,0:T(1,128)S(1...) custom-call(s32[1]{0:T(128)} %bitcast.1.refs_0_, ...), custom_call_target="tpu_custom_call" | custom-call | flops 4227858432 | bytes 15728640 | tf_op jit(solution)/shard_map/pallas_call | solution.py:308
  96.3 17.1 %all-to-all-done.1 = f32[32,2,32,128]{3,2,1,0:T(8,128)S(1)} async-done(((f32[32,2,32,128]{3,2,1,0:T(8,128)}), f32[32,2,32,128]{3,2,1,0:T(8,128)S(1)}, u32[]{:S(2)}, u32[]{:S(2)}) %all-to-all-start.1) | async-done | bytes 1048608 | tf_op jit(solution)/shard_map/all_to_all | solution.py:646
  113.3 3.2 %shard_map.205 = (f32[16,12,32,128]{3,2,1,0:T(8,128)}, f32[16,12,32,128]{3,2,1,0:T(8,128)}) custom-call(s32[1]{0:T(128)} %bitcast.1.refs_0_, s32[1]{0:T(128)} %bitcast.2.refs_1_, f32[3,2,128,1]{3,2,1,0:T(8,128)S(1)} %get-tuple-element.14.refs_2_, f32[2,1,256]{2,1,0:T(1,128)S(1)} %get-tuple-element.15.refs_3_, ...), custom_call_target="tpu_custom_call", output_to_operand_aliasing={{0}: (8, {}), {1}: (9, {})} | custom-call | flops 1409286144 | bytes 5242880 | tf_op jit(solution)/shard_map/pallas_call | solution.py:308
  116.5 40.8 %all_to_all.31.refs_6_ = f32[16,12,32,128]{3,2,1,0:T(8,128)} all-to-all(f32[16,12,32,128]{3,2,1,0:T(8,128)} %get-tuple-element.22), channel_id=1, replica_groups={{0,1,4,5,8,9,12,13,16,17,20,21,24,25,28,29},{2,3,6,7,10,11,14,15,18,19,..., dimensions={0} | all-to-all | bytes 6291456 | tf_op jit(solution)/shard_map/all_to_all | solution.py:646
  157.4 5.3 %all-to-all-start.4 = ((f32[16,12,32,128]{3,2,1,0:T(8,128)}), f32[16,12,32,128]{3,2,1,0:T(8,128)S(1)}, u32[]{:S(2)}, u32[]{:S(2)}) async-start(f32[16,12,32,128]{3,2,1,0:T(8,128)} %get-tuple-element.23), calls=%async_computation.4 | async-start | bytes 6291456 | tf_op jit(solution)/shard_map/all_to_all | solution.py:646
  162.7 14.2 %shard_map.206 = f32[8,4,128,128]{3,2,1,0:T(8,128)} custom-call(f32[6,512,1]{2,1,0:T(8,128)} %constant.70.clone.refs_0_, f32[6,1,512]{2,1,0:T(1,128)} %constant.71.clone.refs_1_, bf16[2,2,256,256]{3,2,1,0:T(8,128)(2,1)} %constant.68.clone.refs_5_.refs_2_, bf16[2,256,256]{2,1,0:T(8,128)(2,1)} %constant.72.clone.refs_3_, ...), custom_call_target="tpu_custom_call" | custom-call | flops 7247757312 | bytes 7340032 | tf_op jit(solution)/shard_map/pallas_call | solution.py:485
  176.9 25.1 %all-to-all-done.4.refs_6_ = f32[16,12,32,128]{3,2,1,0:T(8,128)S(1)} async-done(((f32[16,12,32,128]{3,2,1,0:T(8,128)}), f32[16,12,32,128]{3,2,1,0:T(8,128)S(1)}, u32[]{:S(2)}, u32[]{:S(2)}) %all-to-all-start.4) | async-done | bytes 3145760 | tf_op jit(solution)/shard_map/all_to_all | solution.py:646
  202.1 5.3 %all-to-all-start.3 = ((f32[32,128,128]{2,1,0:T(8,128)}), f32[32,128,128]{2,1,0:T(8,128)}, u32[]{:S(2)}, u32[]{:S(2)}) async-start(f32[32,128,128]{2,1,0:T(8,128)} %bitcast.16), calls=%async_computation.3 | async-start | bytes 4194304 | tf_op jit(solution)/shard_map/all_to_all | solution.py:646
  207.4 13.9 %shard_map.207 = f32[8,4,128,128]{3,2,1,0:T(8,128)} custom-call(f32[6,512,1]{2,1,0:T(8,128)} %constant.75.clone.refs_0_, f32[6,1,512]{2,1,0:T(1,128)} %constant.71.clone.refs_1_, bf16[2,2,256,256]{3,2,1,0:T(8,128)(2,1)} %constant.68.clone.refs_5_.refs_2_, bf16[2,256,256]{2,1,0:T(8,128)(2,1)} %constant.76.clone.refs_3_, ...), custom_call_target="tpu_custom_call" | custom-call | flops 7247757312 | bytes 7340032 | tf_op jit(solution)/shard_map/pallas_call | solution.py:485
  221.3 34.4 %all-to-all-done.3 = f32[32,128,128]{2,1,0:T(8,128)} async-done(((f32[32,128,128]{2,1,0:T(8,128)}), f32[32,128,128]{2,1,0:T(8,128)}, u32[]{:S(2)}, u32[]{:S(2)}) %all-to-all-start.3) | async-done | bytes 2097184 | tf_op jit(solution)/shard_map/all_to_all | solution.py:646
  255.7 3.4 %all-to-all-start.5 = ((f32[32,128,128]{2,1,0:T(8,128)}), f32[32,128,128]{2,1,0:T(8,128)S(1)}, u32[]{:S(2)}, u32[]{:S(2)}) async-start(f32[32,128,128]{2,1,0:T(8,128)} %bitcast.15), calls=%async_computation.5 | async-start | bytes 4194304 | tf_op jit(solution)/shard_map/all_to_all | solution.py:646
  259.1 48.2 %all-to-all-done.5 = f32[32,128,128]{2,1,0:T(8,128)S(1)} async-done(((f32[32,128,128]{2,1,0:T(8,128)}), f32[32,128,128]{2,1,0:T(8,128)S(1)}, u32[]{:S(2)}, u32[]{:S(2)}) %all-to-all-start.5) | async-done | bytes 2097184 | tf_op jit(solution)/shard_map/all_to_all | solution.py:646
  307.4 5.6 %shard_map.208 = (f32[64,32,256]{2,1,0:T(8,128)}, f32[64,32,256]{2,1,0:T(8,128)}) custom-call(s32[1]{0:T(128)} %bitcast.refs_0_, bf16[2,2,256,256]{3,2,1,0:T(8,128)(2,1)} %constant.77.clone.refs_1_, f32[8,2,2,128,128]{4,3,2,1,0:T(8,128)} %bitcast.8.refs_2_, f32[8,2,2,128,128]{4,3,2,1,0:T(8,128)S(1)} %bitcast.13), custom_call_target="tpu_custom_call" | custom-call | flops 1610612736 | bytes 8388608 | tf_op jit(solution)/shard_map/pallas_call | solution.py:616
Async XLA Ops:
  83.8 29.5 %all-to-all-start.1 = ((f32[32,2,32,128]{3,2,1,0:T(8,128)}), f32[32,2,32,128]{3,2,1,0:T(8,128)S(1)}, u32[]{:S(2)}, u32[]{:S(2)}) async-start(f32[32,2,32,128]{3,2,1,0:T(8,128)} %bitcast.5), calls=%async_computation.1 | async-start | bytes 2097152 | tf_op jit(solution)/shard_map/all_to_all | solution.py:646
  157.4 44.7 %all-to-all-start.4 = ((f32[16,12,32,128]{3,2,1,0:T(8,128)}), f32[16,12,32,128]{3,2,1,0:T(8,128)S(1)}, u32[]{:S(2)}, u32[]{:S(2)}) async-start(f32[16,12,32,128]{3,2,1,0:T(8,128)} %get-tuple-element.23), calls=%async_computation.4 | async-start | bytes 6291456 | tf_op jit(solution)/shard_map/all_to_all | solution.py:646
  202.1 53.6 %all-to-all-start.3 = ((f32[32,128,128]{2,1,0:T(8,128)}), f32[32,128,128]{2,1,0:T(8,128)}, u32[]{:S(2)}, u32[]{:S(2)}) async-start(f32[32,128,128]{2,1,0:T(8,128)} %bitcast.16), calls=%async_computation.3 | async-start | bytes 4194304 | tf_op jit(solution)/shard_map/all_to_all | solution.py:646
  255.7 51.7 %all-to-all-start.5 = ((f32[32,128,128]{2,1,0:T(8,128)}), f32[32,128,128]{2,1,0:T(8,128)S(1)}, u32[]{:S(2)}, u32[]{:S(2)}) async-start(f32[32,128,128]{2,1,0:T(8,128)} %bitcast.15), calls=%async_computation.5 | async-start | bytes 4194304 | tf_op jit(solution)/shard_map/all_to_all | solution.py:646

commit v17 on v16

--- a/solution.py
+++ b/solution.py
@@ -71,32 +71,53 @@
     return pl.CostEstimate(flops=6 * macs, bytes_accessed=moved, transcendentals=0)
 
 
-def third_kernel(counts, table_ref, density_ref, *outs):
-    step_x, rows_y, length = density_ref.shape
-    wide, sides, ranks, _, rows_x, _ = outs[0].shape
+def third_kernel(counts, pieces, table_in, density_in, *refs):
+    outs, (table_ref, density_ref, second_ref, in_sems, out_sems) = refs[:-5], refs[-5:]
+    rows_x, rows_y, length = density_ref.shape
+    wide, sides, ranks = outs[0].shape[:3]
+    step_x = rows_x // pieces
     half = length // 2
-    flats = [ref.reshape(math.prod(ref.shape[:5]), 2 * rows_y) for ref in outs]
+    table_copy = pltpu.make_async_copy(table_in, table_ref, in_sems.at[pieces])
+    table_copy.start()
+    in_copies = []
+    for piece in range(pieces):
+        at = pl.ds(piece * step_x, step_x)
+        copy = pltpu.make_async_copy(density_in.at[at], density_ref.at[at], in_sems.at[piece])
+        copy.start()
+        in_copies.append(copy)
+    table_copy.wait()
     table = pair(table_ref)
-    group = step_x
-    start_x = pl.program_id(0) * step_x
-    for first in range(0, step_x, group):
-        block = density_ref[first : first + group].reshape(group * rows_y, length)
+    targets = [outs[0], second_ref][: len(counts)]
+    flats = [ref.reshape(math.prod(ref.shape[:5]), 2 * rows_y) for ref in targets]
+    out_copies = []
+    for piece in range(pieces):
+        in_copies[piece].wait()
+        first = piece * step_x
+        block = density_ref[first : first + step_x].reshape(step_x * rows_y, length)
         result = product(split(block), table)
-        for inner in range(group):
+        for inner in range(step_x):
             rows = slice(inner * rows_y, (inner + 1) * rows_y)
             value = jnp.concatenate([result[rows, :half], result[rows, half:]], axis=0).T
             start = 0
             for flat, count in zip(flats, counts):
                 for c in range(count):
                     for rank in range(ranks):
-                        at = (rank * count + c) * rows_x + first + inner + start_x
+                        at = (rank * count + c) * rows_x + first + inner
                         stride = sides * ranks * count * rows_x
                         flat[pl.ds(at, wide, stride=stride), :] = value[start : start + wide]
                         start += wide
-    for ref in outs:
-        rows = pl.ds(pl.multiple_of(start_x, step_x), step_x)
-        for side in range(1, sides):
-            ref[:, side, :, :, rows] = ref[:, 0, :, :, rows]
+        rows = pl.ds(first, step_x)
+        for ref in targets[::-1]:
+            for side in range(1, sides):
+                ref[:, side, :, :, rows] = ref[:, 0, :, :, rows]
+            if ref is second_ref:
+                copy = pltpu.make_async_copy(
+                    ref.at[:, :, :, :, rows], outs[1].at[:, :, :, :, rows], out_sems.at[piece]
+                )
+                copy.start()
+                out_copies.append(copy)
+    for copy in out_copies:
+        copy.wait()
 
 
 def third_pass(density, wide, sides, ranks, counts):
@@ -106,24 +127,28 @@
     order = np.arange(half).reshape(wide, ranks, per_c).transpose(2, 1, 0).reshape(-1)
     angle = angles(np.arange(length), order, length)
     table = split_table(np.concatenate([np.cos(angle), -np.sin(angle)], axis=1))
-    step = max(rows_x // 2, min(8, rows_x))
+    pieces = max(1, rows_x // 8)
+    shapes = [(wide, sides, ranks, count, rows_x, 2 * rows_y) for count in counts]
+    anywhere = pl.BlockSpec(memory_space=pl.ANY)
 
     def body(*refs):
-        third_kernel(counts, *refs)
+        third_kernel(counts, pieces, *refs)
 
     return pl.pallas_call(
         body,
-        grid=(rows_x // step,),
-        in_specs=[
-            whole(table.shape),
-            pl.BlockSpec((step, rows_y, length), lambda i: (i, 0, 0)),
+        grid=(1,),
+        in_specs=[anywhere] * 2,
+        out_specs=[whole(shapes[0])] + [anywhere] * (len(counts) - 1),
+        out_shape=[
+            (pltpu.HBM if spot else pltpu.VMEM)(shape, jnp.float32)
+            for spot, shape in enumerate(shapes)
         ],
-        out_specs=[
-            whole((wide, sides, ranks, count, rows_x, 2 * rows_y)) for count in counts
-        ],
-        out_shape=[
-            pltpu.VMEM((wide, sides, ranks, count, rows_x, 2 * rows_y), jnp.float32)
-            for count in counts
+        scratch_shapes=[
+            pltpu.VMEM(table.shape, table.dtype),
+            pltpu.VMEM(density.shape, jnp.float32),
+            pltpu.VMEM(shapes[1] if len(counts) == 2 else (8, TILE), jnp.float32),
+            pltpu.SemaphoreType.DMA((pieces + 1,)),
+            pltpu.SemaphoreType.DMA((pieces,)),
         ],
         compiler_params=params(1),
         cost_estimate=cost(density.size * length, 12 * density.size),
@@ -510,8 +535,13 @@
     half = length // 2
     slots = lanes // rows_b
     steps = rows_c // (slots * joined) // pieces
-    table_copy = pltpu.make_async_copy(table_in, table_ref, in_sems.at[pieces])
-    table_copy.start()
+    table_copies = []
+    for join in range(joined):
+        copy = pltpu.make_async_copy(
+            table_in.at[join], table_ref.at[join], in_sems.at[pieces + join]
+        )
+        copy.start()
+        table_copies.append(copy)
     in_copies = []
     if joined == 2:
         for piece in range(pieces):
@@ -522,7 +552,8 @@
             copy.start()
             in_copies.append(copy)
         ins[0] = first_ref
-    table_copy.wait()
+    for copy in table_copies:
+        copy.wait()
     spot_row = lax.broadcasted_iota(jnp.int32, (lanes, half), 0)
     spot_a = lax.broadcasted_iota(jnp.int32, (lanes, half), 1)
     anchor = (spot_row == 0) & (spot_a == 0) & (anchor_ref[0] == 1)
@@ -534,7 +565,7 @@
             own, other = [
                 ref[:, side, :, at].reshape(wide * ranks, 2 * count, lanes) for ref in ins
             ]
-            both = jnp.where(upper, own, other), pltpu.roll(jnp.where(upper, other, own), count, 1)
+            both = jnp.where(upper, own, other), jnp.where(upper, other, own)
             return [value.reshape(half, lanes).T for value in both]
         flat = ins[0].reshape(wide * sides * ranks * rows, lanes)
         run = rows // count
@@ -554,31 +585,35 @@
     for piece in range(pieces):
         if in_copies:
             in_copies[piece].wait()
-        sums = []
-        for side in range(sides):
-            tiles = [
-                [gathered(side, piece * steps + step, part) for part in range(2)] for step in range(steps)
+        tiles = [
+            [
+                [gathered(side, piece * steps + step, part) for part in range(2)]
+                for step in range(steps)
             ]
-            left = jnp.concatenate(
-                [
-                    jnp.concatenate([part[join] for part in parts], axis=1)
-                    for parts in tiles
-                    for join in range(joined)
-                ],
-                axis=0,
-            )
-            sums.append(product(split(left), pair(table_ref.at[side])))
-        even, odd = sums
+            for side in range(sides)
+        ]
         first = piece * steps * joined * slots
-        for far, value in enumerate((even + odd, even - odd)):
-            columns = slice(far * half, (far + 1) * half)
-            for at in range(steps * joined):
-                for part, ref in enumerate((real_ref, imag_ref)):
-                    here = value[at * lanes : (at + 1) * lanes, part * half : (part + 1) * half]
-                    if first + at == 0 and far == 0:
-                        here = jnp.where(anchor, 0.0, here)
-                    spots = slice(first + at * slots, first + (at + 1) * slots)
-                    ref[spots, :, columns] = here.reshape(slots, rows_b, half)
+        for join in range(joined):
+            sums = []
+            for side in range(sides):
+                left = jnp.concatenate(
+                    [
+                        jnp.concatenate([part[join] for part in parts], axis=1)
+                        for parts in tiles[side]
+                    ],
+                    axis=0,
+                )
+                sums.append(product(split(left), pair(table_ref.at[join, side])))
+            even, odd = sums
+            for far, value in enumerate((even + odd, even - odd)):
+                columns = slice(far * half, (far + 1) * half)
+                for step in range(steps):
+                    for part, ref in enumerate((real_ref, imag_ref)):
+                        here = value[step * lanes : (step + 1) * lanes, part * half : (part + 1) * half]
+                        at = first + (step * joined + join) * slots
+                        if at == 0 and far == 0:
+                            here = jnp.where(anchor, 0.0, here)
+                        ref[at : at + slots, :, columns] = here.reshape(slots, rows_b, half)
         at = pl.ds(first, steps * joined * slots)
         for part, (ref, out) in enumerate(((real_ref, real_out), (imag_ref, imag_out))):
             copy = pltpu.make_async_copy(ref.at[at], out.at[at], out_sems.at[2 * piece + part])
@@ -588,12 +623,16 @@
         copy.wait()
 
 
-def first_table(length, devices, sides):
+def first_table(length, devices, joined, count, sides):
     scale = 1.0 / float(length) ** 1.5
-    order = np.arange(length).reshape(devices, -1, sides).transpose(2, 0, 1).reshape(sides, -1)
-    return np.stack(
-        [split_table(scale * turn(-angles(np.arange(length // 2), x, length)).T) for x in order]
-    )
+    index = np.arange(length).reshape(devices, joined, count, sides)
+    tables = []
+    for join in range(joined):
+        order = index[:, :: 1 - 2 * join].transpose(3, 0, 1, 2).reshape(sides, -1)
+        tables.append(
+            [split_table(scale * turn(-angles(np.arange(length // 2), x, length)).T) for x in order]
+        )
+    return np.stack([np.stack(each) for each in tables])
 
 
 def first_pass(parts, table, is_anchor, length, wide, sides, count):
@@ -629,7 +668,7 @@
             pltpu.VMEM(out_shape, jnp.float32),
             pltpu.VMEM(out_shape, jnp.float32),
             pltpu.VMEM(first_shape, jnp.float32),
-            pltpu.SemaphoreType.DMA((pieces + 1,)),
+            pltpu.SemaphoreType.DMA((pieces + joined,)),
             pltpu.SemaphoreType.DMA((2 * pieces,)),
         ],
         compiler_params=params(1),
@@ -681,7 +720,7 @@
             start += count
         is_anchor = ((spot_wide == 0) & (spot_narrow == 0)).astype(jnp.int32).reshape(1)
         parts = []
-        table = first_table(length, devices, sides)
+        table = first_table(length, devices, groups, slab // groups, sides)
         for group, chunk in enumerate(chunks):
             received = keep(transpose(chunk, members), pltpu.VMEM if group else pltpu.HBM)
             (part,) = shear_pass(received, wide, narrow, per_c, group, groups)

time: 314 us -> 314 us (level)
  no operation moved by 1% of the time
where the time goes in v17:
time: 314 us
  waiting for transfers between devices  125 us (40%)
  blocking collectives  119 us (38%)
  Pallas kernels  51.7 us (16%)
  starting transfers between devices  17.3 us (6%)
    all_to_all x4, waiting for transfers between devices, transpose(): lax.all_to_all(value, AXES, split_axis=0, concat_axis=0, tiled=True, axis...  125 us
    all_to_all x2, blocking collectives, transpose(): lax.all_to_all(value, AXES, split_axis=0, concat_axis=0, tiled=True, axis...  119 us
    pallas_call x2, Pallas kernels, shear_pass(): pl.pallas_call(body, grid=(6,), in_specs=[pl.BlockSpec((1, count * half,...  28.1 us
    all_to_all x4, starting transfers between devices, transpose(): lax.all_to_all(value, AXES, split_axis=0, concat_axis=0, tiled=True, axis...  17.3 us
    pallas_call x2, Pallas kernels, spectrum_pass(): pl.pallas_call(body, grid_spec=pltpu.PrefetchScalarGridSpec(num_scalar_pr...  12.5 us
  transfers between devices with their start and end apart: 4, of which 4 were waited for; matrix products, arithmetic and copies ran while one was open for 0% of the time, Pallas kernels for 12%

profile of v17, /device:TPU:1, one launch (start us, length us, event | category | flops | bytes accessed | tf_op | source)
XLA Modules:
  0.0 313.8 jit_solution(17301386592556442710)
XLA Ops:
  0.6 5.8 %shard_map.203 = (f32[8,2,2,6,32,128]{5,4,3,2,1,0:T(8,128)S(1)}, f32[8,2,2,2,32,128]{5,4,3,2,1,0:T(8,128)}) custom-call(bf16[2,256,256]{2,1,0:T(8,128)(2,1)} %constant.64.clone.refs_0_, f32[32,64,256]{2,1,0:T(8,128)} %refs_1_.4), custom_call_target="tpu_custom_call" | custom-call | flops 805306368 | bytes 6291456 | tf_op jit(solution)/shard_map/pallas_call | solution.py:137
  6.4 78.3 %all_to_all.30 = f32[32,6,32,128]{3,2,1,0:T(8,128)} all-to-all(f32[32,6,32,128]{3,2,1,0:T(8,128)S(1)} %bitcast.12), channel_id=1, replica_groups=mesh['wide'=8,'narrow'=4] {'wide','narrow'}, dimensions={0} | all-to-all | bytes 6291456 | tf_op jit(solution)/shard_map/all_to_all | solution.py:685
  84.8 3.2 %all-to-all-start.1 = ((f32[32,2,32,128]{3,2,1,0:T(8,128)}), f32[32,2,32,128]{3,2,1,0:T(8,128)S(1)}, u32[]{:S(2)}, u32[]{:S(2)}) async-start(f32[32,2,32,128]{3,2,1,0:T(8,128)} %bitcast.5), calls=%async_computation.1 | async-start | bytes 2097152 | tf_op jit(solution)/shard_map/all_to_all | solution.py:685
  87.9 9.3 %shard_map.204 = (f32[16,12,32,128]{3,2,1,0:T(8,128)}, f32[16,12,32,128]{3,2,1,0:T(8,128)}, f32[3,2,128,1]{3,2,1,0:T(8,128)S(1)}, f32[2,1,256]{2,1,0:T(1,128)S(1...) custom-call(s32[1]{0:T(128)} %bitcast.1.refs_0_, ...), custom_call_target="tpu_custom_call" | custom-call | flops 4227858432 | bytes 15728640 | tf_op jit(solution)/shard_map/pallas_call | solution.py:333
  97.2 17.1 %all-to-all-done.1 = f32[32,2,32,128]{3,2,1,0:T(8,128)S(1)} async-done(((f32[32,2,32,128]{3,2,1,0:T(8,128)}), f32[32,2,32,128]{3,2,1,0:T(8,128)S(1)}, u32[]{:S(2)}, u32[]{:S(2)}) %all-to-all-start.1) | async-done | bytes 1048608 | tf_op jit(solution)/shard_map/all_to_all | solution.py:685
  114.3 3.2 %shard_map.205 = (f32[16,12,32,128]{3,2,1,0:T(8,128)}, f32[16,12,32,128]{3,2,1,0:T(8,128)}) custom-call(s32[1]{0:T(128)} %bitcast.1.refs_0_, s32[1]{0:T(128)} %bitcast.2.refs_1_, f32[3,2,128,1]{3,2,1,0:T(8,128)S(1)} %get-tuple-element.14.refs_2_, f32[2,1,256]{2,1,0:T(1,128)S(1)} %get-tuple-element.15.refs_3_, ...), custom_call_target="tpu_custom_call", output_to_operand_aliasing={{0}: (8, {}), {1}: (9, {})} | custom-call | flops 1409286144 | bytes 5242880 | tf_op jit(solution)/shard_map/pallas_call | solution.py:333
  117.5 40.8 %all_to_all.31.refs_6_ = f32[16,12,32,128]{3,2,1,0:T(8,128)} all-to-all(f32[16,12,32,128]{3,2,1,0:T(8,128)} %get-tuple-element.22), channel_id=1, replica_groups={{0,1,4,5,8,9,12,13,16,17,20,21,24,25,28,29},{2,3,6,7,10,11,14,15,18,19,..., dimensions={0} | all-to-all | bytes 6291456 | tf_op jit(solution)/shard_map/all_to_all | solution.py:685
  158.3 5.4 %all-to-all-start.4 = ((f32[16,12,32,128]{3,2,1,0:T(8,128)}), f32[16,12,32,128]{3,2,1,0:T(8,128)S(1)}, u32[]{:S(2)}, u32[]{:S(2)}) async-start(f32[16,12,32,128]{3,2,1,0:T(8,128)} %get-tuple-element.23), calls=%async_computation.4 | async-start | bytes 6291456 | tf_op jit(solution)/shard_map/all_to_all | solution.py:685
  163.6 14.2 %shard_map.206 = f32[8,4,128,128]{3,2,1,0:T(8,128)} custom-call(f32[6,512,1]{2,1,0:T(8,128)} %constant.70.clone.refs_0_, f32[6,1,512]{2,1,0:T(1,128)} %constant.71.clone.refs_1_, bf16[2,2,256,256]{3,2,1,0:T(8,128)(2,1)} %constant.68.clone.refs_5_.refs_2_, bf16[2,256,256]{2,1,0:T(8,128)(2,1)} %constant.72.clone.refs_3_, ...), custom_call_target="tpu_custom_call" | custom-call | flops 7247757312 | bytes 7340032 | tf_op jit(solution)/shard_map/pallas_call | solution.py:510
  177.9 25.1 %all-to-all-done.4.refs_6_ = f32[16,12,32,128]{3,2,1,0:T(8,128)S(1)} async-done(((f32[16,12,32,128]{3,2,1,0:T(8,128)}), f32[16,12,32,128]{3,2,1,0:T(8,128)S(1)}, u32[]{:S(2)}, u32[]{:S(2)}) %all-to-all-start.4) | async-done | bytes 3145760 | tf_op jit(solution)/shard_map/all_to_all | solution.py:685
  203.0 5.3 %all-to-all-start.3 = ((f32[32,128,128]{2,1,0:T(8,128)}), f32[32,128,128]{2,1,0:T(8,128)}, u32[]{:S(2)}, u32[]{:S(2)}) async-start(f32[32,128,128]{2,1,0:T(8,128)} %bitcast.16), calls=%async_computation.3 | async-start | bytes 4194304 | tf_op jit(solution)/shard_map/all_to_all | solution.py:685
  208.3 13.9 %shard_map.207 = f32[8,4,128,128]{3,2,1,0:T(8,128)} custom-call(f32[6,512,1]{2,1,0:T(8,128)} %constant.75.clone.refs_0_, f32[6,1,512]{2,1,0:T(1,128)} %constant.71.clone.refs_1_, bf16[2,2,256,256]{3,2,1,0:T(8,128)(2,1)} %constant.68.clone.refs_5_.refs_2_, bf16[2,256,256]{2,1,0:T(8,128)(2,1)} %constant.76.clone.refs_3_, ...), custom_call_target="tpu_custom_call" | custom-call | flops 7247757312 | bytes 7340032 | tf_op jit(solution)/shard_map/pallas_call | solution.py:510
  222.2 34.4 %all-to-all-done.3 = f32[32,128,128]{2,1,0:T(8,128)} async-done(((f32[32,128,128]{2,1,0:T(8,128)}), f32[32,128,128]{2,1,0:T(8,128)}, u32[]{:S(2)}, u32[]{:S(2)}) %all-to-all-start.3) | async-done | bytes 2097184 | tf_op jit(solution)/shard_map/all_to_all | solution.py:685
  256.6 3.4 %all-to-all-start.5 = ((f32[32,128,128]{2,1,0:T(8,128)}), f32[32,128,128]{2,1,0:T(8,128)S(1)}, u32[]{:S(2)}, u32[]{:S(2)}) async-start(f32[32,128,128]{2,1,0:T(8,128)} %bitcast.15), calls=%async_computation.5 | async-start | bytes 4194304 | tf_op jit(solution)/shard_map/all_to_all | solution.py:685
  260.1 48.2 %all-to-all-done.5 = f32[32,128,128]{2,1,0:T(8,128)S(1)} async-done(((f32[32,128,128]{2,1,0:T(8,128)}), f32[32,128,128]{2,1,0:T(8,128)S(1)}, u32[]{:S(2)}, u32[]{:S(2)}) %all-to-all-start.5) | async-done | bytes 2097184 | tf_op jit(solution)/shard_map/all_to_all | solution.py:685
  308.3 5.3 %shard_map.208 = (f32[64,32,256]{2,1,0:T(8,128)}, f32[64,32,256]{2,1,0:T(8,128)}) custom-call(s32[1]{0:T(128)} %bitcast.refs_0_, bf16[2,2,2,256,256]{4,3,2,1,0:T(8,128)(2,1)} %constant.77.clone.refs_1_, f32[8,2,2,128,128]{4,3,2,1,0:T(8,128)} %bitcast.8.refs_2_, f32[8,2,2,128,128]{4,3,2,1,0:T(8,128)S(1)} %bitcast.13), custom_call_target="tpu_custom_call" | custom-call | flops 1610612736 | bytes 8388608 | tf_op jit(solution)/shard_map/pallas_call | solution.py:655
Async XLA Ops:
  84.8 29.5 %all-to-all-start.1 = ((f32[32,2,32,128]{3,2,1,0:T(8,128)}), f32[32,2,32,128]{3,2,1,0:T(8,128)S(1)}, u32[]{:S(2)}, u32[]{:S(2)}) async-start(f32[32,2,32,128]{3,2,1,0:T(8,128)} %bitcast.5), calls=%async_computation.1 | async-start | bytes 2097152 | tf_op jit(solution)/shard_map/all_to_all | solution.py:685
  158.3 44.7 %all-to-all-start.4 = ((f32[16,12,32,128]{3,2,1,0:T(8,128)}), f32[16,12,32,128]{3,2,1,0:T(8,128)S(1)}, u32[]{:S(2)}, u32[]{:S(2)}) async-start(f32[16,12,32,128]{3,2,1,0:T(8,128)} %get-tuple-element.23), calls=%async_computation.4 | async-start | bytes 6291456 | tf_op jit(solution)/shard_map/all_to_all | solution.py:685
  203.0 53.6 %all-to-all-start.3 = ((f32[32,128,128]{2,1,0:T(8,128)}), f32[32,128,128]{2,1,0:T(8,128)}, u32[]{:S(2)}, u32[]{:S(2)}) async-start(f32[32,128,128]{2,1,0:T(8,128)} %bitcast.16), calls=%async_computation.3 | async-start | bytes 4194304 | tf_op jit(solution)/shard_map/all_to_all | solution.py:685
  256.6 51.7 %all-to-all-start.5 = ((f32[32,128,128]{2,1,0:T(8,128)}), f32[32,128,128]{2,1,0:T(8,128)S(1)}, u32[]{:S(2)}, u32[]{:S(2)}) async-start(f32[32,128,128]{2,1,0:T(8,128)} %bitcast.15), calls=%async_computation.5 | async-start | bytes 4194304 | tf_op jit(solution)/shard_map/all_to_all | solution.py:685

commit v18 on v11

--- a/solution.py
+++ b/solution.py
@@ -9,7 +9,7 @@
 from jax.experimental.pallas import tpu as pltpu
 from jax.sharding import PartitionSpec as P
 
-AXES = ("wide", "narrow")
+AXES = ("narrow", "wide")
 TILE = 128
 LIMIT = 16 * 1024 * 1024
 
@@ -73,7 +73,7 @@
 
 def third_kernel(counts, table_ref, density_ref, *outs):
     step_x, rows_y, length = density_ref.shape
-    wide, sides, ranks, _, rows_x, _ = outs[0].shape
+    sides, ranks, wide, _, rows_x, _ = outs[0].shape
     half = length // 2
     flats = [ref.reshape(math.prod(ref.shape[:5]), 2 * rows_y) for ref in outs]
     table = pair(table_ref)
@@ -89,14 +89,14 @@
             for flat, count in zip(flats, counts):
                 for c in range(count):
                     for rank in range(ranks):
-                        at = (rank * count + c) * rows_x + first + inner + start_x
-                        stride = sides * ranks * count * rows_x
+                        at = (rank * wide * count + c) * rows_x + first + inner + start_x
+                        stride = count * rows_x
                         flat[pl.ds(at, wide, stride=stride), :] = value[start : start + wide]
                         start += wide
     for ref in outs:
         rows = pl.ds(pl.multiple_of(start_x, step_x), step_x)
         for side in range(1, sides):
-            ref[:, side, :, :, rows] = ref[:, 0, :, :, rows]
+            ref[side, :, :, :, rows] = ref[0, :, :, :, rows]
 
 
 def third_pass(density, wide, sides, ranks, counts):
@@ -119,10 +119,10 @@
             pl.BlockSpec((step, rows_y, length), lambda i: (i, 0, 0)),
         ],
         out_specs=[
-            whole((wide, sides, ranks, count, rows_x, 2 * rows_y)) for count in counts
+            whole((sides, ranks, wide, count, rows_x, 2 * rows_y)) for count in counts
         ],
         out_shape=[
-            pltpu.VMEM((wide, sides, ranks, count, rows_x, 2 * rows_y), jnp.float32)
+            pltpu.VMEM((sides, ranks, wide, count, rows_x, 2 * rows_y), jnp.float32)
             for count in counts
         ],
         compiler_params=params(1),
@@ -150,7 +150,7 @@
     a_ref, b_ref, second_ref, first_ref, back_ref = tables
     hand_on(tables, outs[groups:])
     outs = outs[:groups]
-    wide, narrow, _, rows_x, lanes = in_ref.shape
+    narrow, wide, _, rows_x, lanes = in_ref.shape
     length = wide * rows_x
     half = length // 2
     quarter = half // 2
@@ -159,7 +159,7 @@
     sign_back = 1.0 - 2.0 * side_ref[0].astype(jnp.float32)
 
     def column(c, n):
-        return in_ref[:, n, c].reshape(length, lanes)
+        return in_ref[n, :, c].reshape(length, lanes)
 
     def columns(numbers):
         return jnp.concatenate(
@@ -256,7 +256,7 @@
 
 
 def spectrum_pass(received, side, start_c, devices, groups, steps, first_step, filled, carried):
-    wide, narrow, per_c, rows_x, lanes = received.shape
+    narrow, wide, per_c, rows_x, lanes = received.shape
     length = wide * rows_x
     rows_y = lanes // 2
     half = length // 2
@@ -313,7 +313,7 @@
             in_specs=[
                 *table_specs,
                 last_spec,
-                pl.BlockSpec((wide, narrow, PAIR, rows_x, lanes), lambda i, *_: (0, 0, i, 0, 0)),
+                pl.BlockSpec((narrow, wide, PAIR, rows_x, lanes), lambda i, *_: (0, 0, i, 0, 0)),
                 *[pl.BlockSpec(memory_space=pl.ANY)] * len(filled),
             ],
             out_specs=[pl.BlockSpec(block, lambda i, *_: (0, 0, first_step + i, 0))] * groups
@@ -405,7 +405,7 @@
             axis=0,
         )
         value = product(pair(last_ref), split(ahead))
-        wide, narrow, message_out, _ = out_ref.shape
+        narrow, wide, message_out, _ = out_ref.shape
         rows_b = length // wide
         slots = tile // rows_b
         rows = 2 * length // slots
@@ -427,7 +427,7 @@
                         for join in range(joined):
                             start = ((n * 2 + part) * joined + join) * run
                             piece = moved[start : start + run]
-                            at = (w * narrow + n) * message_out
+                            at = (n * wide + w) * message_out
                             if joined == 2:
                                 at += part * 2 * count + (join ^ group) * count + x
                                 out[pl.ds(at, run, stride=4 * count), :] = piece
@@ -476,7 +476,7 @@
         [one_lane, wave_lanes, one_lane, wave_lanes**2, wave_lanes, one_lane]
     ).astype(np.float32)[:, None, :]
     tables = [second] + [split_table(table) for table in (third, ahead, last)]
-    out_shape = (wide, narrow, count * 2 * length // (narrow * slots), TILE)
+    out_shape = (narrow, wide, count * 2 * length // (narrow * slots), TILE)
 
     def body(*refs):
         shear_kernel(per_c, group, joined, *refs)
@@ -509,7 +509,7 @@
 
 def first_kernel(count, rows_b, anchor_ref, table_ref, *refs):
     ins, (real_ref, imag_ref) = refs[:-2], refs[-2:]
-    wide, sides, ranks, rows, lanes = ins[0].shape
+    sides, ranks, wide, rows, lanes = ins[0].shape
     length = real_ref.shape[2]
     half = length // 2
     slots = lanes // rows_b
@@ -527,22 +527,14 @@
             at = ((start + step) * 2 + part) * 2 * count
             at = pl.ds(pl.multiple_of(at, 2 * count), 2 * count)
             own, other = [
-                ref[:, side, :, at].reshape(wide * ranks, 2 * count, lanes) for ref in ins
+                ref[side, :, :, at].reshape(wide * ranks, 2 * count, lanes) for ref in ins
             ]
             both = [jnp.where(upper, own, other), jnp.where(upper, other, own)]
             return [value.reshape(half, lanes).T for value in both]
         flat = ins[0].reshape(wide * sides * ranks * rows, lanes)
         run = rows // count
-        value = jnp.concatenate(
-            [
-                flat[
-                    pl.ds((w * sides + side) * ranks * rows + part * steps + step, ranks * count, stride=run),
-                    :,
-                ]
-                for w in range(wide)
-            ],
-            axis=0,
-        )
+        start_row = side * ranks * wide * rows + part * steps + step
+        value = flat[pl.ds(start_row, ranks * wide * count, stride=run), :]
         return [value.T]
 
     lefts = []
@@ -572,9 +564,10 @@
                     ref[at : at + slots, :, columns] = here.reshape(slots, rows_b, half)
 
 
-def first_table(length, devices, joined, count, sides):
+def first_table(length, wide, ranks, joined, count, sides):
     scale = 1.0 / float(length) ** 1.5
-    index = np.arange(length).reshape(devices, joined, count, sides)
+    index = np.arange(length).reshape(wide, ranks, joined, count, sides)
+    index = index.swapaxes(0, 1).reshape(wide * ranks, joined, count, sides)
     tables = []
     for join in range(joined):
         order = index[:, :: 1 - 2 * join].transpose(3, 0, 1, 2).reshape(sides, -1)
@@ -592,7 +585,7 @@
     slots = lanes // rows_b
     total = rows // (2 * joined * count) if joined == 2 else rows // (2 * count)
     grid = 4 if joined == 2 and total % 4 == 0 else 1
-    parts = [part.reshape(wide, sides, ranks, rows, lanes) for part in parts]
+    parts = [part.reshape(sides, ranks, wide, rows, lanes) for part in parts]
 
     def body(*refs):
         first_kernel(count, rows_b, *refs)
@@ -605,7 +598,7 @@
         in_specs=[
             pl.BlockSpec(memory_space=pltpu.SMEM),
             whole(table.shape),
-            *[whole((wide, sides, ranks, rows, lanes))] * joined,
+            *[whole((sides, ranks, wide, rows, lanes))] * joined,
         ],
         out_specs=[pl.BlockSpec((rows_c // grid, rows_b, length), lambda i: (i, 0, 0))] * 2,
         out_shape=[out_shape] * 2,
@@ -626,7 +619,7 @@
     ranks = narrow // sides
     devices = wide * ranks
     members = [
-        [w * narrow + side * ranks + rank for w in range(wide) for rank in range(ranks)]
+        [(side * ranks + rank) * wide + w for w in range(wide) for rank in range(ranks)]
         for side in range(sides)
     ]
 
@@ -645,7 +638,7 @@
         chunks, carried, start = [], [], 0
         for planes, count in zip(third_pass(density, wide, sides, ranks, counts), counts):
             planes = transpose(planes.reshape(wide * narrow, count, rows_x, 2 * rows_y))
-            planes = planes.reshape(wide, narrow, count, rows_x, 2 * rows_y)
+            planes = planes.reshape(narrow, wide, count, rows_x, 2 * rows_y)
             planes = keep(planes, pltpu.VMEM if start else pltpu.HBM)
             chunks, carried = spectrum_pass(
                 planes, side, start_c, devices, groups, steps, start // PAIR, chunks, carried
@@ -653,7 +646,7 @@
             start += count
         is_anchor = ((spot_wide == 0) & (spot_narrow == 0)).astype(jnp.int32).reshape(1)
         parts = []
-        table = first_table(length, devices, groups, slab // groups, sides)
+        table = first_table(length, wide, ranks, groups, slab // groups, sides)
         for group, chunk in enumerate(chunks):
             carry = [table] if group == groups - 1 else []
             received = keep(transpose(chunk, members), pltpu.VMEM if group else pltpu.HBM)

time: 313 us -> 316 us (level)
  no operation moved by 1% of the time
where the time goes in v18:
time: 316 us; the launch traced here: 315 us
  waiting for transfers between devices  123 us (39%)
  blocking collectives  119 us (38%)
  Pallas kernels  51.6 us (16%)
  starting transfers between devices  19.8 us (6%)
    all_to_all x4, waiting for transfers between devices, transpose(): lax.all_to_all(value, AXES, split_axis=0, concat_axis=0, tiled=True, axis...  123 us
    all_to_all x2, blocking collectives, transpose(): lax.all_to_all(value, AXES, split_axis=0, concat_axis=0, tiled=True, axis...  119 us
    pallas_call x2, Pallas kernels, shear_pass(): pl.pallas_call(body, grid=(6,), in_specs=[pl.BlockSpec((1, count * half,...  28.5 us
    all_to_all x4, starting transfers between devices, transpose(): lax.all_to_all(value, AXES, split_axis=0, concat_axis=0, tiled=True, axis...  19.8 us
    pallas_call x2, Pallas kernels, spectrum_pass(): pl.pallas_call(body, grid_spec=pltpu.PrefetchScalarGridSpec(num_scalar_pr...  12.4 us
  transfers between devices with their start and end apart: 4, of which 4 were waited for; matrix products, arithmetic and copies ran while one was open for 0% of the time, Pallas kernels for 12%

profile of v18, /device:TPU:1, one launch (start us, length us, event | category | flops | bytes accessed | tf_op | source)
XLA Modules:
  0.0 314.6 jit_solution(1374648058869473622)
XLA Ops:
  0.6 5.0 %shard_map.203 = (f32[2,2,8,6,32,128]{5,4,3,2,1,0:T(8,128)S(1)}, f32[2,2,8,2,32,128]{5,4,3,2,1,0:T(8,128)}) custom-call(bf16[2,256,256]{2,1,0:T(8,128)(2,1)} %constant.64.clone.refs_0_, f32[32,64,256]{2,1,0:T(8,128)} %refs_1_.3), custom_call_target="tpu_custom_call" | custom-call | flops 805306368 | bytes 6291456 | tf_op jit(solution)/shard_map/pallas_call | solution.py:114
  5.6 77.3 %all_to_all.30 = f32[32,6,32,128]{3,2,1,0:T(8,128)} all-to-all(f32[32,6,32,128]{3,2,1,0:T(8,128)S(1)} %bitcast.12), channel_id=1, replica_groups=mesh['wide'=8,'narrow'=4] {'narrow','wide'}, dimensions={0} | all-to-all | bytes 6291456 | tf_op jit(solution)/shard_map/all_to_all | solution.py:611
  82.9 4.6 %all-to-all-start.1 = ((f32[32,2,32,128]{3,2,1,0:T(8,128)}), f32[32,2,32,128]{3,2,1,0:T(8,128)S(1)}, u32[]{:S(2)}, u32[]{:S(2)}) async-start(f32[32,2,32,128]{3,2,1,0:T(8,128)} %bitcast.5), calls=%async_computation.1 | async-start | bytes 2097152 | tf_op jit(solution)/shard_map/all_to_all | solution.py:611
  87.5 9.3 %shard_map.204 = (f32[16,12,32,128]{3,2,1,0:T(8,128)}, f32[16,12,32,128]{3,2,1,0:T(8,128)}, f32[3,2,128,1]{3,2,1,0:T(8,128)S(1)}, f32[2,1,256]{2,1,0:T(1,128)S(1...) custom-call(s32[1]{0:T(128)} %bitcast.1.refs_0_, ...), custom_call_target="tpu_custom_call" | custom-call | flops 4227858432 | bytes 15728640 | tf_op jit(solution)/shard_map/pallas_call | solution.py:308
  96.8 16.1 %all-to-all-done.1 = f32[32,2,32,128]{3,2,1,0:T(8,128)S(1)} async-done(((f32[32,2,32,128]{3,2,1,0:T(8,128)}), f32[32,2,32,128]{3,2,1,0:T(8,128)S(1)}, u32[]{:S(2)}, u32[]{:S(2)}) %all-to-all-start.1) | async-done | bytes 1048608 | tf_op jit(solution)/shard_map/all_to_all | solution.py:611
  112.8 3.2 %shard_map.205 = (f32[16,12,32,128]{3,2,1,0:T(8,128)}, f32[16,12,32,128]{3,2,1,0:T(8,128)}) custom-call(s32[1]{0:T(128)} %bitcast.1.refs_0_, s32[1]{0:T(128)} %bitcast.2.refs_1_, f32[3,2,128,1]{3,2,1,0:T(8,128)S(1)} %get-tuple-element.16.refs_2_, f32[2,1,256]{2,1,0:T(1,128)S(1)} %get-tuple-element.17.refs_3_, ...), custom_call_target="tpu_custom_call", output_to_operand_aliasing={{0}: (8, {}), {1}: (9, {})} | custom-call | flops 1409286144 | bytes 5242880 | tf_op jit(solution)/shard_map/pallas_call | solution.py:308
  116.0 41.6 %all_to_all.31.refs_6_ = f32[16,12,32,128]{3,2,1,0:T(8,128)S(1)} all-to-all(f32[16,12,32,128]{3,2,1,0:T(8,128)} %get-tuple-element.24), channel_id=1, replica_groups={{0,1,4,5,8,9,12,13,16,17,20,21,24,25,28,29},{2,3,6,7,10,11,14,15,18,19,..., dimensions={0} | all-to-all | bytes 6291456 | tf_op jit(solution)/shard_map/all_to_all | solution.py:611
  157.6 4.4 %all-to-all-start.3 = ((f32[16,12,32,128]{3,2,1,0:T(8,128)}), f32[16,12,32,128]{3,2,1,0:T(8,128)}, u32[]{:S(2)}, u32[]{:S(2)}) async-start(f32[16,12,32,128]{3,2,1,0:T(8,128)} %get-tuple-element.26), calls=%async_computation.3 | async-start | bytes 6291456 | tf_op jit(solution)/shard_map/all_to_all | solution.py:611
  162.0 14.3 %shard_map.206 = (f32[4,8,128,128]{3,2,1,0:T(8,128)}, bf16[2,2,2,256,256]{4,3,2,1,0:T(8,128)(2,1)S(1)}) custom-call(f32[6,512,1]{2,1,0:T(8,128)} %constant.75.clone.refs_0_, f32[6,1,512]{2,1,0:T(1,128)} %constant.71.clone.refs_1_, bf16[2,2,256,256]{3,2,1,0:T(8,128)(2,1)} %constant.68.clone.refs_5_.refs_2_, bf16[2,256,256]{2,1,0:T(8,128)(2,1)} %constant.76.clone.refs_3_, ...), custom_call_target="tpu_custom_call" | custom-call | flops 7247757312 | bytes 7340032 | tf_op jit(solution)/shard_map/pallas_call | solution.py:487
  176.3 0.0 copy-start
  176.3 1.0 copy-done
  177.3 24.2 %all-to-all-done.3.refs_6_ = f32[16,12,32,128]{3,2,1,0:T(8,128)} async-done(((f32[16,12,32,128]{3,2,1,0:T(8,128)}), f32[16,12,32,128]{3,2,1,0:T(8,128)}, u32[]{:S(2)}, u32[]{:S(2)}) %all-to-all-start.3) | async-done | bytes 3145760 | tf_op jit(solution)/shard_map/all_to_all | solution.py:611
  201.5 6.2 %all-to-all-start.5 = ((f32[32,128,128]{2,1,0:T(8,128)}), f32[32,128,128]{2,1,0:T(8,128)S(1)}, u32[]{:S(2)}, u32[]{:S(2)}) async-start(f32[32,128,128]{2,1,0:T(8,128)} %bitcast.16), calls=%async_computation.5 | async-start | bytes 4194304 | tf_op jit(solution)/shard_map/all_to_all | solution.py:611
  207.7 14.2 %shard_map.207 = f32[4,8,128,128]{3,2,1,0:T(8,128)} custom-call(f32[6,512,1]{2,1,0:T(8,128)} %constant.70.clone.refs_0_, f32[6,1,512]{2,1,0:T(1,128)} %constant.71.clone.refs_1_, bf16[2,2,256,256]{3,2,1,0:T(8,128)(2,1)} %constant.68.clone.refs_5_.refs_2_, bf16[2,256,256]{2,1,0:T(8,128)(2,1)} %constant.72.clone.refs_3_, ...), custom_call_target="tpu_custom_call" | custom-call | flops 7247757312 | bytes 7340032 | tf_op jit(solution)/shard_map/pallas_call | solution.py:487
  221.9 34.1 %all-to-all-done.5 = f32[32,128,128]{2,1,0:T(8,128)S(1)} async-done(((f32[32,128,128]{2,1,0:T(8,128)}), f32[32,128,128]{2,1,0:T(8,128)S(1)}, u32[]{:S(2)}, u32[]{:S(2)}) %all-to-all-start.5) | async-done | bytes 2097184 | tf_op jit(solution)/shard_map/all_to_all | solution.py:611
  256.0 0.0 copy-start.1
  256.0 4.6 %all-to-all-start.4 = ((f32[32,128,128]{2,1,0:T(8,128)}), f32[32,128,128]{2,1,0:T(8,128)}, u32[]{:S(2)}, u32[]{:S(2)}) async-start(f32[32,128,128]{2,1,0:T(8,128)} %bitcast.15), calls=%async_computation.4 | async-start | bytes 4194304 | tf_op jit(solution)/shard_map/all_to_all | solution.py:611
  260.6 48.3 %all-to-all-done.4 = f32[32,128,128]{2,1,0:T(8,128)} async-done(((f32[32,128,128]{2,1,0:T(8,128)}), f32[32,128,128]{2,1,0:T(8,128)}, u32[]{:S(2)}, u32[]{:S(2)}) %all-to-all-start.4) | async-done | bytes 2097184 | tf_op jit(solution)/shard_map/all_to_all | solution.py:611
  309.0 0.0 copy-done.1
  309.0 5.7 %shard_map.208 = (f32[64,32,256]{2,1,0:T(8,128)}, f32[64,32,256]{2,1,0:T(8,128)}) custom-call(s32[1]{0:T(128)} %bitcast.refs_0_, bf16[2,2,2,256,256]{4,3,2,1,0:T(8,128)(2,1)S(1)} %copy-done.1, f32[2,2,8,128,128]{4,3,2,1,0:T(8,128)} %bitcast.8.refs_2_, f32[2,2,8,128,128]{4,3,2,1,0:T(8,128)S(1)} %bitcast.13), custom_call_target="tpu_custom_call" | custom-call | flops 1610612736 | bytes 8388608 | tf_op jit(solution)/shard_map/pallas_call | solution.py:595
Async XLA Ops:
  82.9 29.9 %all-to-all-start.1 = ((f32[32,2,32,128]{3,2,1,0:T(8,128)}), f32[32,2,32,128]{3,2,1,0:T(8,128)S(1)}, u32[]{:S(2)}, u32[]{:S(2)}) async-start(f32[32,2,32,128]{3,2,1,0:T(8,128)} %bitcast.5), calls=%async_computation.1 | async-start | bytes 2097152 | tf_op jit(solution)/shard_map/all_to_all | solution.py:611
  157.6 43.8 %all-to-all-start.3 = ((f32[16,12,32,128]{3,2,1,0:T(8,128)}), f32[16,12,32,128]{3,2,1,0:T(8,128)}, u32[]{:S(2)}, u32[]{:S(2)}) async-start(f32[16,12,32,128]{3,2,1,0:T(8,128)} %get-tuple-element.26), calls=%async_computation.3 | async-start | bytes 6291456 | tf_op jit(solution)/shard_map/all_to_all | solution.py:611
  176.3 1.0 copy-start
  201.5 54.5 %all-to-all-start.5 = ((f32[32,128,128]{2,1,0:T(8,128)}), f32[32,128,128]{2,1,0:T(8,128)S(1)}, u32[]{:S(2)}, u32[]{:S(2)}) async-start(f32[32,128,128]{2,1,0:T(8,128)} %bitcast.16), calls=%async_computation.5 | async-start | bytes 4194304 | tf_op jit(solution)/shard_map/all_to_all | solution.py:611
  256.0 53.0 %copy-start.1 = (bf16[2,2,2,256,256]{4,3,2,1,0:T(8,128)(2,1)S(1)}, bf16[2,2,2,256,256]{4,3,2,1,0:T(8,128)(2,1)}, u32[]{:S(2)}) copy-start(bf16[2,2,2,256,256]{4,3,2,1,0:T(8,128)(2,1)} %copy-done) | copy-start | bytes 3145732
  256.0 53.0 %all-to-all-start.4 = ((f32[32,128,128]{2,1,0:T(8,128)}), f32[32,128,128]{2,1,0:T(8,128)}, u32[]{:S(2)}, u32[]{:S(2)}) async-start(f32[32,128,128]{2,1,0:T(8,128)} %bitcast.15), calls=%async_computation.4 | async-start | bytes 4194304 | tf_op jit(solution)/shard_map/all_to_all | solution.py:611

commit v19 on v16

--- a/solution.py
+++ b/solution.py
@@ -77,7 +77,7 @@
     half = length // 2
     flats = [ref.reshape(math.prod(ref.shape[:5]), 2 * rows_y) for ref in outs]
     table = pair(table_ref)
-    group = step_x
+    group = 4
     start_x = pl.program_id(0) * step_x
     for first in range(0, step_x, group):
         block = density_ref[first : first + group].reshape(group * rows_y, length)
@@ -284,7 +284,7 @@
     a_table = np.stack([wave, wave**2, scale]).astype(np.float32)[..., None]
     b_table = np.stack([wave**2, scale]).astype(np.float32).reshape(2, 1, length)
     message = PAIR * slab // groups
-    spaces = [pltpu.HBM] * groups
+    spaces = [pltpu.VMEM, pltpu.HBM][:groups]
     out_shape = (devices, 3 * 2 * length // TILE, steps * message, TILE)
     block = out_shape[:2] + (message, TILE)
 
@@ -336,7 +336,9 @@
 def shear_kernel(
     per_c, group, joined, row_ref, lane_ref, second_ref, third_ref, ahead_ref, last_ref, in_ref, *refs
 ):
-    out_ref, shear_ref = refs
+    shear_ref = refs[-1]
+    out_ref, carry_refs = refs[len(refs) // 2 - 1], refs[: len(refs) // 2 - 1]
+    hand_on(carry_refs, refs[len(refs) // 2 : -1])
     step = pl.program_id(0)
     length = shear_ref.shape[0]
     half = length // 2
@@ -434,7 +436,7 @@
                                 out[pl.ds(at, run), :] = piece
 
 
-def shear_pass(received, wide, narrow, per_c, group, joined):
+def shear_pass(received, wide, narrow, per_c, group, joined, carry):
     devices, tiles, message, tile = received.shape
     count = message // per_c
     length = tiles * tile // 6
@@ -490,28 +492,29 @@
             pl.BlockSpec((1, 1, 2 * length), lambda i: (i, 0, 0)),
             *[whole(table.shape) for table in tables],
             pl.BlockSpec((devices, tiles // 3, message, tile), which),
+            *[whole(each.shape) for each in carry],
         ],
-        out_specs=[whole(out_shape)],
-        out_shape=[pltpu.HBM(out_shape, jnp.float32)],
+        out_specs=[whole(out_shape)] + [whole(each.shape) for each in carry],
+        out_shape=[pltpu.HBM(out_shape, jnp.float32)]
+        + [pltpu.VMEM(each.shape, each.dtype) for each in carry],
         scratch_shapes=[pltpu.VMEM((length, count * length), jnp.float32)],
         compiler_params=params(1),
         cost_estimate=cost(count * 18 * length**3, 4 * received.size + 4 * 2**20),
     )(
         *[in_hbm(value) for value in (row_factor, lane_factor, *tables)],
         received,
-    )
-
-
-def first_kernel(count, rows_b, joined, pieces, anchor_ref, table_in, *refs):
+        *[in_hbm(each) for each in carry],
+    )
+
+
+def first_kernel(count, rows_b, joined, pieces, anchor_ref, table_ref, *refs):
     ins, (real_out, imag_out) = list(refs[:joined]), refs[joined : joined + 2]
-    table_ref, real_ref, imag_ref, first_ref, in_sems, out_sems = refs[joined + 2 :]
+    real_ref, imag_ref, first_ref, in_sems, out_sems = refs[joined + 2 :]
     wide, sides, ranks, rows, lanes = ins[-1].shape
     rows_c, _, length = real_ref.shape
     half = length // 2
     slots = lanes // rows_b
     steps = rows_c // (slots * joined) // pieces
-    table_copy = pltpu.make_async_copy(table_in, table_ref, in_sems.at[pieces])
-    table_copy.start()
     in_copies = []
     if joined == 2:
         for piece in range(pieces):
@@ -522,7 +525,6 @@
             copy.start()
             in_copies.append(copy)
         ins[0] = first_ref
-    table_copy.wait()
     spot_row = lax.broadcasted_iota(jnp.int32, (lanes, half), 0)
     spot_a = lax.broadcasted_iota(jnp.int32, (lanes, half), 1)
     anchor = (spot_row == 0) & (spot_a == 0) & (anchor_ref[0] == 1)
@@ -534,7 +536,7 @@
             own, other = [
                 ref[:, side, :, at].reshape(wide * ranks, 2 * count, lanes) for ref in ins
             ]
-            both = jnp.where(upper, own, other), pltpu.roll(jnp.where(upper, other, own), count, 1)
+            both = jnp.where(upper, own, other), jnp.where(upper, other, own)
             return [value.reshape(half, lanes).T for value in both]
         flat = ins[0].reshape(wide * sides * ranks * rows, lanes)
         run = rows // count
@@ -554,31 +556,35 @@
     for piece in range(pieces):
         if in_copies:
             in_copies[piece].wait()
-        sums = []
-        for side in range(sides):
-            tiles = [
-                [gathered(side, piece * steps + step, part) for part in range(2)] for step in range(steps)
+        tiles = [
+            [
+                [gathered(side, piece * steps + step, part) for part in range(2)]
+                for step in range(steps)
             ]
-            left = jnp.concatenate(
-                [
-                    jnp.concatenate([part[join] for part in parts], axis=1)
-                    for parts in tiles
-                    for join in range(joined)
-                ],
-                axis=0,
-            )
-            sums.append(product(split(left), pair(table_ref.at[side])))
-        even, odd = sums
+            for side in range(sides)
+        ]
         first = piece * steps * joined * slots
-        for far, value in enumerate((even + odd, even - odd)):
-            columns = slice(far * half, (far + 1) * half)
-            for at in range(steps * joined):
-                for part, ref in enumerate((real_ref, imag_ref)):
-                    here = value[at * lanes : (at + 1) * lanes, part * half : (part + 1) * half]
-                    if first + at == 0 and far == 0:
-                        here = jnp.where(anchor, 0.0, here)
-                    spots = slice(first + at * slots, first + (at + 1) * slots)
-                    ref[spots, :, columns] = here.reshape(slots, rows_b, half)
+        for join in range(joined):
+            sums = []
+            for side in range(sides):
+                left = jnp.concatenate(
+                    [
+                        jnp.concatenate([part[join] for part in parts], axis=1)
+                        for parts in tiles[side]
+                    ],
+                    axis=0,
+                )
+                sums.append(product(split(left), pair(table_ref.at[join, side])))
+            even, odd = sums
+            for far, value in enumerate((even + odd, even - odd)):
+                columns = slice(far * half, (far + 1) * half)
+                for step in range(steps):
+                    for part, ref in enumerate((real_ref, imag_ref)):
+                        here = value[step * lanes : (step + 1) * lanes, part * half : (part + 1) * half]
+                        at = first + (step * joined + join) * slots
+                        if at == 0 and far == 0:
+                            here = jnp.where(anchor, 0.0, here)
+                        ref[at : at + slots, :, columns] = here.reshape(slots, rows_b, half)
         at = pl.ds(first, steps * joined * slots)
         for part, (ref, out) in enumerate(((real_ref, real_out), (imag_ref, imag_out))):
             copy = pltpu.make_async_copy(ref.at[at], out.at[at], out_sems.at[2 * piece + part])
@@ -588,12 +594,16 @@
         copy.wait()
 
 
-def first_table(length, devices, sides):
+def first_table(length, devices, joined, count, sides):
     scale = 1.0 / float(length) ** 1.5
-    order = np.arange(length).reshape(devices, -1, sides).transpose(2, 0, 1).reshape(sides, -1)
-    return np.stack(
-        [split_table(scale * turn(-angles(np.arange(length // 2), x, length)).T) for x in order]
-    )
+    index = np.arange(length).reshape(devices, joined, count, sides)
+    tables = []
+    for join in range(joined):
+        order = index[:, :: 1 - 2 * join].transpose(3, 0, 1, 2).reshape(sides, -1)
+        tables.append(
+            [split_table(scale * turn(-angles(np.arange(length // 2), x, length)).T) for x in order]
+        )
+    return np.stack([np.stack(each) for each in tables])
 
 
 def first_pass(parts, table, is_anchor, length, wide, sides, count):
@@ -618,25 +628,24 @@
         grid=(1,),
         in_specs=[
             pl.BlockSpec(memory_space=pltpu.SMEM),
-            anywhere,
+            whole(table.shape),
             *[anywhere] * (joined - 1),
             whole(parts[-1].shape),
         ],
         out_specs=[anywhere] * 2,
         out_shape=[pltpu.HBM(out_shape, jnp.float32)] * 2,
         scratch_shapes=[
-            pltpu.VMEM(table.shape, table.dtype),
             pltpu.VMEM(out_shape, jnp.float32),
             pltpu.VMEM(out_shape, jnp.float32),
             pltpu.VMEM(first_shape, jnp.float32),
-            pltpu.SemaphoreType.DMA((pieces + 1,)),
+            pltpu.SemaphoreType.DMA((pieces,)),
             pltpu.SemaphoreType.DMA((2 * pieces,)),
         ],
         compiler_params=params(1),
         cost_estimate=cost(rows_c * 2 * rows_b * length * length, 16 * rows_c * rows_b * length),
     )(
         is_anchor,
-        in_hbm(table),
+        keep(table, pltpu.VMEM),
         *[in_hbm(part) for part in parts[:-1]],
         keep(parts[-1], pltpu.VMEM),
     )
@@ -681,12 +690,13 @@
             start += count
         is_anchor = ((spot_wide == 0) & (spot_narrow == 0)).astype(jnp.int32).reshape(1)
         parts = []
-        table = first_table(length, devices, sides)
+        table = first_table(length, devices, groups, slab // groups, sides)
         for group, chunk in enumerate(chunks):
+            carry = [table] if group == groups - 1 else []
             received = keep(transpose(chunk, members), pltpu.VMEM if group else pltpu.HBM)
-            (part,) = shear_pass(received, wide, narrow, per_c, group, groups)
+            part, *carry = shear_pass(received, wide, narrow, per_c, group, groups, carry)
             parts.append(transpose(part.reshape((wide * narrow,) + part.shape[2:])))
-        return tuple(first_pass(parts, table, is_anchor, length, wide, sides, slab // groups))
+        return tuple(first_pass(parts, *carry, is_anchor, length, wide, sides, slab // groups))
 
     return jax.shard_map(
         per_device,

time: 314 us -> 313 us (level)
  no operation moved by 1% of the time
where the time goes in v19:
time: 313 us; the launch traced here: 312 us
  waiting for transfers between devices  124 us (40%)
  blocking collectives  118 us (38%)
  Pallas kernels  51 us (16%)
  starting transfers between devices  17.3 us (6%)
    all_to_all x4, waiting for transfers between devices, transpose(): lax.all_to_all(value, AXES, split_axis=0, concat_axis=0, tiled=True, axis...  124 us
    all_to_all x2, blocking collectives, transpose(): lax.all_to_all(value, AXES, split_axis=0, concat_axis=0, tiled=True, axis...  118 us
    pallas_call x2, Pallas kernels, shear_pass(): pl.pallas_call(body, grid=(6,), in_specs=[pl.BlockSpec((1, count * half,...  28.5 us
    all_to_all x4, starting transfers between devices, transpose(): lax.all_to_all(value, AXES, split_axis=0, concat_axis=0, tiled=True, axis...  17.3 us
    pallas_call x2, Pallas kernels, spectrum_pass(): pl.pallas_call(body, grid_spec=pltpu.PrefetchScalarGridSpec(num_scalar_pr...  12.5 us
  transfers between devices with their start and end apart: 4, of which 4 were waited for; matrix products, arithmetic and copies ran while one was open for 0% of the time, Pallas kernels for 12%

profile of v19, /device:TPU:1, one launch (start us, length us, event | category | flops | bytes accessed | tf_op | source)
XLA Modules:
  0.0 312.1 jit_solution(1073632559739992956)
XLA Ops:
  0.6 5.0 %shard_map.203 = (f32[8,2,2,6,32,128]{5,4,3,2,1,0:T(8,128)S(1)}, f32[8,2,2,2,32,128]{5,4,3,2,1,0:T(8,128)}) custom-call(bf16[2,256,256]{2,1,0:T(8,128)(2,1)} %constant.64.clone.refs_0_, f32[32,64,256]{2,1,0:T(8,128)} %refs_1_.3), custom_call_target="tpu_custom_call" | custom-call | flops 805306368 | bytes 6291456 | tf_op jit(solution)/shard_map/pallas_call | solution.py:114
  5.6 78.3 %all_to_all.30 = f32[32,6,32,128]{3,2,1,0:T(8,128)} all-to-all(f32[32,6,32,128]{3,2,1,0:T(8,128)S(1)} %bitcast.12), channel_id=1, replica_groups=mesh['wide'=8,'narrow'=4] {'wide','narrow'}, dimensions={0} | all-to-all | bytes 6291456 | tf_op jit(solution)/shard_map/all_to_all | solution.py:655
  83.9 3.2 %all-to-all-start.1 = ((f32[32,2,32,128]{3,2,1,0:T(8,128)}), f32[32,2,32,128]{3,2,1,0:T(8,128)S(1)}, u32[]{:S(2)}, u32[]{:S(2)}) async-start(f32[32,2,32,128]{3,2,1,0:T(8,128)} %bitcast.5), calls=%async_computation.1 | async-start | bytes 2097152 | tf_op jit(solution)/shard_map/all_to_all | solution.py:655
  87.1 9.3 %shard_map.204 = (f32[16,12,32,128]{3,2,1,0:T(8,128)}, f32[16,12,32,128]{3,2,1,0:T(8,128)}, f32[3,2,128,1]{3,2,1,0:T(8,128)S(1)}, f32[2,1,256]{2,1,0:T(1,128)S(1...) custom-call(s32[1]{0:T(128)} %bitcast.1.refs_0_, ...), custom_call_target="tpu_custom_call" | custom-call | flops 4227858432 | bytes 15728640 | tf_op jit(solution)/shard_map/pallas_call | solution.py:308
  96.4 17.1 %all-to-all-done.1 = f32[32,2,32,128]{3,2,1,0:T(8,128)S(1)} async-done(((f32[32,2,32,128]{3,2,1,0:T(8,128)}), f32[32,2,32,128]{3,2,1,0:T(8,128)S(1)}, u32[]{:S(2)}, u32[]{:S(2)}) %all-to-all-start.1) | async-done | bytes 1048608 | tf_op jit(solution)/shard_map/all_to_all | solution.py:655
  113.4 3.2 %shard_map.205 = (f32[16,12,32,128]{3,2,1,0:T(8,128)}, f32[16,12,32,128]{3,2,1,0:T(8,128)}) custom-call(s32[1]{0:T(128)} %bitcast.1.refs_0_, s32[1]{0:T(128)} %bitcast.2.refs_1_, f32[3,2,128,1]{3,2,1,0:T(8,128)S(1)} %get-tuple-element.16.refs_2_, f32[2,1,256]{2,1,0:T(1,128)S(1)} %get-tuple-element.17.refs_3_, ...), custom_call_target="tpu_custom_call", output_to_operand_aliasing={{0}: (8, {}), {1}: (9, {})} | custom-call | flops 1409286144 | bytes 5242880 | tf_op jit(solution)/shard_map/pallas_call | solution.py:308
  116.6 40.1 %all_to_all.31.refs_6_ = f32[16,12,32,128]{3,2,1,0:T(8,128)S(1)} all-to-all(f32[16,12,32,128]{3,2,1,0:T(8,128)} %get-tuple-element.24), channel_id=1, replica_groups={{0,1,4,5,8,9,12,13,16,17,20,21,24,25,28,29},{2,3,6,7,10,11,14,15,18,19,..., dimensions={0} | all-to-all | bytes 6291456 | tf_op jit(solution)/shard_map/all_to_all | solution.py:655
  156.8 4.4 %all-to-all-start.3 = ((f32[16,12,32,128]{3,2,1,0:T(8,128)}), f32[16,12,32,128]{3,2,1,0:T(8,128)}, u32[]{:S(2)}, u32[]{:S(2)}) async-start(f32[16,12,32,128]{3,2,1,0:T(8,128)} %get-tuple-element.26), calls=%async_computation.3 | async-start | bytes 6291456 | tf_op jit(solution)/shard_map/all_to_all | solution.py:655
  161.1 14.3 %shard_map.206 = (f32[8,4,128,128]{3,2,1,0:T(8,128)}, bf16[2,2,2,256,256]{4,3,2,1,0:T(8,128)(2,1)S(1)}) custom-call(f32[6,512,1]{2,1,0:T(8,128)} %constant.75.clone.refs_0_, f32[6,1,512]{2,1,0:T(1,128)} %constant.71.clone.refs_1_, bf16[2,2,256,256]{3,2,1,0:T(8,128)(2,1)} %constant.68.clone.refs_5_.refs_2_, bf16[2,256,256]{2,1,0:T(8,128)(2,1)} %constant.76.clone.refs_3_, ...), custom_call_target="tpu_custom_call" | custom-call | flops 7247757312 | bytes 7340032 | tf_op jit(solution)/shard_map/pallas_call | solution.py:487
  175.4 0.0 copy-start
  175.4 1.0 copy-done
  176.4 24.2 %all-to-all-done.3.refs_6_ = f32[16,12,32,128]{3,2,1,0:T(8,128)} async-done(((f32[16,12,32,128]{3,2,1,0:T(8,128)}), f32[16,12,32,128]{3,2,1,0:T(8,128)}, u32[]{:S(2)}, u32[]{:S(2)}) %all-to-all-start.3) | async-done | bytes 3145760 | tf_op jit(solution)/shard_map/all_to_all | solution.py:655
  200.6 6.3 %all-to-all-start.5 = ((f32[32,128,128]{2,1,0:T(8,128)}), f32[32,128,128]{2,1,0:T(8,128)S(1)}, u32[]{:S(2)}, u32[]{:S(2)}) async-start(f32[32,128,128]{2,1,0:T(8,128)} %bitcast.16), calls=%async_computation.5 | async-start | bytes 4194304 | tf_op jit(solution)/shard_map/all_to_all | solution.py:655
  206.9 14.2 %shard_map.207 = f32[8,4,128,128]{3,2,1,0:T(8,128)} custom-call(f32[6,512,1]{2,1,0:T(8,128)} %constant.70.clone.refs_0_, f32[6,1,512]{2,1,0:T(1,128)} %constant.71.clone.refs_1_, bf16[2,2,256,256]{3,2,1,0:T(8,128)(2,1)} %constant.68.clone.refs_5_.refs_2_, bf16[2,256,256]{2,1,0:T(8,128)(2,1)} %constant.72.clone.refs_3_, ...), custom_call_target="tpu_custom_call" | custom-call | flops 7247757312 | bytes 7340032 | tf_op jit(solution)/shard_map/pallas_call | solution.py:487
  221.2 34.0 %all-to-all-done.5 = f32[32,128,128]{2,1,0:T(8,128)S(1)} async-done(((f32[32,128,128]{2,1,0:T(8,128)}), f32[32,128,128]{2,1,0:T(8,128)S(1)}, u32[]{:S(2)}, u32[]{:S(2)}) %all-to-all-start.5) | async-done | bytes 2097184 | tf_op jit(solution)/shard_map/all_to_all | solution.py:655
  255.2 0.0 copy-start.1
  255.2 3.5 %all-to-all-start.4 = ((f32[32,128,128]{2,1,0:T(8,128)}), f32[32,128,128]{2,1,0:T(8,128)}, u32[]{:S(2)}, u32[]{:S(2)}) async-start(f32[32,128,128]{2,1,0:T(8,128)} %bitcast.15), calls=%async_computation.4 | async-start | bytes 4194304 | tf_op jit(solution)/shard_map/all_to_all | solution.py:655
  258.7 48.3 %all-to-all-done.4 = f32[32,128,128]{2,1,0:T(8,128)} async-done(((f32[32,128,128]{2,1,0:T(8,128)}), f32[32,128,128]{2,1,0:T(8,128)}, u32[]{:S(2)}, u32[]{:S(2)}) %all-to-all-start.4) | async-done | bytes 2097184 | tf_op jit(solution)/shard_map/all_to_all | solution.py:655
  306.9 0.0 copy-done.1
  306.9 5.0 %shard_map.208 = (f32[64,32,256]{2,1,0:T(8,128)}, f32[64,32,256]{2,1,0:T(8,128)}) custom-call(s32[1]{0:T(128)} %bitcast.refs_0_, bf16[2,2,2,256,256]{4,3,2,1,0:T(8,128)(2,1)S(1)} %copy-done.1, f32[8,2,2,128,128]{4,3,2,1,0:T(8,128)} %bitcast.8.refs_2_, f32[8,2,2,128,128]{4,3,2,1,0:T(8,128)S(1)} %bitcast.13), custom_call_target="tpu_custom_call" | custom-call | flops 1610612736 | bytes 8388608 | tf_op jit(solution)/shard_map/pallas_call | solution.py:626
Async XLA Ops:
  83.9 29.5 %all-to-all-start.1 = ((f32[32,2,32,128]{3,2,1,0:T(8,128)}), f32[32,2,32,128]{3,2,1,0:T(8,128)S(1)}, u32[]{:S(2)}, u32[]{:S(2)}) async-start(f32[32,2,32,128]{3,2,1,0:T(8,128)} %bitcast.5), calls=%async_computation.1 | async-start | bytes 2097152 | tf_op jit(solution)/shard_map/all_to_all | solution.py:655
  156.8 43.8 %all-to-all-start.3 = ((f32[16,12,32,128]{3,2,1,0:T(8,128)}), f32[16,12,32,128]{3,2,1,0:T(8,128)}, u32[]{:S(2)}, u32[]{:S(2)}) async-start(f32[16,12,32,128]{3,2,1,0:T(8,128)} %get-tuple-element.26), calls=%async_computation.3 | async-start | bytes 6291456 | tf_op jit(solution)/shard_map/all_to_all | solution.py:655
  175.4 1.0 copy-start
  200.6 54.6 %all-to-all-start.5 = ((f32[32,128,128]{2,1,0:T(8,128)}), f32[32,128,128]{2,1,0:T(8,128)S(1)}, u32[]{:S(2)}, u32[]{:S(2)}) async-start(f32[32,128,128]{2,1,0:T(8,128)} %bitcast.16), calls=%async_computation.5 | async-start | bytes 4194304 | tf_op jit(solution)/shard_map/all_to_all | solution.py:655
  255.2 51.8 %copy-start.1 = (bf16[2,2,2,256,256]{4,3,2,1,0:T(8,128)(2,1)S(1)}, bf16[2,2,2,256,256]{4,3,2,1,0:T(8,128)(2,1)}, u32[]{:S(2)}) copy-start(bf16[2,2,2,256,256]{4,3,2,1,0:T(8,128)(2,1)} %copy-done) | copy-start | bytes 3145732
  255.2 51.8 %all-to-all-start.4 = ((f32[32,128,128]{2,1,0:T(8,128)}), f32[32,128,128]{2,1,0:T(8,128)}, u32[]{:S(2)}, u32[]{:S(2)}) async-start(f32[32,128,128]{2,1,0:T(8,128)} %bitcast.15), calls=%async_computation.4 | async-start | bytes 4194304 | tf_op jit(solution)/shard_map/all_to_all | solution.py:655
